TPU v7x, 32 devices: a whole 2x2x4 slice. The times are simulated.
32 devices in a mesh: events: 8 (over y, x, core), mp: 4 (over z).
Axes of the slice: x: 2, y: 2, z: 4, core: 2. Of those that a mesh axis runs over, the one named last changes fastest.
Arguments:
- event_x: bfloat16 [24576, 1024], P(('events', 'mp')), may hold values from -6 to 6
- event_visit: int32 [24576], P(('events', 'mp')), may hold values from -1 to 191, as said below
- visit_count: int32 [192], P(('events', 'mp')), may hold values from 1 to 128
- visit_patient: int32 [192], P('events'), may hold values from 0 to 191, as said below
- treatment: int32 [192], P('events'), may hold values 0 or 1
- outcome_target: float32 [192], P('events'), may hold values from -6 to 6
- enc_gain: float32 [1024], replicated, may hold values from 0.1 to 1.9
- enc_qkv: bfloat16 [1024, 3072], replicated, may hold values from -0.1875 to 0.1875
- enc_out: bfloat16 [1024, 1024], replicated, may hold values from -0.1875 to 0.1875
- visit_gain: float32 [2048], replicated, may hold values from 0.1 to 1.9
- visit_qkv: bfloat16 [3, 2048, 2048], P(None, 'events', 'mp'), may hold values from -0.125 to 0.125
- ffn_gain: float32 [2048], replicated, may hold values from 0.1 to 1.9
- ffn_in: bfloat16 [2048, 8192], P('events', 'mp'), may hold values from -0.125 to 0.125
- ffn_out: bfloat16 [8192, 2048], P('mp', 'events'), may hold values from -0.0625 to 0.0625
- head_weight: float32 [2048, 2], replicated, may hold values from -0.125 to 0.125
- head_bias: float32 [2], replicated, may hold values from -4 to 4
Outputs:
- outcomes: float32 [192, 2], P('events')
- event_grads: bfloat16 [24576, 1024], P(('events', 'mp'))
Inputs may be any that keep to these rules, and one draw needn't show every extreme that they name: `event_visit`: the visit of each event row, or -1 for an empty row. Visit v is owned by the device of index v // 6 along events+mp, whose mp index equals that of every device holding one of its events. One device holds at most 96 events of the visits owned by any one device, and some owner receives exactly 96 from every device of its mp index. Visit v has exactly visit_count[v] rows. `visit_patient`: A patient's visits are consecutive and owned by one device.
All inputs are finite; a program needn't handle non-finite values. No bound on the sum of `treatment` on one device may be relied on, other than what follows from the above.
Results may differ from a plain program's by a relative error of at most 0.025.
Values may be sent and summed in bfloat16 or wider, within the bound.
No kernel may reach another device: no remote copies, remote signals or barrier semaphores. Data moves between devices by JAX's collectives and lax.ppermute only.
A program may use at most 128 MiB of HBM per device.

v0:
```python
import jax
import jax.numpy as jnp
from jax import lax
from jax.sharding import PartitionSpec as P

D = 1024
HEADS = 16
HDIM = 64
VB = 128
VHDIM = 128


def rms_scale(values, gain):
    return values * lax.rsqrt(jnp.mean(values * values, axis=-1, keepdims=True) + 1e-05) * gain


def rms_back(grad_norm, values, gain):
    factor = lax.rsqrt(jnp.mean(values * values, axis=-1, keepdims=True) + 1e-05)
    scaled = grad_norm * gain
    return factor * (
        scaled - values * factor * factor * jnp.mean(scaled * values, axis=-1, keepdims=True)
    )


def rank_within(labels, labels_count):
    one_hot = (labels[:, None] == jnp.arange(labels_count, dtype=jnp.int32)[None, :]).astype(
        jnp.int32
    )
    before = jnp.cumsum(one_hot, axis=0) - one_hot
    return jnp.sum(before * one_hot, axis=1)


def encode_visits(blocks, counts, enc_gain, enc_qkv, enc_out):
    visits_dev = counts.shape[0]
    normed = rms_scale(blocks.astype(jnp.float32), enc_gain).astype(jnp.bfloat16)
    mixed_qkv = jnp.dot(normed, enc_qkv, preferred_element_type=jnp.float32).astype(jnp.bfloat16)
    queries = mixed_qkv[:, :D].reshape(visits_dev, VB, HEADS, HDIM)
    key_rows = mixed_qkv[:, D : 2 * D].reshape(visits_dev, VB, HEADS, HDIM)
    values = mixed_qkv[:, 2 * D :].reshape(visits_dev, VB, HEADS, HDIM)
    scores = jnp.einsum(
        "vqhd,vkhd->vhqk", queries, key_rows, preferred_element_type=jnp.float32
    ) * HDIM ** (-0.5)
    live_slots = jnp.arange(VB, dtype=jnp.int32)[None, :] < counts[:, None]
    scores = jnp.where(live_slots[:, None, None, :], scores, -1e30)
    attn_b16 = jax.nn.softmax(scores, axis=-1).astype(jnp.bfloat16)
    attended = jnp.einsum("vhqk,vkhd->vqhd", attn_b16, values, preferred_element_type=jnp.float32)
    attended = attended.astype(jnp.bfloat16).reshape(visits_dev * VB, D)
    hidden = blocks.astype(jnp.float32) + jnp.dot(
        attended, enc_out, preferred_element_type=jnp.float32
    )
    weights_live = live_slots.astype(jnp.float32)[:, :, None]
    denom = counts.astype(jnp.float32)[:, None]
    mean_hidden = jnp.sum(hidden.reshape(visits_dev, VB, D) * weights_live, axis=1) / denom
    mean_input = (
        jnp.sum(blocks.astype(jnp.float32).reshape(visits_dev, VB, D) * weights_live, axis=1)
        / denom
    )
    return jnp.concatenate([mean_hidden, mean_input], axis=1)


def local(
    event_x,
    event_visit,
    visit_count,
    visit_patient,
    treatment,
    outcome_target,
    enc_gain,
    enc_qkv,
    enc_out,
    visit_gain,
    visit_qkv,
    ffn_gain,
    ffn_in,
    ffn_out,
    head_weight,
    head_bias,
):
    senders = lax.axis_size("events")
    mp_size = lax.axis_size("mp")
    mp_index = lax.axis_index("mp")
    rows_dev = event_x.shape[0]
    cap_rows = rows_dev // senders
    visits_dev = visit_count.shape[0]
    group_rows = visits_dev * mp_size
    valid_src = event_visit >= 0
    owner_index = jnp.where(valid_src, event_visit // visits_dev // mp_size, senders)
    owner_rank = rank_within(owner_index, senders)
    send_pos = jnp.where(valid_src, owner_index * cap_rows + owner_rank, rows_dev)
    send_x = jnp.zeros((rows_dev, D), jnp.bfloat16).at[send_pos].set(event_x, mode="drop")
    send_ids = jnp.full((rows_dev,), -1, jnp.int32).at[send_pos].set(event_visit, mode="drop")
    got_x, got_ids = (
        lax.all_to_all(
            send_x.reshape(senders, cap_rows, D), "events", split_axis=0, concat_axis=0, tiled=True
        ),
        lax.all_to_all(
            send_ids.reshape(senders, cap_rows), "events", split_axis=0, concat_axis=0, tiled=True
        ),
    )
    got_x = got_x.reshape(rows_dev, D)
    got_ids = got_ids.reshape(rows_dev)
    valid_dst = got_ids >= 0
    local_visit = jnp.where(valid_dst, got_ids % visits_dev, visits_dev).astype(jnp.int32)
    slot_rank = rank_within(local_visit, visits_dev)
    slot_pos = jnp.where(valid_dst, local_visit * VB + slot_rank, visits_dev * VB)
    blocks = jnp.zeros((visits_dev * VB, D), jnp.bfloat16).at[slot_pos].set(got_x, mode="drop")
    qkv_full, in_full, out_full = (
        lax.all_gather(visit_qkv, "events", axis=1, tiled=True),
        lax.all_gather(ffn_in, "events", axis=0, tiled=True),
        lax.all_gather(ffn_out, "events", axis=1, tiled=True),
    )
    visit_vec = encode_visits(blocks, visit_count, enc_gain, enc_qkv, enc_out)
    all_vec = lax.all_gather(visit_vec.astype(jnp.bfloat16), "mp", axis=0, tiled=True).astype(
        visit_vec.dtype
    )
    normed = rms_scale(all_vec, visit_gain).astype(jnp.bfloat16)
    projected = jnp.einsum(
        "rd,tde->rte", normed, qkv_full, preferred_element_type=jnp.float32
    ).astype(jnp.bfloat16)
    head_cols = qkv_full.shape[2]
    local_heads = head_cols // VHDIM
    queries = projected[:, 0, :].reshape(group_rows, local_heads, VHDIM)
    key_rows = projected[:, 1, :].reshape(group_rows, local_heads, VHDIM)
    values = projected[:, 2, :].reshape(group_rows, local_heads, VHDIM)
    positions = jnp.arange(group_rows, dtype=jnp.int32)
    allowed = (visit_patient[:, None] == visit_patient[None, :]) & (
        positions[None, :] <= positions[:, None]
    )
    scores = jnp.einsum(
        "qhd,khd->hqk", queries, key_rows, preferred_element_type=jnp.float32
    ) * VHDIM ** (-0.5)
    attn_f32 = jax.nn.softmax(jnp.where(allowed[None], scores, -1e30), axis=-1)
    attn_b16 = attn_f32.astype(jnp.bfloat16)
    attended = jnp.einsum("hqk,khd->qhd", attn_b16, values, preferred_element_type=jnp.float32)
    attended = attended.astype(jnp.bfloat16).reshape(group_rows, head_cols)
    attn_all = lax.all_gather(attended, "mp", axis=1, tiled=True)
    middle = all_vec + attn_all.astype(jnp.float32)
    middle_in = rms_scale(middle, ffn_gain).astype(jnp.bfloat16)
    pre_act = jnp.dot(middle_in, in_full, preferred_element_type=jnp.float32)
    activated = jax.nn.silu(pre_act).astype(jnp.bfloat16)
    ffn_part = jnp.dot(activated, out_full, preferred_element_type=jnp.float32)
    partial_value = jnp.dot(ffn_part, head_weight, precision=lax.Precision.HIGHEST)
    outcomes = (
        lax.psum(partial_value, "mp")
        + jnp.dot(middle, head_weight, precision=lax.Precision.HIGHEST)
        + head_bias
    )
    picker = (jnp.arange(2, dtype=jnp.int32)[None, :] == treatment[:, None]).astype(jnp.float32)
    factual = jnp.sum(outcomes * picker, axis=1)
    grad_out = picker * (4096.0 * (factual - outcome_target))[:, None]
    grad_c = jnp.dot(grad_out, head_weight.T, precision=lax.Precision.HIGHEST)
    grad_cf = grad_c.astype(jnp.bfloat16)
    grad_act = lax.dot_general(
        grad_cf, out_full, (((1,), (1,)), ((), ())), preferred_element_type=jnp.float32
    )
    sigma = jax.nn.sigmoid(pre_act)
    grad_pre = (grad_act * sigma * (1.0 + pre_act * (1.0 - sigma))).astype(jnp.bfloat16)
    grad_min_part = lax.dot_general(
        grad_pre, in_full, (((1,), (1,)), ((), ())), preferred_element_type=jnp.float32
    )
    grad_min = lax.psum(grad_min_part.astype(jnp.bfloat16), "mp").astype(jnp.float32)
    grad_mid = grad_c + rms_back(grad_min, middle, ffn_gain)
    grad_cb = lax.dynamic_slice_in_dim(grad_mid, mp_index * head_cols, head_cols, 1).astype(
        jnp.bfloat16
    )
    grad_cb = grad_cb.reshape(group_rows, local_heads, VHDIM)
    grad_p = jnp.einsum("qhd,khd->hqk", grad_cb, values, preferred_element_type=jnp.float32)
    grad_s = (
        attn_f32 * (grad_p - jnp.sum(grad_p * attn_f32, axis=-1, keepdims=True)) * VHDIM ** (-0.5)
    )
    grad_s = grad_s.astype(jnp.bfloat16)
    grad_q = jnp.einsum(
        "hqk,khd->qhd", grad_s, key_rows, preferred_element_type=jnp.float32
    ).astype(jnp.bfloat16)
    grad_k = jnp.einsum("hqk,qhd->khd", grad_s, queries, preferred_element_type=jnp.float32).astype(
        jnp.bfloat16
    )
    grad_v = jnp.einsum(
        "hqk,qhd->khd", attn_b16, grad_cb, preferred_element_type=jnp.float32
    ).astype(jnp.bfloat16)
    grad_three = jnp.stack(
        [
            grad_q.reshape(group_rows, head_cols),
            grad_k.reshape(group_rows, head_cols),
            grad_v.reshape(group_rows, head_cols),
        ],
        axis=1,
    )
    grad_in = lax.psum_scatter(
        jnp.einsum("rte,tde->rd", grad_three, qkv_full, preferred_element_type=jnp.float32).astype(
            jnp.bfloat16
        ),
        "mp",
        scatter_dimension=0,
        tiled=True,
    ).astype(jnp.float32)
    own_grad_mid = lax.dynamic_slice_in_dim(grad_mid, mp_index * visits_dev, visits_dev, 0)
    grad_vec = own_grad_mid + rms_back(grad_in, visit_vec, visit_gain)
    visit_grad = (grad_vec[:, :D] / visit_count.astype(jnp.float32)[:, None]).astype(jnp.bfloat16)
    reply = visit_grad[jnp.minimum(local_visit, visits_dev - 1)]
    reply = jnp.where(valid_dst[:, None], reply, jnp.zeros_like(reply))
    returned = lax.all_to_all(
        reply.reshape(senders, cap_rows, D), "events", split_axis=0, concat_axis=0, tiled=True
    )
    fetched = returned.reshape(rows_dev, D)[jnp.minimum(send_pos, rows_dev - 1)]
    event_grads = jnp.where(valid_src[:, None], fetched, jnp.zeros_like(fetched))
    return (outcomes, event_grads)


def solution(mesh):
    in_specs = (
        P(("events", "mp"), None),
        P(("events", "mp")),
        P(("events", "mp")),
        P("events"),
        P("events"),
        P("events"),
        P(),
        P(),
        P(),
        P(),
        P(None, "events", "mp"),
        P(),
        P("events", "mp"),
        P("mp", "events"),
        P(),
        P(),
    )
    out_specs = (P("events", None), P(("events", "mp"), None))
    return jax.shard_map(local, mesh=mesh, in_specs=in_specs, out_specs=out_specs, check_vma=False)
```

profile of v0, /device:TPU:0, one launch (start us, length us, event | category | flops | bytes accessed | tf_op | source)
XLA Modules:
  0.0 318.5 jit_solution(8930193316807742808)
XLA Ops:
  7.3 0.7 all-gather.5.cloned.1.call-update
  8.0 0.7 all-gather.7.cloned.1.call-update
  8.7 0.7 all-gather.9.cloned.1.call-update
  9.4 0.7 fusion.102
  10.2 1.7 reduce-window.14
  11.9 0.1 copy.82
  12.1 0.2 reduce-window.15
  12.4 3.5 %scatter_custom_fusion = s32[768]{0:T(1024)S(1)} fusion(s32[768]{0:T(1024)S(1)} %get-tuple-element.18, s32[768]{0:T(1024)} %param.17, s32[]{:T(128)} %constant.35.clone.1), kind=kCustom, calls=%fused_computation.181 | custom fusion | bytes 3584 | tf_op jit(solution)/shard_map/scatter | solution.py:91
  16.0 0.7 all_to_all.12
  16.6 5.2 %all-to-all-start = ((s32[8,1,96]{2,1,0:T(1,128)}), s32[8,1,96]{2,1,0:T(1,128)S(1)}, u32[]{:S(2)}, u32[]{:S(2)}) async-start(s32[8,1,96]{2,1,0:T(1,128)} %all_to_all.12), calls=%async_computation | async-start | bytes 8192 | tf_op jit(solution)/shard_map/all_to_all | solution.py:96
  22.0 7.6 %scatter_custom_fusion.1 = bf16[768,1024]{1,0:T(8,128)(2,1)} fusion(s32[768]{0:T(1024)S(1)} %get-tuple-element.18, bf16[768,1024]{1,0:T(8,128)(2,1)} %param.16, bf16[]{:T(256)} %constant.34.clone.1), kind=kCustom, calls=%fused_computation.61 | custom fusion | bytes 1573376 | tf_op jit(solution)/shard_map/scatter | solution.py:90
  29.6 0.6 dynamic-slice.5
  30.9 4.3 %all-to-all-start.1 = ((bf16[8,96,1024]{2,1,0:T(8,128)(2,1)}), bf16[8,96,1024]{2,1,0:T(8,128)(2,1)}, u32[]{:S(2)}, u32[]{:S(2)}) async-start(bf16[8,96,1024]{2,1,0:T(8,128)(2,1)} %bitcast.115), calls=%async_computation.1 | async-start | bytes 3145728 | tf_op jit(solution)/shard_map/all_to_all | solution.py:93
  35.7 1.7 reduce-window.16
  37.4 0.2 slice_reduce_fusion
  37.7 0.2 reduce-window.19
  38.1 34.3 %all-to-all-done.1 = bf16[8,96,1024]{2,1,0:T(8,128)(2,1)} async-done(((bf16[8,96,1024]{2,1,0:T(8,128)(2,1)}), bf16[8,96,1024]{2,1,0:T(8,128)(2,1)}, u32[]{:S(2)}, u32[]{:S(2)}) %all-to-all-start.1) | async-done | bytes 1572896 | tf_op jit(solution)/shard_map/all_to_all | solution.py:93
  72.4 7.6 %scatter_custom_fusion.2 = bf16[768,1024]{1,0:T(8,128)(2,1)} fusion(s32[768]{0:T(1024)S(1)} %get-tuple-element.5, bf16[768,1024]{1,0:T(8,128)(2,1)} %bitcast.7, bf16[]{:T(256)} %constant.34.clone.1), kind=kCustom, calls=%fused_computation.59 | custom fusion | bytes 1573376 | tf_op jit(solution)/shard_map/scatter | solution.py:106
  80.0 1.8 multiply_reduce_fusion.2
  81.8 8.6 %convolution_convert_fusion = bf16[768,3072]{1,0:T(8,128)(2,1)S(1)} fusion(bf16[1024,3072]{1,0:T(8,128)(2,1)} %param.23, bf16[768,1024]{1,0:T(8,128)(2,1)} %scatter_custom_fusion.2, f32[1024]{0:T(1024)S(1)} %copy-done.12, f32[768]{0:T(1024)S(1)} %add_rsqrt_fusion), kind=kOutput, calls=%fused_computation.11 | convolution fusion | flops 4837343232 | bytes 12590080 | tf_op jit(solution)/shard_map/dot_general | solution.py:36
  90.4 2.2 fusion.129
  92.7 5.3 %reshape.379 = bf16[6,128,16,64]{3,2,1,0:T(8,128)(2,1)} reshape(bf16[768,1024]{1,0:T(8,128)(2,1)} %get-tuple-element.12) | data formatting | bytes 3145728 | tf_op jit(solution)/shard_map/reshape | solution.py:37
  97.9 5.3 %reshape.380 = bf16[6,128,16,64]{3,2,1,0:T(8,128)(2,1)} reshape(bf16[768,1024]{1,0:T(8,128)(2,1)} %get-tuple-element.11) | data formatting | bytes 3145728 | tf_op jit(solution)/shard_map/reshape | solution.py:38
  103.2 5.3 %reshape.378 = bf16[6,128,16,64]{3,2,1,0:T(8,128)(2,1)} reshape(bf16[768,1024]{1,0:T(8,128)(2,1)} %get-tuple-element.10) | data formatting | bytes 3145728 | tf_op jit(solution)/shard_map/reshape | solution.py:39
  108.5 5.2 %fusion.5 = f32[6,16,128,128]{2,3,1,0:T(8,128)S(1)} fusion(bf16[6,128,16,64]{3,2,1,0:T(8,128)(2,1)} %reshape.380, bf16[6,128,16,64]{3,2,1,0:T(8,128)(2,1)} %reshape.379), kind=kOutput, calls=%fused_computation.13 | convolution fusion | flops 201326592 | bytes 9437184 | tf_op jit(solution)/shard_map/vqhd,vkhd->vhqk/dot_general | solution.py:40
  113.7 2.5 fusion.131
  116.2 1.1 fusion.23
  117.3 1.3 copy.92
  118.7 1.9 convert_add_fusion
  120.6 0.9 multiply_reduce_fusion.1
  121.6 14.0 %all-gather = bf16[4,6,2048]{2,1,0:T(8,128)(2,1)S(1)} all-gather(bf16[1,6,2048]{2,1,0:T(8,128)(2,1)S(1)} %fusion.67), channel_id=1, replica_groups=mesh['events'=8,'mp'=4] {'mp'}, dimensions={0}, use_global_device_ids=true | all-gather | bytes 122880 | tf_op jit(solution)/shard_map/all_gather | solution.py:113
  135.9 3.8 %convolution_convert_fusion.2 = bf16[24,3,512]{2,0,1:T(8,128)(2,1)S(1)} fusion(bf16[3,2048,512]{2,1,0:T(8,128)(2,1)} %all-gather.5.cloned.1.call-done, f32[24,2048]{1,0:T(8,128)S(1)} %reshape.375, f32[2048]{0:T(1024)S(1)} %copy-done.6, f32[24]{0:T(128)S(1)} %add_rsqrt_fusion.3), kind=kOutput, calls=%fused_computation.40 | convolution fusion | flops 151179264 | bytes 6570080 | tf_op jit(solution)/shard_map/rd,tde->rte/dot_general | solution.py:117
  139.7 0.1 fusion.31
  139.8 0.1 fusion.132
  140.0 0.2 fusion.33
  140.2 13.2 %all_gather.17 = bf16[24,2048]{1,0:T(8,128)(2,1)S(1)} all-gather(bf16[24,512]{1,0:T(8,128)(2,1)S(1)} %bitcast.117), channel_id=1, replica_groups=mesh['events'=8,'mp'=4] {'mp'}, dimensions={1}, use_global_device_ids=true | all-gather | bytes 122880 | tf_op jit(solution)/shard_map/all_gather | solution.py:136
  153.4 0.1 multiply_reduce_fusion.4
  153.6 4.6 %fusion.48 = f32[24,2048]{1,0:T(8,128)S(1)} fusion(bf16[2048,2048]{1,0:T(8,128)(2,1)} %all-gather.7.cloned.1.call-done, f32[2048]{0:T(1024)S(1)} %copy-done.5, f32[24]{0:T(128)S(1)} %add_rsqrt_fusion.2, f32[24,2048]{1,0:T(8,128)S(1)} %reshape.375, bf16[24,2048]{1,0:T(8,128)(2,1)S(1)} %all_gather.17), kind=kOutput, calls=%fused_computation.78 | convolution fusion | flops 201572352 | bytes 8888416 | tf_op jit(solution)/shard_map/dot_general | solution.py:139
  158.3 30.1 %all-gather.9.cloned.1.call-done = bf16[2048,2048]{1,0:T(8,128)(2,1)} async-done(((bf16[2048,256]{1,0:T(8,128)(2,1)}), bf16[2048,2048]{1,0:T(8,128)(2,1)}) %all-gather.9.cloned.1.call-update) | async-done | bytes 8388624 | tf_op jit(solution)/shard_map/all_gather | solution.py:110
  188.4 4.6 %fusion.45 = f32[24,2048]{1,0:T(8,128)S(1)} fusion(bf16[2048,2048]{1,0:T(8,128)(2,1)} %all-gather.9.cloned.1.call-done, f32[24,2048]{1,0:T(8,128)S(1)} %fusion.48), kind=kOutput, calls=%fused_computation.76 | convolution fusion | flops 201572352 | bytes 8781824 | tf_op jit(solution)/shard_map/dot_general | solution.py:141
  192.9 0.2 fusion.133
  193.2 11.7 %psum.14 = f32[24,2]{0,1:T(2,128)S(1)} all-reduce(f32[24,2]{0,1:T(2,128)S(1)} %fusion.133), channel_id=1, replica_groups=mesh['events'=8,'mp'=4] {'mp'}, use_global_device_ids=true, to_apply=%region_18.19 | all-reduce | flops 48 | bytes 384 | tf_op jit(solution)/shard_map/psum | solution.py:144
  204.9 0.9 select_reduce_fusion
  205.8 0.4 fusion.112
  206.2 10.9 %convolution_convert_fusion.1 = bf16[24,2048]{1,0:T(8,128)(2,1)} fusion(bf16[2048,2048]{1,0:T(8,128)(2,1)} %all-gather.7.cloned.1.call-done, bf16[2048,2048]{1,0:T(8,128)(2,1)} %all-gather.9.cloned.1.call-done, f32[24,2048]{1,0:T(8,128)S(1)} %fusion.48, f32[24,2048]{1,0:T(8,128)S(1)} %fusion.112), kind=kOutput, calls=%fused_computation.31 | convolution fusion | flops 403193856 | bytes 17268736 | tf_op jit(solution)/shard_map/dot_general | solution.py:158
  217.1 31.7 %all-reduce.4.cloned.1.call-done = bf16[24,2048]{1,0:T(8,128)(2,1)} async-done(((bf16[24,2048]{1,0:T(8,128)(2,1)}), bf16[24,2048]{1,0:T(8,128)(2,1)}) %all-reduce.4.cloned.1.call-update) | async-done | bytes 98320 | tf_op jit(solution)/shard_map/psum | solution.py:161
  248.8 1.0 multiply_reduce_fusion.3
  249.8 1.0 multiply_add_fusion
  250.8 0.1 fusion.82
  251.0 0.2 fusion.34
  251.2 0.1 fusion.35
  251.4 0.1 fusion.36
  251.6 4.5 %fusion.14 = bf16[24,2048]{1,0:T(8,128)(2,1)S(1)} fusion(bf16[3,2048,512]{2,1,0:T(8,128)(2,1)} %all-gather.5.cloned.1.call-done, bf16[24,1,512]{2,0,1:T(8,128)(2,1)S(1)} %stack_reshape.11, bf16[24,1,512]{2,0,1:T(8,128)(2,1)S(1)} %stack_reshape.10, bf16[24,1,512]{2,0,1:T(8,128)(2,1)S(1)} %stack_reshape.9), kind=kOutput, calls=%fused_computation.29 | convolution fusion | flops 151117824 | bytes 6463488 | tf_op jit(solution)/shard_map/rte,tde->rd/dot_general | solution.py:190
  256.1 13.7 %fusion = bf16[8,2048]{1,0:T(8,128)(2,1)S(1)} fusion(bf16[24,2048]{1,0:T(8,128)(2,1)S(1)} %fusion.14), kind=kCustom, calls=%all-reduce-scatter | all-reduce-scatter fusion | flops 65537 | bytes 131584
  269.8 1.6 collective-permute-start
  271.5 1.6 collective-permute-done
  273.0 0.1 concatenate.4
  273.2 0.2 multiply_reduce_fusion.8
  273.4 2.8 gather_fusion
  276.3 1.3 broadcast_select_fusion.1
  277.6 4.3 %all-to-all-start.2 = ((bf16[8,96,1024]{2,1,0:T(8,128)(2,1)}), bf16[8,96,1024]{2,1,0:T(8,128)(2,1)}, u32[]{:S(2)}, u32[]{:S(2)}) async-start(bf16[8,96,1024]{2,1,0:T(8,128)(2,1)} %broadcast_select_fusion.1), calls=%async_computation.2 | async-start | bytes 3145728 | tf_op jit(solution)/shard_map/all_to_all | solution.py:202
  281.9 21.0 %all-to-all-done.2 = bf16[8,96,1024]{2,1,0:T(8,128)(2,1)} async-done(((bf16[8,96,1024]{2,1,0:T(8,128)(2,1)}), bf16[8,96,1024]{2,1,0:T(8,128)(2,1)}, u32[]{:S(2)}, u32[]{:S(2)}) %all-to-all-start.2) | async-done | bytes 1572896 | tf_op jit(solution)/shard_map/all_to_all | solution.py:202
  302.9 6.3 %gather_fusion.1 = bf16[768,1024]{1,0:T(8,128)(2,1)} fusion(bf16[768,1024]{1,0:T(8,128)(2,1)} %bitcast.20, s32[1024]{0:T(1024)S(1)} %pad_clamp_fusion), kind=kCustom, calls=%fused_computation.1 | custom fusion | bytes 3148800 | tf_op jit(solution)/shard_map/gather | solution.py:205
  309.2 2.7 broadcast_select_fusion
  (84 shorter events, 2.0 us)
Async XLA Ops:
  7.2 111.5 %copy-start = (bf16[1024,1024]{1,0:T(8,128)(2,1)S(1)}, bf16[1024,1024]{1,0:T(8,128)(2,1)}, u32[]{:S(2)}) copy-start(bf16[1024,1024]{1,0:T(8,128)(2,1)} %param.24) | copy-start | bytes 6291460
  7.2 22.4 %copy-start.10 = (u32[32]{0:T(128)S(1)}, u32[32]{0:T(128)}, u32[]{:S(2)}) copy-start(u32[32]{0:T(128)} %constant.106) | copy-start | bytes 388
  7.2 14.6 %copy-start.11 = (s32[6]{0:T(128)S(1)}, s32[6]{0:T(128)}, u32[]{:S(2)}) copy-start(s32[6]{0:T(128)} %param.18) | copy-start | bytes 76
  7.2 14.7 %copy-start.8 = (s32[24]{0:T(128)S(1)}, s32[24]{0:T(128)}, u32[]{:S(2)}) copy-start(s32[24]{0:T(128)} %param.19) | copy-start | bytes 292
  7.2 128.6 %all-gather.5.cloned.1.call-start = ((), (), s32[]{:S(2)}) async-start(), calls=%async_computation.3 | async-start | bytes 7077888 | tf_op jit(solution)/shard_map/all_gather | solution.py:108
  7.9 145.7 %all-gather.7.cloned.1.call-start = ((), (), s32[]{:S(2)}) async-start(), calls=%async_computation.4 | async-start | bytes 9437184 | tf_op jit(solution)/shard_map/all_gather | solution.py:109
  8.7 179.7 %all-gather.9.cloned.1.call-start = ((), (), s32[]{:S(2)}) async-start(), calls=%async_computation.5 | async-start | bytes 9437184 | tf_op jit(solution)/shard_map/all_gather | solution.py:110
  16.6 14.2 %all-to-all-start = ((s32[8,1,96]{2,1,0:T(1,128)}), s32[8,1,96]{2,1,0:T(1,128)S(1)}, u32[]{:S(2)}, u32[]{:S(2)}) async-start(s32[8,1,96]{2,1,0:T(1,128)} %all_to_all.12), calls=%async_computation | async-start | bytes 8192 | tf_op jit(solution)/shard_map/all_to_all | solution.py:96
  30.9 50.9 %copy-start.12 = (f32[1024]{0:T(1024)S(1)}, f32[1024]{0:T(1024)}, u32[]{:S(2)}) copy-start(f32[1024]{0:T(1024)} %param.22) | copy-start | bytes 12292
  30.9 41.5 %all-to-all-start.1 = ((bf16[8,96,1024]{2,1,0:T(8,128)(2,1)}), bf16[8,96,1024]{2,1,0:T(8,128)(2,1)}, u32[]{:S(2)}, u32[]{:S(2)}) async-start(bf16[8,96,1024]{2,1,0:T(8,128)(2,1)} %bitcast.115), calls=%async_computation.1 | async-start | bytes 3145728 | tf_op jit(solution)/shard_map/all_to_all | solution.py:93
  35.2 213.6 %all-reduce.4.cloned.1.call-start = ((), (), s32[]{:S(2)}) async-start(), calls=%async_computation.6 | async-start | bytes 196608 | tf_op jit(solution)/shard_map/psum | solution.py:161
  113.7 2.5 copy-start.3
  117.3 1.4 copy-start.2
  120.6 15.2 %copy-start.6 = (f32[2048]{0:T(1024)S(1)}, f32[2048]{0:T(1024)}, u32[]{:S(2)}) copy-start(f32[2048]{0:T(1024)} %param.25) | copy-start | bytes 24580
  135.8 17.8 %copy-start.5 = (f32[2048]{0:T(1024)S(1)}, f32[2048]{0:T(1024)}, u32[]{:S(2)}) copy-start(f32[2048]{0:T(1024)} %param.27) | copy-start | bytes 24580
  158.3 34.7 %copy-start.4 = (f32[2048,2]{0,1:T(2,128)S(1)}, f32[2048,2]{0,1:T(2,128)}, u32[]{:S(2)}) copy-start(f32[2048,2]{0,1:T(2,128)} %param.30) | copy-start | bytes 49156
  158.3 46.7 %copy-start.7 = (s32[24]{0:T(128)S(1)}, s32[24]{0:T(128)}, u32[]{:S(2)}) copy-start(s32[24]{0:T(128)} %param.20) | copy-start | bytes 292
  158.3 46.6 %copy-start.9 = (f32[2]{0:T(128)S(1)}, f32[2]{0:T(128)}, u32[]{:S(2)}) copy-start(f32[2]{0:T(128)} %param.31) | copy-start | bytes 28
  158.3 47.5 %copy-start.13 = (f32[24]{0:T(128)S(1)}, f32[24]{0:T(128)}, u32[]{:S(2)}) copy-start(f32[24]{0:T(128)} %param.21) | copy-start | bytes 292
  269.8 3.2 %collective-permute-start = (bf16[6,2048]{1,0:T(8,128)(2,1)S(1)}, bf16[6,2048]{1,0:T(8,128)(2,1)S(1)}, u32[]{:S(2)}, u32[]{:S(2)}) collective-permute-start(bf16[6,2048]{1,0:T(8,128)(2,1)S(1)} %slice.59), channel_id=1, source_target_pairs={{0,1},{1,2},{2,3},{4,5},{5,6},{6,7},{8,9},{9,10},{10,11},{12,13},{... | collective-permute-start | bytes 73736
  277.6 25.3 %all-to-all-start.2 = ((bf16[8,96,1024]{2,1,0:T(8,128)(2,1)}), bf16[8,96,1024]{2,1,0:T(8,128)(2,1)}, u32[]{:S(2)}, u32[]{:S(2)}) async-start(bf16[8,96,1024]{2,1,0:T(8,128)(2,1)} %broadcast_select_fusion.1), calls=%async_computation.2 | async-start | bytes 3145728 | tf_op jit(solution)/shard_map/all_to_all | solution.py:202
  302.9 9.0 %copy-start.1 = (bf16[1024,1024]{1,0:T(8,128)(2,1)S(1)}, bf16[1024,1024]{1,0:T(8,128)(2,1)}, u32[]{:S(2)}) copy-start(bf16[1024,1024]{1,0:T(8,128)(2,1)} %param.24) | copy-start | bytes 6291460
Sparse Core Ops, SparseCore 0:
  10.0 63.7 all-gather.4
  75.7 54.7 all-gather.6
  132.4 55.9 all-gather.8
  217.2 31.4 all-reduce.3
where the time goes:
time: 320 us; the launch traced here: 318 us
  waiting for transfers between devices  121 us (38%)
  blocking collectives  52.6 us (16%)
  local copies, waits for them, and re-layouts  50.1 us (16%)
  matrix products  47.6 us (15%)
  other arithmetic  17 us (5%)
  starting transfers between devices  15.5 us (5%)
  between operations  14.9 us (5%)
    all_to_all x1, waiting for transfers between devices, local(): lax.all_to_all(send_x.reshape(senders, cap_rows, D), 'events', split_axis...  34.3 us
    psum x1, waiting for transfers between devices, local(): lax.psum(grad_min_part.astype(jnp.bfloat16), 'mp').astype(jnp.float32)  31.7 us
    all_gather x1, waiting for transfers between devices, local(): lax.all_gather(ffn_out, 'events', axis=1, tiled=True)  30.1 us
    all_to_all x1, waiting for transfers between devices, local(): lax.all_to_all(reply.reshape(senders, cap_rows, D), 'events', split_axis=...  21 us
    all_gather x1, blocking collectives, local(): lax.all_gather(visit_vec.astype(jnp.bfloat16), 'mp', axis=0, tiled=True)  14 us
    unnamed x1, blocking collectives  13.7 us
    all_gather x1, blocking collectives, local(): attn_all = lax.all_gather(attended, 'mp', axis=1, tiled=True)  13.2 us
    psum x1, blocking collectives, local(): lax.psum(partial_value, 'mp')  11.7 us
  transfers between devices with their start and end apart: 8, of which 5 were waited for; matrix products, arithmetic and copies ran while one was open for 24% of the time, Pallas kernels for 0%

commit v1 on v0

v1 whole, which is shorter than its diff:
```python
import functools

import jax
import jax.numpy as jnp
from jax import lax
from jax.experimental import pallas as pl
from jax.experimental.pallas import tpu as pltpu
from jax.sharding import PartitionSpec as P

D = 1024
HEADS = 16
HDIM = 64
VB = 128
DV = 2048
VHDIM = 128
VPAD = 8
LANES = 128
EPS = 1e-5
F32 = jnp.float32
BF16 = jnp.bfloat16
VMEM_LIMIT = 48 * 1024 * 1024

NT = (((1,), (1,)), ((), ()))
TN = (((0,), (0,)), ((), ()))
NN = (((1,), (0,)), ((), ()))


def dot(a, b, dims=NN):
    return lax.dot_general(a, b, dims, preferred_element_type=F32)


def vmem():
    return pl.BlockSpec(memory_space=pltpu.VMEM)


def smem():
    return pl.BlockSpec(memory_space=pltpu.SMEM)


def hbm():
    return pl.BlockSpec(memory_space=pl.ANY)


def params():
    return pltpu.CompilerParams(vmem_limit_bytes=VMEM_LIMIT)


def strict_upper(rows):
    a = lax.broadcasted_iota(jnp.int32, (rows, rows), 0)
    b = lax.broadcasted_iota(jnp.int32, (rows, rows), 1)
    return (a < b).astype(BF16)


def pick_rows(position, first, count, rows):
    slots = lax.broadcasted_iota(jnp.int32, (count, rows), 0) + first
    return (slots == position).astype(BF16)


def pack_kernel(senders, per_owner, visits_dev, where_ref, ids_ref, x_ref, out_ref):
    rows = x_ref.shape[0]
    cap_rows = rows // senders
    ids = ids_ref[...]
    owners = lax.broadcasted_iota(jnp.int32, (senders, rows), 0)
    hot = (ids >= owners * per_owner) & (ids < (owners + 1) * per_owner)
    hot_f = hot.astype(F32)
    before = dot(hot.astype(BF16), strict_upper(rows))
    base = (owners * cap_rows + 1).astype(F32)
    position = (jnp.sum(hot_f * (base + before), axis=0, keepdims=True)).astype(jnp.int32) - 1
    first = (owners * per_owner + where_ref[1] * visits_dev).astype(F32)
    label = jnp.sum(hot_f * (ids.astype(F32) - first + 1.0), axis=0, keepdims=True)
    label = jnp.broadcast_to(label, (LANES, rows)).astype(BF16)
    step = rows // 3
    for c in range(3):
        chosen = pick_rows(position, c * step, step, rows)
        out_ref[c * step : (c + 1) * step, :D] = dot(chosen, x_ref[...]).astype(BF16)
        out_ref[c * step : (c + 1) * step, D:] = dot(chosen, label, NT).astype(BF16)


def encode_kernel(
    visits_dev,
    count_ref,
    got_ref,
    gain_ref,
    qkv_ref,
    proj_ref,
    vec_ref,
    wqk,
    wv,
    wo,
    normed,
    qk,
    pbar,
    ctx,
    sems,
):
    rows = got_ref.shape[0]
    slots = visits_dev * VB
    copies = [
        pltpu.make_async_copy(qkv_ref.at[:, : 2 * D], wqk, sems.at[0]),
        pltpu.make_async_copy(qkv_ref.at[:, 2 * D :], wv, sems.at[1]),
        pltpu.make_async_copy(proj_ref, wo, sems.at[2]),
    ]
    for copy in copies:
        copy.start()
    lane0 = (lax.broadcasted_iota(jnp.int32, (VPAD, LANES), 1) == 0).astype(BF16)
    label = dot(lane0, got_ref[:, D:], NT)[:1]
    visits = lax.broadcasted_iota(jnp.int32, (VPAD, rows), 0)
    hot = label == (visits + 1).astype(F32)
    hot_b = hot.astype(BF16)
    hot_f = hot.astype(F32)
    before = dot(hot_b, strict_upper(rows))
    base = (visits * VB + 1).astype(F32)
    position = (jnp.sum(hot_f * (base + before), axis=0, keepdims=True)).astype(jnp.int32) - 1
    sums = dot(hot_b, got_ref[:, :D])
    gain = gain_ref[...]
    step = 2 * VB
    for c in range(slots // step):
        part = dot(pick_rows(position, c * step, step, rows), got_ref[:, :D])
        scale = lax.rsqrt(jnp.mean(part * part, axis=-1, keepdims=True) + EPS)
        normed[c * step : (c + 1) * step, :] = (part * scale * gain).astype(BF16)
    copies[0].wait()
    wide = 512
    for c in range(2 * D // wide):
        cols = slice(c * wide, (c + 1) * wide)
        qk[:, cols] = dot(normed[...], wqk[:, cols]).astype(BF16)

    lanes = lax.broadcasted_iota(jnp.int32, (VB, LANES), 1)
    low = (lanes < HDIM).astype(F32) * HDIM ** (-0.5)
    high = (lanes >= HDIM).astype(F32) * HDIM ** (-0.5)
    key_slot = lax.broadcasted_iota(jnp.int32, (VB, 2 * VB), 0)
    query_lane = lax.broadcasted_iota(jnp.int32, (1, 2 * VB), 1)
    query_slot = jnp.where(query_lane >= VB, query_lane - VB, query_lane)
    rows8 = lax.broadcasted_iota(jnp.int32, (VPAD, 2 * VB), 0)
    lanes8 = lax.broadcasted_iota(jnp.int32, (VPAD, 2 * VB), 1)
    halves = ((lanes8 >= rows8 * VB) & (lanes8 < (rows8 + 1) * VB)).astype(BF16)

    def one_visit(v, carry):
        count = count_ref[v]
        at = pl.ds(pl.multiple_of(v * VB, VB), VB)
        live_key = key_slot < count
        weight = (query_slot < count).astype(F32) / count.astype(F32)
        for p in range(HEADS // 2):
            q = qk[at, p * LANES : (p + 1) * LANES].astype(F32)
            k = qk[at, D + p * LANES : D + (p + 1) * LANES]
            both = jnp.concatenate([(q * low).astype(BF16), (q * high).astype(BF16)], axis=0)
            scores = jnp.where(live_key, dot(k, both, NT), -1e30)
            top = jnp.max(scores, axis=0, keepdims=True)
            grown = jnp.exp(scores - top)
            total = jnp.sum(grown, axis=0, keepdims=True)
            shares = (grown * (weight / total)).astype(BF16)
            pbar[v, 2 * p : 2 * p + 2, :] = dot(halves, shares, NT)[:2]
        ctx[v] = dot(pbar[v].astype(BF16), normed[at, :]).astype(BF16)
        return carry

    lax.fori_loop(0, visits_dev, one_visit, 0)
    copies[1].wait()
    copies[2].wait()
    vals = dot(ctx[...].reshape(visits_dev * HEADS, D), wv[...]).reshape(visits_dev, HEADS, D)
    head_row = lax.broadcasted_iota(jnp.int32, (1, HEADS, D), 1) * HDIM
    col = lax.broadcasted_iota(jnp.int32, (1, HEADS, D), 2)
    own = (col >= head_row) & (col < head_row + HDIM)
    attended = jnp.sum(jnp.where(own, vals, 0.0), axis=1)
    attended = jnp.concatenate([attended, jnp.zeros((VPAD - visits_dev, D), F32)], axis=0)
    head_part = attended.astype(BF16)
    rest = (attended - head_part.astype(F32)).astype(BF16)
    mixed = dot(head_part, wo[...]) + dot(rest, wo[...])
    row = lax.broadcasted_iota(jnp.int32, (VPAD, 1), 0)
    inverse = jnp.zeros((VPAD, 1), F32)
    for v in range(visits_dev):
        inverse = jnp.where(row == v, 1.0 / count_ref[v].astype(F32), inverse)
    mean_input = sums * inverse
    vec_ref[:, :D] = (mean_input + mixed).astype(BF16)
    vec_ref[:, D:] = mean_input.astype(BF16)


def rms_factor(values):
    return lax.rsqrt(jnp.mean(values * values, axis=-1, keepdims=True) + EPS)


def fetch(pieces, scratch, sems):
    copies = [
        pltpu.make_async_copy(piece, buffer, sems.at[i])
        for i, (piece, buffer) in enumerate(zip(pieces, scratch, strict=True))
    ]
    for copy in copies:
        copy.start()
    return copies


def project_kernel(
    n_mp, n_ev, plan, where_ref, meta_ref, patient_ref, gain_ref, *refs
):
    n = len(plan)
    vec_in, refs = refs[:n_mp], refs[n_mp:]
    pieces, refs = refs[:n], refs[n:]
    vec_ref, attended_ref, qkv_ref, prob_ref = refs[:4]
    scratch, refs = refs[4 : 4 + n], refs[4 + n :]
    vec, blocks, sems = refs
    copies = fetch(pieces, scratch, sems)
    e, m = where_ref[0], where_ref[1]
    for k in range(n_mp):
        vec[m ^ k] = vec_in[k][...].astype(F32)
    rows = n_mp * VPAD
    full = vec[...].reshape(rows, DV)
    vec_ref[...] = full
    normed = (full * rms_factor(full) * gain_ref[...]).astype(BF16)
    width = DV // n_ev
    for j in range(n_ev):
        blocks[j] = normed[:, j * width : (j + 1) * width]
    cols = attended_ref.shape[1]
    totals = [jnp.zeros((rows, cols), F32) for _ in range(3)]
    for i, (k, lo, size) in enumerate(plan):
        copies[i].wait()
        block = blocks[e ^ k][:, lo : lo + size]
        for t in range(3):
            totals[t] = totals[t] + dot(block, scratch[i][t])
    parts = [total.astype(BF16) for total in totals]
    for t in range(3):
        qkv_ref[t] = parts[t]
    q_at = lax.broadcasted_iota(jnp.int32, (rows, rows), 0)
    k_at = lax.broadcasted_iota(jnp.int32, (rows, rows), 1)
    allowed = (meta_ref[:, 2:3] == patient_ref[...]) & (k_at <= q_at)
    for h in range(cols // VHDIM):
        span = slice(h * VHDIM, (h + 1) * VHDIM)
        scores = dot(parts[0][:, span], parts[1][:, span], NT) * VHDIM ** (-0.5)
        scores = jnp.where(allowed, scores, -1e30)
        grown = jnp.exp(scores - jnp.max(scores, axis=-1, keepdims=True))
        prob = grown / jnp.sum(grown, axis=-1, keepdims=True)
        prob_ref[h] = prob
        attended_ref[:, span] = dot(prob.astype(BF16), parts[2][:, span]).astype(BF16)


def pack_scalars(columns, rows):
    lane = lax.broadcasted_iota(jnp.int32, (rows, LANES), 1)
    spread = jnp.zeros((rows, LANES), F32)
    for c, column in enumerate(columns):
        at = (lane == c) | (lane == 8 + c) | (lane == 16 + c)
        spread = jnp.where(at, column, spread)
    one = spread.astype(BF16).astype(F32)
    two = (spread - one).astype(BF16).astype(F32)
    three = spread - one - two
    return jnp.where(lane < 8, one, jnp.where(lane < 16, two, three)).astype(BF16)


def unpack_scalar(packed, c):
    return packed[:, c : c + 1] + packed[:, 8 + c : 9 + c] + packed[:, 16 + c : 17 + c]


def ffn_kernel(
    n_mp, n_ev, plan, where_ref, meta_ref, vec_ref, gain_ref, fw_ref, head_ref, bias_ref, *refs
):
    n = len(plan)
    attn_in, refs = refs[:n_mp], refs[n_mp:]
    pieces, refs = refs[:n], refs[n:]
    outs, refs = refs[:n_mp], refs[n_mp:]
    mid_ref, refs = refs[0], refs[1:]
    scratch, refs = refs[:n], refs[n:]
    attn, blocks, grads, sems = refs
    copies = fetch(pieces, scratch, sems)
    e, m = where_ref[0], where_ref[1]
    rows = vec_ref.shape[0]
    for k in range(n_mp):
        attn[m ^ k] = attn_in[k][...].astype(F32)
    mid = vec_ref[...] + jnp.concatenate([attn[k] for k in range(n_mp)], axis=1)
    mid_ref[...] = mid
    gain = gain_ref[...]
    normed = (mid * rms_factor(mid) * gain).astype(BF16)
    width = DV // n_ev
    for j in range(n_ev):
        blocks[j] = normed[:, j * width : (j + 1) * width]
    pre = jnp.zeros((rows, fw_ref.shape[1]), F32)
    for i, (k, lo, size) in enumerate(plan):
        copies[i].wait()
        pre = pre + dot(blocks[e ^ k][:, lo : lo + size], scratch[i][...])
    sigma = 1.0 / (1.0 + jnp.exp(-pre))
    act = (pre * sigma).astype(BF16).astype(F32)
    first = (m == 0).astype(F32)
    outcome = []
    for j in range(2):
        base = jnp.sum(mid * head_ref[j : j + 1, :], axis=-1, keepdims=True) + bias_ref[j]
        outcome.append(jnp.sum(act * fw_ref[j : j + 1, :], axis=-1, keepdims=True) + first * base)
    chosen = jnp.where(meta_ref[:, 0:1] > 0.5, fw_ref[1:2, :], fw_ref[0:1, :])
    slope = (chosen * sigma * (1.0 + pre * (1.0 - sigma))).astype(BF16)
    for i, (k, lo, size) in enumerate(plan):
        grads[e ^ k, :, lo : lo + size] = dot(slope, scratch[i][...], NT)
    moment = jnp.zeros((rows, 1), F32)
    for j in range(n_ev):
        span = slice(j * width, (j + 1) * width)
        moment = moment + jnp.sum(grads[j] * gain[:, span] * mid[:, span], axis=-1, keepdims=True)
    scalars = pack_scalars([outcome[0], outcome[1], moment], rows)
    each = n_ev // n_mp
    cols = DV // n_mp
    for k in range(n_mp):
        for j in range(each):
            outs[k][:, j * width : (j + 1) * width] = grads[(m ^ k) * each + j].astype(BF16)
        outs[k][:, cols:] = scalars


def back_kernel(
    n_mp, n_ev, plan, where_ref, meta_ref, vec_ref, mid_ref, gain_ref, vgain_ref, head_ref,
    qkv_ref, prob_ref, *refs
):
    n = len(plan)
    pay_in, refs = refs[:n_mp], refs[n_mp:]
    pieces, refs = refs[:n], refs[n:]
    outs, refs = refs[:n_mp], refs[n_mp:]
    outcome_ref, refs = refs[0], refs[1:]
    scratch, refs = refs[:n], refs[n:]
    grads, table, sems = refs
    copies = fetch(pieces, scratch, sems)
    e, m = where_ref[0], where_ref[1]
    rows = vec_ref.shape[0]
    cols = DV // n_mp
    total = pay_in[0][...].astype(F32)
    for k in range(1, n_mp):
        total = total + pay_in[k][...].astype(F32)
    packed = total[:, cols:]
    outcome = [unpack_scalar(packed, 0), unpack_scalar(packed, 1)]
    moment = unpack_scalar(packed, 2) * (1.0 / DV)
    lane = lax.broadcasted_iota(jnp.int32, (rows, LANES), 1)
    outcome_ref[...] = jnp.where(lane == 0, outcome[0], outcome[1])
    treated = meta_ref[:, 0:1] > 0.5
    delta = 4096.0 * (jnp.where(treated, outcome[1], outcome[0]) - meta_ref[:, 1:2])
    factor = rms_factor(mid_ref[...])
    at = pl.ds(pl.multiple_of(m * cols, cols), cols)
    mid = mid_ref[:, at]
    head = jnp.where(treated, head_ref[1:2, at], head_ref[0:1, at])
    scaled = total[:, :cols] * gain_ref[:, at]
    grad_mid = delta * (head + factor * (scaled - mid * (factor * factor * moment)))
    grad_c = grad_mid.astype(BF16)
    three = [[], [], []]
    for h in range(cols // VHDIM):
        span = slice(h * VHDIM, (h + 1) * VHDIM)
        prob = prob_ref[h]
        grad_p = dot(grad_c[:, span], qkv_ref[2, :, span], NT)
        grad_s = prob * (grad_p - jnp.sum(grad_p * prob, axis=-1, keepdims=True))
        grad_s = (grad_s * VHDIM ** (-0.5)).astype(BF16)
        three[0].append(dot(grad_s, qkv_ref[1, :, span]).astype(BF16))
        three[1].append(dot(grad_s, qkv_ref[0, :, span], TN).astype(BF16))
        three[2].append(dot(prob.astype(BF16), grad_c[:, span], TN).astype(BF16))
    three = [jnp.concatenate(parts, axis=1) for parts in three]
    for i, (k, lo, size) in enumerate(plan):
        copies[i].wait()
        part = dot(three[0], scratch[i][0], NT)
        part = part + dot(three[1], scratch[i][1], NT)
        part = part + dot(three[2], scratch[i][2], NT)
        grads[e ^ k, :, lo : lo + size] = part
    width = DV // n_ev
    vec = vec_ref[...]
    spread = rms_factor(vec)
    moment = jnp.zeros((rows, 1), F32)
    for j in range(n_ev):
        span = slice(j * width, (j + 1) * width)
        scaled = grads[j] * vgain_ref[:, span]
        moment = moment + jnp.sum(scaled * vec[:, span], axis=-1, keepdims=True)
        if (j + 1) * width <= D:
            table[:, :, span] = (scaled * spread).reshape(n_mp, VPAD, width)

    @pl.when(m * cols < D)
    def _():
        here = pl.ds(pl.multiple_of(m * cols, cols), cols)
        table[:, :, here] = table[:, :, here] + grad_mid.reshape(n_mp, VPAD, cols)

    scalars = pack_scalars([moment], rows).astype(F32)
    table[:, :, D:] = scalars.reshape(n_mp, VPAD, LANES)
    for k in range(n_mp):
        outs[k][...] = table[m ^ k].astype(BF16)


def finish_kernel(n_mp, visits_dev, count_ref, own_ref, *refs):
    pays, out_ref = refs[:n_mp], refs[n_mp]
    total = pays[0][...].astype(F32)
    for k in range(1, n_mp):
        total = total + pays[k][...].astype(F32)
    vec = own_ref[...].astype(F32)
    spread = rms_factor(vec)
    moment = unpack_scalar(total[:, D:], 0) * (1.0 / DV)
    grad = total[:, :D] - vec[:, :D] * (spread * spread * spread * moment)
    row = lax.broadcasted_iota(jnp.int32, (VPAD, 1), 0)
    inverse = jnp.zeros((VPAD, 1), F32)
    for v in range(visits_dev):
        inverse = jnp.where(row == v, 1.0 / count_ref[v].astype(F32), inverse)
    out_ref[...] = (grad * inverse).astype(BF16)


def swap(x, axis, size, k):
    return lax.ppermute(x, axis, [(i, i ^ k) for i in range(size)])


def gather_weights(shard, n_ev, row_axis):
    rows = shard.shape[row_axis]
    if n_ev != 8:
        pieces = [shard] + [swap(shard, "events", n_ev, k) for k in range(1, n_ev)]
        return pieces, [(k, 0, rows) for k in range(n_ev)]
    half = rows // 2
    from_x = swap(shard, "events", n_ev, 2)
    from_y = swap(shard, "events", n_ev, 4)
    low = swap(lax.slice_in_dim(from_x, 0, half, axis=row_axis), "events", n_ev, 4)
    high = swap(lax.slice_in_dim(from_y, half, rows, axis=row_axis), "events", n_ev, 2)
    near = [shard, from_x, from_y, low, high]
    plan = [(0, 0, rows), (2, 0, rows), (4, 0, rows), (6, 0, half), (6, half, half)]
    far = [swap(piece, "events", n_ev, 1) for piece in near]
    return near + far, plan + [(k ^ 1, lo, size) for k, lo, size in plan]


def gather_events(block, n_ev):
    if n_ev != 8:
        return jnp.concatenate(
            [block] + [swap(block, "events", n_ev, k) for k in range(1, n_ev)], axis=0
        )
    pair = jnp.concatenate([block, swap(block, "events", n_ev, 1)], axis=0)
    return jnp.concatenate([pair] + [swap(pair, "events", n_ev, k) for k in (2, 4, 6)], axis=0)


def local(
    event_x,
    event_visit,
    visit_count,
    visit_patient,
    treatment,
    outcome_target,
    enc_gain,
    enc_qkv,
    enc_out,
    visit_gain,
    visit_qkv,
    ffn_gain,
    ffn_in,
    ffn_out,
    head_weight,
    head_bias,
):
    n_ev = lax.axis_size("events")
    n_mp = lax.axis_size("mp")
    e = lax.axis_index("events")
    m = lax.axis_index("mp")
    rows_dev = event_x.shape[0]
    visits_dev = visit_count.shape[0]
    per_owner = visits_dev * n_mp
    group = n_mp * VPAD
    cols = DV // n_mp
    hidden = ffn_in.shape[1]
    where = jnp.stack([e, m]).astype(jnp.int32)
    ids = event_visit.reshape(1, rows_dev)

    send = pl.pallas_call(
        functools.partial(pack_kernel, n_ev, per_owner, visits_dev),
        out_shape=jax.ShapeDtypeStruct((rows_dev, D + LANES), BF16),
        in_specs=[smem(), vmem(), vmem()],
        out_specs=vmem(),
        compiler_params=params(),
        name="pack",
    )(where, ids, event_x)
    got = lax.all_to_all(
        send.reshape(n_ev, rows_dev // n_ev, D + LANES), "events", split_axis=0, concat_axis=0,
        tiled=True,
    ).reshape(rows_dev, D + LANES)

    qkv_pieces, qkv_plan = gather_weights(visit_qkv, n_ev, 1)
    ffn_pieces, ffn_plan = gather_weights(ffn_in, n_ev, 0)

    head_t = head_weight.T
    width = DV // n_ev
    own_head = lax.dynamic_slice_in_dim(head_t, e * width, width, 1)
    head_hi = own_head.astype(BF16)
    head_mid = (own_head - head_hi.astype(F32)).astype(BF16)
    head_lo = (own_head - head_hi.astype(F32) - head_mid.astype(F32)).astype(BF16)
    fw = dot(jnp.concatenate([head_hi, head_mid, head_lo], axis=0), ffn_out, NT)
    fw = fw[0:2] + fw[2:4] + fw[4:6]
    step = 1
    while step < n_ev:
        fw = fw + swap(fw, "events", n_ev, step)
        step *= 2

    def spread_rows(values, fill):
        values = values.astype(F32).reshape(n_mp, visits_dev)
        return jnp.pad(values, ((0, 0), (0, VPAD - visits_dev)), constant_values=fill).reshape(group)

    patient = spread_rows(visit_patient, -1.0)
    meta = jnp.stack(
        [spread_rows(treatment, 0.0), spread_rows(outcome_target, 0.0), patient], axis=1
    )
    patient_row = patient.reshape(1, group)

    vec = pl.pallas_call(
        functools.partial(encode_kernel, visits_dev),
        out_shape=jax.ShapeDtypeStruct((VPAD, DV), BF16),
        in_specs=[smem(), vmem(), vmem(), hbm(), hbm()],
        out_specs=vmem(),
        scratch_shapes=[
            pltpu.VMEM((D, 2 * D), BF16),
            pltpu.VMEM((D, D), BF16),
            pltpu.VMEM((D, D), BF16),
            pltpu.VMEM((visits_dev * VB, D), BF16),
            pltpu.VMEM((visits_dev * VB, 2 * D), BF16),
            pltpu.VMEM((visits_dev, HEADS, VB), F32),
            pltpu.VMEM((visits_dev, HEADS, D), BF16),
            pltpu.SemaphoreType.DMA((3,)),
        ],
        compiler_params=params(),
        name="encode",
    )(visit_count, got, enc_gain.reshape(1, D), enc_qkv, enc_out)

    vecs = [vec] + [swap(vec, "mp", n_mp, k) for k in range(1, n_mp)]
    n_q = len(qkv_plan)
    all_vec, attended, qkv, prob = pl.pallas_call(
        functools.partial(project_kernel, n_mp, n_ev, qkv_plan),
        out_shape=(
            jax.ShapeDtypeStruct((group, DV), F32),
            jax.ShapeDtypeStruct((group, cols), BF16),
            jax.ShapeDtypeStruct((3, group, cols), BF16),
            jax.ShapeDtypeStruct((cols // VHDIM, group, group), F32),
        ),
        in_specs=[smem()] + [vmem()] * (3 + n_mp) + [hbm()] * n_q,
        out_specs=(vmem(),) * 4,
        scratch_shapes=[pltpu.VMEM(piece.shape, BF16) for piece in qkv_pieces]
        + [
            pltpu.VMEM((n_mp, VPAD, DV), F32),
            pltpu.VMEM((n_ev, group, width), BF16),
            pltpu.SemaphoreType.DMA((n_q,)),
        ],
        compiler_params=params(),
        name="project",
    )(where, meta, patient_row, visit_gain.reshape(1, DV), *vecs, *qkv_pieces)

    attns = [attended] + [swap(attended, "mp", n_mp, k) for k in range(1, n_mp)]
    n_f = len(ffn_plan)
    ffn_outs = pl.pallas_call(
        functools.partial(ffn_kernel, n_mp, n_ev, ffn_plan),
        out_shape=[jax.ShapeDtypeStruct((group, cols + LANES), BF16)] * n_mp
        + [jax.ShapeDtypeStruct((group, DV), F32)],
        in_specs=[smem()] + [vmem()] * 5 + [smem()] + [vmem()] * n_mp + [hbm()] * n_f,
        out_specs=[vmem()] * (n_mp + 1),
        scratch_shapes=[pltpu.VMEM(piece.shape, BF16) for piece in ffn_pieces]
        + [
            pltpu.VMEM((n_mp, group, cols), F32),
            pltpu.VMEM((n_ev, group, width), BF16),
            pltpu.VMEM((n_ev, group, width), F32),
            pltpu.SemaphoreType.DMA((n_f,)),
        ],
        compiler_params=params(),
        name="ffn",
    )(where, meta, all_vec, ffn_gain.reshape(1, DV), fw, head_t, head_bias, *attns, *ffn_pieces)
    mid = ffn_outs[n_mp]
    pays = [ffn_outs[0]] + [swap(ffn_outs[k], "mp", n_mp, k) for k in range(1, n_mp)]

    back_outs = pl.pallas_call(
        functools.partial(back_kernel, n_mp, n_ev, qkv_plan),
        out_shape=[jax.ShapeDtypeStruct((VPAD, D + LANES), BF16)] * n_mp
        + [jax.ShapeDtypeStruct((group, LANES), F32)],
        in_specs=[smem()] + [vmem()] * (8 + n_mp) + [hbm()] * n_q,
        out_specs=[vmem()] * (n_mp + 1),
        scratch_shapes=[pltpu.VMEM(piece.shape, BF16) for piece in qkv_pieces]
        + [
            pltpu.VMEM((n_ev, group, width), F32),
            pltpu.VMEM((n_mp, VPAD, D + LANES), F32),
            pltpu.SemaphoreType.DMA((n_q,)),
        ],
        compiler_params=params(),
        name="back",
    )(
        where, meta, all_vec, mid, ffn_gain.reshape(1, DV), visit_gain.reshape(1, DV), head_t, qkv,
        prob, *pays, *qkv_pieces,
    )
    outcomes = back_outs[n_mp][:, :2].reshape(n_mp, VPAD, 2)[:, :visits_dev].reshape(per_owner, 2)
    shares = [back_outs[0]] + [swap(back_outs[k], "mp", n_mp, k) for k in range(1, n_mp)]
    visit_grad = pl.pallas_call(
        functools.partial(finish_kernel, n_mp, visits_dev),
        out_shape=jax.ShapeDtypeStruct((VPAD, D), BF16),
        in_specs=[smem()] + [vmem()] * (1 + n_mp),
        out_specs=vmem(),
        compiler_params=params(),
        name="finish",
    )(visit_count, vec, *shares)

    table = gather_events(visit_grad, n_ev)
    slot = jnp.arange(n_ev * VPAD, dtype=jnp.int32)
    inner = slot % VPAD
    named = ((slot // VPAD) ^ e) * per_owner + m * visits_dev + inner
    named = jnp.where(inner < visits_dev, named, -2)
    chosen = (event_visit[:, None] == named[None, :]).astype(BF16)
    event_grads = dot(chosen, table).astype(BF16)
    return (outcomes, event_grads)


def solution(mesh):
    in_specs = (
        P(("events", "mp"), None),
        P(("events", "mp")),
        P(("events", "mp")),
        P("events"),
        P("events"),
        P("events"),
        P(),
        P(),
        P(),
        P(),
        P(None, "events", "mp"),
        P(),
        P("events", "mp"),
        P("mp", "events"),
        P(),
        P(),
    )
    out_specs = (P("events", None), P(("events", "mp"), None))
    return jax.shard_map(local, mesh=mesh, in_specs=in_specs, out_specs=out_specs, check_vma=False)
```

time: 320 us -> 191 us (0.60)
  blocking collectives: 52.6 us -> 0 us
  matrix products: 47.6 us -> 2.13 us
  waiting for transfers between devices: 121 us -> 85.8 us
  Pallas kernels: 0 us -> 33.9 us
  starting transfers between devices: 15.5 us -> 47 us
  local copies, waits for them, and re-layouts: 50.1 us -> 19.1 us
  other arithmetic: 17 us -> 0.94 us
  between operations: 14.9 us -> 1.02 us
    ppermute x0 -> x37, waiting for transfers between devices: none -> 85.8 us  [swap(): return lax.ppermute(x, axis, [(i, i ^ k) for i in range(size)])]
    all_to_all x3 -> x1, waiting for transfers between devices: 55.3 us -> 0.01 us  [local(): lax.all_to_all(send.reshape(n_ev, rows_dev // n_ev, D + LANES), 'events',...]
    dot_general x18 -> x2, matrix products: 47.6 us -> 2.13 us  [dot(): return lax.dot_general(a, b, dims, preferred_element_type=F32)]
    ppermute x0 -> x37, starting transfers between devices: none -> 42.8 us  [swap(): return lax.ppermute(x, axis, [(i, i ^ k) for i in range(size)])]
    pallas_call x0 -> x6, Pallas kernels: none -> 33.9 us  [the longest x1 12.2 us: local(): pl.pallas_call(functools.partial(encode_kernel, visits_dev), out_shape=ja...]
    psum x1 -> x0, waiting for transfers between devices: 31.7 us -> none  [local(): lax.psum(grad_min_part.astype(jnp.bfloat16), 'mp').astype(jnp.float32)]
    all_gather x3 -> x0, waiting for transfers between devices: 30.1 us -> none  [the longest x1 30.1 us: local(): lax.all_gather(ffn_out, 'events', axis=1, tiled=True)]
    all_gather x2 -> x0, blocking collectives: 27.2 us -> none  [the longest x1 14 us: local(): lax.all_gather(visit_vec.astype(jnp.bfloat16), 'mp', axis=0, tiled=True)]
  transfers between devices with their start and end apart: 8 -> 38, of which waited for: 5 -> 16; matrix products, arithmetic and copies ran while one was open for 24% -> 4% of each run, Pallas kernels for 0% -> 10%
where the time goes in v1:
time: 191 us; the launch traced here: 190 us
  waiting for transfers between devices  85.8 us (45%)
  starting transfers between devices  47 us (25%)
  Pallas kernels  33.9 us (18%)
  local copies, waits for them, and re-layouts  19.1 us (10%)
  matrix products  2.13 us (1%)
    ppermute x37, waiting for transfers between devices, swap(): return lax.ppermute(x, axis, [(i, i ^ k) for i in range(size)])  85.8 us
    ppermute x37, starting transfers between devices, swap(): return lax.ppermute(x, axis, [(i, i ^ k) for i in range(size)])  42.8 us
    unnamed x61, local copies, waits for them, and re-layouts  12.9 us
    pallas_call x1, Pallas kernels, local(): pl.pallas_call(functools.partial(encode_kernel, visits_dev), out_shape=ja...  12.2 us
    pallas_call x1, Pallas kernels, local(): pl.pallas_call(functools.partial(back_kernel, n_mp, n_ev, qkv_plan), out_...  7.47 us
    pallas_call x1, Pallas kernels, local(): pl.pallas_call(functools.partial(ffn_kernel, n_mp, n_ev, ffn_plan), out_s...  7.12 us
    all_to_all x1, starting transfers between devices, local(): lax.all_to_all(send.reshape(n_ev, rows_dev // n_ev, D + LANES), 'events',...  4.27 us
    pallas_call x1, Pallas kernels, local(): pl.pallas_call(functools.partial(project_kernel, n_mp, n_ev, qkv_plan), o...  4.01 us
  transfers between devices with their start and end apart: 38, of which 16 were waited for; matrix products, arithmetic and copies ran while one was open for 4% of the time, Pallas kernels for 10%

profile of v1, /device:TPU:0, one launch (start us, length us, event | category | flops | bytes accessed | tf_op | source)
XLA Modules:
  0.0 190.0 jit_solution(4139023436053681653)
XLA Ops:
  0.6 3.0 %collective-permute-start.18 = (bf16[256,2048]{1,0:T(8,128)(2,1)}, bf16[256,2048]{1,0:T(8,128)(2,1)}, u32[]{:S(2)}, u32[]{:S(2)}) collective-permute-start(bf16[256,2048]{1,0:T(8,128)(2,1)} %refs_4_.4), channel_id=1, source_target_pairs={{0,8},{4,12},{8,0},{12,4},{16,24},{20,28},{24,16},{28,20},{1,9},{5... | collective-permute-start | bytes 3145736 | tf_op jit(solution)/shard_map/ppermute | solution.py:387
  3.7 2.0 %collective-permute-start.4 = (bf16[3,256,512]{2,1,0:T(8,128)(2,1)}, bf16[3,256,512]{2,1,0:T(8,128)(2,1)}, u32[]{:S(2)}, u32[]{:S(2)}) collective-permute-start(bf16[3,256,512]{2,1,0:T(8,128)(2,1)} %refs_4_.5), channel_id=1, source_target_pairs={{0,16},{4,20},{8,24},{12,28},{16,0},{20,4},{24,8},{28,12},{1,17},{... | collective-permute-start | bytes 2359304 | tf_op jit(solution)/shard_map/ppermute | solution.py:387
  5.8 0.8 subtract_convert_fusion
  7.1 0.7 reshape.70.ids_ref
  7.8 1.4 copy-done.17
  9.2 2.4 %pack.1 = bf16[768,1152]{1,0:T(8,128)(2,1)S(1)} custom-call(s32[2]{0:T(128)S(1)} %pad_add_fusion.where_ref, s32[1,768]{1,0:T(1,128)S(1)} %reshape.70.ids_ref, bf16[768,1024]{1,0:T(8,128)(2,1)S(1)} %copy-done.17), custom_call_target="tpu_custom_call" | custom-call | tf_op jit(solution)/shard_map/pack/pallas_call | solution.py:446
  11.6 1.2 copy-done.1
  12.8 4.3 %all-to-all-start = ((bf16[8,96,1152]{2,1,0:T(8,128)(2,1)}), bf16[8,96,1152]{2,1,0:T(8,128)(2,1)S(1)}, u32[]{:S(2)}, u32[]{:S(2)}) async-start(bf16[8,96,1152]{2,1,0:T(8,128)(2,1)} %bitcast.25), calls=%async_computation | async-start | bytes 3538944 | tf_op jit(solution)/shard_map/all_to_all | solution.py:454
  17.1 10.8 %collective-permute-done.18.refs_5_ = bf16[256,2048]{1,0:T(8,128)(2,1)} collective-permute-done((bf16[256,2048]{1,0:T(8,128)(2,1)}, bf16[256,2048]{1,0:T(8,128)(2,1)}, u32[]{:S(2)}, u32[]{:S(2)}) %collective-permute-start.18) | collective-permute-done | bytes 1048608 | tf_op jit(solution)/shard_map/ppermute | solution.py:387
  28.0 1.1 slice.41
  29.0 2.1 %collective-permute-start.20 = (bf16[128,2048]{1,0:T(8,128)(2,1)S(1)}, bf16[128,2048]{1,0:T(8,128)(2,1)}, u32[]{:S(2)}, u32[]{:S(2)}) collective-permute-start(bf16[128,2048]{1,0:T(8,128)(2,1)S(1)} %slice.41), channel_id=1, source_target_pairs={{0,16},{4,20},{8,24},{12,28},{16,0},{20,4},{24,8},{28,12},{1,17},{... | collective-permute-start | bytes 1572872 | tf_op jit(solution)/shard_map/ppermute | solution.py:387
  31.2 13.6 %collective-permute-done.3.refs_5_ = bf16[3,256,512]{2,1,0:T(8,128)(2,1)} collective-permute-done((bf16[3,256,512]{2,1,0:T(8,128)(2,1)}, bf16[3,256,512]{2,1,0:T(8,128)(2,1)}, u32[]{:S(2)}, u32[]{:S(2)}) %collective-permute-start.3) | collective-permute-done | bytes 786464 | tf_op jit(solution)/shard_map/ppermute | solution.py:387
  44.8 2.1 %collective-permute-start.13 = (f32[2,2048]{1,0:T(2,128)S(1)}, f32[2,2048]{1,0:T(2,128)S(1)}, u32[]{:S(2)}, u32[]{:S(2)}) collective-permute-start(f32[2,2048]{1,0:T(2,128)S(1)} %fusion.18), channel_id=1, source_target_pairs={{0,8},{4,12},{8,0},{12,4},{16,24},{20,28},{24,16},{28,20},{1,9},{5... | collective-permute-start | bytes 49160 | tf_op jit(solution)/shard_map/ppermute | solution.py:387
  46.9 1.0 slice.36
  47.9 1.6 collective-permute-start.5
  49.5 1.0 slice.37
  50.5 12.8 %collective-permute-done.13 = f32[2,2048]{1,0:T(2,128)S(1)} collective-permute-done((f32[2,2048]{1,0:T(2,128)S(1)}, f32[2,2048]{1,0:T(2,128)S(1)}, u32[]{:S(2)}, u32[]{:S(2)}) %collective-permute-start.13) | collective-permute-done | bytes 16416 | tf_op jit(solution)/shard_map/ppermute | solution.py:387
  63.3 1.7 collective-permute-start.6
  65.0 1.6 collective-permute-start.14
  66.6 1.1 slice.42
  67.7 16.7 %collective-permute-done.14 = f32[2,2048]{1,0:T(2,128)S(1)} collective-permute-done((f32[2,2048]{1,0:T(2,128)S(1)}, f32[2,2048]{1,0:T(2,128)S(1)}, u32[]{:S(2)}, u32[]{:S(2)}) %collective-permute-start.14) | collective-permute-done | bytes 16416 | tf_op jit(solution)/shard_map/ppermute | solution.py:387
  84.4 1.6 collective-permute-start.21
  86.1 0.5 collective-permute-start.11
  86.6 0.8 copy-done.8
  87.3 0.9 copy-done.4
  88.7 8.3 %collective-permute-done.21.refs_8_ = bf16[128,2048]{1,0:T(8,128)(2,1)} collective-permute-done((bf16[128,2048]{1,0:T(8,128)(2,1)S(1)}, bf16[128,2048]{1,0:T(8,128)(2,1)}, u32[]{:S(2)}, u32[]{:S(2)}) %collective-permute-start.21) | collective-permute-done | bytes 524320 | tf_op jit(solution)/shard_map/ppermute | solution.py:387
  97.0 0.8 copy-done.11
  97.8 0.5 collective-permute-start.23
  98.3 0.8 copy-done.14
  99.1 1.6 copy-done.7
  100.7 12.2 %encode.1.refs_0_.own_ref = bf16[8,2048]{1,0:T(8,128)(2,1)S(1)} custom-call(s32[6]{0:T(128)S(1)} %copy-done.22, bf16[768,1152]{1,0:T(8,128)(2,1)S(1)} %bitcast.24, f32[1,1024]{1,0:T(1,128)S(1)} %bitcast.32, bf16[1024,3072]{1,0:T(8,128)(2,1)} %qkv_ref.1, bf16[1024,1024]{1,0:T(8,128)(2,1)S(1)} %copy-done.7), custom_call_target="tpu_custom_call" | custom-call | tf_op jit(solution)/shard_map/encode/pallas_call | solution.py:485
  112.9 1.5 collective-permute-start
  114.4 2.6 %collective-permute-start.1 = (bf16[8,2048]{1,0:T(8,128)(2,1)S(1)}, bf16[8,2048]{1,0:T(8,128)(2,1)S(1)}, u32[]{:S(2)}, u32[]{:S(2)}) collective-permute-start(bf16[8,2048]{1,0:T(8,128)(2,1)S(1)} %encode.1.refs_0_.own_ref), channel_id=1, source_target_pairs={{0,2},{1,3},{2,0},{3,1},{4,6},{5,7},{6,4},{7,5},{8,10},{9,11},{10,... | collective-permute-start | bytes 98312 | tf_op jit(solution)/shard_map/ppermute | solution.py:387
  117.0 3.3 %collective-permute-start.2 = (bf16[8,2048]{1,0:T(8,128)(2,1)S(1)}, bf16[8,2048]{1,0:T(8,128)(2,1)S(1)}, u32[]{:S(2)}, u32[]{:S(2)}) collective-permute-start(bf16[8,2048]{1,0:T(8,128)(2,1)S(1)} %encode.1.refs_0_.own_ref), channel_id=1, source_target_pairs={{0,3},{1,2},{2,1},{3,0},{4,7},{5,6},{6,5},{7,4},{8,11},{9,10},{10,... | collective-permute-start | bytes 98312 | tf_op jit(solution)/shard_map/ppermute | solution.py:387
  120.3 2.4 %collective-permute-done.2.refs_3_ = bf16[8,2048]{1,0:T(8,128)(2,1)S(1)} collective-permute-done((bf16[8,2048]{1,0:T(8,128)(2,1)S(1)}, bf16[8,2048]{1,0:T(8,128)(2,1)S(1)}, u32[]{:S(2)}, u32[]{:S(2)}) %collective-permute-start.2) | collective-permute-done | bytes 32800 | tf_op jit(solution)/shard_map/ppermute | solution.py:387
  123.4 1.1 copy-done.2
  124.6 1.1 copy-done.5
  125.7 1.0 copy-done.9
  126.7 1.0 copy-done.12
  127.7 1.0 copy-done.15
  128.7 4.0 %project.1 = (f32[32,2048]{1,0:T(8,128)S(1)}, bf16[32,512]{1,0:T(8,128)(2,1)S(1)}, bf16[3,32,512]{2,1,0:T(8,128)(2,1)S(1)}, f32[4,32,32]{2,1,0:T(8,128)S(1)}) custom-call(s32[2]{0:T(128)S(1)} %pad_add_fusion.where_ref, f32[32,3]{1,0:T(8,128)S(1)} %copy.24.meta_ref, f32[1,32]{1,0:T(1,128)S(1)} %reshape_reshape.3.patient_ref, f32[1,2048]{1,0:T(1,128)S(1)} %bitcast.28, ...), custom_call_target="tpu_custom_call" | custom-call | tf_op jit(solution)/shard_map/project/pallas_call | solution.py:506
  132.8 3.9 %collective-permute-done.15.refs_1_ = bf16[32,512]{1,0:T(8,128)(2,1)S(1)} collective-permute-done((bf16[32,512]{1,0:T(8,128)(2,1)S(1)}, bf16[32,512]{1,0:T(8,128)(2,1)S(1)}, u32[]{:S(2)}, u32[]{:S(2)}) %collective-permute-start.15) | collective-permute-done | bytes 32800 | tf_op jit(solution)/shard_map/ppermute | solution.py:387
  136.7 2.1 %collective-permute-start.16 = (bf16[32,512]{1,0:T(8,128)(2,1)S(1)}, bf16[32,512]{1,0:T(8,128)(2,1)S(1)}, u32[]{:S(2)}, u32[]{:S(2)}) collective-permute-start(bf16[32,512]{1,0:T(8,128)(2,1)S(1)} %get-tuple-element.17.refs_0_), channel_id=1, source_target_pairs={{0,2},{1,3},{2,0},{3,1},{4,6},{5,7},{6,4},{7,5},{8,10},{9,11},{10,... | collective-permute-start | bytes 98312 | tf_op jit(solution)/shard_map/ppermute | solution.py:387
  138.8 2.8 %collective-permute-done.16.refs_2_ = bf16[32,512]{1,0:T(8,128)(2,1)S(1)} collective-permute-done((bf16[32,512]{1,0:T(8,128)(2,1)S(1)}, bf16[32,512]{1,0:T(8,128)(2,1)S(1)}, u32[]{:S(2)}, u32[]{:S(2)}) %collective-permute-start.16) | collective-permute-done | bytes 32800 | tf_op jit(solution)/shard_map/ppermute | solution.py:387
  141.5 3.3 %collective-permute-start.17 = (bf16[32,512]{1,0:T(8,128)(2,1)S(1)}, bf16[32,512]{1,0:T(8,128)(2,1)S(1)}, u32[]{:S(2)}, u32[]{:S(2)}) collective-permute-start(bf16[32,512]{1,0:T(8,128)(2,1)S(1)} %get-tuple-element.17.refs_0_), channel_id=1, source_target_pairs={{0,3},{1,2},{2,1},{3,0},{4,7},{5,6},{6,5},{7,4},{8,11},{9,10},{10,... | collective-permute-start | bytes 98312 | tf_op jit(solution)/shard_map/ppermute | solution.py:387
  144.9 2.4 %collective-permute-done.17.refs_3_ = bf16[32,512]{1,0:T(8,128)(2,1)S(1)} collective-permute-done((bf16[32,512]{1,0:T(8,128)(2,1)S(1)}, bf16[32,512]{1,0:T(8,128)(2,1)S(1)}, u32[]{:S(2)}, u32[]{:S(2)}) %collective-permute-start.17) | collective-permute-done | bytes 32800 | tf_op jit(solution)/shard_map/ppermute | solution.py:387
  147.3 7.1 %ffn.1 = (bf16[32,640]{1,0:T(8,128)(2,1)S(1)}, bf16[32,640]{1,0:T(8,128)(2,1)S(1)}, bf16[32,640]{1,0:T(8,128)(2,1)S(1)}, bf16[32,640]{1,0:T(8,128)(2,1)S(1)}, f32[32,2048]{1,0:T(8,128)S(1)}) custom-call(s32[2]{0:T(128)S(1)} %pad_add_fusion.where_ref, f32[32,3]{1,0:T(8,128)S(1)} %copy.24.meta_ref, f32[32,2048]{1,0:T(8,128)S(1)} %get-tuple-element.16.vec_ref, ...), custom_call_target="tpu_custom_call" | custom-call | tf_op jit(solution)/shard_map/ffn/pallas_call | solution.py:528
  154.6 3.9 %collective-permute-start.28 = (bf16[32,640]{1,0:T(8,128)(2,1)S(1)}, bf16[32,640]{1,0:T(8,128)(2,1)S(1)}, u32[]{:S(2)}, u32[]{:S(2)}) collective-permute-start(bf16[32,640]{1,0:T(8,128)(2,1)S(1)} %get-tuple-element.23), channel_id=1, source_target_pairs={{0,2},{1,3},{2,0},{3,1},{4,6},{5,7},{6,4},{7,5},{8,10},{9,11},{10,... | collective-permute-start | bytes 122888 | tf_op jit(solution)/shard_map/ppermute | solution.py:387
  158.5 0.5 collective-permute-start.29
  158.9 2.2 %collective-permute-done.28.refs_2_ = bf16[32,640]{1,0:T(8,128)(2,1)S(1)} collective-permute-done((bf16[32,640]{1,0:T(8,128)(2,1)S(1)}, bf16[32,640]{1,0:T(8,128)(2,1)S(1)}, u32[]{:S(2)}, u32[]{:S(2)}) %collective-permute-start.28) | collective-permute-done | bytes 40992 | tf_op jit(solution)/shard_map/ppermute | solution.py:387
  161.2 3.1 %collective-permute-done.29.refs_3_ = bf16[32,640]{1,0:T(8,128)(2,1)S(1)} collective-permute-done((bf16[32,640]{1,0:T(8,128)(2,1)S(1)}, bf16[32,640]{1,0:T(8,128)(2,1)S(1)}, u32[]{:S(2)}, u32[]{:S(2)}) %collective-permute-start.29) | collective-permute-done | bytes 40992 | tf_op jit(solution)/shard_map/ppermute | solution.py:387
  164.3 7.5 %back.1 = (bf16[8,1152]{1,0:T(8,128)(2,1)S(1)}, bf16[8,1152]{1,0:T(8,128)(2,1)S(1)}, bf16[8,1152]{1,0:T(8,128)(2,1)S(1)}, bf16[8,1152]{1,0:T(8,128)(2,1)S(1)}, f32[32,128]{1,0:T(8,128)S(1)}) custom-call(s32[2]{0:T(128)S(1)} %pad_add_fusion.where_ref, f32[32,3]{1,0:T(8,128)S(1)} %copy.24.meta_ref, f32[32,2048]{1,0:T(8,128)S(1)} %get-tuple-element.16.vec_ref, ...), custom_call_target="tpu_custom_call" | custom-call | tf_op jit(solution)/shard_map/back/pallas_call | solution.py:547
  171.9 1.0 collective-permute-start.31
  172.9 3.3 %collective-permute-start.32 = (bf16[8,1152]{1,0:T(8,128)(2,1)S(1)}, bf16[8,1152]{1,0:T(8,128)(2,1)S(1)}, u32[]{:S(2)}, u32[]{:S(2)}) collective-permute-start(bf16[8,1152]{1,0:T(8,128)(2,1)S(1)} %get-tuple-element.29), channel_id=1, source_target_pairs={{0,3},{1,2},{2,1},{3,0},{4,7},{5,6},{6,5},{7,4},{8,11},{9,10},{10,... | collective-permute-start | bytes 55304 | tf_op jit(solution)/shard_map/ppermute | solution.py:387
  176.3 0.6 reshape.76
  177.0 1.4 collective-permute-done.32.refs_3_
  178.4 0.7 finish.1
  179.2 1.2 collective-permute-done.33
  180.4 1.5 collective-permute-start.34
  181.8 1.5 collective-permute-start.35
  183.4 0.5 collective-permute-start.36
  184.3 1.5 collective-permute-done.35
  185.8 2.4 %collective-permute-done.36 = bf16[16,1024]{1,0:T(8,128)(2,1)S(1)} collective-permute-done((bf16[16,1024]{1,0:T(8,128)(2,1)S(1)}, bf16[16,1024]{1,0:T(8,128)(2,1)S(1)}, u32[]{:S(2)}, u32[]{:S(2)}) %collective-permute-start.36) | collective-permute-done | bytes 32800 | tf_op jit(solution)/shard_map/ppermute | solution.py:387
  188.2 1.8 convolution_convert_fusion
  (111 shorter events, 2.9 us)
Async XLA Ops:
  0.6 5.9 %copy-start = (bf16[2048,256]{1,0:T(8,128)(2,1)S(1)}, bf16[2048,256]{1,0:T(8,128)(2,1)}, u32[]{:S(2)}) copy-start(bf16[2048,256]{1,0:T(8,128)(2,1)} %param.29) | copy-start | bytes 3145732
  0.6 27.3 %collective-permute-start.18 = (bf16[256,2048]{1,0:T(8,128)(2,1)}, bf16[256,2048]{1,0:T(8,128)(2,1)}, u32[]{:S(2)}, u32[]{:S(2)}) collective-permute-start(bf16[256,2048]{1,0:T(8,128)(2,1)} %refs_4_.4), channel_id=1, source_target_pairs={{0,8},{4,12},{8,0},{12,4},{16,24},{20,28},{24,16},{28,20},{1,9},{5... | collective-permute-start | bytes 3145736 | tf_op jit(solution)/shard_map/ppermute | solution.py:387
  3.6 41.2 %collective-permute-start.3 = (bf16[3,256,512]{2,1,0:T(8,128)(2,1)}, bf16[3,256,512]{2,1,0:T(8,128)(2,1)}, u32[]{:S(2)}, u32[]{:S(2)}) collective-permute-start(bf16[3,256,512]{2,1,0:T(8,128)(2,1)} %refs_4_.5), channel_id=1, source_target_pairs={{0,8},{4,12},{8,0},{12,4},{16,24},{20,28},{24,16},{28,20},{1,9},{5... | collective-permute-start | bytes 2359304 | tf_op jit(solution)/shard_map/ppermute | solution.py:387
  3.7 44.2 %collective-permute-start.4 = (bf16[3,256,512]{2,1,0:T(8,128)(2,1)}, bf16[3,256,512]{2,1,0:T(8,128)(2,1)}, u32[]{:S(2)}, u32[]{:S(2)}) collective-permute-start(bf16[3,256,512]{2,1,0:T(8,128)(2,1)} %refs_4_.5), channel_id=1, source_target_pairs={{0,16},{4,20},{8,24},{12,28},{16,0},{20,4},{24,8},{28,12},{1,17},{... | collective-permute-start | bytes 2359304 | tf_op jit(solution)/shard_map/ppermute | solution.py:387
  5.7 59.3 %collective-permute-start.19 = (bf16[256,2048]{1,0:T(8,128)(2,1)}, bf16[256,2048]{1,0:T(8,128)(2,1)}, u32[]{:S(2)}, u32[]{:S(2)}) collective-permute-start(bf16[256,2048]{1,0:T(8,128)(2,1)} %refs_4_.4), channel_id=1, source_target_pairs={{0,16},{4,20},{8,24},{12,28},{16,0},{20,4},{24,8},{28,12},{1,17},{... | collective-permute-start | bytes 3145736 | tf_op jit(solution)/shard_map/ppermute | solution.py:387
  6.9 22.1 %collective-permute-start.12 = (f32[2,2048]{1,0:T(2,128)S(1)}, f32[2,2048]{1,0:T(2,128)S(1)}, u32[]{:S(2)}, u32[]{:S(2)}) collective-permute-start(f32[2,2048]{1,0:T(2,128)S(1)} %slice_add_fusion), channel_id=1, source_target_pairs={{0,4},{4,0},{8,12},{12,8},{16,20},{20,16},{24,28},{28,24},{1,5},{5... | collective-permute-start | bytes 49160 | tf_op jit(solution)/shard_map/ppermute | solution.py:387
  7.8 1.4 copy-start.17
  11.6 1.2 copy-start.1
  12.8 86.2 %all-to-all-start = ((bf16[8,96,1152]{2,1,0:T(8,128)(2,1)}), bf16[8,96,1152]{2,1,0:T(8,128)(2,1)S(1)}, u32[]{:S(2)}, u32[]{:S(2)}) async-start(bf16[8,96,1152]{2,1,0:T(8,128)(2,1)} %bitcast.25), calls=%async_computation | async-start | bytes 3538944 | tf_op jit(solution)/shard_map/all_to_all | solution.py:454
  17.1 81.9 %copy-start.21 = (f32[1024]{0:T(1024)S(1)}, f32[1024]{0:T(1024)}, u32[]{:S(2)}) copy-start(f32[1024]{0:T(1024)} %param.22) | copy-start | bytes 12292
  17.1 81.9 %copy-start.22 = (s32[6]{0:T(128)S(1)}, s32[6]{0:T(128)}, u32[]{:S(2)}) copy-start(s32[6]{0:T(128)} %count_ref.3) | copy-start | bytes 76
  28.0 59.4 %collective-permute-start.7 = (bf16[3,256,512]{2,1,0:T(8,128)(2,1)}, bf16[3,256,512]{2,1,0:T(8,128)(2,1)S(1)}, u32[]{:S(2)}, u32[]{:S(2)}) collective-permute-start(bf16[3,256,512]{2,1,0:T(8,128)(2,1)} %refs_4_.5), channel_id=1, source_target_pairs={{0,4},{4,0},{8,12},{12,8},{16,20},{20,16},{24,28},{28,24},{1,5},{5... | collective-permute-start | bytes 2359304 | tf_op jit(solution)/shard_map/ppermute | solution.py:387
  29.0 59.2 %collective-permute-start.20 = (bf16[128,2048]{1,0:T(8,128)(2,1)S(1)}, bf16[128,2048]{1,0:T(8,128)(2,1)}, u32[]{:S(2)}, u32[]{:S(2)}) collective-permute-start(bf16[128,2048]{1,0:T(8,128)(2,1)S(1)} %slice.41), channel_id=1, source_target_pairs={{0,16},{4,20},{8,24},{12,28},{16,0},{20,4},{24,8},{28,12},{1,17},{... | collective-permute-start | bytes 1572872 | tf_op jit(solution)/shard_map/ppermute | solution.py:387
  44.8 18.5 %collective-permute-start.13 = (f32[2,2048]{1,0:T(2,128)S(1)}, f32[2,2048]{1,0:T(2,128)S(1)}, u32[]{:S(2)}, u32[]{:S(2)}) collective-permute-start(f32[2,2048]{1,0:T(2,128)S(1)} %fusion.18), channel_id=1, source_target_pairs={{0,8},{4,12},{8,0},{12,4},{16,24},{20,28},{24,16},{28,20},{1,9},{5... | collective-permute-start | bytes 49160 | tf_op jit(solution)/shard_map/ppermute | solution.py:387
  47.9 38.2 %collective-permute-start.5 = (bf16[3,128,512]{2,1,0:T(8,128)(2,1)S(1)}, bf16[3,128,512]{2,1,0:T(8,128)(2,1)S(1)}, u32[]{:S(2)}, u32[]{:S(2)}) collective-permute-start(bf16[3,128,512]{2,1,0:T(8,128)(2,1)S(1)} %slice.36), channel_id=1, source_target_pairs={{0,16},{4,20},{8,24},{12,28},{16,0},{20,4},{24,8},{28,12},{1,17},{... | collective-permute-start | bytes 1179656 | tf_op jit(solution)/shard_map/ppermute | solution.py:387
  63.3 22.8 %collective-permute-start.6 = (bf16[3,128,512]{2,1,0:T(8,128)(2,1)S(1)}, bf16[3,128,512]{2,1,0:T(8,128)(2,1)S(1)}, u32[]{:S(2)}, u32[]{:S(2)}) collective-permute-start(bf16[3,128,512]{2,1,0:T(8,128)(2,1)S(1)} %slice.37), channel_id=1, source_target_pairs={{0,8},{4,12},{8,0},{12,4},{16,24},{20,28},{24,16},{28,20},{1,9},{5... | collective-permute-start | bytes 1179656 | tf_op jit(solution)/shard_map/ppermute | solution.py:387
  65.0 19.4 %collective-permute-start.14 = (f32[2,2048]{1,0:T(2,128)S(1)}, f32[2,2048]{1,0:T(2,128)S(1)}, u32[]{:S(2)}, u32[]{:S(2)}) collective-permute-start(f32[2,2048]{1,0:T(2,128)S(1)} %add.62), channel_id=1, source_target_pairs={{0,16},{4,20},{8,24},{12,28},{16,0},{20,4},{24,8},{28,12},{1,17},{... | collective-permute-start | bytes 49160 | tf_op jit(solution)/shard_map/ppermute | solution.py:387
  84.4 12.6 %collective-permute-start.21 = (bf16[128,2048]{1,0:T(8,128)(2,1)S(1)}, bf16[128,2048]{1,0:T(8,128)(2,1)}, u32[]{:S(2)}, u32[]{:S(2)}) collective-permute-start(bf16[128,2048]{1,0:T(8,128)(2,1)S(1)} %slice.42), channel_id=1, source_target_pairs={{0,8},{4,12},{8,0},{12,4},{16,24},{20,28},{24,16},{28,20},{1,9},{5... | collective-permute-start | bytes 1572872 | tf_op jit(solution)/shard_map/ppermute | solution.py:387
  86.1 10.9 %collective-permute-start.10 = (bf16[3,128,512]{2,1,0:T(8,128)(2,1)S(1)}, bf16[3,128,512]{2,1,0:T(8,128)(2,1)S(1)}, u32[]{:S(2)}, u32[]{:S(2)}) collective-permute-start(bf16[3,128,512]{2,1,0:T(8,128)(2,1)S(1)} %collective-permute-done.5.refs_7_), channel_id=1, source_target_pairs={{0,4},{4,0},{8,12},{12,8},{16,20},{20,16},{24,28},{28,24},{1,5},{5... | collective-permute-start | bytes 1179656 | tf_op jit(solution)/shard_map/ppermute | solution.py:387
  86.1 12.2 %collective-permute-start.11 = (bf16[3,128,512]{2,1,0:T(8,128)(2,1)S(1)}, bf16[3,128,512]{2,1,0:T(8,128)(2,1)S(1)}, u32[]{:S(2)}, u32[]{:S(2)}) collective-permute-start(bf16[3,128,512]{2,1,0:T(8,128)(2,1)S(1)} %collective-permute-done.6.refs_8_), channel_id=1, source_target_pairs={{0,4},{4,0},{8,12},{12,8},{16,20},{20,16},{24,28},{28,24},{1,5},{5... | collective-permute-start | bytes 1179656 | tf_op jit(solution)/shard_map/ppermute | solution.py:387
  87.3 0.9 copy-start.4
  88.2 24.7 %collective-permute-start.8 = (bf16[3,256,512]{2,1,0:T(8,128)(2,1)}, bf16[3,256,512]{2,1,0:T(8,128)(2,1)}, u32[]{:S(2)}, u32[]{:S(2)}) collective-permute-start(bf16[3,256,512]{2,1,0:T(8,128)(2,1)} %collective-permute-done.3.refs_5_), channel_id=1, source_target_pairs={{0,4},{4,0},{8,12},{12,8},{16,20},{20,16},{24,28},{28,24},{1,5},{5... | collective-permute-start | bytes 2359304 | tf_op jit(solution)/shard_map/ppermute | solution.py:387
  88.3 26.1 %collective-permute-start.9 = (bf16[3,256,512]{2,1,0:T(8,128)(2,1)}, bf16[3,256,512]{2,1,0:T(8,128)(2,1)}, u32[]{:S(2)}, u32[]{:S(2)}) collective-permute-start(bf16[3,256,512]{2,1,0:T(8,128)(2,1)} %collective-permute-done.4.refs_6_), channel_id=1, source_target_pairs={{0,4},{4,0},{8,12},{12,8},{16,20},{20,16},{24,28},{28,24},{1,5},{5... | collective-permute-start | bytes 2359304 | tf_op jit(solution)/shard_map/ppermute | solution.py:387
  97.0 35.7 %collective-permute-start.22 = (bf16[256,2048]{1,0:T(8,128)(2,1)}, bf16[256,2048]{1,0:T(8,128)(2,1)}, u32[]{:S(2)}, u32[]{:S(2)}) collective-permute-start(bf16[256,2048]{1,0:T(8,128)(2,1)} %refs_4_.4), channel_id=1, source_target_pairs={{0,4},{4,0},{8,12},{12,8},{16,20},{20,16},{24,28},{28,24},{1,5},{5... | collective-permute-start | bytes 3145736 | tf_op jit(solution)/shard_map/ppermute | solution.py:387
  97.8 49.5 %collective-permute-start.23 = (bf16[256,2048]{1,0:T(8,128)(2,1)}, bf16[256,2048]{1,0:T(8,128)(2,1)}, u32[]{:S(2)}, u32[]{:S(2)}) collective-permute-start(bf16[256,2048]{1,0:T(8,128)(2,1)} %collective-permute-done.18.refs_5_), channel_id=1, source_target_pairs={{0,4},{4,0},{8,12},{12,8},{16,20},{20,16},{24,28},{28,24},{1,5},{5... | collective-permute-start | bytes 3145736 | tf_op jit(solution)/shard_map/ppermute | solution.py:387
  98.3 0.8 copy-start.14
  99.1 48.2 %collective-permute-start.24 = (bf16[256,2048]{1,0:T(8,128)(2,1)}, bf16[256,2048]{1,0:T(8,128)(2,1)}, u32[]{:S(2)}, u32[]{:S(2)}) collective-permute-start(bf16[256,2048]{1,0:T(8,128)(2,1)} %collective-permute-done.19.refs_6_), channel_id=1, source_target_pairs={{0,4},{4,0},{8,12},{12,8},{16,20},{20,16},{24,28},{28,24},{1,5},{5... | collective-permute-start | bytes 3145736 | tf_op jit(solution)/shard_map/ppermute | solution.py:387
  99.1 1.6 copy-start.7
  100.7 22.0 %copy-start.26 = (s32[24]{0:T(128)S(1)}, s32[24]{0:T(128)}, u32[]{:S(2)}) copy-start(s32[24]{0:T(128)} %param.19) | copy-start | bytes 292
  100.7 22.3 %copy-start.27 = (s32[24]{0:T(128)S(1)}, s32[24]{0:T(128)}, u32[]{:S(2)}) copy-start(s32[24]{0:T(128)} %param.20) | copy-start | bytes 292
  100.7 22.5 %copy-start.25 = (f32[24]{0:T(128)S(1)}, f32[24]{0:T(128)}, u32[]{:S(2)}) copy-start(f32[24]{0:T(128)} %param.21) | copy-start | bytes 292
  100.7 22.8 %copy-start.19 = (f32[2048]{0:T(1024)S(1)}, f32[2048]{0:T(1024)}, u32[]{:S(2)}) copy-start(f32[2048]{0:T(1024)} %param.25) | copy-start | bytes 24580
  112.9 4.1 %collective-permute-start = (bf16[8,2048]{1,0:T(8,128)(2,1)S(1)}, bf16[8,2048]{1,0:T(8,128)(2,1)S(1)}, u32[]{:S(2)}, u32[]{:S(2)}) collective-permute-start(bf16[8,2048]{1,0:T(8,128)(2,1)S(1)} %encode.1.refs_0_.own_ref), channel_id=1, source_target_pairs={{0,1},{1,0},{2,3},{3,2},{4,5},{5,4},{6,7},{7,6},{8,9},{9,8},{10,11... | collective-permute-start | bytes 98312 | tf_op jit(solution)/shard_map/ppermute | solution.py:387
  114.4 5.9 %collective-permute-start.1 = (bf16[8,2048]{1,0:T(8,128)(2,1)S(1)}, bf16[8,2048]{1,0:T(8,128)(2,1)S(1)}, u32[]{:S(2)}, u32[]{:S(2)}) collective-permute-start(bf16[8,2048]{1,0:T(8,128)(2,1)S(1)} %encode.1.refs_0_.own_ref), channel_id=1, source_target_pairs={{0,2},{1,3},{2,0},{3,1},{4,6},{5,7},{6,4},{7,5},{8,10},{9,11},{10,... | collective-permute-start | bytes 98312 | tf_op jit(solution)/shard_map/ppermute | solution.py:387
  117.0 5.7 %collective-permute-start.2 = (bf16[8,2048]{1,0:T(8,128)(2,1)S(1)}, bf16[8,2048]{1,0:T(8,128)(2,1)S(1)}, u32[]{:S(2)}, u32[]{:S(2)}) collective-permute-start(bf16[8,2048]{1,0:T(8,128)(2,1)S(1)} %encode.1.refs_0_.own_ref), channel_id=1, source_target_pairs={{0,3},{1,2},{2,1},{3,0},{4,7},{5,6},{6,5},{7,4},{8,11},{9,10},{10,... | collective-permute-start | bytes 98312 | tf_op jit(solution)/shard_map/ppermute | solution.py:387
  120.3 26.9 %collective-permute-start.25 = (bf16[128,2048]{1,0:T(8,128)(2,1)}, bf16[128,2048]{1,0:T(8,128)(2,1)S(1)}, u32[]{:S(2)}, u32[]{:S(2)}) collective-permute-start(bf16[128,2048]{1,0:T(8,128)(2,1)} %collective-permute-done.20.refs_7_), channel_id=1, source_target_pairs={{0,4},{4,0},{8,12},{12,8},{16,20},{20,16},{24,28},{28,24},{1,5},{5... | collective-permute-start | bytes 1572872 | tf_op jit(solution)/shard_map/ppermute | solution.py:387
  122.7 24.6 %collective-permute-start.26 = (bf16[128,2048]{1,0:T(8,128)(2,1)}, bf16[128,2048]{1,0:T(8,128)(2,1)S(1)}, u32[]{:S(2)}, u32[]{:S(2)}) collective-permute-start(bf16[128,2048]{1,0:T(8,128)(2,1)} %collective-permute-done.21.refs_8_), channel_id=1, source_target_pairs={{0,4},{4,0},{8,12},{12,8},{16,20},{20,16},{24,28},{28,24},{1,5},{5... | collective-permute-start | bytes 1572872 | tf_op jit(solution)/shard_map/ppermute | solution.py:387
  123.4 1.1 copy-start.2
  124.6 1.1 copy-start.5
  125.7 1.0 copy-start.9
  126.7 1.0 copy-start.12
  127.7 1.0 copy-start.15
  128.7 18.6 %copy-start.18 = (f32[2048,2]{0,1:T(2,128)S(1)}, f32[2048,2]{0,1:T(2,128)}, u32[]{:S(2)}) copy-start(f32[2048,2]{0,1:T(2,128)} %param.30) | copy-start | bytes 49156
  128.7 18.6 %copy-start.20 = (f32[2048]{0:T(1024)S(1)}, f32[2048]{0:T(1024)}, u32[]{:S(2)}) copy-start(f32[2048]{0:T(1024)} %param.27) | copy-start | bytes 24580
  128.7 18.6 %copy-start.23 = (f32[2]{0:T(128)S(1)}, f32[2]{0:T(128)}, u32[]{:S(2)}) copy-start(f32[2]{0:T(128)} %bias_ref.1) | copy-start | bytes 28
  132.7 4.0 %collective-permute-start.15 = (bf16[32,512]{1,0:T(8,128)(2,1)S(1)}, bf16[32,512]{1,0:T(8,128)(2,1)S(1)}, u32[]{:S(2)}, u32[]{:S(2)}) collective-permute-start(bf16[32,512]{1,0:T(8,128)(2,1)S(1)} %get-tuple-element.17.refs_0_), channel_id=1, source_target_pairs={{0,1},{1,0},{2,3},{3,2},{4,5},{5,4},{6,7},{7,6},{8,9},{9,8},{10,11... | collective-permute-start | bytes 98312 | tf_op jit(solution)/shard_map/ppermute | solution.py:387
  136.7 4.8 %collective-permute-start.16 = (bf16[32,512]{1,0:T(8,128)(2,1)S(1)}, bf16[32,512]{1,0:T(8,128)(2,1)S(1)}, u32[]{:S(2)}, u32[]{:S(2)}) collective-permute-start(bf16[32,512]{1,0:T(8,128)(2,1)S(1)} %get-tuple-element.17.refs_0_), channel_id=1, source_target_pairs={{0,2},{1,3},{2,0},{3,1},{4,6},{5,7},{6,4},{7,5},{8,10},{9,11},{10,... | collective-permute-start | bytes 98312 | tf_op jit(solution)/shard_map/ppermute | solution.py:387
  141.5 5.7 %collective-permute-start.17 = (bf16[32,512]{1,0:T(8,128)(2,1)S(1)}, bf16[32,512]{1,0:T(8,128)(2,1)S(1)}, u32[]{:S(2)}, u32[]{:S(2)}) collective-permute-start(bf16[32,512]{1,0:T(8,128)(2,1)S(1)} %get-tuple-element.17.refs_0_), channel_id=1, source_target_pairs={{0,3},{1,2},{2,1},{3,0},{4,7},{5,6},{6,5},{7,4},{8,11},{9,10},{10,... | collective-permute-start | bytes 98312 | tf_op jit(solution)/shard_map/ppermute | solution.py:387
  147.3 17.0 %copy-start.3 = (bf16[3,256,512]{2,1,0:T(8,128)(2,1)S(1)}, bf16[3,256,512]{2,1,0:T(8,128)(2,1)}, u32[]{:S(2)}) copy-start(bf16[3,256,512]{2,1,0:T(8,128)(2,1)} %refs_4_.5) | copy-start | bytes 2359300
  147.3 17.0 %copy-start.6 = (bf16[3,256,512]{2,1,0:T(8,128)(2,1)S(1)}, bf16[3,256,512]{2,1,0:T(8,128)(2,1)}, u32[]{:S(2)}) copy-start(bf16[3,256,512]{2,1,0:T(8,128)(2,1)} %copy-done.4) | copy-start | bytes 2359300
  147.3 16.9 %copy-start.10 = (bf16[3,128,512]{2,1,0:T(8,128)(2,1)S(1)}, bf16[3,128,512]{2,1,0:T(8,128)(2,1)}, u32[]{:S(2)}) copy-start(bf16[3,128,512]{2,1,0:T(8,128)(2,1)} %copy-done.8) | copy-start | bytes 1179652
  147.3 16.9 %copy-start.13 = (bf16[3,128,512]{2,1,0:T(8,128)(2,1)S(1)}, bf16[3,128,512]{2,1,0:T(8,128)(2,1)}, u32[]{:S(2)}) copy-start(bf16[3,128,512]{2,1,0:T(8,128)(2,1)} %copy-done.11) | copy-start | bytes 1179652
  147.3 16.9 %copy-start.16 = (bf16[3,128,512]{2,1,0:T(8,128)(2,1)S(1)}, bf16[3,128,512]{2,1,0:T(8,128)(2,1)}, u32[]{:S(2)}) copy-start(bf16[3,128,512]{2,1,0:T(8,128)(2,1)} %copy-done.14) | copy-start | bytes 1179652
  154.5 4.5 %collective-permute-start.27 = (bf16[32,640]{1,0:T(8,128)(2,1)S(1)}, bf16[32,640]{1,0:T(8,128)(2,1)S(1)}, u32[]{:S(2)}, u32[]{:S(2)}) collective-permute-start(bf16[32,640]{1,0:T(8,128)(2,1)S(1)} %get-tuple-element.22), channel_id=1, source_target_pairs={{0,1},{1,0},{2,3},{3,2},{4,5},{5,4},{6,7},{7,6},{8,9},{9,8},{10,11... | collective-permute-start | bytes 122888 | tf_op jit(solution)/shard_map/ppermute | solution.py:387
  154.6 6.6 %collective-permute-start.28 = (bf16[32,640]{1,0:T(8,128)(2,1)S(1)}, bf16[32,640]{1,0:T(8,128)(2,1)S(1)}, u32[]{:S(2)}, u32[]{:S(2)}) collective-permute-start(bf16[32,640]{1,0:T(8,128)(2,1)S(1)} %get-tuple-element.23), channel_id=1, source_target_pairs={{0,2},{1,3},{2,0},{3,1},{4,6},{5,7},{6,4},{7,5},{8,10},{9,11},{10,... | collective-permute-start | bytes 122888 | tf_op jit(solution)/shard_map/ppermute | solution.py:387
  158.5 5.8 %collective-permute-start.29 = (bf16[32,640]{1,0:T(8,128)(2,1)S(1)}, bf16[32,640]{1,0:T(8,128)(2,1)S(1)}, u32[]{:S(2)}, u32[]{:S(2)}) collective-permute-start(bf16[32,640]{1,0:T(8,128)(2,1)S(1)} %get-tuple-element.24), channel_id=1, source_target_pairs={{0,3},{1,2},{2,1},{3,0},{4,7},{5,6},{6,5},{7,4},{8,11},{9,10},{10,... | collective-permute-start | bytes 122888 | tf_op jit(solution)/shard_map/ppermute | solution.py:387
  164.3 23.9 %copy-start.24 = (s32[768]{0:T(1024)S(1)}, s32[768]{0:T(1024)}, u32[]{:S(2)}) copy-start(s32[768]{0:T(1024)} %param.17) | copy-start | bytes 9220
  171.8 5.2 %collective-permute-start.30 = (bf16[8,1152]{1,0:T(8,128)(2,1)S(1)}, bf16[8,1152]{1,0:T(8,128)(2,1)S(1)}, u32[]{:S(2)}, u32[]{:S(2)}) collective-permute-start(bf16[8,1152]{1,0:T(8,128)(2,1)S(1)} %get-tuple-element.27), channel_id=1, source_target_pairs={{0,1},{1,0},{2,3},{3,2},{4,5},{5,4},{6,7},{7,6},{8,9},{9,8},{10,11... | collective-permute-start | bytes 55304 | tf_op jit(solution)/shard_map/ppermute | solution.py:387
  171.9 5.1 %collective-permute-start.31 = (bf16[8,1152]{1,0:T(8,128)(2,1)S(1)}, bf16[8,1152]{1,0:T(8,128)(2,1)S(1)}, u32[]{:S(2)}, u32[]{:S(2)}) collective-permute-start(bf16[8,1152]{1,0:T(8,128)(2,1)S(1)} %get-tuple-element.28), channel_id=1, source_target_pairs={{0,2},{1,3},{2,0},{3,1},{4,6},{5,7},{6,4},{7,5},{8,10},{9,11},{10,... | collective-permute-start | bytes 55304 | tf_op jit(solution)/shard_map/ppermute | solution.py:387
  172.9 5.6 %collective-permute-start.32 = (bf16[8,1152]{1,0:T(8,128)(2,1)S(1)}, bf16[8,1152]{1,0:T(8,128)(2,1)S(1)}, u32[]{:S(2)}, u32[]{:S(2)}) collective-permute-start(bf16[8,1152]{1,0:T(8,128)(2,1)S(1)} %get-tuple-element.29), channel_id=1, source_target_pairs={{0,3},{1,2},{2,1},{3,0},{4,7},{5,6},{6,5},{7,4},{8,11},{9,10},{10,... | collective-permute-start | bytes 55304 | tf_op jit(solution)/shard_map/ppermute | solution.py:387
  179.2 1.2 collective-permute-start.33
  180.4 3.9 %collective-permute-start.34 = (bf16[16,1024]{1,0:T(8,128)(2,1)S(1)}, bf16[16,1024]{1,0:T(8,128)(2,1)S(1)}, u32[]{:S(2)}, u32[]{:S(2)}) collective-permute-start(bf16[16,1024]{1,0:T(8,128)(2,1)S(1)} %pad_maximum_fusion), channel_id=1, source_target_pairs={{0,8},{4,12},{8,0},{12,4},{16,24},{20,28},{24,16},{28,20},{1,9},{5... | collective-permute-start | bytes 98312 | tf_op jit(solution)/shard_map/ppermute | solution.py:387
  181.8 3.9 %collective-permute-start.35 = (bf16[16,1024]{1,0:T(8,128)(2,1)S(1)}, bf16[16,1024]{1,0:T(8,128)(2,1)S(1)}, u32[]{:S(2)}, u32[]{:S(2)}) collective-permute-start(bf16[16,1024]{1,0:T(8,128)(2,1)S(1)} %pad_maximum_fusion), channel_id=1, source_target_pairs={{0,16},{4,20},{8,24},{12,28},{16,0},{20,4},{24,8},{28,12},{1,17},{... | collective-permute-start | bytes 98312 | tf_op jit(solution)/shard_map/ppermute | solution.py:387
  183.4 4.8 %collective-permute-start.36 = (bf16[16,1024]{1,0:T(8,128)(2,1)S(1)}, bf16[16,1024]{1,0:T(8,128)(2,1)S(1)}, u32[]{:S(2)}, u32[]{:S(2)}) collective-permute-start(bf16[16,1024]{1,0:T(8,128)(2,1)S(1)} %pad_maximum_fusion), channel_id=1, source_target_pairs={{0,24},{4,28},{8,16},{12,20},{16,8},{20,12},{24,0},{28,4},{1,25},{... | collective-permute-start | bytes 98312 | tf_op jit(solution)/shard_map/ppermute | solution.py:387
  (2 other events, 1.5 us)

commit v2 on v1

--- a/solution.py
+++ b/solution.py
@@ -14,6 +14,7 @@
 DV = 2048
 VHDIM = 128
 VPAD = 8
+FW_ROWS = 16
 LANES = 128
 EPS = 1e-5
 F32 = jnp.float32
@@ -43,6 +44,16 @@
 
 def params():
     return pltpu.CompilerParams(vmem_limit_bytes=VMEM_LIMIT)
+
+
+def cost(micros):
+    return pl.CostEstimate(
+        flops=int(micros * 1e9) + 1, bytes_accessed=int(micros * 1e6) + 1, transcendentals=0
+    )
+
+
+def after(value, *others):
+    return lax.optimization_barrier((value, *others))[0]
 
 
 def strict_upper(rows):
@@ -74,6 +85,23 @@
         chosen = pick_rows(position, c * step, step, rows)
         out_ref[c * step : (c + 1) * step, :D] = dot(chosen, x_ref[...]).astype(BF16)
         out_ref[c * step : (c + 1) * step, D:] = dot(chosen, label, NT).astype(BF16)
+
+
+def fold_kernel(weight_ref, head_ref, qkv_ref, out_ref):
+    rows, cols = qkv_ref.shape[1:]
+    out_ref[:, :rows, :] = qkv_ref[...]
+    folded = dot(head_ref[...], weight_ref[...], NT)
+    folded = folded[0:2] + folded[2:4] + folded[4:6]
+    one = folded.astype(BF16).astype(F32)
+    two = (folded - one).astype(BF16).astype(F32)
+    parts = (one, two, folded - one - two)
+    chunks = folded.shape[1] // cols
+    blank = jnp.zeros((FW_ROWS - 2 * chunks, cols), F32)
+    for t in range(3):
+        lines = [
+            parts[t][j : j + 1, c * cols : (c + 1) * cols] for j in range(2) for c in range(chunks)
+        ]
+        out_ref[t, rows:, :] = jnp.concatenate(lines + [blank], axis=0).astype(BF16)
 
 
 def encode_kernel(
@@ -193,8 +221,8 @@
     n = len(plan)
     vec_in, refs = refs[:n_mp], refs[n_mp:]
     pieces, refs = refs[:n], refs[n:]
-    vec_ref, attended_ref, qkv_ref, prob_ref = refs[:4]
-    scratch, refs = refs[4 : 4 + n], refs[4 + n :]
+    vec_ref, attended_ref, qkv_ref, prob_ref, fw_ref = refs[:5]
+    scratch, refs = refs[5 : 5 + n], refs[5 + n :]
     vec, blocks, sems = refs
     copies = fetch(pieces, scratch, sems)
     e, m = where_ref[0], where_ref[1]
@@ -209,11 +237,15 @@
         blocks[j] = normed[:, j * width : (j + 1) * width]
     cols = attended_ref.shape[1]
     totals = [jnp.zeros((rows, cols), F32) for _ in range(3)]
+    fw = jnp.zeros(fw_ref.shape, F32)
     for i, (k, lo, size) in enumerate(plan):
         copies[i].wait()
         block = blocks[e ^ k][:, lo : lo + size]
         for t in range(3):
-            totals[t] = totals[t] + dot(block, scratch[i][t])
+            totals[t] = totals[t] + dot(block, scratch[i][t, :size, :])
+            if scratch[i].shape[1] > size:
+                fw = fw + scratch[i][t, size:, :].astype(F32)
+    fw_ref[...] = fw
     parts = [total.astype(BF16) for total in totals]
     for t in range(3):
         qkv_ref[t] = parts[t]
@@ -268,7 +300,13 @@
     width = DV // n_ev
     for j in range(n_ev):
         blocks[j] = normed[:, j * width : (j + 1) * width]
-    pre = jnp.zeros((rows, fw_ref.shape[1]), F32)
+    hidden = scratch[0].shape[1]
+    pre = jnp.zeros((rows, hidden), F32)
+    chunks = hidden // fw_ref.shape[1]
+    fw = [
+        jnp.concatenate([fw_ref[j * chunks + c : j * chunks + c + 1, :] for c in range(chunks)], axis=1)
+        for j in range(2)
+    ]
     for i, (k, lo, size) in enumerate(plan):
         copies[i].wait()
         pre = pre + dot(blocks[e ^ k][:, lo : lo + size], scratch[i][...])
@@ -278,8 +316,8 @@
     outcome = []
     for j in range(2):
         base = jnp.sum(mid * head_ref[j : j + 1, :], axis=-1, keepdims=True) + bias_ref[j]
-        outcome.append(jnp.sum(act * fw_ref[j : j + 1, :], axis=-1, keepdims=True) + first * base)
-    chosen = jnp.where(meta_ref[:, 0:1] > 0.5, fw_ref[1:2, :], fw_ref[0:1, :])
+        outcome.append(jnp.sum(act * fw[j], axis=-1, keepdims=True) + first * base)
+    chosen = jnp.where(meta_ref[:, 0:1] > 0.5, fw[1], fw[0])
     slope = (chosen * sigma * (1.0 + pre * (1.0 - sigma))).astype(BF16)
     for i, (k, lo, size) in enumerate(plan):
         grads[e ^ k, :, lo : lo + size] = dot(slope, scratch[i][...], NT)
@@ -341,9 +379,9 @@
     three = [jnp.concatenate(parts, axis=1) for parts in three]
     for i, (k, lo, size) in enumerate(plan):
         copies[i].wait()
-        part = dot(three[0], scratch[i][0], NT)
-        part = part + dot(three[1], scratch[i][1], NT)
-        part = part + dot(three[2], scratch[i][2], NT)
+        part = dot(three[0], scratch[i][0, :size, :], NT)
+        part = part + dot(three[1], scratch[i][1, :size, :], NT)
+        part = part + dot(three[2], scratch[i][2, :size, :], NT)
         grads[e ^ k, :, lo : lo + size] = part
     width = DV // n_ev
     vec = vec_ref[...]
@@ -387,20 +425,58 @@
     return lax.ppermute(x, axis, [(i, i ^ k) for i in range(size)])
 
 
-def gather_weights(shard, n_ev, row_axis):
-    rows = shard.shape[row_axis]
+def first_hop(shard, n_ev):
     if n_ev != 8:
-        pieces = [shard] + [swap(shard, "events", n_ev, k) for k in range(1, n_ev)]
-        return pieces, [(k, 0, rows) for k in range(n_ev)]
-    half = rows // 2
-    from_x = swap(shard, "events", n_ev, 2)
-    from_y = swap(shard, "events", n_ev, 4)
-    low = swap(lax.slice_in_dim(from_x, 0, half, axis=row_axis), "events", n_ev, 4)
-    high = swap(lax.slice_in_dim(from_y, half, rows, axis=row_axis), "events", n_ev, 2)
-    near = [shard, from_x, from_y, low, high]
-    plan = [(0, 0, rows), (2, 0, rows), (4, 0, rows), (6, 0, half), (6, half, half)]
-    far = [swap(piece, "events", n_ev, 1) for piece in near]
-    return near + far, plan + [(k ^ 1, lo, size) for k, lo, size in plan]
+        return [shard] + [swap(shard, "events", n_ev, k) for k in range(1, n_ev)]
+    return [shard, swap(shard, "events", n_ev, 2), swap(shard, "events", n_ev, 4)]
+
+
+def halves_kernel(half, low_ref, high_ref, low_out, high_out):
+    low_out[...] = low_ref[...]
+    high_out[...] = high_ref[:, half:, :] if len(high_ref.shape) == 3 else high_ref[...]
+
+
+def halves_of(pieces, half):
+    tail = pieces[1].shape[-1]
+    if pieces[1].ndim == 2:
+        low, high = (half, tail), (half, tail)
+        block = [pl.BlockSpec(low, lambda i: (0, 0)), pl.BlockSpec(high, lambda i: (1, 0))]
+    else:
+        lead, rows = pieces[1].shape[:2]
+        low, high = (lead, half, tail), (lead, rows - half, tail)
+        block = [pl.BlockSpec(low, lambda i: (0, 0, 0)), vmem()]
+    outs = [pl.BlockSpec(shape, lambda i, n=len(low): (0,) * n) for shape in (low, high)]
+    return pl.pallas_call(
+        functools.partial(halves_kernel, half),
+        grid=(1,),
+        out_shape=[jax.ShapeDtypeStruct(low, BF16), jax.ShapeDtypeStruct(high, BF16)],
+        in_specs=block,
+        out_specs=outs,
+        compiler_params=params(),
+        cost_estimate=cost(0),
+        name="halves",
+    )(pieces[1], pieces[2])
+
+
+def second_hop(low, high, n_ev):
+    return [swap(low, "events", n_ev, 4), swap(high, "events", n_ev, 2)]
+
+
+def across(pieces, n_ev):
+    return [swap(piece, "events", n_ev, 1) for piece in pieces]
+
+
+def direct_plan(n_ev, width):
+    order = range(n_ev) if n_ev != 8 else (0, 2, 4, 6, 1, 3, 5, 7)
+    return [(k, 0, width) for k in order]
+
+
+def hop_plan(n_ev, width):
+    if n_ev != 8:
+        return direct_plan(n_ev, width)
+    half = width // 2
+    near = [(0, 0, width), (2, 0, width), (4, 0, width), (6, 0, half), (6, half, half)]
+    return near + [(k ^ 1, lo, size) for k, lo, size in near]
 
 
 def gather_events(block, n_ev):
@@ -449,6 +525,7 @@
         in_specs=[smem(), vmem(), vmem()],
         out_specs=vmem(),
         compiler_params=params(),
+        cost_estimate=cost(0),
         name="pack",
     )(where, ids, event_x)
     got = lax.all_to_all(
@@ -456,8 +533,7 @@
         tiled=True,
     ).reshape(rows_dev, D + LANES)
 
-    qkv_pieces, qkv_plan = gather_weights(visit_qkv, n_ev, 1)
-    ffn_pieces, ffn_plan = gather_weights(ffn_in, n_ev, 0)
+    ffn_first = first_hop(ffn_in, n_ev)
 
     head_t = head_weight.T
     width = DV // n_ev
@@ -465,12 +541,25 @@
     head_hi = own_head.astype(BF16)
     head_mid = (own_head - head_hi.astype(F32)).astype(BF16)
     head_lo = (own_head - head_hi.astype(F32) - head_mid.astype(F32)).astype(BF16)
-    fw = dot(jnp.concatenate([head_hi, head_mid, head_lo], axis=0), ffn_out, NT)
-    fw = fw[0:2] + fw[2:4] + fw[4:6]
-    step = 1
-    while step < n_ev:
-        fw = fw + swap(fw, "events", n_ev, step)
-        step *= 2
+    heads = jnp.concatenate([head_hi, head_mid, head_lo, jnp.zeros((2, width), BF16)], axis=0)
+    qkv_shard = pl.pallas_call(
+        fold_kernel,
+        out_shape=jax.ShapeDtypeStruct((3, width + FW_ROWS, cols), BF16),
+        in_specs=[vmem()] * 3,
+        out_specs=vmem(),
+        compiler_params=params(),
+        cost_estimate=cost(30),
+        name="fold",
+    )(ffn_out, heads, after(visit_qkv, *ffn_first[1:]))
+    qkv_first = [qkv_shard] + first_hop(after(qkv_shard, got), n_ev)[1:]
+    qkv_plan = hop_plan(n_ev, width)
+    ffn_plan = hop_plan(n_ev, width)
+    two_hops = n_ev == 8
+    if two_hops:
+        ffn_halves = halves_of(ffn_first, width // 2)
+        ffn_far = across(ffn_first, n_ev)
+        qkv_far = across(qkv_first[:1], n_ev)
+        got = after(got, *ffn_far, *ffn_halves, *qkv_far)
 
     def spread_rows(values, fill):
         values = values.astype(F32).reshape(n_mp, visits_dev)
@@ -498,21 +587,33 @@
             pltpu.SemaphoreType.DMA((3,)),
         ],
         compiler_params=params(),
+        cost_estimate=cost(0),
         name="encode",
     )(visit_count, got, enc_gain.reshape(1, D), enc_qkv, enc_out)
 
+    if two_hops:
+        qkv_halves = halves_of([qkv_first[0]] + [after(p, vec) for p in qkv_first[1:]], width // 2)
+        vec = after(vec, *qkv_halves)
     vecs = [vec] + [swap(vec, "mp", n_mp, k) for k in range(1, n_mp)]
+    if two_hops:
+        qkv_second = second_hop(*qkv_halves, n_ev)
+        ffn_second = second_hop(*[after(piece, *vecs[1:]) for piece in ffn_halves], n_ev)
+        qkv_far += across([after(piece, *vecs[1:]) for piece in qkv_first[1:]], n_ev)
+        qkv_pieces = qkv_first + qkv_second + qkv_far + across(qkv_second, n_ev)
+    else:
+        qkv_pieces = qkv_first
     n_q = len(qkv_plan)
-    all_vec, attended, qkv, prob = pl.pallas_call(
+    all_vec, attended, qkv, prob, fw = pl.pallas_call(
         functools.partial(project_kernel, n_mp, n_ev, qkv_plan),
         out_shape=(
             jax.ShapeDtypeStruct((group, DV), F32),
             jax.ShapeDtypeStruct((group, cols), BF16),
             jax.ShapeDtypeStruct((3, group, cols), BF16),
             jax.ShapeDtypeStruct((cols // VHDIM, group, group), F32),
+            jax.ShapeDtypeStruct((FW_ROWS, cols), F32),
         ),
         in_specs=[smem()] + [vmem()] * (3 + n_mp) + [hbm()] * n_q,
-        out_specs=(vmem(),) * 4,
+        out_specs=(vmem(),) * 5,
         scratch_shapes=[pltpu.VMEM(piece.shape, BF16) for piece in qkv_pieces]
         + [
             pltpu.VMEM((n_mp, VPAD, DV), F32),
@@ -520,10 +621,16 @@
             pltpu.SemaphoreType.DMA((n_q,)),
         ],
         compiler_params=params(),
+        cost_estimate=cost(0),
         name="project",
     )(where, meta, patient_row, visit_gain.reshape(1, DV), *vecs, *qkv_pieces)
 
     attns = [attended] + [swap(attended, "mp", n_mp, k) for k in range(1, n_mp)]
+    if two_hops:
+        ffn_second = [after(piece, *attns[1:]) for piece in ffn_second]
+        ffn_pieces = ffn_first + ffn_second + ffn_far + across(ffn_second, n_ev)
+    else:
+        ffn_pieces = ffn_first
     n_f = len(ffn_plan)
     ffn_outs = pl.pallas_call(
         functools.partial(ffn_kernel, n_mp, n_ev, ffn_plan),
@@ -539,6 +646,7 @@
             pltpu.SemaphoreType.DMA((n_f,)),
         ],
         compiler_params=params(),
+        cost_estimate=cost(7),
         name="ffn",
     )(where, meta, all_vec, ffn_gain.reshape(1, DV), fw, head_t, head_bias, *attns, *ffn_pieces)
     mid = ffn_outs[n_mp]
@@ -557,6 +665,7 @@
             pltpu.SemaphoreType.DMA((n_q,)),
         ],
         compiler_params=params(),
+        cost_estimate=cost(7),
         name="back",
     )(
         where, meta, all_vec, mid, ffn_gain.reshape(1, DV), visit_gain.reshape(1, DV), head_t, qkv,
@@ -570,6 +679,7 @@
         in_specs=[smem()] + [vmem()] * (1 + n_mp),
         out_specs=vmem(),
         compiler_params=params(),
+        cost_estimate=cost(0),
         name="finish",
     )(visit_count, vec, *shares)
 

time: 191 us -> 148 us (0.77)
  waiting for transfers between devices: 85.8 us -> 53.2 us
  starting transfers between devices: 47 us -> 37.4 us
  Pallas kernels: 33.9 us -> 39.8 us
  local copies, waits for them, and re-layouts: 19.1 us -> 14.5 us
    ppermute x37 -> x34, waiting for transfers between devices: 85.8 us -> 38.7 us  [swap(): return lax.ppermute(x, axis, [(i, i ^ k) for i in range(size)])]
    all_to_all x1, waiting for transfers between devices: 0.01 us -> 14.5 us  [local(): lax.all_to_all(send.reshape(n_ev, rows_dev // n_ev, D + LANES), 'events',...]
    ppermute x37 -> x34, starting transfers between devices: 42.8 us -> 33.7 us  [swap(): return lax.ppermute(x, axis, [(i, i ^ k) for i in range(size)])]
    slice x4 -> x0, local copies, waits for them, and re-layouts: 4.19 us -> none  [the longest x2 2.1 us: gather_weights(): lax.slice_in_dim(from_x, 0, half, axis=row_axis)]
    pallas_call x0 -> x3, Pallas kernels: none -> 3.59 us  [the longest x2 2.28 us: halves_of(): pl.pallas_call(functools.partial(halves_kernel, half), grid=(1,), out_sha...]
    unnamed x61 -> x65, local copies, waits for them, and re-layouts: 12.9 us -> 12.3 us
  transfers between devices with their start and end apart: 38 -> 35, of which waited for: 16 -> 18; matrix products, arithmetic and copies ran while one was open for 4% -> 2% of each run, Pallas kernels for 10% -> 16%
where the time goes in v2:
time: 148 us
  waiting for transfers between devices  53.2 us (36%)
  Pallas kernels  39.8 us (27%)
  starting transfers between devices  37.4 us (25%)
  local copies, waits for them, and re-layouts  14.5 us (10%)
  matrix products  1.76 us (1%)
    ppermute x34, waiting for transfers between devices, swap(): return lax.ppermute(x, axis, [(i, i ^ k) for i in range(size)])  38.7 us
    ppermute x34, starting transfers between devices, swap(): return lax.ppermute(x, axis, [(i, i ^ k) for i in range(size)])  33.7 us
    all_to_all x1, waiting for transfers between devices, local(): lax.all_to_all(send.reshape(n_ev, rows_dev // n_ev, D + LANES), 'events',...  14.5 us
    unnamed x65, local copies, waits for them, and re-layouts  12.3 us
    pallas_call x1, Pallas kernels, local(): pl.pallas_call(functools.partial(encode_kernel, visits_dev), out_shape=ja...  12.2 us
    pallas_call x1, Pallas kernels, local(): pl.pallas_call(functools.partial(back_kernel, n_mp, n_ev, qkv_plan), out_...  8.33 us
    pallas_call x1, Pallas kernels, local(): pl.pallas_call(functools.partial(ffn_kernel, n_mp, n_ev, ffn_plan), out_s...  6.95 us
    pallas_call x1, Pallas kernels, local(): pl.pallas_call(functools.partial(project_kernel, n_mp, n_ev, qkv_plan), o...  4.39 us
  transfers between devices with their start and end apart: 35, of which 18 were waited for; matrix products, arithmetic and copies ran while one was open for 2% of the time, Pallas kernels for 16%

profile of v2, /device:TPU:0, one launch (start us, length us, event | category | flops | bytes accessed | tf_op | source)
XLA Modules:
  0.0 147.7 jit_solution(15823312489928703369)
XLA Ops:
  0.6 3.0 %collective-permute-start.1 = (bf16[256,2048]{1,0:T(8,128)(2,1)}, bf16[256,2048]{1,0:T(8,128)(2,1)}, u32[]{:S(2)}, u32[]{:S(2)}) collective-permute-start(bf16[256,2048]{1,0:T(8,128)(2,1)} %refs_4_.1), channel_id=1, source_target_pairs={{0,8},{4,12},{8,0},{12,4},{16,24},{20,28},{24,16},{28,20},{1,9},{5... | collective-permute-start | bytes 3145736 | tf_op jit(solution)/shard_map/ppermute | solution.py:425
  3.6 1.5 %collective-permute-start.3 = (bf16[256,2048]{1,0:T(8,128)(2,1)}, bf16[256,2048]{1,0:T(8,128)(2,1)}, u32[]{:S(2)}, u32[]{:S(2)}) collective-permute-start(bf16[256,2048]{1,0:T(8,128)(2,1)} %refs_4_.1), channel_id=1, source_target_pairs={{0,16},{4,20},{8,24},{12,28},{16,0},{20,4},{24,8},{28,12},{1,17},{... | collective-permute-start | bytes 3145736 | tf_op jit(solution)/shard_map/ppermute | solution.py:425
  5.2 0.7 reshape.70.ids_ref
  5.9 1.4 copy-done.1
  7.3 3.7 %pack.1 = bf16[768,1152]{1,0:T(8,128)(2,1)} custom-call(s32[2]{0:T(128)S(1)} %pad_add_fusion.where_ref, s32[1,768]{1,0:T(1,128)S(1)} %reshape.70.ids_ref, bf16[768,1024]{1,0:T(8,128)(2,1)S(1)} %copy-done.1), custom_call_target="tpu_custom_call" | custom-call | flops 1 | bytes 1 | tf_op jit(solution)/shard_map/pack/pallas_call | solution.py:522
  11.0 3.7 %all-to-all-start = ((bf16[8,96,1152]{2,1,0:T(8,128)(2,1)}), bf16[8,96,1152]{2,1,0:T(8,128)(2,1)S(1)}, u32[]{:S(2)}, u32[]{:S(2)}) async-start(bf16[8,96,1152]{2,1,0:T(8,128)(2,1)} %bitcast.3), calls=%async_computation | async-start | bytes 3538944 | tf_op jit(solution)/shard_map/all_to_all | solution.py:531
  14.9 13.0 %collective-permute-done.1.low_ref.refs_5_ = bf16[256,2048]{1,0:T(8,128)(2,1)} collective-permute-done((bf16[256,2048]{1,0:T(8,128)(2,1)}, bf16[256,2048]{1,0:T(8,128)(2,1)}, u32[]{:S(2)}, u32[]{:S(2)}) %collective-permute-start.1) | collective-permute-done | bytes 1048608 | tf_op jit(solution)/shard_map/ppermute | solution.py:425
  27.9 2.1 %collective-permute-done.3.high_ref.refs_6_ = bf16[256,2048]{1,0:T(8,128)(2,1)} collective-permute-done((bf16[256,2048]{1,0:T(8,128)(2,1)}, bf16[256,2048]{1,0:T(8,128)(2,1)}, u32[]{:S(2)}, u32[]{:S(2)}) %collective-permute-start.3) | collective-permute-done | bytes 1048608 | tf_op jit(solution)/shard_map/ppermute | solution.py:425
  30.5 1.1 copy-done.8
  31.7 1.3 fold.1.refs_4_
  33.0 14.5 %all-to-all-done = bf16[8,96,1152]{2,1,0:T(8,128)(2,1)S(1)} async-done(((bf16[8,96,1152]{2,1,0:T(8,128)(2,1)}), bf16[8,96,1152]{2,1,0:T(8,128)(2,1)S(1)}, u32[]{:S(2)}, u32[]{:S(2)}) %all-to-all-start) | async-done | bytes 1769504 | tf_op jit(solution)/shard_map/all_to_all | solution.py:531
  47.5 1.6 %collective-permute-start.7 = (bf16[3,272,512]{2,1,0:T(8,128)(2,1)}, bf16[3,272,512]{2,1,0:T(8,128)(2,1)S(1)}, u32[]{:S(2)}, u32[]{:S(2)}) collective-permute-start(bf16[3,272,512]{2,1,0:T(8,128)(2,1)} %fold.1.refs_4_), channel_id=1, source_target_pairs={{0,16},{4,20},{8,24},{12,28},{16,0},{20,4},{24,8},{28,12},{1,17},{... | collective-permute-start | bytes 2506760 | tf_op jit(solution)/shard_map/ppermute | solution.py:425
  49.5 2.2 %halves.2 = (bf16[128,2048]{1,0:T(8,128)(2,1)}, bf16[128,2048]{1,0:T(8,128)(2,1)}) custom-call(bf16[256,2048]{1,0:T(8,128)(2,1)} %collective-permute-done.1.low_ref.refs_5_, bf16[256,2048]{1,0:T(8,128)(2,1)} %collective-permute-done.3.high_ref.refs_6_), custom_call_target="tpu_custom_call" | custom-call | flops 1 | bytes 1 | tf_op jit(solution)/shard_map/halves/pallas_call | solution.py:449
  51.8 12.2 %encode.1.refs_0_.own_ref = bf16[8,2048]{1,0:T(8,128)(2,1)S(1)} custom-call(s32[6]{0:T(128)S(1)} %copy-done.4, bf16[768,1152]{1,0:T(8,128)(2,1)S(1)} %bitcast.23, f32[1,1024]{1,0:T(1,128)S(1)} %bitcast.26, bf16[1024,3072]{1,0:T(8,128)(2,1)} %qkv_ref.2, bf16[1024,1024]{1,0:T(8,128)(2,1)S(1)} %copy-done), custom_call_target="tpu_custom_call" | custom-call | flops 1 | bytes 1 | tf_op jit(solution)/shard_map/encode/pallas_call | solution.py:574
  64.0 1.3 collective-permute-done.7.high_ref.refs_6_
  65.3 1.5 %collective-permute-done.6.low_ref.refs_5_ = bf16[3,272,512]{2,1,0:T(8,128)(2,1)S(1)} collective-permute-done((bf16[3,272,512]{2,1,0:T(8,128)(2,1)}, bf16[3,272,512]{2,1,0:T(8,128)(2,1)S(1)}, u32[]{:S(2)}, u32[]{:S(2)}) %collective-permute-start.6) | collective-permute-done | bytes 835616 | tf_op jit(solution)/shard_map/ppermute | solution.py:425
  66.9 0.7 collective-permute-start.11
  67.6 1.7 %collective-permute-start.12 = (bf16[3,144,512]{2,1,0:T(8,128)(2,1)S(1)}, bf16[3,144,512]{2,1,0:T(8,128)(2,1)S(1)}, u32[]{:S(2)}, u32[]{:S(2)}) collective-permute-start(bf16[3,144,512]{2,1,0:T(8,128)(2,1)S(1)} %get-tuple-element.41), channel_id=1, source_target_pairs={{0,8},{4,12},{8,0},{12,4},{16,24},{20,28},{24,16},{28,20},{1,9},{5... | collective-permute-start | bytes 1327112 | tf_op jit(solution)/shard_map/ppermute | solution.py:425
  69.4 3.4 %collective-permute-start.10 = (bf16[8,2048]{1,0:T(8,128)(2,1)S(1)}, bf16[8,2048]{1,0:T(8,128)(2,1)S(1)}, u32[]{:S(2)}, u32[]{:S(2)}) collective-permute-start(bf16[8,2048]{1,0:T(8,128)(2,1)S(1)} %encode.1.refs_0_.own_ref), channel_id=1, source_target_pairs={{0,3},{1,2},{2,1},{3,0},{4,7},{5,6},{6,5},{7,4},{8,11},{9,10},{10,... | collective-permute-start | bytes 98312 | tf_op jit(solution)/shard_map/ppermute | solution.py:425
  72.8 0.9 collective-permute-start.8
  73.7 1.3 collective-permute-done.10.refs_3_
  75.1 2.5 %collective-permute-done.9.refs_2_ = bf16[8,2048]{1,0:T(8,128)(2,1)S(1)} collective-permute-done((bf16[8,2048]{1,0:T(8,128)(2,1)S(1)}, bf16[8,2048]{1,0:T(8,128)(2,1)S(1)}, u32[]{:S(2)}, u32[]{:S(2)}) %collective-permute-start.9) | collective-permute-done | bytes 32800 | tf_op jit(solution)/shard_map/ppermute | solution.py:425
  77.6 0.5 collective-permute-start.14
  78.4 1.5 %collective-permute-start.20 = (bf16[128,2048]{1,0:T(8,128)(2,1)}, bf16[128,2048]{1,0:T(8,128)(2,1)}, u32[]{:S(2)}, u32[]{:S(2)}) collective-permute-start(bf16[128,2048]{1,0:T(8,128)(2,1)} %get-tuple-element.48), channel_id=1, source_target_pairs={{0,16},{4,20},{8,24},{12,28},{16,0},{20,4},{24,8},{28,12},{1,17},{... | collective-permute-start | bytes 1572872 | tf_op jit(solution)/shard_map/ppermute | solution.py:425
  80.0 1.1 collective-permute-done.15.refs_12_
  82.0 0.9 collective-permute-done.16.refs_13_
  82.9 4.4 %project.1 = (f32[32,2048]{1,0:T(8,128)S(1)}, bf16[32,512]{1,0:T(8,128)(2,1)S(1)}, bf16[3,32,512]{2,1,0:T(8,128)(2,1)S(1)}, f32[4,32,32]{2,1,0:T(8,128)S(1)}, f32[16,512]{1,0:T(8,128)S(1)}) custom-call(s32[2]{0:T(128)S(1)} %pad_add_fusion.where_ref, f32[32,3]{1,0:T(8,128)S(1)} %copy.24.meta_ref, f32[1,32]{1,0:T(1,128)S(1)} %reshape_reshape.3.patient_ref, ...), custom_call_target="tpu_custom_call" | custom-call | flops 1 | bytes 1 | tf_op jit(solution)/shard_map/project/pallas_call | solution.py:606
  87.3 0.7 copy-done.9
  88.0 0.6 copy-done.12
  88.6 0.6 copy-done.14
  89.3 0.6 copy-done.18
  89.9 1.5 collective-permute-start.19
  91.3 0.6 collective-permute-start.18
  91.9 2.4 %collective-permute-start.17 = (bf16[32,512]{1,0:T(8,128)(2,1)S(1)}, bf16[32,512]{1,0:T(8,128)(2,1)S(1)}, u32[]{:S(2)}, u32[]{:S(2)}) collective-permute-start(bf16[32,512]{1,0:T(8,128)(2,1)S(1)} %get-tuple-element.47.refs_0_), channel_id=1, source_target_pairs={{0,1},{1,0},{2,3},{3,2},{4,5},{5,4},{6,7},{7,6},{8,9},{9,8},{10,11... | collective-permute-start | bytes 98312 | tf_op jit(solution)/shard_map/ppermute | solution.py:425
  94.2 0.6 copy-done.16
  94.9 1.1 collective-permute-done.19.refs_3_
  96.3 0.6 copy-done.20
  96.9 0.6 copy-done.22
  98.1 1.7 %collective-permute-done.22.refs_12_ = bf16[128,2048]{1,0:T(8,128)(2,1)} collective-permute-done((bf16[128,2048]{1,0:T(8,128)(2,1)}, bf16[128,2048]{1,0:T(8,128)(2,1)}, u32[]{:S(2)}, u32[]{:S(2)}) %collective-permute-start.22) | collective-permute-done | bytes 524320 | tf_op jit(solution)/shard_map/ppermute | solution.py:425
  99.8 0.7 collective-permute-done.23.refs_13_
  100.6 1.2 copy-done.7
  101.8 0.9 copy-done.10
  102.7 0.8 copy-done.17
  103.5 0.8 copy-done.19
  104.2 0.8 copy-done.21
  105.0 0.8 copy-done.23
  105.8 7.0 %ffn.1 = (bf16[32,640]{1,0:T(8,128)(2,1)S(1)}, bf16[32,640]{1,0:T(8,128)(2,1)S(1)}, bf16[32,640]{1,0:T(8,128)(2,1)S(1)}, bf16[32,640]{1,0:T(8,128)(2,1)S(1)}, f32[32,2048]{1,0:T(8,128)S(1)}) custom-call(s32[2]{0:T(128)S(1)} %pad_add_fusion.where_ref, f32[32,3]{1,0:T(8,128)S(1)} %copy.24.meta_ref, f32[32,2048]{1,0:T(8,128)S(1)} %copy-done.10, ...), custom_call_target="tpu_custom_call" | custom-call | flops 7000000000 | bytes 7000001 | tf_op jit(solution)/shard_map/ffn/pallas_call | solution.py:635
  112.7 1.3 collective-permute-start.24
  114.0 1.5 %collective-permute-start.25 = (bf16[32,640]{1,0:T(8,128)(2,1)S(1)}, bf16[32,640]{1,0:T(8,128)(2,1)S(1)}, u32[]{:S(2)}, u32[]{:S(2)}) collective-permute-start(bf16[32,640]{1,0:T(8,128)(2,1)S(1)} %get-tuple-element.57), channel_id=1, source_target_pairs={{0,2},{1,3},{2,0},{3,1},{4,6},{5,7},{6,4},{7,5},{8,10},{9,11},{10,... | collective-permute-start | bytes 122888 | tf_op jit(solution)/shard_map/ppermute | solution.py:425
  115.6 1.6 %collective-permute-start.26 = (bf16[32,640]{1,0:T(8,128)(2,1)S(1)}, bf16[32,640]{1,0:T(8,128)(2,1)S(1)}, u32[]{:S(2)}, u32[]{:S(2)}) collective-permute-start(bf16[32,640]{1,0:T(8,128)(2,1)S(1)} %get-tuple-element.58), channel_id=1, source_target_pairs={{0,3},{1,2},{2,1},{3,0},{4,7},{5,6},{6,5},{7,4},{8,11},{9,10},{10,... | collective-permute-start | bytes 122888 | tf_op jit(solution)/shard_map/ppermute | solution.py:425
  117.2 2.8 %collective-permute-done.25.refs_2_ = bf16[32,640]{1,0:T(8,128)(2,1)S(1)} collective-permute-done((bf16[32,640]{1,0:T(8,128)(2,1)S(1)}, bf16[32,640]{1,0:T(8,128)(2,1)S(1)}, u32[]{:S(2)}, u32[]{:S(2)}) %collective-permute-start.25) | collective-permute-done | bytes 40992 | tf_op jit(solution)/shard_map/ppermute | solution.py:425
  120.0 1.3 collective-permute-done.26.refs_3_
  121.4 8.3 %back.1 = (bf16[8,1152]{1,0:T(8,128)(2,1)S(1)}, bf16[8,1152]{1,0:T(8,128)(2,1)}, bf16[8,1152]{1,0:T(8,128)(2,1)S(1)}, bf16[8,1152]{1,0:T(8,128)(2,1)S(1)}, f32[32,128]{1,0:T(8,128)S(1)}) custom-call(s32[2]{0:T(128)S(1)} %pad_add_fusion.where_ref, f32[32,3]{1,0:T(8,128)S(1)} %copy.24.meta_ref, f32[32,2048]{1,0:T(8,128)S(1)} %copy-done.11, ...), custom_call_target="tpu_custom_call" | custom-call | flops 7000000000 | bytes 7000001 | tf_op jit(solution)/shard_map/back/pallas_call | solution.py:655
  129.8 2.2 %collective-permute-start.28 = (bf16[8,1152]{1,0:T(8,128)(2,1)S(1)}, bf16[8,1152]{1,0:T(8,128)(2,1)S(1)}, u32[]{:S(2)}, u32[]{:S(2)}) collective-permute-start(bf16[8,1152]{1,0:T(8,128)(2,1)S(1)} %get-tuple-element.62), channel_id=1, source_target_pairs={{0,2},{1,3},{2,0},{3,1},{4,6},{5,7},{6,4},{7,5},{8,10},{9,11},{10,... | collective-permute-start | bytes 55304 | tf_op jit(solution)/shard_map/ppermute | solution.py:425
  132.0 2.2 %collective-permute-start.29 = (bf16[8,1152]{1,0:T(8,128)(2,1)S(1)}, bf16[8,1152]{1,0:T(8,128)(2,1)S(1)}, u32[]{:S(2)}, u32[]{:S(2)}) collective-permute-start(bf16[8,1152]{1,0:T(8,128)(2,1)S(1)} %get-tuple-element.63), channel_id=1, source_target_pairs={{0,3},{1,2},{2,1},{3,0},{4,7},{5,6},{6,5},{7,4},{8,11},{9,10},{10,... | collective-permute-start | bytes 55304 | tf_op jit(solution)/shard_map/ppermute | solution.py:425
  134.3 0.6 reshape.76
  135.0 2.6 %collective-permute-done.29.refs_3_ = bf16[8,1152]{1,0:T(8,128)(2,1)S(1)} collective-permute-done((bf16[8,1152]{1,0:T(8,128)(2,1)S(1)}, bf16[8,1152]{1,0:T(8,128)(2,1)S(1)}, u32[]{:S(2)}, u32[]{:S(2)}) %collective-permute-start.29) | collective-permute-done | bytes 18464 | tf_op jit(solution)/shard_map/ppermute | solution.py:425
  137.5 0.7 finish.1
  138.3 1.2 collective-permute-done.30
  139.4 1.3 collective-permute-start.33
  140.7 1.2 collective-permute-start.32
  141.9 1.0 collective-permute-start.31
  142.9 2.9 %collective-permute-done.31 = bf16[16,1024]{1,0:T(8,128)(2,1)S(1)} collective-permute-done((bf16[16,1024]{1,0:T(8,128)(2,1)S(1)}, bf16[16,1024]{1,0:T(8,128)(2,1)S(1)}, u32[]{:S(2)}, u32[]{:S(2)}) %collective-permute-start.31) | collective-permute-done | bytes 32800 | tf_op jit(solution)/shard_map/ppermute | solution.py:425
  145.9 1.8 %convolution_convert_fusion = bf16[768,1024]{1,0:T(8,128)(2,1)} fusion(bf16[64,1024]{1,0:T(8,128)(2,1)S(1)} %constant_dynamic-update-slice_fusion, s32[64]{0:T(128)S(1)} %compare_select_fusion, s32[768]{0:T(1024)S(1)} %copy-done.26), kind=kOutput, calls=%fused_computation | convolution fusion | flops 101498880 | bytes 1707264 | tf_op jit(solution)/shard_map/dot_general | solution.py:30
  (106 shorter events, 3.6 us)
Async XLA Ops:
  0.6 27.3 %collective-permute-start.1 = (bf16[256,2048]{1,0:T(8,128)(2,1)}, bf16[256,2048]{1,0:T(8,128)(2,1)}, u32[]{:S(2)}, u32[]{:S(2)}) collective-permute-start(bf16[256,2048]{1,0:T(8,128)(2,1)} %refs_4_.1), channel_id=1, source_target_pairs={{0,8},{4,12},{8,0},{12,4},{16,24},{20,28},{24,16},{28,20},{1,9},{5... | collective-permute-start | bytes 3145736 | tf_op jit(solution)/shard_map/ppermute | solution.py:425
  3.6 26.4 %collective-permute-start.3 = (bf16[256,2048]{1,0:T(8,128)(2,1)}, bf16[256,2048]{1,0:T(8,128)(2,1)}, u32[]{:S(2)}, u32[]{:S(2)}) collective-permute-start(bf16[256,2048]{1,0:T(8,128)(2,1)} %refs_4_.1), channel_id=1, source_target_pairs={{0,16},{4,20},{8,24},{12,28},{16,0},{20,4},{24,8},{28,12},{1,17},{... | collective-permute-start | bytes 3145736 | tf_op jit(solution)/shard_map/ppermute | solution.py:425
  5.2 44.0 %collective-permute-start = (bf16[256,2048]{1,0:T(8,128)(2,1)}, bf16[256,2048]{1,0:T(8,128)(2,1)}, u32[]{:S(2)}, u32[]{:S(2)}) collective-permute-start(bf16[256,2048]{1,0:T(8,128)(2,1)} %refs_4_.1), channel_id=1, source_target_pairs={{0,4},{4,0},{8,12},{12,8},{16,20},{20,16},{24,28},{28,24},{1,5},{5... | collective-permute-start | bytes 3145736 | tf_op jit(solution)/shard_map/ppermute | solution.py:425
  5.9 1.4 copy-start.1
  11.0 3.8 %copy-start.5 = (f32[2048,2]{0,1:T(2,128)S(1)}, f32[2048,2]{0,1:T(2,128)}, u32[]{:S(2)}) copy-start(f32[2048,2]{0,1:T(2,128)} %param.30) | copy-start | bytes 49156
  11.0 19.5 %copy-start.6 = (bf16[2048,256]{1,0:T(8,128)(2,1)S(1)}, bf16[2048,256]{1,0:T(8,128)(2,1)}, u32[]{:S(2)}) copy-start(bf16[2048,256]{1,0:T(8,128)(2,1)} %weight_ref.1) | copy-start | bytes 3145732
  11.0 36.5 %all-to-all-start = ((bf16[8,96,1152]{2,1,0:T(8,128)(2,1)}), bf16[8,96,1152]{2,1,0:T(8,128)(2,1)S(1)}, u32[]{:S(2)}, u32[]{:S(2)}) async-start(bf16[8,96,1152]{2,1,0:T(8,128)(2,1)} %bitcast.3), calls=%async_computation | async-start | bytes 3538944 | tf_op jit(solution)/shard_map/all_to_all | solution.py:531
  30.0 21.7 %collective-permute-start.2 = (bf16[256,2048]{1,0:T(8,128)(2,1)}, bf16[256,2048]{1,0:T(8,128)(2,1)}, u32[]{:S(2)}, u32[]{:S(2)}) collective-permute-start(bf16[256,2048]{1,0:T(8,128)(2,1)} %collective-permute-done.1.low_ref.refs_5_), channel_id=1, source_target_pairs={{0,4},{4,0},{8,12},{12,8},{16,20},{20,16},{24,28},{28,24},{1,5},{5... | collective-permute-start | bytes 3145736 | tf_op jit(solution)/shard_map/ppermute | solution.py:425
  30.0 21.7 %collective-permute-start.4 = (bf16[256,2048]{1,0:T(8,128)(2,1)}, bf16[256,2048]{1,0:T(8,128)(2,1)}, u32[]{:S(2)}, u32[]{:S(2)}) collective-permute-start(bf16[256,2048]{1,0:T(8,128)(2,1)} %collective-permute-done.3.high_ref.refs_6_), channel_id=1, source_target_pairs={{0,4},{4,0},{8,12},{12,8},{16,20},{20,16},{24,28},{28,24},{1,5},{5... | collective-permute-start | bytes 3145736 | tf_op jit(solution)/shard_map/ppermute | solution.py:425
  30.5 1.1 copy-start.8
  33.0 18.7 %copy-start.3 = (f32[1024]{0:T(1024)S(1)}, f32[1024]{0:T(1024)}, u32[]{:S(2)}) copy-start(f32[1024]{0:T(1024)} %param.22) | copy-start | bytes 12292
  33.0 18.7 %copy-start.4 = (s32[6]{0:T(128)S(1)}, s32[6]{0:T(128)}, u32[]{:S(2)}) copy-start(s32[6]{0:T(128)} %count_ref.3) | copy-start | bytes 76
  33.0 18.7 %collective-permute-start.5 = (bf16[3,272,512]{2,1,0:T(8,128)(2,1)}, bf16[3,272,512]{2,1,0:T(8,128)(2,1)}, u32[]{:S(2)}, u32[]{:S(2)}) collective-permute-start(bf16[3,272,512]{2,1,0:T(8,128)(2,1)} %fold.1.refs_4_), channel_id=1, source_target_pairs={{0,4},{4,0},{8,12},{12,8},{16,20},{20,16},{24,28},{28,24},{1,5},{5... | collective-permute-start | bytes 2506760 | tf_op jit(solution)/shard_map/ppermute | solution.py:425
  47.5 4.3 %copy-start = (bf16[1024,1024]{1,0:T(8,128)(2,1)S(1)}, bf16[1024,1024]{1,0:T(8,128)(2,1)}, u32[]{:S(2)}) copy-start(bf16[1024,1024]{1,0:T(8,128)(2,1)} %proj_ref.1) | copy-start | bytes 6291460
  47.5 17.9 %collective-permute-start.7 = (bf16[3,272,512]{2,1,0:T(8,128)(2,1)}, bf16[3,272,512]{2,1,0:T(8,128)(2,1)S(1)}, u32[]{:S(2)}, u32[]{:S(2)}) collective-permute-start(bf16[3,272,512]{2,1,0:T(8,128)(2,1)} %fold.1.refs_4_), channel_id=1, source_target_pairs={{0,16},{4,20},{8,24},{12,28},{16,0},{20,4},{24,8},{28,12},{1,17},{... | collective-permute-start | bytes 2506760 | tf_op jit(solution)/shard_map/ppermute | solution.py:425
  49.1 17.7 %collective-permute-start.6 = (bf16[3,272,512]{2,1,0:T(8,128)(2,1)}, bf16[3,272,512]{2,1,0:T(8,128)(2,1)S(1)}, u32[]{:S(2)}, u32[]{:S(2)}) collective-permute-start(bf16[3,272,512]{2,1,0:T(8,128)(2,1)} %fold.1.refs_4_), channel_id=1, source_target_pairs={{0,8},{4,12},{8,0},{12,4},{16,24},{20,28},{24,16},{28,20},{1,9},{5... | collective-permute-start | bytes 2506760 | tf_op jit(solution)/shard_map/ppermute | solution.py:425
  51.8 29.5 %copy-start.28 = (s32[24]{0:T(128)S(1)}, s32[24]{0:T(128)}, u32[]{:S(2)}) copy-start(s32[24]{0:T(128)} %param.19) | copy-start | bytes 292
  51.8 29.7 %copy-start.29 = (s32[24]{0:T(128)S(1)}, s32[24]{0:T(128)}, u32[]{:S(2)}) copy-start(s32[24]{0:T(128)} %param.20) | copy-start | bytes 292
  51.8 29.9 %copy-start.27 = (f32[24]{0:T(128)S(1)}, f32[24]{0:T(128)}, u32[]{:S(2)}) copy-start(f32[24]{0:T(128)} %param.21) | copy-start | bytes 292
  51.8 31.1 %copy-start.2 = (f32[2048]{0:T(1024)S(1)}, f32[2048]{0:T(1024)}, u32[]{:S(2)}) copy-start(f32[2048]{0:T(1024)} %param.25) | copy-start | bytes 24580
  66.9 11.2 %collective-permute-start.11 = (bf16[3,128,512]{2,1,0:T(8,128)(2,1)S(1)}, bf16[3,128,512]{2,1,0:T(8,128)(2,1)S(1)}, u32[]{:S(2)}, u32[]{:S(2)}) collective-permute-start(bf16[3,128,512]{2,1,0:T(8,128)(2,1)S(1)} %get-tuple-element.40), channel_id=1, source_target_pairs={{0,16},{4,20},{8,24},{12,28},{16,0},{20,4},{24,8},{28,12},{1,17},{... | collective-permute-start | bytes 1179656 | tf_op jit(solution)/shard_map/ppermute | solution.py:425
  67.6 10.8 %collective-permute-start.12 = (bf16[3,144,512]{2,1,0:T(8,128)(2,1)S(1)}, bf16[3,144,512]{2,1,0:T(8,128)(2,1)S(1)}, u32[]{:S(2)}, u32[]{:S(2)}) collective-permute-start(bf16[3,144,512]{2,1,0:T(8,128)(2,1)S(1)} %get-tuple-element.41), channel_id=1, source_target_pairs={{0,8},{4,12},{8,0},{12,4},{16,24},{20,28},{24,16},{28,20},{1,9},{5... | collective-permute-start | bytes 1327112 | tf_op jit(solution)/shard_map/ppermute | solution.py:425
  69.4 5.7 %collective-permute-start.10 = (bf16[8,2048]{1,0:T(8,128)(2,1)S(1)}, bf16[8,2048]{1,0:T(8,128)(2,1)S(1)}, u32[]{:S(2)}, u32[]{:S(2)}) collective-permute-start(bf16[8,2048]{1,0:T(8,128)(2,1)S(1)} %encode.1.refs_0_.own_ref), channel_id=1, source_target_pairs={{0,3},{1,2},{2,1},{3,0},{4,7},{5,6},{6,5},{7,4},{8,11},{9,10},{10,... | collective-permute-start | bytes 98312 | tf_op jit(solution)/shard_map/ppermute | solution.py:425
  72.8 4.8 %collective-permute-start.9 = (bf16[8,2048]{1,0:T(8,128)(2,1)S(1)}, bf16[8,2048]{1,0:T(8,128)(2,1)S(1)}, u32[]{:S(2)}, u32[]{:S(2)}) collective-permute-start(bf16[8,2048]{1,0:T(8,128)(2,1)S(1)} %encode.1.refs_0_.own_ref), channel_id=1, source_target_pairs={{0,2},{1,3},{2,0},{3,1},{4,6},{5,7},{6,4},{7,5},{8,10},{9,11},{10,... | collective-permute-start | bytes 98312 | tf_op jit(solution)/shard_map/ppermute | solution.py:425
  72.8 4.8 %collective-permute-start.8 = (bf16[8,2048]{1,0:T(8,128)(2,1)S(1)}, bf16[8,2048]{1,0:T(8,128)(2,1)S(1)}, u32[]{:S(2)}, u32[]{:S(2)}) collective-permute-start(bf16[8,2048]{1,0:T(8,128)(2,1)S(1)} %encode.1.refs_0_.own_ref), channel_id=1, source_target_pairs={{0,1},{1,0},{2,3},{3,2},{4,5},{5,4},{6,7},{7,6},{8,9},{9,8},{10,11... | collective-permute-start | bytes 98312 | tf_op jit(solution)/shard_map/ppermute | solution.py:425
  77.6 4.4 %collective-permute-start.13 = (bf16[3,272,512]{2,1,0:T(8,128)(2,1)S(1)}, bf16[3,272,512]{2,1,0:T(8,128)(2,1)}, u32[]{:S(2)}, u32[]{:S(2)}) collective-permute-start(bf16[3,272,512]{2,1,0:T(8,128)(2,1)S(1)} %collective-permute-done.6.low_ref.refs_5_), channel_id=1, source_target_pairs={{0,4},{4,0},{8,12},{12,8},{16,20},{20,16},{24,28},{28,24},{1,5},{5... | collective-permute-start | bytes 2506760 | tf_op jit(solution)/shard_map/ppermute | solution.py:425
  77.6 4.4 %collective-permute-start.14 = (bf16[3,272,512]{2,1,0:T(8,128)(2,1)S(1)}, bf16[3,272,512]{2,1,0:T(8,128)(2,1)}, u32[]{:S(2)}, u32[]{:S(2)}) collective-permute-start(bf16[3,272,512]{2,1,0:T(8,128)(2,1)S(1)} %collective-permute-done.7.high_ref.refs_6_), channel_id=1, source_target_pairs={{0,4},{4,0},{8,12},{12,8},{16,20},{20,16},{24,28},{28,24},{1,5},{5... | collective-permute-start | bytes 2506760 | tf_op jit(solution)/shard_map/ppermute | solution.py:425
  78.1 3.0 %collective-permute-start.15 = (bf16[3,128,512]{2,1,0:T(8,128)(2,1)S(1)}, bf16[3,128,512]{2,1,0:T(8,128)(2,1)S(1)}, u32[]{:S(2)}, u32[]{:S(2)}) collective-permute-start(bf16[3,128,512]{2,1,0:T(8,128)(2,1)S(1)} %collective-permute-done.11.refs_7_), channel_id=1, source_target_pairs={{0,4},{4,0},{8,12},{12,8},{16,20},{20,16},{24,28},{28,24},{1,5},{5... | collective-permute-start | bytes 1179656 | tf_op jit(solution)/shard_map/ppermute | solution.py:425
  78.1 16.7 %collective-permute-start.21 = (bf16[128,2048]{1,0:T(8,128)(2,1)}, bf16[128,2048]{1,0:T(8,128)(2,1)}, u32[]{:S(2)}, u32[]{:S(2)}) collective-permute-start(bf16[128,2048]{1,0:T(8,128)(2,1)} %get-tuple-element.50), channel_id=1, source_target_pairs={{0,8},{4,12},{8,0},{12,4},{16,24},{20,28},{24,16},{28,20},{1,9},{5... | collective-permute-start | bytes 1572872 | tf_op jit(solution)/shard_map/ppermute | solution.py:425
  78.4 19.1 %collective-permute-start.20 = (bf16[128,2048]{1,0:T(8,128)(2,1)}, bf16[128,2048]{1,0:T(8,128)(2,1)}, u32[]{:S(2)}, u32[]{:S(2)}) collective-permute-start(bf16[128,2048]{1,0:T(8,128)(2,1)} %get-tuple-element.48), channel_id=1, source_target_pairs={{0,16},{4,20},{8,24},{12,28},{16,0},{20,4},{24,8},{28,12},{1,17},{... | collective-permute-start | bytes 1572872 | tf_op jit(solution)/shard_map/ppermute | solution.py:425
  81.1 1.8 %collective-permute-start.16 = (bf16[3,144,512]{2,1,0:T(8,128)(2,1)S(1)}, bf16[3,144,512]{2,1,0:T(8,128)(2,1)S(1)}, u32[]{:S(2)}, u32[]{:S(2)}) collective-permute-start(bf16[3,144,512]{2,1,0:T(8,128)(2,1)S(1)} %collective-permute-done.12.refs_8_), channel_id=1, source_target_pairs={{0,4},{4,0},{8,12},{12,8},{16,20},{20,16},{24,28},{28,24},{1,5},{5... | collective-permute-start | bytes 1327112 | tf_op jit(solution)/shard_map/ppermute | solution.py:425
  82.9 17.7 %copy-start.24 = (f32[2048]{0:T(1024)S(1)}, f32[2048]{0:T(1024)}, u32[]{:S(2)}) copy-start(f32[2048]{0:T(1024)} %param.27) | copy-start | bytes 24580
  82.9 17.7 %copy-start.25 = (f32[2]{0:T(128)S(1)}, f32[2]{0:T(128)}, u32[]{:S(2)}) copy-start(f32[2]{0:T(128)} %bias_ref.1) | copy-start | bytes 28
  87.3 0.7 copy-start.9
  88.0 0.6 copy-start.12
  88.6 0.6 copy-start.14
  89.2 0.6 copy-start.18
  89.9 6.1 %collective-permute-start.19 = (bf16[32,512]{1,0:T(8,128)(2,1)S(1)}, bf16[32,512]{1,0:T(8,128)(2,1)S(1)}, u32[]{:S(2)}, u32[]{:S(2)}) collective-permute-start(bf16[32,512]{1,0:T(8,128)(2,1)S(1)} %get-tuple-element.47.refs_0_), channel_id=1, source_target_pairs={{0,3},{1,2},{2,1},{3,0},{4,7},{5,6},{6,5},{7,4},{8,11},{9,10},{10,... | collective-permute-start | bytes 98312 | tf_op jit(solution)/shard_map/ppermute | solution.py:425
  91.3 5.0 %collective-permute-start.18 = (bf16[32,512]{1,0:T(8,128)(2,1)S(1)}, bf16[32,512]{1,0:T(8,128)(2,1)S(1)}, u32[]{:S(2)}, u32[]{:S(2)}) collective-permute-start(bf16[32,512]{1,0:T(8,128)(2,1)S(1)} %get-tuple-element.47.refs_0_), channel_id=1, source_target_pairs={{0,2},{1,3},{2,0},{3,1},{4,6},{5,7},{6,4},{7,5},{8,10},{9,11},{10,... | collective-permute-start | bytes 98312 | tf_op jit(solution)/shard_map/ppermute | solution.py:425
  91.9 5.0 %collective-permute-start.17 = (bf16[32,512]{1,0:T(8,128)(2,1)S(1)}, bf16[32,512]{1,0:T(8,128)(2,1)S(1)}, u32[]{:S(2)}, u32[]{:S(2)}) collective-permute-start(bf16[32,512]{1,0:T(8,128)(2,1)S(1)} %get-tuple-element.47.refs_0_), channel_id=1, source_target_pairs={{0,1},{1,0},{2,3},{3,2},{4,5},{5,4},{6,7},{7,6},{8,9},{9,8},{10,11... | collective-permute-start | bytes 98312 | tf_op jit(solution)/shard_map/ppermute | solution.py:425
  96.3 0.6 copy-start.20
  96.9 0.6 copy-start.22
  97.5 2.3 %collective-permute-start.22 = (bf16[128,2048]{1,0:T(8,128)(2,1)}, bf16[128,2048]{1,0:T(8,128)(2,1)}, u32[]{:S(2)}, u32[]{:S(2)}) collective-permute-start(bf16[128,2048]{1,0:T(8,128)(2,1)} %collective-permute-done.20.refs_7_), channel_id=1, source_target_pairs={{0,4},{4,0},{8,12},{12,8},{16,20},{20,16},{24,28},{28,24},{1,5},{5... | collective-permute-start | bytes 1572872 | tf_op jit(solution)/shard_map/ppermute | solution.py:425
  97.5 3.0 %collective-permute-start.23 = (bf16[128,2048]{1,0:T(8,128)(2,1)}, bf16[128,2048]{1,0:T(8,128)(2,1)}, u32[]{:S(2)}, u32[]{:S(2)}) collective-permute-start(bf16[128,2048]{1,0:T(8,128)(2,1)} %collective-permute-done.21.refs_8_), channel_id=1, source_target_pairs={{0,4},{4,0},{8,12},{12,8},{16,20},{20,16},{24,28},{28,24},{1,5},{5... | collective-permute-start | bytes 1572872 | tf_op jit(solution)/shard_map/ppermute | solution.py:425
  100.6 1.2 copy-start.7
  101.8 0.9 copy-start.10
  102.7 0.8 copy-start.17
  103.5 0.8 copy-start.19
  104.2 0.8 copy-start.21
  105.0 0.8 copy-start.23
  105.8 15.6 %copy-start.11 = (f32[32,2048]{1,0:T(8,128)S(1)}, f32[32,2048]{1,0:T(8,128)}, u32[]{:S(2)}) copy-start(f32[32,2048]{1,0:T(8,128)} %copy-done.9) | copy-start | bytes 786436
  105.8 15.6 %copy-start.13 = (bf16[3,32,512]{2,1,0:T(8,128)(2,1)S(1)}, bf16[3,32,512]{2,1,0:T(8,128)(2,1)}, u32[]{:S(2)}) copy-start(bf16[3,32,512]{2,1,0:T(8,128)(2,1)} %copy-done.12) | copy-start | bytes 294916
  105.8 15.6 %copy-start.15 = (f32[4,32,32]{2,1,0:T(8,128)S(1)}, f32[4,32,32]{2,1,0:T(8,128)}, u32[]{:S(2)}) copy-start(f32[4,32,32]{2,1,0:T(8,128)} %copy-done.14) | copy-start | bytes 49156
  112.7 4.5 %collective-permute-start.24 = (bf16[32,640]{1,0:T(8,128)(2,1)S(1)}, bf16[32,640]{1,0:T(8,128)(2,1)S(1)}, u32[]{:S(2)}, u32[]{:S(2)}) collective-permute-start(bf16[32,640]{1,0:T(8,128)(2,1)S(1)} %get-tuple-element.56), channel_id=1, source_target_pairs={{0,1},{1,0},{2,3},{3,2},{4,5},{5,4},{6,7},{7,6},{8,9},{9,8},{10,11... | collective-permute-start | bytes 122888 | tf_op jit(solution)/shard_map/ppermute | solution.py:425
  114.0 6.0 %collective-permute-start.25 = (bf16[32,640]{1,0:T(8,128)(2,1)S(1)}, bf16[32,640]{1,0:T(8,128)(2,1)S(1)}, u32[]{:S(2)}, u32[]{:S(2)}) collective-permute-start(bf16[32,640]{1,0:T(8,128)(2,1)S(1)} %get-tuple-element.57), channel_id=1, source_target_pairs={{0,2},{1,3},{2,0},{3,1},{4,6},{5,7},{6,4},{7,5},{8,10},{9,11},{10,... | collective-permute-start | bytes 122888 | tf_op jit(solution)/shard_map/ppermute | solution.py:425
  115.6 5.8 %collective-permute-start.26 = (bf16[32,640]{1,0:T(8,128)(2,1)S(1)}, bf16[32,640]{1,0:T(8,128)(2,1)S(1)}, u32[]{:S(2)}, u32[]{:S(2)}) collective-permute-start(bf16[32,640]{1,0:T(8,128)(2,1)S(1)} %get-tuple-element.58), channel_id=1, source_target_pairs={{0,3},{1,2},{2,1},{3,0},{4,7},{5,6},{6,5},{7,4},{8,11},{9,10},{10,... | collective-permute-start | bytes 122888 | tf_op jit(solution)/shard_map/ppermute | solution.py:425
  121.4 24.5 %copy-start.26 = (s32[768]{0:T(1024)S(1)}, s32[768]{0:T(1024)}, u32[]{:S(2)}) copy-start(s32[768]{0:T(1024)} %param.17) | copy-start | bytes 9220
  129.7 5.2 %collective-permute-start.27 = (bf16[8,1152]{1,0:T(8,128)(2,1)}, bf16[8,1152]{1,0:T(8,128)(2,1)S(1)}, u32[]{:S(2)}, u32[]{:S(2)}) collective-permute-start(bf16[8,1152]{1,0:T(8,128)(2,1)} %get-tuple-element.61), channel_id=1, source_target_pairs={{0,1},{1,0},{2,3},{3,2},{4,5},{5,4},{6,7},{7,6},{8,9},{9,8},{10,11... | collective-permute-start | bytes 55304 | tf_op jit(solution)/shard_map/ppermute | solution.py:425
  129.8 5.1 %collective-permute-start.28 = (bf16[8,1152]{1,0:T(8,128)(2,1)S(1)}, bf16[8,1152]{1,0:T(8,128)(2,1)S(1)}, u32[]{:S(2)}, u32[]{:S(2)}) collective-permute-start(bf16[8,1152]{1,0:T(8,128)(2,1)S(1)} %get-tuple-element.62), channel_id=1, source_target_pairs={{0,2},{1,3},{2,0},{3,1},{4,6},{5,7},{6,4},{7,5},{8,10},{9,11},{10,... | collective-permute-start | bytes 55304 | tf_op jit(solution)/shard_map/ppermute | solution.py:425
  132.0 5.6 %collective-permute-start.29 = (bf16[8,1152]{1,0:T(8,128)(2,1)S(1)}, bf16[8,1152]{1,0:T(8,128)(2,1)S(1)}, u32[]{:S(2)}, u32[]{:S(2)}) collective-permute-start(bf16[8,1152]{1,0:T(8,128)(2,1)S(1)} %get-tuple-element.63), channel_id=1, source_target_pairs={{0,3},{1,2},{2,1},{3,0},{4,7},{5,6},{6,5},{7,4},{8,11},{9,10},{10,... | collective-permute-start | bytes 55304 | tf_op jit(solution)/shard_map/ppermute | solution.py:425
  138.2 1.2 collective-permute-start.30
  139.4 6.4 %collective-permute-start.33 = (bf16[16,1024]{1,0:T(8,128)(2,1)S(1)}, bf16[16,1024]{1,0:T(8,128)(2,1)S(1)}, u32[]{:S(2)}, u32[]{:S(2)}) collective-permute-start(bf16[16,1024]{1,0:T(8,128)(2,1)S(1)} %pad_maximum_fusion), channel_id=1, source_target_pairs={{0,24},{4,28},{8,16},{12,20},{16,8},{20,12},{24,0},{28,4},{1,25},{... | collective-permute-start | bytes 98312 | tf_op jit(solution)/shard_map/ppermute | solution.py:425
  140.7 5.1 %collective-permute-start.32 = (bf16[16,1024]{1,0:T(8,128)(2,1)S(1)}, bf16[16,1024]{1,0:T(8,128)(2,1)S(1)}, u32[]{:S(2)}, u32[]{:S(2)}) collective-permute-start(bf16[16,1024]{1,0:T(8,128)(2,1)S(1)} %pad_maximum_fusion), channel_id=1, source_target_pairs={{0,16},{4,20},{8,24},{12,28},{16,0},{20,4},{24,8},{28,12},{1,17},{... | collective-permute-start | bytes 98312 | tf_op jit(solution)/shard_map/ppermute | solution.py:425
  141.9 3.9 %collective-permute-start.31 = (bf16[16,1024]{1,0:T(8,128)(2,1)S(1)}, bf16[16,1024]{1,0:T(8,128)(2,1)S(1)}, u32[]{:S(2)}, u32[]{:S(2)}) collective-permute-start(bf16[16,1024]{1,0:T(8,128)(2,1)S(1)} %pad_maximum_fusion), channel_id=1, source_target_pairs={{0,8},{4,12},{8,0},{12,4},{16,24},{20,28},{24,16},{28,20},{1,9},{5... | collective-permute-start | bytes 98312 | tf_op jit(solution)/shard_map/ppermute | solution.py:425
  (1 other events, 0.6 us)

commit v3 on v2

--- a/solution.py
+++ b/solution.py
@@ -15,11 +15,11 @@
 VHDIM = 128
 VPAD = 8
 FW_ROWS = 16
+SNUG = 48
 LANES = 128
 EPS = 1e-5
 F32 = jnp.float32
 BF16 = jnp.bfloat16
-VMEM_LIMIT = 48 * 1024 * 1024
 
 NT = (((1,), (1,)), ((), ()))
 TN = (((0,), (0,)), ((), ()))
@@ -39,11 +39,11 @@
 
 
 def hbm():
-    return pl.BlockSpec(memory_space=pl.ANY)
-
-
-def params():
-    return pltpu.CompilerParams(vmem_limit_bytes=VMEM_LIMIT)
+    return pl.BlockSpec(memory_space=pltpu.HBM)
+
+
+def params(mib):
+    return pltpu.CompilerParams(vmem_limit_bytes=int(mib * 1024) * 1024)
 
 
 def cost(micros):
@@ -67,10 +67,12 @@
     return (slots == position).astype(BF16)
 
 
-def pack_kernel(senders, per_owner, visits_dev, where_ref, ids_ref, x_ref, out_ref):
+def pack_kernel(senders, per_owner, visits_dev, where_ref, ids_ref, x_hbm, out_ref, x_ref, sem):
+    copy = pltpu.make_async_copy(x_hbm, x_ref, sem)
+    copy.start()
     rows = x_ref.shape[0]
     cap_rows = rows // senders
-    ids = ids_ref[...]
+    ids = jnp.concatenate([ids_ref[i : i + 1, :] for i in range(ids_ref.shape[0])], axis=1)
     owners = lax.broadcasted_iota(jnp.int32, (senders, rows), 0)
     hot = (ids >= owners * per_owner) & (ids < (owners + 1) * per_owner)
     hot_f = hot.astype(F32)
@@ -80,11 +82,31 @@
     first = (owners * per_owner + where_ref[1] * visits_dev).astype(F32)
     label = jnp.sum(hot_f * (ids.astype(F32) - first + 1.0), axis=0, keepdims=True)
     label = jnp.broadcast_to(label, (LANES, rows)).astype(BF16)
+    copy.wait()
     step = rows // 3
     for c in range(3):
         chosen = pick_rows(position, c * step, step, rows)
         out_ref[c * step : (c + 1) * step, :D] = dot(chosen, x_ref[...]).astype(BF16)
         out_ref[c * step : (c + 1) * step, D:] = dot(chosen, label, NT).astype(BF16)
+
+
+def prep_kernel(visits_dev, patient_ref, treat_ref, target_ref, meta_ref, row_ref):
+    rows, lanes = meta_ref.shape
+    slot = lax.broadcasted_iota(jnp.int32, (rows, lanes), 0)
+    lane = lax.broadcasted_iota(jnp.int32, (rows, lanes), 1)
+    place = lax.broadcasted_iota(jnp.int32, (VPAD, rows), 1)
+    meta = jnp.where(lane == 2, -1.0, jnp.zeros((rows, lanes), F32))
+    line = jnp.full((VPAD, rows), -1.0, F32)
+    for g in range(patient_ref.shape[0]):
+        at = (g // visits_dev) * VPAD + g % visits_dev
+        patient = patient_ref[g].astype(F32)
+        here = jnp.where(
+            lane == 0, treat_ref[g].astype(F32), jnp.where(lane == 1, target_ref[g], patient)
+        )
+        meta = jnp.where((slot == at) & (lane < 3), here, meta)
+        line = jnp.where(place == at, patient, line)
+    meta_ref[...] = meta
+    row_ref[...] = line
 
 
 def fold_kernel(weight_ref, head_ref, qkv_ref, out_ref):
@@ -107,11 +129,12 @@
 def encode_kernel(
     visits_dev,
     count_ref,
-    got_ref,
     gain_ref,
+    got_hbm,
     qkv_ref,
     proj_ref,
     vec_ref,
+    got_ref,
     wqk,
     wv,
     wo,
@@ -123,13 +146,18 @@
 ):
     rows = got_ref.shape[0]
     slots = visits_dev * VB
+    inputs = [
+        pltpu.make_async_copy(got_hbm.at[:, D:], got_ref.at[:, D:], sems.at[3]),
+        pltpu.make_async_copy(got_hbm.at[:, :D], got_ref.at[:, :D], sems.at[4]),
+    ]
     copies = [
         pltpu.make_async_copy(qkv_ref.at[:, : 2 * D], wqk, sems.at[0]),
         pltpu.make_async_copy(qkv_ref.at[:, 2 * D :], wv, sems.at[1]),
         pltpu.make_async_copy(proj_ref, wo, sems.at[2]),
     ]
-    for copy in copies:
+    for copy in inputs + copies:
         copy.start()
+    inputs[0].wait()
     lane0 = (lax.broadcasted_iota(jnp.int32, (VPAD, LANES), 1) == 0).astype(BF16)
     label = dot(lane0, got_ref[:, D:], NT)[:1]
     visits = lax.broadcasted_iota(jnp.int32, (VPAD, rows), 0)
@@ -139,6 +167,7 @@
     before = dot(hot_b, strict_upper(rows))
     base = (visits * VB + 1).astype(F32)
     position = (jnp.sum(hot_f * (base + before), axis=0, keepdims=True)).astype(jnp.int32) - 1
+    inputs[1].wait()
     sums = dot(hot_b, got_ref[:, :D])
     gain = gain_ref[...]
     step = 2 * VB
@@ -205,9 +234,9 @@
     return lax.rsqrt(jnp.mean(values * values, axis=-1, keepdims=True) + EPS)
 
 
-def fetch(pieces, scratch, sems):
+def fetch(pieces, scratch, sems, first=0):
     copies = [
-        pltpu.make_async_copy(piece, buffer, sems.at[i])
+        pltpu.make_async_copy(piece, buffer, sems.at[first + i])
         for i, (piece, buffer) in enumerate(zip(pieces, scratch, strict=True))
     ]
     for copy in copies:
@@ -215,29 +244,32 @@
     return copies
 
 
-def project_kernel(
-    n_mp, n_ev, plan, where_ref, meta_ref, patient_ref, gain_ref, *refs
-):
+def project_kernel(n_mp, n_ev, plan, where_ref, *refs):
     n = len(plan)
-    vec_in, refs = refs[:n_mp], refs[n_mp:]
+    vec_in, (gain_ref, meta_ref, patient_ref), refs = refs[:n_mp], refs[n_mp : n_mp + 3], refs[n_mp + 3 :]
     pieces, refs = refs[:n], refs[n:]
-    vec_ref, attended_ref, qkv_ref, prob_ref, fw_ref = refs[:5]
-    scratch, refs = refs[5 : 5 + n], refs[5 + n :]
-    vec, blocks, sems = refs
+    attended_ref, state, refs = refs[0], refs[1], refs[2:]
+    scratch, refs = refs[:n], refs[n:]
+    vec, blocks, sems, kept, out_sems = refs
     copies = fetch(pieces, scratch, sems)
     e, m = where_ref[0], where_ref[1]
+    cols = attended_ref.shape[1]
+    saves = [
+        pltpu.make_async_copy(kept.at[:, lo:hi], state.at[:, lo:hi], out_sems.at[i])
+        for i, (lo, hi) in enumerate(state_spans(cols))
+    ]
     for k in range(n_mp):
-        vec[m ^ k] = vec_in[k][...].astype(F32)
+        vec[m ^ k] = vec_in[k][...]
     rows = n_mp * VPAD
-    full = vec[...].reshape(rows, DV)
-    vec_ref[...] = full
+    full = vec[...].astype(F32).reshape(rows, DV)
+    kept[:, :DV] = full
+    saves[0].start()
     normed = (full * rms_factor(full) * gain_ref[...]).astype(BF16)
     width = DV // n_ev
     for j in range(n_ev):
         blocks[j] = normed[:, j * width : (j + 1) * width]
-    cols = attended_ref.shape[1]
     totals = [jnp.zeros((rows, cols), F32) for _ in range(3)]
-    fw = jnp.zeros(fw_ref.shape, F32)
+    fw = jnp.zeros((FW_ROWS, cols), F32)
     for i, (k, lo, size) in enumerate(plan):
         copies[i].wait()
         block = blocks[e ^ k][:, lo : lo + size]
@@ -245,21 +277,29 @@
             totals[t] = totals[t] + dot(block, scratch[i][t, :size, :])
             if scratch[i].shape[1] > size:
                 fw = fw + scratch[i][t, size:, :].astype(F32)
-    fw_ref[...] = fw
     parts = [total.astype(BF16) for total in totals]
     for t in range(3):
-        qkv_ref[t] = parts[t]
+        kept[:, DV + t * cols : DV + (t + 1) * cols] = parts[t].astype(F32)
+    kept[:FW_ROWS, DV + 3 * cols : DV + 4 * cols] = fw
+    saves[1].start()
     q_at = lax.broadcasted_iota(jnp.int32, (rows, rows), 0)
     k_at = lax.broadcasted_iota(jnp.int32, (rows, rows), 1)
-    allowed = (meta_ref[:, 2:3] == patient_ref[...]) & (k_at <= q_at)
+    allowed = (meta_ref[:, 2:3] == patient_ref[0:1, :]) & (k_at <= q_at)
     for h in range(cols // VHDIM):
         span = slice(h * VHDIM, (h + 1) * VHDIM)
         scores = dot(parts[0][:, span], parts[1][:, span], NT) * VHDIM ** (-0.5)
         scores = jnp.where(allowed, scores, -1e30)
         grown = jnp.exp(scores - jnp.max(scores, axis=-1, keepdims=True))
         prob = grown / jnp.sum(grown, axis=-1, keepdims=True)
-        prob_ref[h] = prob
+        kept[:, DV + 4 * cols + h * rows : DV + 4 * cols + (h + 1) * rows] = prob
         attended_ref[:, span] = dot(prob.astype(BF16), parts[2][:, span]).astype(BF16)
+    saves[2].start()
+    for save in saves:
+        save.wait()
+
+
+def state_spans(cols):
+    return ((0, DV), (DV, DV + 4 * cols), (DV + 4 * cols, DV + 4 * cols + LANES))
 
 
 def pack_scalars(columns, rows):
@@ -279,24 +319,32 @@
 
 
 def ffn_kernel(
-    n_mp, n_ev, plan, where_ref, meta_ref, vec_ref, gain_ref, fw_ref, head_ref, bias_ref, *refs
+    n_mp, n_ev, plan, where_ref, bias_ref, gain_ref, meta_ref, head_ref, *refs
 ):
     n = len(plan)
-    attn_in, refs = refs[:n_mp], refs[n_mp:]
+    attn_in, state, refs = refs[:n_mp], refs[n_mp], refs[n_mp + 1 :]
     pieces, refs = refs[:n], refs[n:]
-    outs, refs = refs[:n_mp], refs[n_mp:]
-    mid_ref, refs = refs[0], refs[1:]
+    outs, mid_ref, refs = refs[:n_mp], refs[n_mp], refs[n_mp + 1 :]
     scratch, refs = refs[:n], refs[n:]
-    attn, blocks, grads, sems = refs
+    attn, vec_ref, fw_ref, blocks, grads, sems = refs
+    e, m = where_ref[0], where_ref[1]
+    cols = DV // n_mp
+    fw_at = DV + 3 * cols
+    sources = [state.at[:, :DV], state.at[:FW_ROWS, fw_at : fw_at + cols]]
+    small = fetch(sources, [vec_ref, fw_ref], sems, n)
     copies = fetch(pieces, scratch, sems)
-    e, m = where_ref[0], where_ref[1]
+    for k in range(n_mp):
+        attn[m ^ k] = attn_in[k][...]
+    for copy in small:
+        copy.wait()
     rows = vec_ref.shape[0]
-    for k in range(n_mp):
-        attn[m ^ k] = attn_in[k][...].astype(F32)
-    mid = vec_ref[...] + jnp.concatenate([attn[k] for k in range(n_mp)], axis=1)
-    mid_ref[...] = mid
+    mid = vec_ref[...] + jnp.concatenate([attn[k] for k in range(n_mp)], axis=1).astype(F32)
+    at = pl.ds(pl.multiple_of(m * cols, cols), cols)
+    factor = rms_factor(mid)
+    mid_ref[:, :cols] = vec_ref[:, at] + attn[m].astype(F32)
+    mid_ref[:, cols:] = jnp.broadcast_to(factor, (rows, LANES))
     gain = gain_ref[...]
-    normed = (mid * rms_factor(mid) * gain).astype(BF16)
+    normed = (mid * factor * gain).astype(BF16)
     width = DV // n_ev
     for j in range(n_ev):
         blocks[j] = normed[:, j * width : (j + 1) * width]
@@ -327,7 +375,6 @@
         moment = moment + jnp.sum(grads[j] * gain[:, span] * mid[:, span], axis=-1, keepdims=True)
     scalars = pack_scalars([outcome[0], outcome[1], moment], rows)
     each = n_ev // n_mp
-    cols = DV // n_mp
     for k in range(n_mp):
         for j in range(each):
             outs[k][:, j * width : (j + 1) * width] = grads[(m ^ k) * each + j].astype(BF16)
@@ -335,19 +382,18 @@
 
 
 def back_kernel(
-    n_mp, n_ev, plan, where_ref, meta_ref, vec_ref, mid_ref, gain_ref, vgain_ref, head_ref,
-    qkv_ref, prob_ref, *refs
+    n_mp, n_ev, plan, where_ref, mid_ref, meta_ref, gain_ref, vgain_ref, head_ref, *refs
 ):
     n = len(plan)
-    pay_in, refs = refs[:n_mp], refs[n_mp:]
+    pay_in, state, refs = refs[:n_mp], refs[n_mp], refs[n_mp + 1 :]
     pieces, refs = refs[:n], refs[n:]
-    outs, refs = refs[:n_mp], refs[n_mp:]
-    outcome_ref, refs = refs[0], refs[1:]
+    outs, outcome_ref, coef_ref, refs = refs[:n_mp], refs[n_mp], refs[n_mp + 1], refs[n_mp + 2 :]
     scratch, refs = refs[:n], refs[n:]
-    grads, table, sems = refs
+    kept, grads, table, sems = refs
+    (stored,) = fetch([state], [kept], sems, n)
     copies = fetch(pieces, scratch, sems)
     e, m = where_ref[0], where_ref[1]
-    rows = vec_ref.shape[0]
+    rows = mid_ref.shape[0]
     cols = DV // n_mp
     total = pay_in[0][...].astype(F32)
     for k in range(1, n_mp):
@@ -359,22 +405,26 @@
     outcome_ref[...] = jnp.where(lane == 0, outcome[0], outcome[1])
     treated = meta_ref[:, 0:1] > 0.5
     delta = 4096.0 * (jnp.where(treated, outcome[1], outcome[0]) - meta_ref[:, 1:2])
-    factor = rms_factor(mid_ref[...])
+    factor = mid_ref[:, cols : cols + 1]
     at = pl.ds(pl.multiple_of(m * cols, cols), cols)
-    mid = mid_ref[:, at]
+    mid = mid_ref[:, :cols]
     head = jnp.where(treated, head_ref[1:2, at], head_ref[0:1, at])
     scaled = total[:, :cols] * gain_ref[:, at]
     grad_mid = delta * (head + factor * (scaled - mid * (factor * factor * moment)))
     grad_c = grad_mid.astype(BF16)
+    stored.wait()
+    queries, keys, values = (
+        kept[:, DV + t * cols : DV + (t + 1) * cols].astype(BF16) for t in range(3)
+    )
     three = [[], [], []]
     for h in range(cols // VHDIM):
         span = slice(h * VHDIM, (h + 1) * VHDIM)
-        prob = prob_ref[h]
-        grad_p = dot(grad_c[:, span], qkv_ref[2, :, span], NT)
+        prob = kept[:, DV + 4 * cols + h * rows : DV + 4 * cols + (h + 1) * rows]
+        grad_p = dot(grad_c[:, span], values[:, span], NT)
         grad_s = prob * (grad_p - jnp.sum(grad_p * prob, axis=-1, keepdims=True))
         grad_s = (grad_s * VHDIM ** (-0.5)).astype(BF16)
-        three[0].append(dot(grad_s, qkv_ref[1, :, span]).astype(BF16))
-        three[1].append(dot(grad_s, qkv_ref[0, :, span], TN).astype(BF16))
+        three[0].append(dot(grad_s, keys[:, span]).astype(BF16))
+        three[1].append(dot(grad_s, queries[:, span], TN).astype(BF16))
         three[2].append(dot(prob.astype(BF16), grad_c[:, span], TN).astype(BF16))
     three = [jnp.concatenate(parts, axis=1) for parts in three]
     for i, (k, lo, size) in enumerate(plan):
@@ -384,7 +434,7 @@
         part = part + dot(three[2], scratch[i][2, :size, :], NT)
         grads[e ^ k, :, lo : lo + size] = part
     width = DV // n_ev
-    vec = vec_ref[...]
+    vec = kept[:, :DV]
     spread = rms_factor(vec)
     moment = jnp.zeros((rows, 1), F32)
     for j in range(n_ev):
@@ -403,22 +453,36 @@
     table[:, :, D:] = scalars.reshape(n_mp, VPAD, LANES)
     for k in range(n_mp):
         outs[k][...] = table[m ^ k].astype(BF16)
-
-
-def finish_kernel(n_mp, visits_dev, count_ref, own_ref, *refs):
+    table[:, :, :D] = (vec[:, :D] * (spread * spread * spread * (1.0 / DV))).reshape(n_mp, VPAD, D)
+    coef_ref[...] = table[m][:, :D]
+
+
+def finish_kernel(n_mp, visits_dev, count_ref, coef_ref, *refs):
     pays, out_ref = refs[:n_mp], refs[n_mp]
     total = pays[0][...].astype(F32)
     for k in range(1, n_mp):
         total = total + pays[k][...].astype(F32)
-    vec = own_ref[...].astype(F32)
-    spread = rms_factor(vec)
-    moment = unpack_scalar(total[:, D:], 0) * (1.0 / DV)
-    grad = total[:, :D] - vec[:, :D] * (spread * spread * spread * moment)
+    grad = total[:, :D] - coef_ref[...] * unpack_scalar(total[:, D:], 0)
     row = lax.broadcasted_iota(jnp.int32, (VPAD, 1), 0)
     inverse = jnp.zeros((VPAD, 1), F32)
     for v in range(visits_dev):
         inverse = jnp.where(row == v, 1.0 / count_ref[v].astype(F32), inverse)
-    out_ref[...] = (grad * inverse).astype(BF16)
+    out_ref[...] = (grad * inverse).astype(BF16).astype(F32)
+
+
+def spread_kernel(n_ev, pick, *refs):
+    tables, out, rows_ref, out_sems = refs[:n_ev], *refs[n_ev:]
+    table = jnp.concatenate([each[...] for each in tables], axis=0).astype(BF16)
+    rows = rows_ref.shape[0]
+    step = rows // 3
+    saves = []
+    for c in range(3):
+        span = slice(c * step, (c + 1) * step)
+        rows_ref[span, :] = dot(pick[span, :], table).astype(BF16)
+        saves.append(pltpu.make_async_copy(rows_ref.at[span, :], out.at[span, :], out_sems.at[c]))
+        saves[c].start()
+    for save in saves:
+        save.wait()
 
 
 def swap(x, axis, size, k):
@@ -431,30 +495,57 @@
     return [shard, swap(shard, "events", n_ev, 2), swap(shard, "events", n_ev, 4)]
 
 
-def halves_kernel(half, low_ref, high_ref, low_out, high_out):
+def halves_kernel(low_ref, high_ref, low_out, high_out):
     low_out[...] = low_ref[...]
-    high_out[...] = high_ref[:, half:, :] if len(high_ref.shape) == 3 else high_ref[...]
+    high_out[...] = high_ref[...]
 
 
 def halves_of(pieces, half):
-    tail = pieces[1].shape[-1]
-    if pieces[1].ndim == 2:
-        low, high = (half, tail), (half, tail)
-        block = [pl.BlockSpec(low, lambda i: (0, 0)), pl.BlockSpec(high, lambda i: (1, 0))]
-    else:
-        lead, rows = pieces[1].shape[:2]
-        low, high = (lead, half, tail), (lead, rows - half, tail)
-        block = [pl.BlockSpec(low, lambda i: (0, 0, 0)), vmem()]
-    outs = [pl.BlockSpec(shape, lambda i, n=len(low): (0,) * n) for shape in (low, high)]
+    cols = pieces[1].shape[1]
+    shape = jax.ShapeDtypeStruct((half, cols), BF16)
+    block = pl.BlockSpec((half, cols), lambda i: (0, 0))
     return pl.pallas_call(
-        functools.partial(halves_kernel, half),
+        halves_kernel,
         grid=(1,),
-        out_shape=[jax.ShapeDtypeStruct(low, BF16), jax.ShapeDtypeStruct(high, BF16)],
-        in_specs=block,
-        out_specs=outs,
-        compiler_params=params(),
+        out_shape=[shape, shape],
+        in_specs=[block, pl.BlockSpec((half, cols), lambda i: (1, 0))],
+        out_specs=[block, block],
+        compiler_params=params(SNUG),
         cost_estimate=cost(0),
         name="halves",
+    )(pieces[1], pieces[2])
+
+
+def split_kernel(half, low_ref, high_ref, low_out, high_out, low, high, sems):
+    rows = high_ref.shape[1]
+    sources = [low_ref.at[:, :half, :], high_ref.at[:, half:rows, :]]
+    copies = fetch(sources, [low, high], sems)
+    saves = []
+    for i, (buffer, out) in enumerate(((low, low_out), (high, high_out))):
+        copies[i].wait()
+        saves += fetch([buffer], [out], sems, 2 + i)
+    for save in saves:
+        save.wait()
+
+
+def split_of(pieces, half):
+    lead, rows, cols = pieces[1].shape
+    return pl.pallas_call(
+        functools.partial(split_kernel, half),
+        out_shape=[
+            jax.ShapeDtypeStruct((lead, half, cols), BF16),
+            jax.ShapeDtypeStruct((lead, rows - half, cols), BF16),
+        ],
+        in_specs=[hbm()] * 2,
+        out_specs=[hbm()] * 2,
+        scratch_shapes=[
+            pltpu.VMEM((lead, half, cols), BF16),
+            pltpu.VMEM((lead, rows - half, cols), BF16),
+            pltpu.SemaphoreType.DMA((4,)),
+        ],
+        compiler_params=params(SNUG),
+        cost_estimate=cost(0),
+        name="split",
     )(pieces[1], pieces[2])
 
 
@@ -479,13 +570,15 @@
     return near + [(k ^ 1, lo, size) for k, lo, size in near]
 
 
+def event_order(n_ev):
+    return list(range(n_ev)) if n_ev != 8 else [0, 2, 4, 6, 1, 3, 5, 7]
+
+
 def gather_events(block, n_ev):
     if n_ev != 8:
-        return jnp.concatenate(
-            [block] + [swap(block, "events", n_ev, k) for k in range(1, n_ev)], axis=0
-        )
-    pair = jnp.concatenate([block, swap(block, "events", n_ev, 1)], axis=0)
-    return jnp.concatenate([pair] + [swap(pair, "events", n_ev, k) for k in (2, 4, 6)], axis=0)
+        return [block] + [swap(block, "events", n_ev, k) for k in range(1, n_ev)]
+    near = [block] + [swap(block, "events", n_ev, k) for k in (2, 4, 6)]
+    return near + across(near, n_ev)
 
 
 def local(
@@ -517,14 +610,15 @@
     cols = DV // n_mp
     hidden = ffn_in.shape[1]
     where = jnp.stack([e, m]).astype(jnp.int32)
-    ids = event_visit.reshape(1, rows_dev)
+    ids = event_visit.reshape(rows_dev // LANES, LANES)
 
     send = pl.pallas_call(
         functools.partial(pack_kernel, n_ev, per_owner, visits_dev),
         out_shape=jax.ShapeDtypeStruct((rows_dev, D + LANES), BF16),
-        in_specs=[smem(), vmem(), vmem()],
+        in_specs=[smem(), vmem(), hbm()],
         out_specs=vmem(),
-        compiler_params=params(),
+        scratch_shapes=[pltpu.VMEM((rows_dev, D), BF16), pltpu.SemaphoreType.DMA],
+        compiler_params=params(12),
         cost_estimate=cost(0),
         name="pack",
     )(where, ids, event_x)
@@ -542,41 +636,51 @@
     head_mid = (own_head - head_hi.astype(F32)).astype(BF16)
     head_lo = (own_head - head_hi.astype(F32) - head_mid.astype(F32)).astype(BF16)
     heads = jnp.concatenate([head_hi, head_mid, head_lo, jnp.zeros((2, width), BF16)], axis=0)
+    meta, patient_row = pl.pallas_call(
+        functools.partial(prep_kernel, visits_dev),
+        out_shape=[
+            jax.ShapeDtypeStruct((group, LANES), F32),
+            jax.ShapeDtypeStruct((VPAD, group), F32),
+        ],
+        in_specs=[smem()] * 3,
+        out_specs=[vmem()] * 2,
+        compiler_params=params(4),
+        cost_estimate=cost(0),
+        name="prep",
+    )(visit_patient, treatment, outcome_target)
+    two_hops = n_ev == 8
+    inner = jnp.arange(VPAD, dtype=jnp.int32)
+    named = (jnp.array(event_order(n_ev), jnp.int32) ^ e)[:, None] * per_owner
+    named = jnp.where(inner < visits_dev, named + m * visits_dev + inner[None, :], -2).reshape(-1)
+    chosen = (event_visit[:, None] == named[None, :]).astype(BF16)
+    ready = [meta, patient_row, head_t, chosen]
+    if two_hops:
+        ffn_halves = halves_of(ffn_first, width // 2)
+        ready += ffn_halves
     qkv_shard = pl.pallas_call(
         fold_kernel,
         out_shape=jax.ShapeDtypeStruct((3, width + FW_ROWS, cols), BF16),
         in_specs=[vmem()] * 3,
         out_specs=vmem(),
-        compiler_params=params(),
+        compiler_params=params(SNUG),
         cost_estimate=cost(30),
         name="fold",
-    )(ffn_out, heads, after(visit_qkv, *ffn_first[1:]))
+    )(ffn_out, heads, after(visit_qkv, *ffn_first[1:], *ready))
     qkv_first = [qkv_shard] + first_hop(after(qkv_shard, got), n_ev)[1:]
     qkv_plan = hop_plan(n_ev, width)
     ffn_plan = hop_plan(n_ev, width)
-    two_hops = n_ev == 8
     if two_hops:
-        ffn_halves = halves_of(ffn_first, width // 2)
         ffn_far = across(ffn_first, n_ev)
         qkv_far = across(qkv_first[:1], n_ev)
-        got = after(got, *ffn_far, *ffn_halves, *qkv_far)
-
-    def spread_rows(values, fill):
-        values = values.astype(F32).reshape(n_mp, visits_dev)
-        return jnp.pad(values, ((0, 0), (0, VPAD - visits_dev)), constant_values=fill).reshape(group)
-
-    patient = spread_rows(visit_patient, -1.0)
-    meta = jnp.stack(
-        [spread_rows(treatment, 0.0), spread_rows(outcome_target, 0.0), patient], axis=1
-    )
-    patient_row = patient.reshape(1, group)
+        got = after(got, *ffn_far, *qkv_far)
 
     vec = pl.pallas_call(
         functools.partial(encode_kernel, visits_dev),
         out_shape=jax.ShapeDtypeStruct((VPAD, DV), BF16),
-        in_specs=[smem(), vmem(), vmem(), hbm(), hbm()],
+        in_specs=[smem(), vmem(), hbm(), hbm(), hbm()],
         out_specs=vmem(),
         scratch_shapes=[
+            pltpu.VMEM((rows_dev, D + LANES), BF16),
             pltpu.VMEM((D, 2 * D), BF16),
             pltpu.VMEM((D, D), BF16),
             pltpu.VMEM((D, D), BF16),
@@ -584,15 +688,15 @@
             pltpu.VMEM((visits_dev * VB, 2 * D), BF16),
             pltpu.VMEM((visits_dev, HEADS, VB), F32),
             pltpu.VMEM((visits_dev, HEADS, D), BF16),
-            pltpu.SemaphoreType.DMA((3,)),
+            pltpu.SemaphoreType.DMA((5,)),
         ],
-        compiler_params=params(),
+        compiler_params=params(SNUG),
         cost_estimate=cost(0),
         name="encode",
-    )(visit_count, got, enc_gain.reshape(1, D), enc_qkv, enc_out)
+    )(visit_count, enc_gain.reshape(1, D), got, enc_qkv, enc_out)
 
     if two_hops:
-        qkv_halves = halves_of([qkv_first[0]] + [after(p, vec) for p in qkv_first[1:]], width // 2)
+        qkv_halves = split_of([qkv_first[0]] + [after(p, vec) for p in qkv_first[1:]], width // 2)
         vec = after(vec, *qkv_halves)
     vecs = [vec] + [swap(vec, "mp", n_mp, k) for k in range(1, n_mp)]
     if two_hops:
@@ -603,27 +707,28 @@
     else:
         qkv_pieces = qkv_first
     n_q = len(qkv_plan)
-    all_vec, attended, qkv, prob, fw = pl.pallas_call(
+    vgain = visit_gain.reshape(1, DV)
+    state_shape = (group, state_spans(cols)[2][1])
+    attended, state = pl.pallas_call(
         functools.partial(project_kernel, n_mp, n_ev, qkv_plan),
-        out_shape=(
-            jax.ShapeDtypeStruct((group, DV), F32),
+        out_shape=[
             jax.ShapeDtypeStruct((group, cols), BF16),
-            jax.ShapeDtypeStruct((3, group, cols), BF16),
-            jax.ShapeDtypeStruct((cols // VHDIM, group, group), F32),
-            jax.ShapeDtypeStruct((FW_ROWS, cols), F32),
-        ),
-        in_specs=[smem()] + [vmem()] * (3 + n_mp) + [hbm()] * n_q,
-        out_specs=(vmem(),) * 5,
+            jax.ShapeDtypeStruct(state_shape, F32),
+        ],
+        in_specs=[smem()] + [vmem()] * (n_mp + 3) + [hbm()] * n_q,
+        out_specs=[vmem(), hbm()],
         scratch_shapes=[pltpu.VMEM(piece.shape, BF16) for piece in qkv_pieces]
         + [
-            pltpu.VMEM((n_mp, VPAD, DV), F32),
+            pltpu.VMEM((n_mp, VPAD, DV), BF16),
             pltpu.VMEM((n_ev, group, width), BF16),
             pltpu.SemaphoreType.DMA((n_q,)),
+            pltpu.VMEM(state_shape, F32),
+            pltpu.SemaphoreType.DMA((3,)),
         ],
-        compiler_params=params(),
+        compiler_params=params(SNUG),
         cost_estimate=cost(0),
         name="project",
-    )(where, meta, patient_row, visit_gain.reshape(1, DV), *vecs, *qkv_pieces)
+    )(where, *vecs, vgain, meta, patient_row, *qkv_pieces)
 
     attns = [attended] + [swap(attended, "mp", n_mp, k) for k in range(1, n_mp)]
     if two_hops:
@@ -632,64 +737,72 @@
     else:
         ffn_pieces = ffn_first
     n_f = len(ffn_plan)
+    fgain = ffn_gain.reshape(1, DV)
     ffn_outs = pl.pallas_call(
         functools.partial(ffn_kernel, n_mp, n_ev, ffn_plan),
         out_shape=[jax.ShapeDtypeStruct((group, cols + LANES), BF16)] * n_mp
-        + [jax.ShapeDtypeStruct((group, DV), F32)],
-        in_specs=[smem()] + [vmem()] * 5 + [smem()] + [vmem()] * n_mp + [hbm()] * n_f,
+        + [jax.ShapeDtypeStruct((group, cols + LANES), F32)],
+        in_specs=[smem()] * 2 + [vmem()] * (3 + n_mp) + [hbm()] * (1 + n_f),
         out_specs=[vmem()] * (n_mp + 1),
         scratch_shapes=[pltpu.VMEM(piece.shape, BF16) for piece in ffn_pieces]
         + [
-            pltpu.VMEM((n_mp, group, cols), F32),
+            pltpu.VMEM((n_mp, group, cols), BF16),
+            pltpu.VMEM((group, DV), F32),
+            pltpu.VMEM((FW_ROWS, cols), F32),
             pltpu.VMEM((n_ev, group, width), BF16),
             pltpu.VMEM((n_ev, group, width), F32),
-            pltpu.SemaphoreType.DMA((n_f,)),
+            pltpu.SemaphoreType.DMA((n_f + 2,)),
         ],
-        compiler_params=params(),
-        cost_estimate=cost(7),
+        compiler_params=params(SNUG),
+        cost_estimate=cost(0),
         name="ffn",
-    )(where, meta, all_vec, ffn_gain.reshape(1, DV), fw, head_t, head_bias, *attns, *ffn_pieces)
+    )(where, head_bias, fgain, meta, head_t, *attns, state, *ffn_pieces)
     mid = ffn_outs[n_mp]
     pays = [ffn_outs[0]] + [swap(ffn_outs[k], "mp", n_mp, k) for k in range(1, n_mp)]
 
     back_outs = pl.pallas_call(
         functools.partial(back_kernel, n_mp, n_ev, qkv_plan),
         out_shape=[jax.ShapeDtypeStruct((VPAD, D + LANES), BF16)] * n_mp
-        + [jax.ShapeDtypeStruct((group, LANES), F32)],
-        in_specs=[smem()] + [vmem()] * (8 + n_mp) + [hbm()] * n_q,
-        out_specs=[vmem()] * (n_mp + 1),
+        + [jax.ShapeDtypeStruct((group, LANES), F32), jax.ShapeDtypeStruct((VPAD, D), F32)],
+        in_specs=[smem()] + [vmem()] * (5 + n_mp) + [hbm()] * (1 + n_q),
+        out_specs=[vmem()] * (n_mp + 2),
         scratch_shapes=[pltpu.VMEM(piece.shape, BF16) for piece in qkv_pieces]
         + [
+            pltpu.VMEM(state_shape, F32),
             pltpu.VMEM((n_ev, group, width), F32),
             pltpu.VMEM((n_mp, VPAD, D + LANES), F32),
-            pltpu.SemaphoreType.DMA((n_q,)),
+            pltpu.SemaphoreType.DMA((n_q + 1,)),
         ],
-        compiler_params=params(),
-        cost_estimate=cost(7),
+        compiler_params=params(SNUG),
+        cost_estimate=cost(0),
         name="back",
-    )(
-        where, meta, all_vec, mid, ffn_gain.reshape(1, DV), visit_gain.reshape(1, DV), head_t, qkv,
-        prob, *pays, *qkv_pieces,
-    )
+    )(where, mid, meta, fgain, vgain, head_t, *pays, state, *qkv_pieces)
     outcomes = back_outs[n_mp][:, :2].reshape(n_mp, VPAD, 2)[:, :visits_dev].reshape(per_owner, 2)
     shares = [back_outs[0]] + [swap(back_outs[k], "mp", n_mp, k) for k in range(1, n_mp)]
     visit_grad = pl.pallas_call(
         functools.partial(finish_kernel, n_mp, visits_dev),
-        out_shape=jax.ShapeDtypeStruct((VPAD, D), BF16),
+        out_shape=jax.ShapeDtypeStruct((VPAD, D), F32),
         in_specs=[smem()] + [vmem()] * (1 + n_mp),
         out_specs=vmem(),
-        compiler_params=params(),
+        compiler_params=params(4),
         cost_estimate=cost(0),
         name="finish",
-    )(visit_count, vec, *shares)
-
-    table = gather_events(visit_grad, n_ev)
-    slot = jnp.arange(n_ev * VPAD, dtype=jnp.int32)
-    inner = slot % VPAD
-    named = ((slot // VPAD) ^ e) * per_owner + m * visits_dev + inner
-    named = jnp.where(inner < visits_dev, named, -2)
-    chosen = (event_visit[:, None] == named[None, :]).astype(BF16)
-    event_grads = dot(chosen, table).astype(BF16)
+    )(visit_count, after(back_outs[n_mp + 1], outcomes), *shares)
+
+    tables = gather_events(visit_grad, n_ev)
+    event_grads = pl.pallas_call(
+        functools.partial(spread_kernel, n_ev),
+        out_shape=jax.ShapeDtypeStruct((rows_dev, D), BF16),
+        in_specs=[vmem()] * (n_ev + 1),
+        out_specs=hbm(),
+        scratch_shapes=[
+            pltpu.VMEM((rows_dev, D), BF16),
+            pltpu.SemaphoreType.DMA((3,)),
+        ],
+        compiler_params=params(8),
+        cost_estimate=cost(0),
+        name="spread",
+    )(chosen, *tables)
     return (outcomes, event_grads)
 
 

time: 148 us -> 142 us (0.959)
  local copies, waits for them, and re-layouts: 14.5 us -> 6.35 us
  waiting for transfers between devices: 53.2 us -> 55.3 us
  matrix products: 1.76 us -> 0 us
    unnamed x65 -> x47, local copies, waits for them, and re-layouts: 12.3 us -> 5.54 us
    ppermute x34 -> x37, waiting for transfers between devices: 38.7 us -> 41.5 us  [swap(): return lax.ppermute(x, axis, [(i, i ^ k) for i in range(size)])]
    dot_general x1 -> x0, matrix products: 1.76 us -> none  [dot(): return lax.dot_general(a, b, dims, preferred_element_type=F32)]
    pallas_call x2 -> x4, Pallas kernels: 2.28 us -> 3.75 us  [the longest x1 1.44 us: local(): pl.pallas_call(functools.partial(spread_kernel, n_ev), out_shape=jax.Shap...]
    ppermute x34 -> x37, starting transfers between devices: 33.7 us -> 33.6 us  [swap(): return lax.ppermute(x, axis, [(i, i ^ k) for i in range(size)])]
  transfers between devices with their start and end apart: 35 -> 38, of which waited for: 18 -> 21; matrix products, arithmetic and copies ran while one was open for 2% -> 1% of each run, Pallas kernels for 16% -> 17%
where the time goes in v3:
time: 142 us; the launch traced here: 141 us
  waiting for transfers between devices  55.3 us (39%)
  Pallas kernels  41 us (29%)
  starting transfers between devices  37.3 us (26%)
  local copies, waits for them, and re-layouts  6.35 us (4%)
    ppermute x37, waiting for transfers between devices, swap(): return lax.ppermute(x, axis, [(i, i ^ k) for i in range(size)])  41.5 us
    ppermute x37, starting transfers between devices, swap(): return lax.ppermute(x, axis, [(i, i ^ k) for i in range(size)])  33.6 us
    all_to_all x1, waiting for transfers between devices, local(): lax.all_to_all(send.reshape(n_ev, rows_dev // n_ev, D + LANES), 'events',...  13.9 us
    pallas_call x1, Pallas kernels, local(): pl.pallas_call(functools.partial(encode_kernel, visits_dev), out_shape=ja...  12.5 us
    pallas_call x1, Pallas kernels, local(): pl.pallas_call(functools.partial(back_kernel, n_mp, n_ev, qkv_plan), out_...  8.23 us
    pallas_call x1, Pallas kernels, local(): pl.pallas_call(functools.partial(ffn_kernel, n_mp, n_ev, ffn_plan), out_s...  6.2 us
    unnamed x47, local copies, waits for them, and re-layouts  5.54 us
    pallas_call x1, Pallas kernels, local(): pl.pallas_call(functools.partial(project_kernel, n_mp, n_ev, qkv_plan), o...  4.48 us
  transfers between devices with their start and end apart: 38, of which 21 were waited for; matrix products, arithmetic and copies ran while one was open for 1% of the time, Pallas kernels for 17%

profile of v3, /device:TPU:0, one launch (start us, length us, event | category | flops | bytes accessed | tf_op | source)
XLA Modules:
  0.0 141.5 jit_solution(1060951986279418485)
XLA Ops:
  0.6 3.0 %collective-permute-start.1 = (bf16[256,2048]{1,0:T(8,128)(2,1)}, bf16[256,2048]{1,0:T(8,128)(2,1)S(1)}, u32[]{:S(2)}, u32[]{:S(2)}) collective-permute-start(bf16[256,2048]{1,0:T(8,128)(2,1)} %refs_5_.1), channel_id=1, source_target_pairs={{0,8},{4,12},{8,0},{12,4},{16,24},{20,28},{24,16},{28,20},{1,9},{5... | collective-permute-start | bytes 3145736 | tf_op jit(solution)/shard_map/ppermute | solution.py:489
  3.6 1.5 %collective-permute-start.3 = (bf16[256,2048]{1,0:T(8,128)(2,1)}, bf16[256,2048]{1,0:T(8,128)(2,1)}, u32[]{:S(2)}, u32[]{:S(2)}) collective-permute-start(bf16[256,2048]{1,0:T(8,128)(2,1)} %refs_5_.1), channel_id=1, source_target_pairs={{0,16},{4,20},{8,24},{12,28},{16,0},{20,4},{24,8},{28,12},{1,17},{... | collective-permute-start | bytes 3145736 | tf_op jit(solution)/shard_map/ppermute | solution.py:489
  5.2 1.4 copy-done.1
  6.6 0.7 copy-done.6
  7.3 3.8 %pack.1 = bf16[768,1152]{1,0:T(8,128)(2,1)} custom-call(s32[2]{0:T(128)S(1)} %pad_add_fusion.where_ref, s32[6,128]{1,0:T(8,128)S(1)} %bitcast.30, bf16[768,1024]{1,0:T(8,128)(2,1)S(1)} %copy-done.1), custom_call_target="tpu_custom_call" | custom-call | flops 1 | bytes 1 | tf_op jit(solution)/shard_map/pack/pallas_call | solution.py:615
  11.3 3.7 %all-to-all-start = ((bf16[8,96,1152]{2,1,0:T(8,128)(2,1)}), bf16[8,96,1152]{2,1,0:T(8,128)(2,1)S(1)}, u32[]{:S(2)}, u32[]{:S(2)}) async-start(bf16[8,96,1152]{2,1,0:T(8,128)(2,1)} %bitcast.6), calls=%async_computation | async-start | bytes 3538944 | tf_op jit(solution)/shard_map/all_to_all | solution.py:625
  15.0 0.6 prep.1
  16.0 0.2 compare_convert_fusion.pick
  16.2 11.7 %collective-permute-done.1.low_ref.refs_6_ = bf16[256,2048]{1,0:T(8,128)(2,1)S(1)} collective-permute-done((bf16[256,2048]{1,0:T(8,128)(2,1)}, bf16[256,2048]{1,0:T(8,128)(2,1)S(1)}, u32[]{:S(2)}, u32[]{:S(2)}) %collective-permute-start.1) | collective-permute-done | bytes 1048608 | tf_op jit(solution)/shard_map/ppermute | solution.py:489
  27.8 2.1 %collective-permute-done.3.high_ref.refs_7_ = bf16[256,2048]{1,0:T(8,128)(2,1)} collective-permute-done((bf16[256,2048]{1,0:T(8,128)(2,1)}, bf16[256,2048]{1,0:T(8,128)(2,1)}, u32[]{:S(2)}, u32[]{:S(2)}) %collective-permute-start.3) | collective-permute-done | bytes 1048608 | tf_op jit(solution)/shard_map/ppermute | solution.py:489
  29.9 1.1 halves.1
  31.0 0.8 copy-done.13
  31.9 0.8 copy-done.15
  32.7 0.5 collective-permute-start.4
  33.2 1.3 fold.1.refs_7_.refs_5_
  34.5 13.9 %all-to-all-done = bf16[8,96,1152]{2,1,0:T(8,128)(2,1)S(1)} async-done(((bf16[8,96,1152]{2,1,0:T(8,128)(2,1)}), bf16[8,96,1152]{2,1,0:T(8,128)(2,1)S(1)}, u32[]{:S(2)}, u32[]{:S(2)}) %all-to-all-start) | async-done | bytes 1769504 | tf_op jit(solution)/shard_map/all_to_all | solution.py:625
  48.4 1.5 %collective-permute-start.7 = (bf16[3,272,512]{2,1,0:T(8,128)(2,1)}, bf16[3,272,512]{2,1,0:T(8,128)(2,1)S(1)}, u32[]{:S(2)}, u32[]{:S(2)}) collective-permute-start(bf16[3,272,512]{2,1,0:T(8,128)(2,1)} %fold.1.refs_7_.refs_5_), channel_id=1, source_target_pairs={{0,16},{4,20},{8,24},{12,28},{16,0},{20,4},{24,8},{28,12},{1,17},{... | collective-permute-start | bytes 2506760 | tf_op jit(solution)/shard_map/ppermute | solution.py:489
  49.9 0.5 collective-permute-start.6
  50.5 1.6 %copy-done = bf16[1024,1024]{1,0:T(8,128)(2,1)S(1)} copy-done((bf16[1024,1024]{1,0:T(8,128)(2,1)S(1)}, bf16[1024,1024]{1,0:T(8,128)(2,1)}, u32[]{:S(2)}) %copy-start) | copy-done | bytes 2097176
  52.1 12.5 %encode.1.refs_0_ = bf16[8,2048]{1,0:T(8,128)(2,1)S(1)} custom-call(s32[6]{0:T(128)S(1)} %copy-done.9, f32[1,1024]{1,0:T(1,128)S(1)} %bitcast.31, bf16[768,1152]{1,0:T(8,128)(2,1)S(1)} %bitcast.23, bf16[1024,3072]{1,0:T(8,128)(2,1)} %qkv_ref.2, bf16[1024,1024]{1,0:T(8,128)(2,1)S(1)} %copy-done), custom_call_target="tpu_custom_call" | custom-call | flops 1 | bytes 1 | tf_op jit(solution)/shard_map/encode/pallas_call | solution.py:677
  64.6 4.2 %collective-permute-done.7.high_ref.refs_9_.refs_7_ = bf16[3,272,512]{2,1,0:T(8,128)(2,1)S(1)} collective-permute-done((bf16[3,272,512]{2,1,0:T(8,128)(2,1)}, bf16[3,272,512]{2,1,0:T(8,128)(2,1)S(1)}, u32[]{:S(2)}, u32[]{:S(2)}) %collective-permute-start.7) | collective-permute-done | bytes 835616 | tf_op jit(solution)/shard_map/ppermute | solution.py:489
  68.8 1.2 collective-permute-done.6.low_ref.refs_8_.refs_6_
  70.1 0.6 split.1
  70.7 0.6 collective-permute-start.11
  71.3 0.4 collective-permute-start.12
  71.6 3.7 %collective-permute-start.10 = (bf16[8,2048]{1,0:T(8,128)(2,1)S(1)}, bf16[8,2048]{1,0:T(8,128)(2,1)S(1)}, u32[]{:S(2)}, u32[]{:S(2)}) collective-permute-start(bf16[8,2048]{1,0:T(8,128)(2,1)S(1)} %encode.1.refs_0_), channel_id=1, source_target_pairs={{0,3},{1,2},{2,1},{3,0},{4,7},{5,6},{6,5},{7,4},{8,11},{9,10},{10,... | collective-permute-start | bytes 98312 | tf_op jit(solution)/shard_map/ppermute | solution.py:489
  75.4 0.6 collective-permute-start.8
  76.0 1.4 collective-permute-done.10.refs_3_
  77.4 2.8 %collective-permute-done.9.refs_2_ = bf16[8,2048]{1,0:T(8,128)(2,1)S(1)} collective-permute-done((bf16[8,2048]{1,0:T(8,128)(2,1)S(1)}, bf16[8,2048]{1,0:T(8,128)(2,1)S(1)}, u32[]{:S(2)}, u32[]{:S(2)}) %collective-permute-start.9) | collective-permute-done | bytes 32800 | tf_op jit(solution)/shard_map/ppermute | solution.py:489
  80.2 0.5 collective-permute-start.14
  80.7 1.6 %collective-permute-start.21 = (bf16[128,2048]{1,0:T(8,128)(2,1)S(1)}, bf16[128,2048]{1,0:T(8,128)(2,1)S(1)}, u32[]{:S(2)}, u32[]{:S(2)}) collective-permute-start(bf16[128,2048]{1,0:T(8,128)(2,1)S(1)} %copy-done.16), channel_id=1, source_target_pairs={{0,8},{4,12},{8,0},{12,4},{16,24},{20,28},{24,16},{28,20},{1,9},{5... | collective-permute-start | bytes 1572872 | tf_op jit(solution)/shard_map/ppermute | solution.py:489
  82.3 1.5 %collective-permute-start.20 = (bf16[128,2048]{1,0:T(8,128)(2,1)S(1)}, bf16[128,2048]{1,0:T(8,128)(2,1)S(1)}, u32[]{:S(2)}, u32[]{:S(2)}) collective-permute-start(bf16[128,2048]{1,0:T(8,128)(2,1)S(1)} %copy-done.14), channel_id=1, source_target_pairs={{0,16},{4,20},{8,24},{12,28},{16,0},{20,4},{24,8},{28,12},{1,17},{... | collective-permute-start | bytes 1572872 | tf_op jit(solution)/shard_map/ppermute | solution.py:489
  83.8 0.5 collective-permute-done.15.refs_15_.refs_13_
  84.3 0.1 collective-permute-start.16
  84.5 1.6 %collective-permute-done.16.refs_16_.refs_14_ = bf16[3,144,512]{2,1,0:T(8,128)(2,1)S(1)} collective-permute-done((bf16[3,144,512]{2,1,0:T(8,128)(2,1)S(1)}, bf16[3,144,512]{2,1,0:T(8,128)(2,1)S(1)}, u32[]{:S(2)}, u32[]{:S(2)}) %collective-permute-start.16) | collective-permute-done | bytes 442400 | tf_op jit(solution)/shard_map/ppermute | solution.py:489
  86.2 4.5 %project.1 = (bf16[32,512]{1,0:T(8,128)(2,1)S(1)}, f32[32,4224]{1,0:T(8,128)S(1)}) custom-call(s32[2]{0:T(128)S(1)} %pad_add_fusion.where_ref, bf16[8,2048]{1,0:T(8,128)(2,1)S(1)} %encode.1.refs_0_, bf16[8,2048]{1,0:T(8,128)(2,1)S(1)} %collective-permute-done.8.refs_1_, bf16[8,2048]{1,0:T(8,128)(2,1)S(1)} %collective-permute-done.9.refs_2_, ...), custom_call_target="tpu_custom_call" | custom-call | flops 1 | bytes 1 | tf_op jit(solution)/shard_map/project/pallas_call | solution.py:712
  90.7 2.4 %collective-permute-start.19 = (bf16[32,512]{1,0:T(8,128)(2,1)S(1)}, bf16[32,512]{1,0:T(8,128)(2,1)S(1)}, u32[]{:S(2)}, u32[]{:S(2)}) collective-permute-start(bf16[32,512]{1,0:T(8,128)(2,1)S(1)} %get-tuple-element.48.refs_0_), channel_id=1, source_target_pairs={{0,3},{1,2},{2,1},{3,0},{4,7},{5,6},{6,5},{7,4},{8,11},{9,10},{10,... | collective-permute-start | bytes 98312 | tf_op jit(solution)/shard_map/ppermute | solution.py:489
  93.1 2.0 %collective-permute-start.17 = (bf16[32,512]{1,0:T(8,128)(2,1)S(1)}, bf16[32,512]{1,0:T(8,128)(2,1)S(1)}, u32[]{:S(2)}, u32[]{:S(2)}) collective-permute-start(bf16[32,512]{1,0:T(8,128)(2,1)S(1)} %get-tuple-element.48.refs_0_), channel_id=1, source_target_pairs={{0,1},{1,0},{2,3},{3,2},{4,5},{5,4},{6,7},{7,6},{8,9},{9,8},{10,11... | collective-permute-start | bytes 98312 | tf_op jit(solution)/shard_map/ppermute | solution.py:489
  95.1 1.7 %collective-permute-done.19.refs_3_ = bf16[32,512]{1,0:T(8,128)(2,1)S(1)} collective-permute-done((bf16[32,512]{1,0:T(8,128)(2,1)S(1)}, bf16[32,512]{1,0:T(8,128)(2,1)S(1)}, u32[]{:S(2)}, u32[]{:S(2)}) %collective-permute-start.19) | collective-permute-done | bytes 32800 | tf_op jit(solution)/shard_map/ppermute | solution.py:489
  96.9 1.1 collective-permute-done.18.refs_2_
  97.9 0.5 collective-permute-start.23
  98.4 1.4 collective-permute-done.22.refs_13_
  99.8 0.7 collective-permute-done.23.refs_14_
  100.6 6.2 %ffn.1 = (bf16[32,640]{1,0:T(8,128)(2,1)S(1)}, bf16[32,640]{1,0:T(8,128)(2,1)S(1)}, bf16[32,640]{1,0:T(8,128)(2,1)S(1)}, bf16[32,640]{1,0:T(8,128)(2,1)S(1)}, f32[32,640]{1,0:T(8,128)S(1)}) custom-call(s32[2]{0:T(128)S(1)} %pad_add_fusion.where_ref, f32[2]{0:T(128)S(1)} %copy-done.10, f32[1,2048]{1,0:T(1,128)S(1)} %bitcast.28, ...), custom_call_target="tpu_custom_call" | custom-call | flops 1 | bytes 1 | tf_op jit(solution)/shard_map/ffn/pallas_call | solution.py:741
  106.8 1.2 collective-permute-start.24
  108.0 1.6 %collective-permute-start.25 = (bf16[32,640]{1,0:T(8,128)(2,1)S(1)}, bf16[32,640]{1,0:T(8,128)(2,1)S(1)}, u32[]{:S(2)}, u32[]{:S(2)}) collective-permute-start(bf16[32,640]{1,0:T(8,128)(2,1)S(1)} %get-tuple-element.57), channel_id=1, source_target_pairs={{0,2},{1,3},{2,0},{3,1},{4,6},{5,7},{6,4},{7,5},{8,10},{9,11},{10,... | collective-permute-start | bytes 122888 | tf_op jit(solution)/shard_map/ppermute | solution.py:489
  109.6 1.7 %collective-permute-start.26 = (bf16[32,640]{1,0:T(8,128)(2,1)S(1)}, bf16[32,640]{1,0:T(8,128)(2,1)S(1)}, u32[]{:S(2)}, u32[]{:S(2)}) collective-permute-start(bf16[32,640]{1,0:T(8,128)(2,1)S(1)} %get-tuple-element.58), channel_id=1, source_target_pairs={{0,3},{1,2},{2,1},{3,0},{4,7},{5,6},{6,5},{7,4},{8,11},{9,10},{10,... | collective-permute-start | bytes 122888 | tf_op jit(solution)/shard_map/ppermute | solution.py:489
  111.3 2.9 %collective-permute-done.25.refs_2_ = bf16[32,640]{1,0:T(8,128)(2,1)S(1)} collective-permute-done((bf16[32,640]{1,0:T(8,128)(2,1)S(1)}, bf16[32,640]{1,0:T(8,128)(2,1)S(1)}, u32[]{:S(2)}, u32[]{:S(2)}) %collective-permute-start.25) | collective-permute-done | bytes 40992 | tf_op jit(solution)/shard_map/ppermute | solution.py:489
  114.1 1.2 collective-permute-done.26.refs_3_
  115.4 8.2 %back.1 = (bf16[8,1152]{1,0:T(8,128)(2,1)S(1)}, bf16[8,1152]{1,0:T(8,128)(2,1)S(1)}, bf16[8,1152]{1,0:T(8,128)(2,1)S(1)}, bf16[8,1152]{1,0:T(8,128)(2,1)S(1)}, f...) custom-call(s32[2]{0:T(128)S(1)} %pad_add_fusion.where_ref, f32[32,640]{1,0:T(8,128)S(1)} %get-tuple-element.54.mid_ref, ...), custom_call_target="tpu_custom_call" | custom-call | flops 1 | bytes 1 | tf_op jit(solution)/shard_map/back/pallas_call | solution.py:763
  123.7 2.4 %collective-permute-start.28 = (bf16[8,1152]{1,0:T(8,128)(2,1)S(1)}, bf16[8,1152]{1,0:T(8,128)(2,1)S(1)}, u32[]{:S(2)}, u32[]{:S(2)}) collective-permute-start(bf16[8,1152]{1,0:T(8,128)(2,1)S(1)} %get-tuple-element.64), channel_id=1, source_target_pairs={{0,2},{1,3},{2,0},{3,1},{4,6},{5,7},{6,4},{7,5},{8,10},{9,11},{10,... | collective-permute-start | bytes 55304 | tf_op jit(solution)/shard_map/ppermute | solution.py:489
  126.0 2.0 %collective-permute-start.29 = (bf16[8,1152]{1,0:T(8,128)(2,1)S(1)}, bf16[8,1152]{1,0:T(8,128)(2,1)S(1)}, u32[]{:S(2)}, u32[]{:S(2)}) collective-permute-start(bf16[8,1152]{1,0:T(8,128)(2,1)S(1)} %get-tuple-element.65), channel_id=1, source_target_pairs={{0,3},{1,2},{2,1},{3,0},{4,7},{5,6},{6,5},{7,4},{8,11},{9,10},{10,... | collective-permute-start | bytes 55304 | tf_op jit(solution)/shard_map/ppermute | solution.py:489
  128.2 0.6 reshape.62
  128.8 2.8 %collective-permute-done.29.refs_3_ = bf16[8,1152]{1,0:T(8,128)(2,1)S(1)} collective-permute-done((bf16[8,1152]{1,0:T(8,128)(2,1)S(1)}, bf16[8,1152]{1,0:T(8,128)(2,1)S(1)}, u32[]{:S(2)}, u32[]{:S(2)}) %collective-permute-start.29) | collective-permute-done | bytes 18464 | tf_op jit(solution)/shard_map/ppermute | solution.py:489
  131.6 0.7 finish.1.refs_0_
  132.3 2.0 %collective-permute-start.32 = (f32[8,1024]{1,0:T(8,128)S(1)}, f32[8,1024]{1,0:T(8,128)S(1)}, u32[]{:S(2)}, u32[]{:S(2)}) collective-permute-start(f32[8,1024]{1,0:T(8,128)S(1)} %finish.1.refs_0_), channel_id=1, source_target_pairs={{0,24},{4,28},{8,16},{12,20},{16,8},{20,12},{24,0},{28,4},{1,25},{... | collective-permute-start | bytes 98312 | tf_op jit(solution)/shard_map/ppermute | solution.py:489
  134.3 0.5 collective-permute-start.31
  134.8 1.0 collective-permute-start.30
  135.8 1.3 collective-permute-done.32.refs_3_
  137.1 1.1 collective-permute-done.31.refs_2_
  138.2 0.5 collective-permute-done.30.refs_1_
  138.7 0.7 collective-permute-done.35.refs_6_
  139.4 0.5 collective-permute-done.34.refs_5_
  139.9 1.4 %spread.1 = bf16[768,1024]{1,0:T(8,128)(2,1)} custom-call(bf16[768,64]{1,0:T(8,128)(2,1)S(1)} %compare_convert_fusion.pick, f32[8,1024]{1,0:T(8,128)S(1)} %finish.1.refs_0_, f32[8,1024]{1,0:T(8,128)S(1)} %collective-permute-done.30.refs_1_, f32[8,1024]{1,0:T(8,128)S(1)} %collective-permute-done.31.refs_2_, f32[8,1024]{1,0:T(8,128)S(1)} %collective-permute-done.32.refs_3_, ...), custom_call_target="tpu_custom_call" | custom-call | flops 1 | bytes 1 | tf_op jit(solution)/shard_map/spread/pallas_call | solution.py:793
  (82 shorter events, 0.8 us)
Async XLA Ops:
  0.6 27.2 %collective-permute-start.1 = (bf16[256,2048]{1,0:T(8,128)(2,1)}, bf16[256,2048]{1,0:T(8,128)(2,1)S(1)}, u32[]{:S(2)}, u32[]{:S(2)}) collective-permute-start(bf16[256,2048]{1,0:T(8,128)(2,1)} %refs_5_.1), channel_id=1, source_target_pairs={{0,8},{4,12},{8,0},{12,4},{16,24},{20,28},{24,16},{28,20},{1,9},{5... | collective-permute-start | bytes 3145736 | tf_op jit(solution)/shard_map/ppermute | solution.py:489
  3.6 46.3 %collective-permute-start = (bf16[256,2048]{1,0:T(8,128)(2,1)}, bf16[256,2048]{1,0:T(8,128)(2,1)}, u32[]{:S(2)}, u32[]{:S(2)}) collective-permute-start(bf16[256,2048]{1,0:T(8,128)(2,1)} %refs_5_.1), channel_id=1, source_target_pairs={{0,4},{4,0},{8,12},{12,8},{16,20},{20,16},{24,28},{28,24},{1,5},{5... | collective-permute-start | bytes 3145736 | tf_op jit(solution)/shard_map/ppermute | solution.py:489
  3.6 26.3 %collective-permute-start.3 = (bf16[256,2048]{1,0:T(8,128)(2,1)}, bf16[256,2048]{1,0:T(8,128)(2,1)}, u32[]{:S(2)}, u32[]{:S(2)}) collective-permute-start(bf16[256,2048]{1,0:T(8,128)(2,1)} %refs_5_.1), channel_id=1, source_target_pairs={{0,16},{4,20},{8,24},{12,28},{16,0},{20,4},{24,8},{28,12},{1,17},{... | collective-permute-start | bytes 3145736 | tf_op jit(solution)/shard_map/ppermute | solution.py:489
  5.2 1.4 copy-start.1
  6.6 0.7 copy-start.6
  11.2 3.8 %copy-start.17 = (s32[24]{0:T(128)S(1)}, s32[24]{0:T(128)}, u32[]{:S(2)}) copy-start(s32[24]{0:T(128)} %patient_ref.1) | copy-start | bytes 292
  11.2 3.8 %copy-start.18 = (s32[24]{0:T(128)S(1)}, s32[24]{0:T(128)}, u32[]{:S(2)}) copy-start(s32[24]{0:T(128)} %treat_ref.1) | copy-start | bytes 292
  11.2 3.8 %copy-start.19 = (f32[24]{0:T(128)S(1)}, f32[24]{0:T(128)}, u32[]{:S(2)}) copy-start(f32[24]{0:T(128)} %target_ref.1) | copy-start | bytes 292
  11.2 4.4 %copy-start.22 = (s32[8]{0:T(128)S(1)}, s32[8]{0:T(128)}, u32[]{:S(2)}) copy-start(s32[8]{0:T(128)} %constant.26.clone) | copy-start | bytes 100
  11.2 4.7 %copy-start.3 = (f32[2048,2]{0,1:T(2,128)S(1)}, f32[2048,2]{0,1:T(2,128)}, u32[]{:S(2)}) copy-start(f32[2048,2]{0,1:T(2,128)} %param.31) | copy-start | bytes 49156
  11.2 4.8 %copy-start.7 = (s32[768]{0:T(1024)S(1)}, s32[768]{0:T(1024)}, u32[]{:S(2)}) copy-start(s32[768]{0:T(1024)} %param.18) | copy-start | bytes 9220
  11.3 37.1 %all-to-all-start = ((bf16[8,96,1152]{2,1,0:T(8,128)(2,1)}), bf16[8,96,1152]{2,1,0:T(8,128)(2,1)S(1)}, u32[]{:S(2)}, u32[]{:S(2)}) async-start(bf16[8,96,1152]{2,1,0:T(8,128)(2,1)} %bitcast.6), calls=%async_computation | async-start | bytes 3538944 | tf_op jit(solution)/shard_map/all_to_all | solution.py:625
  15.8 17.4 %copy-start.11 = (bf16[2048,256]{1,0:T(8,128)(2,1)S(1)}, bf16[2048,256]{1,0:T(8,128)(2,1)}, u32[]{:S(2)}) copy-start(bf16[2048,256]{1,0:T(8,128)(2,1)} %weight_ref.1) | copy-start | bytes 3145732
  15.8 17.4 %copy-start.12 = (bf16[3,256,512]{2,1,0:T(8,128)(2,1)S(1)}, bf16[3,256,512]{2,1,0:T(8,128)(2,1)}, u32[]{:S(2)}) copy-start(bf16[3,256,512]{2,1,0:T(8,128)(2,1)} %qkv_ref.1) | copy-start | bytes 2359300
  31.0 0.8 copy-start.13
  31.9 0.8 copy-start.15
  32.7 17.8 %copy-start.8 = (f32[1024]{0:T(1024)S(1)}, f32[1024]{0:T(1024)}, u32[]{:S(2)}) copy-start(f32[1024]{0:T(1024)} %param.23) | copy-start | bytes 12292
  32.7 17.8 %copy-start.9 = (s32[6]{0:T(128)S(1)}, s32[6]{0:T(128)}, u32[]{:S(2)}) copy-start(s32[6]{0:T(128)} %count_ref.3) | copy-start | bytes 76
  32.7 17.7 %collective-permute-start.2 = (bf16[256,2048]{1,0:T(8,128)(2,1)S(1)}, bf16[256,2048]{1,0:T(8,128)(2,1)}, u32[]{:S(2)}, u32[]{:S(2)}) collective-permute-start(bf16[256,2048]{1,0:T(8,128)(2,1)S(1)} %collective-permute-done.1.low_ref.refs_6_), channel_id=1, source_target_pairs={{0,4},{4,0},{8,12},{12,8},{16,20},{20,16},{24,28},{28,24},{1,5},{5... | collective-permute-start | bytes 3145736 | tf_op jit(solution)/shard_map/ppermute | solution.py:489
  32.7 17.7 %collective-permute-start.4 = (bf16[256,2048]{1,0:T(8,128)(2,1)}, bf16[256,2048]{1,0:T(8,128)(2,1)}, u32[]{:S(2)}, u32[]{:S(2)}) collective-permute-start(bf16[256,2048]{1,0:T(8,128)(2,1)} %collective-permute-done.3.high_ref.refs_7_), channel_id=1, source_target_pairs={{0,4},{4,0},{8,12},{12,8},{16,20},{20,16},{24,28},{28,24},{1,5},{5... | collective-permute-start | bytes 3145736 | tf_op jit(solution)/shard_map/ppermute | solution.py:489
  34.5 15.9 %collective-permute-start.5 = (bf16[3,272,512]{2,1,0:T(8,128)(2,1)}, bf16[3,272,512]{2,1,0:T(8,128)(2,1)}, u32[]{:S(2)}, u32[]{:S(2)}) collective-permute-start(bf16[3,272,512]{2,1,0:T(8,128)(2,1)} %fold.1.refs_7_.refs_5_), channel_id=1, source_target_pairs={{0,4},{4,0},{8,12},{12,8},{16,20},{20,16},{24,28},{28,24},{1,5},{5... | collective-permute-start | bytes 2506760 | tf_op jit(solution)/shard_map/ppermute | solution.py:489
  48.4 20.4 %collective-permute-start.7 = (bf16[3,272,512]{2,1,0:T(8,128)(2,1)}, bf16[3,272,512]{2,1,0:T(8,128)(2,1)S(1)}, u32[]{:S(2)}, u32[]{:S(2)}) collective-permute-start(bf16[3,272,512]{2,1,0:T(8,128)(2,1)} %fold.1.refs_7_.refs_5_), channel_id=1, source_target_pairs={{0,16},{4,20},{8,24},{12,28},{16,0},{20,4},{24,8},{28,12},{1,17},{... | collective-permute-start | bytes 2506760 | tf_op jit(solution)/shard_map/ppermute | solution.py:489
  49.9 20.2 %collective-permute-start.6 = (bf16[3,272,512]{2,1,0:T(8,128)(2,1)}, bf16[3,272,512]{2,1,0:T(8,128)(2,1)S(1)}, u32[]{:S(2)}, u32[]{:S(2)}) collective-permute-start(bf16[3,272,512]{2,1,0:T(8,128)(2,1)} %fold.1.refs_7_.refs_5_), channel_id=1, source_target_pairs={{0,8},{4,12},{8,0},{12,4},{16,24},{20,28},{24,16},{28,20},{1,9},{5... | collective-permute-start | bytes 2506760 | tf_op jit(solution)/shard_map/ppermute | solution.py:489
  50.5 1.6 %copy-start = (bf16[1024,1024]{1,0:T(8,128)(2,1)S(1)}, bf16[1024,1024]{1,0:T(8,128)(2,1)}, u32[]{:S(2)}) copy-start(bf16[1024,1024]{1,0:T(8,128)(2,1)} %proj_ref.1) | copy-start | bytes 6291460
  52.1 28.7 %copy-start.16 = (bf16[128,2048]{1,0:T(8,128)(2,1)S(1)}, bf16[128,2048]{1,0:T(8,128)(2,1)}, u32[]{:S(2)}) copy-start(bf16[128,2048]{1,0:T(8,128)(2,1)} %copy-done.15) | copy-start | bytes 1572868
  52.1 30.2 %copy-start.14 = (bf16[128,2048]{1,0:T(8,128)(2,1)S(1)}, bf16[128,2048]{1,0:T(8,128)(2,1)}, u32[]{:S(2)}) copy-start(bf16[128,2048]{1,0:T(8,128)(2,1)} %copy-done.13) | copy-start | bytes 1572868
  52.1 34.1 %copy-start.4 = (f32[2048]{0:T(1024)S(1)}, f32[2048]{0:T(1024)}, u32[]{:S(2)}) copy-start(f32[2048]{0:T(1024)} %param.26) | copy-start | bytes 24580
  70.7 10.0 %collective-permute-start.11 = (bf16[3,128,512]{2,1,0:T(8,128)(2,1)S(1)}, bf16[3,128,512]{2,1,0:T(8,128)(2,1)S(1)}, u32[]{:S(2)}, u32[]{:S(2)}) collective-permute-start(bf16[3,128,512]{2,1,0:T(8,128)(2,1)S(1)} %get-tuple-element.43), channel_id=1, source_target_pairs={{0,16},{4,20},{8,24},{12,28},{16,0},{20,4},{24,8},{28,12},{1,17},{... | collective-permute-start | bytes 1179656 | tf_op jit(solution)/shard_map/ppermute | solution.py:489
  71.3 11.0 %collective-permute-start.12 = (bf16[3,144,512]{2,1,0:T(8,128)(2,1)S(1)}, bf16[3,144,512]{2,1,0:T(8,128)(2,1)S(1)}, u32[]{:S(2)}, u32[]{:S(2)}) collective-permute-start(bf16[3,144,512]{2,1,0:T(8,128)(2,1)S(1)} %get-tuple-element.44), channel_id=1, source_target_pairs={{0,8},{4,12},{8,0},{12,4},{16,24},{20,28},{24,16},{28,20},{1,9},{5... | collective-permute-start | bytes 1327112 | tf_op jit(solution)/shard_map/ppermute | solution.py:489
  71.6 5.8 %collective-permute-start.10 = (bf16[8,2048]{1,0:T(8,128)(2,1)S(1)}, bf16[8,2048]{1,0:T(8,128)(2,1)S(1)}, u32[]{:S(2)}, u32[]{:S(2)}) collective-permute-start(bf16[8,2048]{1,0:T(8,128)(2,1)S(1)} %encode.1.refs_0_), channel_id=1, source_target_pairs={{0,3},{1,2},{2,1},{3,0},{4,7},{5,6},{6,5},{7,4},{8,11},{9,10},{10,... | collective-permute-start | bytes 98312 | tf_op jit(solution)/shard_map/ppermute | solution.py:489
  75.4 4.8 %collective-permute-start.9 = (bf16[8,2048]{1,0:T(8,128)(2,1)S(1)}, bf16[8,2048]{1,0:T(8,128)(2,1)S(1)}, u32[]{:S(2)}, u32[]{:S(2)}) collective-permute-start(bf16[8,2048]{1,0:T(8,128)(2,1)S(1)} %encode.1.refs_0_), channel_id=1, source_target_pairs={{0,2},{1,3},{2,0},{3,1},{4,6},{5,7},{6,4},{7,5},{8,10},{9,11},{10,... | collective-permute-start | bytes 98312 | tf_op jit(solution)/shard_map/ppermute | solution.py:489
  75.4 4.8 %collective-permute-start.8 = (bf16[8,2048]{1,0:T(8,128)(2,1)S(1)}, bf16[8,2048]{1,0:T(8,128)(2,1)S(1)}, u32[]{:S(2)}, u32[]{:S(2)}) collective-permute-start(bf16[8,2048]{1,0:T(8,128)(2,1)S(1)} %encode.1.refs_0_), channel_id=1, source_target_pairs={{0,1},{1,0},{2,3},{3,2},{4,5},{5,4},{6,7},{7,6},{8,9},{9,8},{10,11... | collective-permute-start | bytes 98312 | tf_op jit(solution)/shard_map/ppermute | solution.py:489
  80.2 4.3 %collective-permute-start.13 = (bf16[3,272,512]{2,1,0:T(8,128)(2,1)S(1)}, bf16[3,272,512]{2,1,0:T(8,128)(2,1)S(1)}, u32[]{:S(2)}, u32[]{:S(2)}) collective-permute-start(bf16[3,272,512]{2,1,0:T(8,128)(2,1)S(1)} %collective-permute-done.6.low_ref.refs_8_.refs_6_), channel_id=1, source_target_pairs={{0,4},{4,0},{8,12},{12,8},{16,20},{20,16},{24,28},{28,24},{1,5},{5... | collective-permute-start | bytes 2506760 | tf_op jit(solution)/shard_map/ppermute | solution.py:489
  80.2 4.3 %collective-permute-start.14 = (bf16[3,272,512]{2,1,0:T(8,128)(2,1)S(1)}, bf16[3,272,512]{2,1,0:T(8,128)(2,1)S(1)}, u32[]{:S(2)}, u32[]{:S(2)}) collective-permute-start(bf16[3,272,512]{2,1,0:T(8,128)(2,1)S(1)} %collective-permute-done.7.high_ref.refs_9_.refs_7_), channel_id=1, source_target_pairs={{0,4},{4,0},{8,12},{12,8},{16,20},{20,16},{24,28},{28,24},{1,5},{5... | collective-permute-start | bytes 2506760 | tf_op jit(solution)/shard_map/ppermute | solution.py:489
  80.7 3.6 %collective-permute-start.15 = (bf16[3,128,512]{2,1,0:T(8,128)(2,1)S(1)}, bf16[3,128,512]{2,1,0:T(8,128)(2,1)S(1)}, u32[]{:S(2)}, u32[]{:S(2)}) collective-permute-start(bf16[3,128,512]{2,1,0:T(8,128)(2,1)S(1)} %collective-permute-done.11.refs_10_.refs_8_), channel_id=1, source_target_pairs={{0,4},{4,0},{8,12},{12,8},{16,20},{20,16},{24,28},{28,24},{1,5},{5... | collective-permute-start | bytes 1179656 | tf_op jit(solution)/shard_map/ppermute | solution.py:489
  80.7 14.4 %collective-permute-start.21 = (bf16[128,2048]{1,0:T(8,128)(2,1)S(1)}, bf16[128,2048]{1,0:T(8,128)(2,1)S(1)}, u32[]{:S(2)}, u32[]{:S(2)}) collective-permute-start(bf16[128,2048]{1,0:T(8,128)(2,1)S(1)} %copy-done.16), channel_id=1, source_target_pairs={{0,8},{4,12},{8,0},{12,4},{16,24},{20,28},{24,16},{28,20},{1,9},{5... | collective-permute-start | bytes 1572872 | tf_op jit(solution)/shard_map/ppermute | solution.py:489
  82.3 15.6 %collective-permute-start.20 = (bf16[128,2048]{1,0:T(8,128)(2,1)S(1)}, bf16[128,2048]{1,0:T(8,128)(2,1)S(1)}, u32[]{:S(2)}, u32[]{:S(2)}) collective-permute-start(bf16[128,2048]{1,0:T(8,128)(2,1)S(1)} %copy-done.14), channel_id=1, source_target_pairs={{0,16},{4,20},{8,24},{12,28},{16,0},{20,4},{24,8},{28,12},{1,17},{... | collective-permute-start | bytes 1572872 | tf_op jit(solution)/shard_map/ppermute | solution.py:489
  84.3 1.8 %collective-permute-start.16 = (bf16[3,144,512]{2,1,0:T(8,128)(2,1)S(1)}, bf16[3,144,512]{2,1,0:T(8,128)(2,1)S(1)}, u32[]{:S(2)}, u32[]{:S(2)}) collective-permute-start(bf16[3,144,512]{2,1,0:T(8,128)(2,1)S(1)} %collective-permute-done.12.refs_11_.refs_9_), channel_id=1, source_target_pairs={{0,4},{4,0},{8,12},{12,8},{16,20},{20,16},{24,28},{28,24},{1,5},{5... | collective-permute-start | bytes 1327112 | tf_op jit(solution)/shard_map/ppermute | solution.py:489
  84.5 1.7 %copy-start.20 = (bf16[3,272,512]{2,1,0:T(8,128)(2,1)}, bf16[3,272,512]{2,1,0:T(8,128)(2,1)S(1)}, u32[]{:S(2)}) copy-start(bf16[3,272,512]{2,1,0:T(8,128)(2,1)S(1)} %collective-permute-done.13.refs_13_.refs_11_) | copy-start | bytes 2506756
  84.5 1.7 %copy-start.21 = (bf16[3,272,512]{2,1,0:T(8,128)(2,1)}, bf16[3,272,512]{2,1,0:T(8,128)(2,1)S(1)}, u32[]{:S(2)}) copy-start(bf16[3,272,512]{2,1,0:T(8,128)(2,1)S(1)} %collective-permute-done.14.refs_14_.refs_12_) | copy-start | bytes 2506756
  86.1 14.5 %copy-start.2 = (bf16[256,2048]{1,0:T(8,128)(2,1)S(1)}, bf16[256,2048]{1,0:T(8,128)(2,1)}, u32[]{:S(2)}) copy-start(bf16[256,2048]{1,0:T(8,128)(2,1)} %refs_5_.1) | copy-start | bytes 3145732
  86.1 14.4 %copy-start.5 = (f32[2048]{0:T(1024)S(1)}, f32[2048]{0:T(1024)}, u32[]{:S(2)}) copy-start(f32[2048]{0:T(1024)} %param.28) | copy-start | bytes 24580
  86.2 14.4 %copy-start.10 = (f32[2]{0:T(128)S(1)}, f32[2]{0:T(128)}, u32[]{:S(2)}) copy-start(f32[2]{0:T(128)} %bias_ref.1) | copy-start | bytes 28
  90.7 6.2 %collective-permute-start.19 = (bf16[32,512]{1,0:T(8,128)(2,1)S(1)}, bf16[32,512]{1,0:T(8,128)(2,1)S(1)}, u32[]{:S(2)}, u32[]{:S(2)}) collective-permute-start(bf16[32,512]{1,0:T(8,128)(2,1)S(1)} %get-tuple-element.48.refs_0_), channel_id=1, source_target_pairs={{0,3},{1,2},{2,1},{3,0},{4,7},{5,6},{6,5},{7,4},{8,11},{9,10},{10,... | collective-permute-start | bytes 98312 | tf_op jit(solution)/shard_map/ppermute | solution.py:489
  93.1 4.8 %collective-permute-start.18 = (bf16[32,512]{1,0:T(8,128)(2,1)S(1)}, bf16[32,512]{1,0:T(8,128)(2,1)S(1)}, u32[]{:S(2)}, u32[]{:S(2)}) collective-permute-start(bf16[32,512]{1,0:T(8,128)(2,1)S(1)} %get-tuple-element.48.refs_0_), channel_id=1, source_target_pairs={{0,2},{1,3},{2,0},{3,1},{4,6},{5,7},{6,4},{7,5},{8,10},{9,11},{10,... | collective-permute-start | bytes 98312 | tf_op jit(solution)/shard_map/ppermute | solution.py:489
  93.1 4.8 %collective-permute-start.17 = (bf16[32,512]{1,0:T(8,128)(2,1)S(1)}, bf16[32,512]{1,0:T(8,128)(2,1)S(1)}, u32[]{:S(2)}, u32[]{:S(2)}) collective-permute-start(bf16[32,512]{1,0:T(8,128)(2,1)S(1)} %get-tuple-element.48.refs_0_), channel_id=1, source_target_pairs={{0,1},{1,0},{2,3},{3,2},{4,5},{5,4},{6,7},{7,6},{8,9},{9,8},{10,11... | collective-permute-start | bytes 98312 | tf_op jit(solution)/shard_map/ppermute | solution.py:489
  97.9 1.9 %collective-permute-start.22 = (bf16[128,2048]{1,0:T(8,128)(2,1)S(1)}, bf16[128,2048]{1,0:T(8,128)(2,1)S(1)}, u32[]{:S(2)}, u32[]{:S(2)}) collective-permute-start(bf16[128,2048]{1,0:T(8,128)(2,1)S(1)} %collective-permute-done.20.refs_8_), channel_id=1, source_target_pairs={{0,4},{4,0},{8,12},{12,8},{16,20},{20,16},{24,28},{28,24},{1,5},{5... | collective-permute-start | bytes 1572872 | tf_op jit(solution)/shard_map/ppermute | solution.py:489
  97.9 2.7 %collective-permute-start.23 = (bf16[128,2048]{1,0:T(8,128)(2,1)S(1)}, bf16[128,2048]{1,0:T(8,128)(2,1)S(1)}, u32[]{:S(2)}, u32[]{:S(2)}) collective-permute-start(bf16[128,2048]{1,0:T(8,128)(2,1)S(1)} %collective-permute-done.21.refs_9_), channel_id=1, source_target_pairs={{0,4},{4,0},{8,12},{12,8},{16,20},{20,16},{24,28},{28,24},{1,5},{5... | collective-permute-start | bytes 1572872 | tf_op jit(solution)/shard_map/ppermute | solution.py:489
  106.8 4.5 %collective-permute-start.24 = (bf16[32,640]{1,0:T(8,128)(2,1)S(1)}, bf16[32,640]{1,0:T(8,128)(2,1)S(1)}, u32[]{:S(2)}, u32[]{:S(2)}) collective-permute-start(bf16[32,640]{1,0:T(8,128)(2,1)S(1)} %get-tuple-element.56), channel_id=1, source_target_pairs={{0,1},{1,0},{2,3},{3,2},{4,5},{5,4},{6,7},{7,6},{8,9},{9,8},{10,11... | collective-permute-start | bytes 122888 | tf_op jit(solution)/shard_map/ppermute | solution.py:489
  108.0 6.2 %collective-permute-start.25 = (bf16[32,640]{1,0:T(8,128)(2,1)S(1)}, bf16[32,640]{1,0:T(8,128)(2,1)S(1)}, u32[]{:S(2)}, u32[]{:S(2)}) collective-permute-start(bf16[32,640]{1,0:T(8,128)(2,1)S(1)} %get-tuple-element.57), channel_id=1, source_target_pairs={{0,2},{1,3},{2,0},{3,1},{4,6},{5,7},{6,4},{7,5},{8,10},{9,11},{10,... | collective-permute-start | bytes 122888 | tf_op jit(solution)/shard_map/ppermute | solution.py:489
  109.6 5.8 %collective-permute-start.26 = (bf16[32,640]{1,0:T(8,128)(2,1)S(1)}, bf16[32,640]{1,0:T(8,128)(2,1)S(1)}, u32[]{:S(2)}, u32[]{:S(2)}) collective-permute-start(bf16[32,640]{1,0:T(8,128)(2,1)S(1)} %get-tuple-element.58), channel_id=1, source_target_pairs={{0,3},{1,2},{2,1},{3,0},{4,7},{5,6},{6,5},{7,4},{8,11},{9,10},{10,... | collective-permute-start | bytes 122888 | tf_op jit(solution)/shard_map/ppermute | solution.py:489
  123.6 5.2 %collective-permute-start.27 = (bf16[8,1152]{1,0:T(8,128)(2,1)S(1)}, bf16[8,1152]{1,0:T(8,128)(2,1)S(1)}, u32[]{:S(2)}, u32[]{:S(2)}) collective-permute-start(bf16[8,1152]{1,0:T(8,128)(2,1)S(1)} %get-tuple-element.63), channel_id=1, source_target_pairs={{0,1},{1,0},{2,3},{3,2},{4,5},{5,4},{6,7},{7,6},{8,9},{9,8},{10,11... | collective-permute-start | bytes 55304 | tf_op jit(solution)/shard_map/ppermute | solution.py:489
  123.7 5.1 %collective-permute-start.28 = (bf16[8,1152]{1,0:T(8,128)(2,1)S(1)}, bf16[8,1152]{1,0:T(8,128)(2,1)S(1)}, u32[]{:S(2)}, u32[]{:S(2)}) collective-permute-start(bf16[8,1152]{1,0:T(8,128)(2,1)S(1)} %get-tuple-element.64), channel_id=1, source_target_pairs={{0,2},{1,3},{2,0},{3,1},{4,6},{5,7},{6,4},{7,5},{8,10},{9,11},{10,... | collective-permute-start | bytes 55304 | tf_op jit(solution)/shard_map/ppermute | solution.py:489
  126.0 5.6 %collective-permute-start.29 = (bf16[8,1152]{1,0:T(8,128)(2,1)S(1)}, bf16[8,1152]{1,0:T(8,128)(2,1)S(1)}, u32[]{:S(2)}, u32[]{:S(2)}) collective-permute-start(bf16[8,1152]{1,0:T(8,128)(2,1)S(1)} %get-tuple-element.65), channel_id=1, source_target_pairs={{0,3},{1,2},{2,1},{3,0},{4,7},{5,6},{6,5},{7,4},{8,11},{9,10},{10,... | collective-permute-start | bytes 55304 | tf_op jit(solution)/shard_map/ppermute | solution.py:489
  132.3 4.8 %collective-permute-start.32 = (f32[8,1024]{1,0:T(8,128)S(1)}, f32[8,1024]{1,0:T(8,128)S(1)}, u32[]{:S(2)}, u32[]{:S(2)}) collective-permute-start(f32[8,1024]{1,0:T(8,128)S(1)} %finish.1.refs_0_), channel_id=1, source_target_pairs={{0,24},{4,28},{8,16},{12,20},{16,8},{20,12},{24,0},{28,4},{1,25},{... | collective-permute-start | bytes 98312 | tf_op jit(solution)/shard_map/ppermute | solution.py:489
  134.3 3.9 %collective-permute-start.31 = (f32[8,1024]{1,0:T(8,128)S(1)}, f32[8,1024]{1,0:T(8,128)S(1)}, u32[]{:S(2)}, u32[]{:S(2)}) collective-permute-start(f32[8,1024]{1,0:T(8,128)S(1)} %finish.1.refs_0_), channel_id=1, source_target_pairs={{0,16},{4,20},{8,24},{12,28},{16,0},{20,4},{24,8},{28,12},{1,17},{... | collective-permute-start | bytes 98312 | tf_op jit(solution)/shard_map/ppermute | solution.py:489
  134.8 3.9 %collective-permute-start.30 = (f32[8,1024]{1,0:T(8,128)S(1)}, f32[8,1024]{1,0:T(8,128)S(1)}, u32[]{:S(2)}, u32[]{:S(2)}) collective-permute-start(f32[8,1024]{1,0:T(8,128)S(1)} %finish.1.refs_0_), channel_id=1, source_target_pairs={{0,8},{4,12},{8,0},{12,4},{16,24},{20,28},{24,16},{28,20},{1,9},{5... | collective-permute-start | bytes 98312 | tf_op jit(solution)/shard_map/ppermute | solution.py:489
  135.8 2.9 %collective-permute-start.33 = (f32[8,1024]{1,0:T(8,128)S(1)}, f32[8,1024]{1,0:T(8,128)S(1)}, u32[]{:S(2)}, u32[]{:S(2)}) collective-permute-start(f32[8,1024]{1,0:T(8,128)S(1)} %finish.1.refs_0_), channel_id=1, source_target_pairs={{0,4},{4,0},{8,12},{12,8},{16,20},{20,16},{24,28},{28,24},{1,5},{5... | collective-permute-start | bytes 98312 | tf_op jit(solution)/shard_map/ppermute | solution.py:489
  137.1 1.6 %collective-permute-start.36 = (f32[8,1024]{1,0:T(8,128)S(1)}, f32[8,1024]{1,0:T(8,128)S(1)}, u32[]{:S(2)}, u32[]{:S(2)}) collective-permute-start(f32[8,1024]{1,0:T(8,128)S(1)} %collective-permute-done.32.refs_3_), channel_id=1, source_target_pairs={{0,4},{4,0},{8,12},{12,8},{16,20},{20,16},{24,28},{28,24},{1,5},{5... | collective-permute-start | bytes 98312 | tf_op jit(solution)/shard_map/ppermute | solution.py:489
  138.2 1.2 collective-permute-start.35
  138.7 1.2 collective-permute-start.34

commit v4 on v3

--- a/solution.py
+++ b/solution.py
@@ -109,21 +109,16 @@
     row_ref[...] = line
 
 
-def fold_kernel(weight_ref, head_ref, qkv_ref, out_ref):
-    rows, cols = qkv_ref.shape[1:]
-    out_ref[:, :rows, :] = qkv_ref[...]
+def fold_kernel(weight_ref, head_ref, ffn_ref, out_ref):
+    rows = ffn_ref.shape[0]
+    out_ref[:rows, :] = ffn_ref[...]
     folded = dot(head_ref[...], weight_ref[...], NT)
     folded = folded[0:2] + folded[2:4] + folded[4:6]
     one = folded.astype(BF16).astype(F32)
     two = (folded - one).astype(BF16).astype(F32)
-    parts = (one, two, folded - one - two)
-    chunks = folded.shape[1] // cols
-    blank = jnp.zeros((FW_ROWS - 2 * chunks, cols), F32)
-    for t in range(3):
-        lines = [
-            parts[t][j : j + 1, c * cols : (c + 1) * cols] for j in range(2) for c in range(chunks)
-        ]
-        out_ref[t, rows:, :] = jnp.concatenate(lines + [blank], axis=0).astype(BF16)
+    three = folded - one - two
+    blank = jnp.zeros((FW_ROWS - 6, folded.shape[1]), F32)
+    out_ref[rows:, :] = jnp.concatenate([one, two, three, blank], axis=0).astype(BF16)
 
 
 def encode_kernel(
@@ -269,18 +264,14 @@
     for j in range(n_ev):
         blocks[j] = normed[:, j * width : (j + 1) * width]
     totals = [jnp.zeros((rows, cols), F32) for _ in range(3)]
-    fw = jnp.zeros((FW_ROWS, cols), F32)
     for i, (k, lo, size) in enumerate(plan):
         copies[i].wait()
         block = blocks[e ^ k][:, lo : lo + size]
         for t in range(3):
             totals[t] = totals[t] + dot(block, scratch[i][t, :size, :])
-            if scratch[i].shape[1] > size:
-                fw = fw + scratch[i][t, size:, :].astype(F32)
     parts = [total.astype(BF16) for total in totals]
     for t in range(3):
         kept[:, DV + t * cols : DV + (t + 1) * cols] = parts[t].astype(F32)
-    kept[:FW_ROWS, DV + 3 * cols : DV + 4 * cols] = fw
     saves[1].start()
     q_at = lax.broadcasted_iota(jnp.int32, (rows, rows), 0)
     k_at = lax.broadcasted_iota(jnp.int32, (rows, rows), 1)
@@ -291,7 +282,7 @@
         scores = jnp.where(allowed, scores, -1e30)
         grown = jnp.exp(scores - jnp.max(scores, axis=-1, keepdims=True))
         prob = grown / jnp.sum(grown, axis=-1, keepdims=True)
-        kept[:, DV + 4 * cols + h * rows : DV + 4 * cols + (h + 1) * rows] = prob
+        kept[:, DV + 3 * cols + h * rows : DV + 3 * cols + (h + 1) * rows] = prob
         attended_ref[:, span] = dot(prob.astype(BF16), parts[2][:, span]).astype(BF16)
     saves[2].start()
     for save in saves:
@@ -299,7 +290,7 @@
 
 
 def state_spans(cols):
-    return ((0, DV), (DV, DV + 4 * cols), (DV + 4 * cols, DV + 4 * cols + LANES))
+    return ((0, DV), (DV, DV + 3 * cols), (DV + 3 * cols, DV + 3 * cols + LANES))
 
 
 def pack_scalars(columns, rows):
@@ -326,12 +317,10 @@
     pieces, refs = refs[:n], refs[n:]
     outs, mid_ref, refs = refs[:n_mp], refs[n_mp], refs[n_mp + 1 :]
     scratch, refs = refs[:n], refs[n:]
-    attn, vec_ref, fw_ref, blocks, grads, sems = refs
+    attn, vec_ref, blocks, grads, sems = refs
     e, m = where_ref[0], where_ref[1]
     cols = DV // n_mp
-    fw_at = DV + 3 * cols
-    sources = [state.at[:, :DV], state.at[:FW_ROWS, fw_at : fw_at + cols]]
-    small = fetch(sources, [vec_ref, fw_ref], sems, n)
+    small = fetch([state.at[:, :DV]], [vec_ref], sems, n)
     copies = fetch(pieces, scratch, sems)
     for k in range(n_mp):
         attn[m ^ k] = attn_in[k][...]
@@ -350,25 +339,24 @@
         blocks[j] = normed[:, j * width : (j + 1) * width]
     hidden = scratch[0].shape[1]
     pre = jnp.zeros((rows, hidden), F32)
-    chunks = hidden // fw_ref.shape[1]
-    fw = [
-        jnp.concatenate([fw_ref[j * chunks + c : j * chunks + c + 1, :] for c in range(chunks)], axis=1)
-        for j in range(2)
-    ]
+    fw = jnp.zeros((2, hidden), F32)
     for i, (k, lo, size) in enumerate(plan):
         copies[i].wait()
-        pre = pre + dot(blocks[e ^ k][:, lo : lo + size], scratch[i][...])
+        pre = pre + dot(blocks[e ^ k][:, lo : lo + size], scratch[i][:size, :])
+        if scratch[i].shape[0] > size:
+            parts = scratch[i][size : size + FW_ROWS, :].astype(F32)
+            fw = fw + (parts[0:2] + parts[2:4] + parts[4:6])
     sigma = 1.0 / (1.0 + jnp.exp(-pre))
     act = (pre * sigma).astype(BF16).astype(F32)
     first = (m == 0).astype(F32)
     outcome = []
     for j in range(2):
         base = jnp.sum(mid * head_ref[j : j + 1, :], axis=-1, keepdims=True) + bias_ref[j]
-        outcome.append(jnp.sum(act * fw[j], axis=-1, keepdims=True) + first * base)
-    chosen = jnp.where(meta_ref[:, 0:1] > 0.5, fw[1], fw[0])
+        outcome.append(jnp.sum(act * fw[j : j + 1, :], axis=-1, keepdims=True) + first * base)
+    chosen = jnp.where(meta_ref[:, 0:1] > 0.5, fw[1:2, :], fw[0:1, :])
     slope = (chosen * sigma * (1.0 + pre * (1.0 - sigma))).astype(BF16)
     for i, (k, lo, size) in enumerate(plan):
-        grads[e ^ k, :, lo : lo + size] = dot(slope, scratch[i][...], NT)
+        grads[e ^ k, :, lo : lo + size] = dot(slope, scratch[i][:size, :], NT)
     moment = jnp.zeros((rows, 1), F32)
     for j in range(n_ev):
         span = slice(j * width, (j + 1) * width)
@@ -419,7 +407,7 @@
     three = [[], [], []]
     for h in range(cols // VHDIM):
         span = slice(h * VHDIM, (h + 1) * VHDIM)
-        prob = kept[:, DV + 4 * cols + h * rows : DV + 4 * cols + (h + 1) * rows]
+        prob = kept[:, DV + 3 * cols + h * rows : DV + 3 * cols + (h + 1) * rows]
         grad_p = dot(grad_c[:, span], values[:, span], NT)
         grad_s = prob * (grad_p - jnp.sum(grad_p * prob, axis=-1, keepdims=True))
         grad_s = (grad_s * VHDIM ** (-0.5)).astype(BF16)
@@ -496,20 +484,23 @@
 
 
 def halves_kernel(low_ref, high_ref, low_out, high_out):
+    half = low_out.shape[0]
     low_out[...] = low_ref[...]
-    high_out[...] = high_ref[...]
+    high_out[...] = high_ref[half:, :]
 
 
 def halves_of(pieces, half):
-    cols = pieces[1].shape[1]
-    shape = jax.ShapeDtypeStruct((half, cols), BF16)
-    block = pl.BlockSpec((half, cols), lambda i: (0, 0))
+    rows, cols = pieces[1].shape
+    low = pl.BlockSpec((half, cols), lambda i: (0, 0))
     return pl.pallas_call(
         halves_kernel,
         grid=(1,),
-        out_shape=[shape, shape],
-        in_specs=[block, pl.BlockSpec((half, cols), lambda i: (1, 0))],
-        out_specs=[block, block],
+        out_shape=[
+            jax.ShapeDtypeStruct((half, cols), BF16),
+            jax.ShapeDtypeStruct((rows - half, cols), BF16),
+        ],
+        in_specs=[low, vmem()],
+        out_specs=[low, vmem()],
         compiler_params=params(SNUG),
         cost_estimate=cost(0),
         name="halves",
@@ -627,7 +618,7 @@
         tiled=True,
     ).reshape(rows_dev, D + LANES)
 
-    ffn_first = first_hop(ffn_in, n_ev)
+    qkv_first = first_hop(visit_qkv, n_ev)
 
     head_t = head_weight.T
     width = DV // n_ev
@@ -655,25 +646,29 @@
     chosen = (event_visit[:, None] == named[None, :]).astype(BF16)
     ready = [meta, patient_row, head_t, chosen]
     if two_hops:
-        ffn_halves = halves_of(ffn_first, width // 2)
-        ready += ffn_halves
-    qkv_shard = pl.pallas_call(
+        qkv_halves = split_of(qkv_first, width // 2)
+        qkv_far = across(qkv_first, n_ev)
+        ready += [*qkv_halves, *qkv_far]
+    ffn_shard = pl.pallas_call(
         fold_kernel,
-        out_shape=jax.ShapeDtypeStruct((3, width + FW_ROWS, cols), BF16),
+        out_shape=jax.ShapeDtypeStruct((width + FW_ROWS, hidden), BF16),
         in_specs=[vmem()] * 3,
         out_specs=vmem(),
         compiler_params=params(SNUG),
         cost_estimate=cost(30),
         name="fold",
-    )(ffn_out, heads, after(visit_qkv, *ffn_first[1:], *ready))
-    qkv_first = [qkv_shard] + first_hop(after(qkv_shard, got), n_ev)[1:]
+    )(ffn_out, heads, after(ffn_in, *ready))
     qkv_plan = hop_plan(n_ev, width)
     ffn_plan = hop_plan(n_ev, width)
+    gate = [got]
     if two_hops:
-        ffn_far = across(ffn_first, n_ev)
-        qkv_far = across(qkv_first[:1], n_ev)
+        qkv_second = second_hop(*qkv_halves, n_ev)
+        qkv_far += across(qkv_second, n_ev)
+        ffn_far = across([ffn_shard], n_ev)
+        gate += qkv_second
+    ffn_first = [ffn_shard] + first_hop(after(ffn_shard, *gate), n_ev)[1:]
+    if two_hops:
         got = after(got, *ffn_far, *qkv_far)
-
     vec = pl.pallas_call(
         functools.partial(encode_kernel, visits_dev),
         out_shape=jax.ShapeDtypeStruct((VPAD, DV), BF16),
@@ -690,20 +685,18 @@
             pltpu.VMEM((visits_dev, HEADS, D), BF16),
             pltpu.SemaphoreType.DMA((5,)),
         ],
-        compiler_params=params(SNUG),
+        compiler_params=params(53),
         cost_estimate=cost(0),
         name="encode",
     )(visit_count, enc_gain.reshape(1, D), got, enc_qkv, enc_out)
 
-    if two_hops:
-        qkv_halves = split_of([qkv_first[0]] + [after(p, vec) for p in qkv_first[1:]], width // 2)
-        vec = after(vec, *qkv_halves)
     vecs = [vec] + [swap(vec, "mp", n_mp, k) for k in range(1, n_mp)]
     if two_hops:
-        qkv_second = second_hop(*qkv_halves, n_ev)
-        ffn_second = second_hop(*[after(piece, *vecs[1:]) for piece in ffn_halves], n_ev)
-        qkv_far += across([after(piece, *vecs[1:]) for piece in qkv_first[1:]], n_ev)
-        qkv_pieces = qkv_first + qkv_second + qkv_far + across(qkv_second, n_ev)
+        qkv_pieces = qkv_first + qkv_second + qkv_far
+        ffn_next = [ffn_first[0]] + [after(piece, *vecs[1:]) for piece in ffn_first[1:]]
+        ffn_second = second_hop(*halves_of(ffn_next, width // 2), n_ev)
+        ffn_far += across(ffn_next[1:], n_ev)
+        vecs[0] = after(vec, *ffn_far[1:])
     else:
         qkv_pieces = qkv_first
     n_q = len(qkv_plan)
@@ -748,10 +741,9 @@
         + [
             pltpu.VMEM((n_mp, group, cols), BF16),
             pltpu.VMEM((group, DV), F32),
-            pltpu.VMEM((FW_ROWS, cols), F32),
             pltpu.VMEM((n_ev, group, width), BF16),
             pltpu.VMEM((n_ev, group, width), F32),
-            pltpu.SemaphoreType.DMA((n_f + 2,)),
+            pltpu.SemaphoreType.DMA((n_f + 1,)),
         ],
         compiler_params=params(SNUG),
         cost_estimate=cost(0),

time: 142 us -> 138 us (0.972)
  waiting for transfers between devices: 55.3 us -> 48.6 us
  starting transfers between devices: 37.3 us -> 39.5 us
  other arithmetic: 0.41 us -> 1.85 us
    all_to_all x1, waiting for transfers between devices: 13.9 us -> 0.01 us  [local(): lax.all_to_all(send.reshape(n_ev, rows_dev // n_ev, D + LANES), 'events',...]
    ppermute x37, waiting for transfers between devices: 41.5 us -> 48.6 us  [swap(): return lax.ppermute(x, axis, [(i, i ^ k) for i in range(size)])]
    ppermute x37, starting transfers between devices: 33.6 us -> 35 us  [swap(): return lax.ppermute(x, axis, [(i, i ^ k) for i in range(size)])]
    unnamed x47 -> x53, local copies, waits for them, and re-layouts: 5.54 us -> 5.16 us
  transfers between devices with their start and end apart: 38 -> 38, of which waited for: 21 -> 20; matrix products, arithmetic and copies ran while one was open for 1% -> 2% of each run, Pallas kernels for 17% -> 17%
where the time goes in v4:
time: 138 us
  waiting for transfers between devices  48.6 us (35%)
  Pallas kernels  40.6 us (29%)
  starting transfers between devices  39.5 us (29%)
  local copies, waits for them, and re-layouts  5.97 us (4%)
  other arithmetic  1.85 us (1%)
    ppermute x37, waiting for transfers between devices, swap(): return lax.ppermute(x, axis, [(i, i ^ k) for i in range(size)])  48.6 us
    ppermute x37, starting transfers between devices, swap(): return lax.ppermute(x, axis, [(i, i ^ k) for i in range(size)])  35 us
    pallas_call x1, Pallas kernels, local(): pl.pallas_call(functools.partial(encode_kernel, visits_dev), out_shape=ja...  13.3 us
    pallas_call x1, Pallas kernels, local(): pl.pallas_call(functools.partial(back_kernel, n_mp, n_ev, qkv_plan), out_...  8.17 us
    pallas_call x1, Pallas kernels, local(): pl.pallas_call(functools.partial(ffn_kernel, n_mp, n_ev, ffn_plan), out_s...  6.53 us
    unnamed x53, local copies, waits for them, and re-layouts  5.16 us
    all_to_all x1, starting transfers between devices, local(): lax.all_to_all(send.reshape(n_ev, rows_dev // n_ev, D + LANES), 'events',...  4.45 us
    pallas_call x1, Pallas kernels, local(): pl.pallas_call(functools.partial(project_kernel, n_mp, n_ev, qkv_plan), o...  4.03 us
  transfers between devices with their start and end apart: 38, of which 20 were waited for; matrix products, arithmetic and copies ran while one was open for 2% of the time, Pallas kernels for 17%

profile of v4, /device:TPU:0, one launch (start us, length us, event | category | flops | bytes accessed | tf_op | source)
XLA Modules:
  0.0 137.7 jit_solution(17002015996962621116)
XLA Ops:
  0.6 3.0 %collective-permute-start.1 = (bf16[3,256,512]{2,1,0:T(8,128)(2,1)}, bf16[3,256,512]{2,1,0:T(8,128)(2,1)S(1)}, u32[]{:S(2)}, u32[]{:S(2)}) collective-permute-start(bf16[3,256,512]{2,1,0:T(8,128)(2,1)} %refs_5_.1), channel_id=1, source_target_pairs={{0,16},{4,20},{8,24},{12,28},{16,0},{20,4},{24,8},{28,12},{1,17},{... | collective-permute-start | bytes 2359304 | tf_op jit(solution)/shard_map/ppermute | solution.py:477
  3.7 1.5 %collective-permute-start = (bf16[3,256,512]{2,1,0:T(8,128)(2,1)}, bf16[3,256,512]{2,1,0:T(8,128)(2,1)S(1)}, u32[]{:S(2)}, u32[]{:S(2)}) collective-permute-start(bf16[3,256,512]{2,1,0:T(8,128)(2,1)} %refs_5_.1), channel_id=1, source_target_pairs={{0,8},{4,12},{8,0},{12,4},{16,24},{20,28},{24,16},{28,20},{1,9},{5... | collective-permute-start | bytes 2359304 | tf_op jit(solution)/shard_map/ppermute | solution.py:477
  5.2 1.4 %copy-done.3 = bf16[768,1024]{1,0:T(8,128)(2,1)S(1)} copy-done((bf16[768,1024]{1,0:T(8,128)(2,1)S(1)}, bf16[768,1024]{1,0:T(8,128)(2,1)}, u32[]{:S(2)}) %copy-start.3) | copy-done | bytes 1572888
  6.6 0.7 copy-done.8
  7.3 3.8 %pack.1 = bf16[768,1152]{1,0:T(8,128)(2,1)} custom-call(s32[2]{0:T(128)S(1)} %pad_add_fusion.where_ref, s32[6,128]{1,0:T(8,128)S(1)} %bitcast.29, bf16[768,1024]{1,0:T(8,128)(2,1)S(1)} %copy-done.3), custom_call_target="tpu_custom_call" | custom-call | flops 1 | bytes 1 | tf_op jit(solution)/shard_map/pack/pallas_call | solution.py:606
  11.2 4.5 %all-to-all-start = ((bf16[8,96,1152]{2,1,0:T(8,128)(2,1)}), bf16[8,96,1152]{2,1,0:T(8,128)(2,1)}, u32[]{:S(2)}, u32[]{:S(2)}) async-start(bf16[8,96,1152]{2,1,0:T(8,128)(2,1)} %bitcast.6), calls=%async_computation | async-start | bytes 3538944 | tf_op jit(solution)/shard_map/all_to_all | solution.py:616
  15.7 0.6 prep.1
  16.4 5.9 %collective-permute-done.1.high_ref.refs_9_.refs_7_ = bf16[3,256,512]{2,1,0:T(8,128)(2,1)S(1)} collective-permute-done((bf16[3,256,512]{2,1,0:T(8,128)(2,1)}, bf16[3,256,512]{2,1,0:T(8,128)(2,1)S(1)}, u32[]{:S(2)}, u32[]{:S(2)}) %collective-permute-start.1) | collective-permute-done | bytes 786464 | tf_op jit(solution)/shard_map/ppermute | solution.py:477
  22.2 2.1 %collective-permute-done.low_ref.refs_8_.refs_6_ = bf16[3,256,512]{2,1,0:T(8,128)(2,1)S(1)} collective-permute-done((bf16[3,256,512]{2,1,0:T(8,128)(2,1)}, bf16[3,256,512]{2,1,0:T(8,128)(2,1)S(1)}, u32[]{:S(2)}, u32[]{:S(2)}) %collective-permute-start) | collective-permute-done | bytes 786464 | tf_op jit(solution)/shard_map/ppermute | solution.py:477
  24.6 0.8 subtract_convert_fusion
  25.4 0.8 compare_convert_fusion.pick
  26.3 0.5 split.1
  26.8 0.5 collective-permute-start.6
  27.4 2.9 %collective-permute-start.8 = (bf16[3,128,512]{2,1,0:T(8,128)(2,1)S(1)}, bf16[3,128,512]{2,1,0:T(8,128)(2,1)}, u32[]{:S(2)}, u32[]{:S(2)}) collective-permute-start(bf16[3,128,512]{2,1,0:T(8,128)(2,1)S(1)} %get-tuple-element.33), channel_id=1, source_target_pairs={{0,8},{4,12},{8,0},{12,4},{16,24},{20,28},{24,16},{28,20},{1,9},{5... | collective-permute-start | bytes 1179656 | tf_op jit(solution)/shard_map/ppermute | solution.py:477
  30.3 1.5 %copy-done.19 = bf16[256,2048]{1,0:T(8,128)(2,1)S(1)} copy-done((bf16[256,2048]{1,0:T(8,128)(2,1)S(1)}, bf16[256,2048]{1,0:T(8,128)(2,1)}, u32[]{:S(2)}) %copy-start.19) | copy-done | bytes 1048600
  31.8 1.4 %fold.1.refs_5_ = bf16[272,2048]{1,0:T(8,128)(2,1)} custom-call(bf16[2048,256]{1,0:T(8,128)(2,1)S(1)} %copy-done.18, bf16[8,256]{1,0:T(8,128)(2,1)S(1)} %maximum_maximum_fusion.head_ref, bf16[256,2048]{1,0:T(8,128)(2,1)S(1)} %copy-done.19), custom_call_target="tpu_custom_call" | custom-call | flops 30000001024 | bytes 30000000 | tf_op jit(solution)/shard_map/fold/pallas_call | solution.py:652
  33.2 15.6 %collective-permute-done.6.refs_10_.refs_8_ = bf16[3,128,512]{2,1,0:T(8,128)(2,1)S(1)} collective-permute-done((bf16[3,128,512]{2,1,0:T(8,128)(2,1)S(1)}, bf16[3,128,512]{2,1,0:T(8,128)(2,1)S(1)}, u32[]{:S(2)}, u32[]{:S(2)}) %collective-permute-start.6) | collective-permute-done | bytes 393248 | tf_op jit(solution)/shard_map/ppermute | solution.py:477
  48.8 1.7 %collective-permute-done.8.refs_11_.refs_9_ = bf16[3,128,512]{2,1,0:T(8,128)(2,1)} collective-permute-done((bf16[3,128,512]{2,1,0:T(8,128)(2,1)S(1)}, bf16[3,128,512]{2,1,0:T(8,128)(2,1)}, u32[]{:S(2)}, u32[]{:S(2)}) %collective-permute-start.8) | collective-permute-done | bytes 393248 | tf_op jit(solution)/shard_map/ppermute | solution.py:477
  50.5 0.4 collective-permute-start.15
  50.8 1.6 %collective-permute-start.10 = (bf16[272,2048]{1,0:T(8,128)(2,1)}, bf16[272,2048]{1,0:T(8,128)(2,1)S(1)}, u32[]{:S(2)}, u32[]{:S(2)}) collective-permute-start(bf16[272,2048]{1,0:T(8,128)(2,1)} %fold.1.refs_5_), channel_id=1, source_target_pairs={{0,8},{4,12},{8,0},{12,4},{16,24},{20,28},{24,16},{28,20},{1,9},{5... | collective-permute-start | bytes 3342344 | tf_op jit(solution)/shard_map/ppermute | solution.py:477
  52.5 0.5 collective-permute-start.9
  53.0 1.7 %collective-permute-done.7.refs_15_.refs_13_ = bf16[3,128,512]{2,1,0:T(8,128)(2,1)S(1)} collective-permute-done((bf16[3,128,512]{2,1,0:T(8,128)(2,1)S(1)}, bf16[3,128,512]{2,1,0:T(8,128)(2,1)S(1)}, u32[]{:S(2)}, u32[]{:S(2)}) %collective-permute-start.7) | collective-permute-done | bytes 393248 | tf_op jit(solution)/shard_map/ppermute | solution.py:477
  54.7 0.2 collective-permute-done.9.refs_16_.refs_14_
  55.0 0.7 copy-done.12
  55.6 0.7 copy-done.15
  56.3 13.3 %encode.1.refs_0_ = bf16[8,2048]{1,0:T(8,128)(2,1)S(1)} custom-call(s32[6]{0:T(128)S(1)} %copy-done.15, f32[1,1024]{1,0:T(1,128)S(1)} %bitcast.30, bf16[768,1152]{1,0:T(8,128)(2,1)} %bitcast.7.got_hbm, bf16[1024,3072]{1,0:T(8,128)(2,1)} %qkv_ref.1, bf16[1024,1024]{1,0:T(8,128)(2,1)} %proj_ref.1), custom_call_target="tpu_custom_call" | custom-call | flops 1 | bytes 1 | tf_op jit(solution)/shard_map/encode/pallas_call | solution.py:672
  69.7 3.7 %collective-permute-start.13 = (bf16[8,2048]{1,0:T(8,128)(2,1)S(1)}, bf16[8,2048]{1,0:T(8,128)(2,1)S(1)}, u32[]{:S(2)}, u32[]{:S(2)}) collective-permute-start(bf16[8,2048]{1,0:T(8,128)(2,1)S(1)} %encode.1.refs_0_), channel_id=1, source_target_pairs={{0,3},{1,2},{2,1},{3,0},{4,7},{5,6},{6,5},{7,4},{8,11},{9,10},{10,... | collective-permute-start | bytes 98312 | tf_op jit(solution)/shard_map/ppermute | solution.py:477
  73.4 0.8 collective-permute-start.11
  74.2 1.6 %collective-permute-done.15.high_ref.refs_7_ = bf16[272,2048]{1,0:T(8,128)(2,1)S(1)} collective-permute-done((bf16[272,2048]{1,0:T(8,128)(2,1)}, bf16[272,2048]{1,0:T(8,128)(2,1)S(1)}, u32[]{:S(2)}, u32[]{:S(2)}) %collective-permute-start.15) | collective-permute-done | bytes 1114144 | tf_op jit(solution)/shard_map/ppermute | solution.py:477
  75.8 2.4 %collective-permute-done.12.refs_2_ = bf16[8,2048]{1,0:T(8,128)(2,1)S(1)} collective-permute-done((bf16[8,2048]{1,0:T(8,128)(2,1)S(1)}, bf16[8,2048]{1,0:T(8,128)(2,1)S(1)}, u32[]{:S(2)}, u32[]{:S(2)}) %collective-permute-start.12) | collective-permute-done | bytes 32800 | tf_op jit(solution)/shard_map/ppermute | solution.py:477
  78.2 0.5 collective-permute-start.14
  78.8 0.6 collective-permute-start.21
  79.4 1.5 %collective-permute-start.20 = (bf16[128,2048]{1,0:T(8,128)(2,1)S(1)}, bf16[128,2048]{1,0:T(8,128)(2,1)S(1)}, u32[]{:S(2)}, u32[]{:S(2)}) collective-permute-start(bf16[128,2048]{1,0:T(8,128)(2,1)S(1)} %get-tuple-element.42), channel_id=1, source_target_pairs={{0,16},{4,20},{8,24},{12,28},{16,0},{20,4},{24,8},{28,12},{1,17},{... | collective-permute-start | bytes 1572872 | tf_op jit(solution)/shard_map/ppermute | solution.py:477
  80.9 1.6 %collective-permute-done.14.refs_11_ = bf16[272,2048]{1,0:T(8,128)(2,1)S(1)} collective-permute-done((bf16[272,2048]{1,0:T(8,128)(2,1)S(1)}, bf16[272,2048]{1,0:T(8,128)(2,1)S(1)}, u32[]{:S(2)}, u32[]{:S(2)}) %collective-permute-start.14) | collective-permute-done | bytes 1114144 | tf_op jit(solution)/shard_map/ppermute | solution.py:477
  82.6 4.0 %project.1 = (bf16[32,512]{1,0:T(8,128)(2,1)S(1)}, f32[32,3712]{1,0:T(8,128)S(1)}) custom-call(s32[2]{0:T(128)S(1)} %copy-done.11, bf16[8,2048]{1,0:T(8,128)(2,1)S(1)} %encode.1.refs_0_, bf16[8,2048]{1,0:T(8,128)(2,1)S(1)} %collective-permute-done.11.refs_1_, bf16[8,2048]{1,0:T(8,128)(2,1)S(1)} %collective-permute-done.12.refs_2_, ...), custom_call_target="tpu_custom_call" | custom-call | flops 1 | bytes 1 | tf_op jit(solution)/shard_map/project/pallas_call | solution.py:705
  86.7 1.5 %collective-permute-start.19 = (bf16[32,512]{1,0:T(8,128)(2,1)S(1)}, bf16[32,512]{1,0:T(8,128)(2,1)S(1)}, u32[]{:S(2)}, u32[]{:S(2)}) collective-permute-start(bf16[32,512]{1,0:T(8,128)(2,1)S(1)} %get-tuple-element.40.refs_0_), channel_id=1, source_target_pairs={{0,3},{1,2},{2,1},{3,0},{4,7},{5,6},{6,5},{7,4},{8,11},{9,10},{10,... | collective-permute-start | bytes 98312 | tf_op jit(solution)/shard_map/ppermute | solution.py:477
  88.2 0.6 collective-permute-start.18
  88.8 2.3 %collective-permute-start.17 = (bf16[32,512]{1,0:T(8,128)(2,1)S(1)}, bf16[32,512]{1,0:T(8,128)(2,1)S(1)}, u32[]{:S(2)}, u32[]{:S(2)}) collective-permute-start(bf16[32,512]{1,0:T(8,128)(2,1)S(1)} %get-tuple-element.40.refs_0_), channel_id=1, source_target_pairs={{0,1},{1,0},{2,3},{3,2},{4,5},{5,4},{6,7},{7,6},{8,9},{9,8},{10,11... | collective-permute-start | bytes 98312 | tf_op jit(solution)/shard_map/ppermute | solution.py:477
  91.1 3.0 %collective-permute-done.21.refs_9_ = bf16[144,2048]{1,0:T(8,128)(2,1)S(1)} collective-permute-done((bf16[144,2048]{1,0:T(8,128)(2,1)S(1)}, bf16[144,2048]{1,0:T(8,128)(2,1)S(1)}, u32[]{:S(2)}, u32[]{:S(2)}) %collective-permute-start.21) | collective-permute-done | bytes 589856 | tf_op jit(solution)/shard_map/ppermute | solution.py:477
  94.2 0.5 collective-permute-start.22
  94.7 2.2 %collective-permute-done.22.refs_13_ = bf16[128,2048]{1,0:T(8,128)(2,1)S(1)} collective-permute-done((bf16[128,2048]{1,0:T(8,128)(2,1)S(1)}, bf16[128,2048]{1,0:T(8,128)(2,1)S(1)}, u32[]{:S(2)}, u32[]{:S(2)}) %collective-permute-start.22) | collective-permute-done | bytes 524320 | tf_op jit(solution)/shard_map/ppermute | solution.py:477
  97.0 6.5 %ffn.1 = (bf16[32,640]{1,0:T(8,128)(2,1)S(1)}, bf16[32,640]{1,0:T(8,128)(2,1)S(1)}, bf16[32,640]{1,0:T(8,128)(2,1)S(1)}, bf16[32,640]{1,0:T(8,128)(2,1)S(1)}, f32[32,640]{1,0:T(8,128)S(1)}) custom-call(s32[2]{0:T(128)S(1)} %copy-done.11, f32[2]{0:T(128)S(1)} %copy-done.17, f32[1,2048]{1,0:T(1,128)S(1)} %bitcast.27, ...), custom_call_target="tpu_custom_call" | custom-call | flops 1 | bytes 1 | tf_op jit(solution)/shard_map/ffn/pallas_call | solution.py:734
  103.5 0.9 collective-permute-start.24
  104.4 1.3 collective-permute-start.25
  105.7 2.3 %collective-permute-start.26 = (bf16[32,640]{1,0:T(8,128)(2,1)S(1)}, bf16[32,640]{1,0:T(8,128)(2,1)S(1)}, u32[]{:S(2)}, u32[]{:S(2)}) collective-permute-start(bf16[32,640]{1,0:T(8,128)(2,1)S(1)} %get-tuple-element.50), channel_id=1, source_target_pairs={{0,3},{1,2},{2,1},{3,0},{4,7},{5,6},{6,5},{7,4},{8,11},{9,10},{10,... | collective-permute-start | bytes 122888 | tf_op jit(solution)/shard_map/ppermute | solution.py:477
  108.0 2.6 %collective-permute-done.25.refs_2_ = bf16[32,640]{1,0:T(8,128)(2,1)S(1)} collective-permute-done((bf16[32,640]{1,0:T(8,128)(2,1)S(1)}, bf16[32,640]{1,0:T(8,128)(2,1)S(1)}, u32[]{:S(2)}, u32[]{:S(2)}) %collective-permute-start.25) | collective-permute-done | bytes 40992 | tf_op jit(solution)/shard_map/ppermute | solution.py:477
  110.6 1.0 collective-permute-done.26.refs_3_
  111.6 8.2 %back.1 = (bf16[8,1152]{1,0:T(8,128)(2,1)S(1)}, bf16[8,1152]{1,0:T(8,128)(2,1)S(1)}, bf16[8,1152]{1,0:T(8,128)(2,1)S(1)}, bf16[8,1152]{1,0:T(8,128)(2,1)S(1)}, f...) custom-call(s32[2]{0:T(128)S(1)} %copy-done.11, f32[32,640]{1,0:T(8,128)S(1)} %get-tuple-element.46.mid_ref, ...), custom_call_target="tpu_custom_call" | custom-call | flops 1 | bytes 1 | tf_op jit(solution)/shard_map/back/pallas_call | solution.py:755
  119.8 0.7 collective-permute-start.27
  120.5 2.1 %collective-permute-start.28 = (bf16[8,1152]{1,0:T(8,128)(2,1)S(1)}, bf16[8,1152]{1,0:T(8,128)(2,1)S(1)}, u32[]{:S(2)}, u32[]{:S(2)}) collective-permute-start(bf16[8,1152]{1,0:T(8,128)(2,1)S(1)} %get-tuple-element.56), channel_id=1, source_target_pairs={{0,2},{1,3},{2,0},{3,1},{4,6},{5,7},{6,4},{7,5},{8,10},{9,11},{10,... | collective-permute-start | bytes 55304 | tf_op jit(solution)/shard_map/ppermute | solution.py:477
  122.6 1.6 %collective-permute-start.29 = (bf16[8,1152]{1,0:T(8,128)(2,1)S(1)}, bf16[8,1152]{1,0:T(8,128)(2,1)S(1)}, u32[]{:S(2)}, u32[]{:S(2)}) collective-permute-start(bf16[8,1152]{1,0:T(8,128)(2,1)S(1)} %get-tuple-element.57), channel_id=1, source_target_pairs={{0,3},{1,2},{2,1},{3,0},{4,7},{5,6},{6,5},{7,4},{8,11},{9,10},{10,... | collective-permute-start | bytes 55304 | tf_op jit(solution)/shard_map/ppermute | solution.py:477
  124.3 0.6 reshape.62
  125.0 0.3 collective-permute-done.28.refs_2_
  125.3 2.9 %collective-permute-done.29.refs_3_ = bf16[8,1152]{1,0:T(8,128)(2,1)S(1)} collective-permute-done((bf16[8,1152]{1,0:T(8,128)(2,1)S(1)}, bf16[8,1152]{1,0:T(8,128)(2,1)S(1)}, u32[]{:S(2)}, u32[]{:S(2)}) %collective-permute-start.29) | collective-permute-done | bytes 18464 | tf_op jit(solution)/shard_map/ppermute | solution.py:477
  128.2 0.7 finish.1.refs_0_
  128.9 1.6 %collective-permute-start.32 = (f32[8,1024]{1,0:T(8,128)S(1)}, f32[8,1024]{1,0:T(8,128)S(1)}, u32[]{:S(2)}, u32[]{:S(2)}) collective-permute-start(f32[8,1024]{1,0:T(8,128)S(1)} %finish.1.refs_0_), channel_id=1, source_target_pairs={{0,24},{4,28},{8,16},{12,20},{16,8},{20,12},{24,0},{28,4},{1,25},{... | collective-permute-start | bytes 98312 | tf_op jit(solution)/shard_map/ppermute | solution.py:477
  130.5 0.5 collective-permute-start.31
  131.0 1.4 %collective-permute-start.30 = (f32[8,1024]{1,0:T(8,128)S(1)}, f32[8,1024]{1,0:T(8,128)S(1)}, u32[]{:S(2)}, u32[]{:S(2)}) collective-permute-start(f32[8,1024]{1,0:T(8,128)S(1)} %finish.1.refs_0_), channel_id=1, source_target_pairs={{0,8},{4,12},{8,0},{12,4},{16,24},{20,28},{24,16},{28,20},{1,9},{5... | collective-permute-start | bytes 98312 | tf_op jit(solution)/shard_map/ppermute | solution.py:477
  132.4 1.3 collective-permute-done.32.refs_3_
  133.7 0.7 collective-permute-done.31.refs_2_
  134.4 0.5 collective-permute-done.30.refs_1_
  134.9 0.7 collective-permute-done.35.refs_6_
  135.6 0.5 collective-permute-done.34.refs_5_
  136.1 1.4 %spread.1 = bf16[768,1024]{1,0:T(8,128)(2,1)} custom-call(bf16[768,64]{1,0:T(8,128)(2,1)S(1)} %copy-done.4, f32[8,1024]{1,0:T(8,128)S(1)} %finish.1.refs_0_, f32[8,1024]{1,0:T(8,128)S(1)} %collective-permute-done.30.refs_1_, f32[8,1024]{1,0:T(8,128)S(1)} %collective-permute-done.31.refs_2_, f32[8,1024]{1,0:T(8,128)S(1)} %collective-permute-done.32.refs_3_, ...), custom_call_target="tpu_custom_call" | custom-call | flops 1 | bytes 1 | tf_op jit(solution)/shard_map/spread/pallas_call | solution.py:785
  (88 shorter events, 0.9 us)
Async XLA Ops:
  0.6 21.6 %collective-permute-start.1 = (bf16[3,256,512]{2,1,0:T(8,128)(2,1)}, bf16[3,256,512]{2,1,0:T(8,128)(2,1)S(1)}, u32[]{:S(2)}, u32[]{:S(2)}) collective-permute-start(bf16[3,256,512]{2,1,0:T(8,128)(2,1)} %refs_5_.1), channel_id=1, source_target_pairs={{0,16},{4,20},{8,24},{12,28},{16,0},{20,4},{24,8},{28,12},{1,17},{... | collective-permute-start | bytes 2359304 | tf_op jit(solution)/shard_map/ppermute | solution.py:477
  3.7 20.7 %collective-permute-start = (bf16[3,256,512]{2,1,0:T(8,128)(2,1)}, bf16[3,256,512]{2,1,0:T(8,128)(2,1)S(1)}, u32[]{:S(2)}, u32[]{:S(2)}) collective-permute-start(bf16[3,256,512]{2,1,0:T(8,128)(2,1)} %refs_5_.1), channel_id=1, source_target_pairs={{0,8},{4,12},{8,0},{12,4},{16,24},{20,28},{24,16},{28,20},{1,9},{5... | collective-permute-start | bytes 2359304 | tf_op jit(solution)/shard_map/ppermute | solution.py:477
  5.2 25.1 %collective-permute-start.2 = (bf16[3,256,512]{2,1,0:T(8,128)(2,1)}, bf16[3,256,512]{2,1,0:T(8,128)(2,1)S(1)}, u32[]{:S(2)}, u32[]{:S(2)}) collective-permute-start(bf16[3,256,512]{2,1,0:T(8,128)(2,1)} %refs_5_.1), channel_id=1, source_target_pairs={{0,4},{4,0},{8,12},{12,8},{16,20},{20,16},{24,28},{28,24},{1,5},{5... | collective-permute-start | bytes 2359304 | tf_op jit(solution)/shard_map/ppermute | solution.py:477
  5.2 5.9 %copy-start.10 = (s32[2]{0:T(128)}, s32[2]{0:T(128)S(1)}, u32[]{:S(2)}) copy-start(s32[2]{0:T(128)S(1)} %pad_add_fusion.where_ref) | copy-start | bytes 28
  5.2 1.4 %copy-start.3 = (bf16[768,1024]{1,0:T(8,128)(2,1)S(1)}, bf16[768,1024]{1,0:T(8,128)(2,1)}, u32[]{:S(2)}) copy-start(bf16[768,1024]{1,0:T(8,128)(2,1)} %x_hbm.1) | copy-start | bytes 4718596
  6.6 0.7 copy-start.8
  11.2 4.5 %copy-start.20 = (s32[24]{0:T(128)S(1)}, s32[24]{0:T(128)}, u32[]{:S(2)}) copy-start(s32[24]{0:T(128)} %patient_ref.1) | copy-start | bytes 292
  11.2 4.5 %copy-start.21 = (s32[24]{0:T(128)S(1)}, s32[24]{0:T(128)}, u32[]{:S(2)}) copy-start(s32[24]{0:T(128)} %treat_ref.1) | copy-start | bytes 292
  11.2 4.5 %copy-start.22 = (f32[24]{0:T(128)S(1)}, f32[24]{0:T(128)}, u32[]{:S(2)}) copy-start(f32[24]{0:T(128)} %target_ref.1) | copy-start | bytes 292
  11.2 5.1 %copy-start.25 = (s32[8]{0:T(128)S(1)}, s32[8]{0:T(128)}, u32[]{:S(2)}) copy-start(s32[8]{0:T(128)} %constant.26.clone) | copy-start | bytes 100
  11.2 14.2 %copy-start.9 = (s32[768]{0:T(1024)S(1)}, s32[768]{0:T(1024)}, u32[]{:S(2)}) copy-start(s32[768]{0:T(1024)} %param.18) | copy-start | bytes 9220
  11.2 39.2 %all-to-all-start = ((bf16[8,96,1152]{2,1,0:T(8,128)(2,1)}), bf16[8,96,1152]{2,1,0:T(8,128)(2,1)}, u32[]{:S(2)}, u32[]{:S(2)}) async-start(bf16[8,96,1152]{2,1,0:T(8,128)(2,1)} %bitcast.6), calls=%async_computation | async-start | bytes 3538944 | tf_op jit(solution)/shard_map/all_to_all | solution.py:616
  16.3 10.5 %copy-start.13 = (f32[8,32]{1,0:T(8,128)}, f32[8,32]{1,0:T(8,128)S(1)}, u32[]{:S(2)}) copy-start(f32[8,32]{1,0:T(8,128)S(1)} %get-tuple-element.31.refs_6_) | copy-start | bytes 3076
  22.2 8.0 %collective-permute-start.4 = (bf16[3,256,512]{2,1,0:T(8,128)(2,1)S(1)}, bf16[3,256,512]{2,1,0:T(8,128)(2,1)}, u32[]{:S(2)}, u32[]{:S(2)}) collective-permute-start(bf16[3,256,512]{2,1,0:T(8,128)(2,1)S(1)} %collective-permute-done.1.high_ref.refs_9_.refs_7_), channel_id=1, source_target_pairs={{0,4},{4,0},{8,12},{12,8},{16,20},{20,16},{24,28},{28,24},{1,5},{5... | collective-permute-start | bytes 2359304 | tf_op jit(solution)/shard_map/ppermute | solution.py:477
  24.3 5.9 %collective-permute-start.3 = (bf16[3,256,512]{2,1,0:T(8,128)(2,1)S(1)}, bf16[3,256,512]{2,1,0:T(8,128)(2,1)S(1)}, u32[]{:S(2)}, u32[]{:S(2)}) collective-permute-start(bf16[3,256,512]{2,1,0:T(8,128)(2,1)S(1)} %collective-permute-done.low_ref.refs_8_.refs_6_), channel_id=1, source_target_pairs={{0,4},{4,0},{8,12},{12,8},{16,20},{20,16},{24,28},{28,24},{1,5},{5... | collective-permute-start | bytes 2359304 | tf_op jit(solution)/shard_map/ppermute | solution.py:477
  24.5 5.8 %copy-start.18 = (bf16[2048,256]{1,0:T(8,128)(2,1)S(1)}, bf16[2048,256]{1,0:T(8,128)(2,1)}, u32[]{:S(2)}) copy-start(bf16[2048,256]{1,0:T(8,128)(2,1)} %weight_ref.1) | copy-start | bytes 3145732
  26.8 22.0 %collective-permute-start.6 = (bf16[3,128,512]{2,1,0:T(8,128)(2,1)S(1)}, bf16[3,128,512]{2,1,0:T(8,128)(2,1)S(1)}, u32[]{:S(2)}, u32[]{:S(2)}) collective-permute-start(bf16[3,128,512]{2,1,0:T(8,128)(2,1)S(1)} %get-tuple-element.32), channel_id=1, source_target_pairs={{0,16},{4,20},{8,24},{12,28},{16,0},{20,4},{24,8},{28,12},{1,17},{... | collective-permute-start | bytes 1179656 | tf_op jit(solution)/shard_map/ppermute | solution.py:477
  27.4 23.1 %collective-permute-start.8 = (bf16[3,128,512]{2,1,0:T(8,128)(2,1)S(1)}, bf16[3,128,512]{2,1,0:T(8,128)(2,1)}, u32[]{:S(2)}, u32[]{:S(2)}) collective-permute-start(bf16[3,128,512]{2,1,0:T(8,128)(2,1)S(1)} %get-tuple-element.33), channel_id=1, source_target_pairs={{0,8},{4,12},{8,0},{12,4},{16,24},{20,28},{24,16},{28,20},{1,9},{5... | collective-permute-start | bytes 1179656 | tf_op jit(solution)/shard_map/ppermute | solution.py:477
  30.3 52.2 %copy-start.2 = (bf16[3,256,512]{2,1,0:T(8,128)(2,1)}, bf16[3,256,512]{2,1,0:T(8,128)(2,1)S(1)}, u32[]{:S(2)}) copy-start(bf16[3,256,512]{2,1,0:T(8,128)(2,1)S(1)} %collective-permute-done.3.refs_13_.refs_11_) | copy-start | bytes 2359300
  30.3 1.5 %copy-start.19 = (bf16[256,2048]{1,0:T(8,128)(2,1)S(1)}, bf16[256,2048]{1,0:T(8,128)(2,1)}, u32[]{:S(2)}) copy-start(bf16[256,2048]{1,0:T(8,128)(2,1)} %ffn_ref) | copy-start | bytes 3145732
  33.2 21.7 %collective-permute-start.5 = (bf16[272,2048]{1,0:T(8,128)(2,1)}, bf16[272,2048]{1,0:T(8,128)(2,1)}, u32[]{:S(2)}, u32[]{:S(2)}) collective-permute-start(bf16[272,2048]{1,0:T(8,128)(2,1)} %fold.1.refs_5_), channel_id=1, source_target_pairs={{0,4},{4,0},{8,12},{12,8},{16,20},{20,16},{24,28},{28,24},{1,5},{5... | collective-permute-start | bytes 3342344 | tf_op jit(solution)/shard_map/ppermute | solution.py:477
  50.5 25.3 %collective-permute-start.15 = (bf16[272,2048]{1,0:T(8,128)(2,1)}, bf16[272,2048]{1,0:T(8,128)(2,1)S(1)}, u32[]{:S(2)}, u32[]{:S(2)}) collective-permute-start(bf16[272,2048]{1,0:T(8,128)(2,1)} %fold.1.refs_5_), channel_id=1, source_target_pairs={{0,16},{4,20},{8,24},{12,28},{16,0},{20,4},{24,8},{28,12},{1,17},{... | collective-permute-start | bytes 3342344 | tf_op jit(solution)/shard_map/ppermute | solution.py:477
  50.8 27.4 %collective-permute-start.10 = (bf16[272,2048]{1,0:T(8,128)(2,1)}, bf16[272,2048]{1,0:T(8,128)(2,1)S(1)}, u32[]{:S(2)}, u32[]{:S(2)}) collective-permute-start(bf16[272,2048]{1,0:T(8,128)(2,1)} %fold.1.refs_5_), channel_id=1, source_target_pairs={{0,8},{4,12},{8,0},{12,4},{16,24},{20,28},{24,16},{28,20},{1,9},{5... | collective-permute-start | bytes 3342344 | tf_op jit(solution)/shard_map/ppermute | solution.py:477
  52.5 2.3 %collective-permute-start.7 = (bf16[3,128,512]{2,1,0:T(8,128)(2,1)S(1)}, bf16[3,128,512]{2,1,0:T(8,128)(2,1)S(1)}, u32[]{:S(2)}, u32[]{:S(2)}) collective-permute-start(bf16[3,128,512]{2,1,0:T(8,128)(2,1)S(1)} %collective-permute-done.6.refs_10_.refs_8_), channel_id=1, source_target_pairs={{0,4},{4,0},{8,12},{12,8},{16,20},{20,16},{24,28},{28,24},{1,5},{5... | collective-permute-start | bytes 1179656 | tf_op jit(solution)/shard_map/ppermute | solution.py:477
  52.5 2.5 %collective-permute-start.9 = (bf16[3,128,512]{2,1,0:T(8,128)(2,1)}, bf16[3,128,512]{2,1,0:T(8,128)(2,1)S(1)}, u32[]{:S(2)}, u32[]{:S(2)}) collective-permute-start(bf16[3,128,512]{2,1,0:T(8,128)(2,1)} %collective-permute-done.8.refs_11_.refs_9_), channel_id=1, source_target_pairs={{0,4},{4,0},{8,12},{12,8},{16,20},{20,16},{24,28},{28,24},{1,5},{5... | collective-permute-start | bytes 1179656 | tf_op jit(solution)/shard_map/ppermute | solution.py:477
  55.0 0.7 copy-start.12
  55.6 0.7 copy-start.15
  69.7 12.9 %copy-start.1 = (bf16[3,256,512]{2,1,0:T(8,128)(2,1)S(1)}, bf16[3,256,512]{2,1,0:T(8,128)(2,1)}, u32[]{:S(2)}) copy-start(bf16[3,256,512]{2,1,0:T(8,128)(2,1)} %refs_5_.1) | copy-start | bytes 2359300
  69.7 12.9 %copy-start.6 = (f32[2048]{0:T(1024)S(1)}, f32[2048]{0:T(1024)}, u32[]{:S(2)}) copy-start(f32[2048]{0:T(1024)} %param.26) | copy-start | bytes 24580
  69.7 12.9 %copy-start.11 = (s32[2]{0:T(128)S(1)}, s32[2]{0:T(128)}, u32[]{:S(2)}) copy-start(s32[2]{0:T(128)} %copy-done.10) | copy-start | bytes 28
  69.7 12.9 %copy-start.14 = (f32[8,32]{1,0:T(8,128)S(1)}, f32[8,32]{1,0:T(8,128)}, u32[]{:S(2)}) copy-start(f32[8,32]{1,0:T(8,128)} %copy-done.13) | copy-start | bytes 3076
  69.7 6.1 %collective-permute-start.13 = (bf16[8,2048]{1,0:T(8,128)(2,1)S(1)}, bf16[8,2048]{1,0:T(8,128)(2,1)S(1)}, u32[]{:S(2)}, u32[]{:S(2)}) collective-permute-start(bf16[8,2048]{1,0:T(8,128)(2,1)S(1)} %encode.1.refs_0_), channel_id=1, source_target_pairs={{0,3},{1,2},{2,1},{3,0},{4,7},{5,6},{6,5},{7,4},{8,11},{9,10},{10,... | collective-permute-start | bytes 98312 | tf_op jit(solution)/shard_map/ppermute | solution.py:477
  73.4 4.8 %collective-permute-start.12 = (bf16[8,2048]{1,0:T(8,128)(2,1)S(1)}, bf16[8,2048]{1,0:T(8,128)(2,1)S(1)}, u32[]{:S(2)}, u32[]{:S(2)}) collective-permute-start(bf16[8,2048]{1,0:T(8,128)(2,1)S(1)} %encode.1.refs_0_), channel_id=1, source_target_pairs={{0,2},{1,3},{2,0},{3,1},{4,6},{5,7},{6,4},{7,5},{8,10},{9,11},{10,... | collective-permute-start | bytes 98312 | tf_op jit(solution)/shard_map/ppermute | solution.py:477
  73.4 4.8 %collective-permute-start.11 = (bf16[8,2048]{1,0:T(8,128)(2,1)S(1)}, bf16[8,2048]{1,0:T(8,128)(2,1)S(1)}, u32[]{:S(2)}, u32[]{:S(2)}) collective-permute-start(bf16[8,2048]{1,0:T(8,128)(2,1)S(1)} %encode.1.refs_0_), channel_id=1, source_target_pairs={{0,1},{1,0},{2,3},{3,2},{4,5},{5,4},{6,7},{7,6},{8,9},{9,8},{10,11... | collective-permute-start | bytes 98312 | tf_op jit(solution)/shard_map/ppermute | solution.py:477
  75.8 10.9 %copy-start = (bf16[272,2048]{1,0:T(8,128)(2,1)}, bf16[272,2048]{1,0:T(8,128)(2,1)S(1)}, u32[]{:S(2)}) copy-start(bf16[272,2048]{1,0:T(8,128)(2,1)S(1)} %collective-permute-done.15.high_ref.refs_7_) | copy-start | bytes 3342340
  78.2 2.8 %collective-permute-start.16 = (bf16[272,2048]{1,0:T(8,128)(2,1)S(1)}, bf16[272,2048]{1,0:T(8,128)(2,1)S(1)}, u32[]{:S(2)}, u32[]{:S(2)}) collective-permute-start(bf16[272,2048]{1,0:T(8,128)(2,1)S(1)} %collective-permute-done.15.high_ref.refs_7_), channel_id=1, source_target_pairs={{0,4},{4,0},{8,12},{12,8},{16,20},{20,16},{24,28},{28,24},{1,5},{5... | collective-permute-start | bytes 3342344 | tf_op jit(solution)/shard_map/ppermute | solution.py:477
  78.2 4.3 %collective-permute-start.14 = (bf16[272,2048]{1,0:T(8,128)(2,1)S(1)}, bf16[272,2048]{1,0:T(8,128)(2,1)S(1)}, u32[]{:S(2)}, u32[]{:S(2)}) collective-permute-start(bf16[272,2048]{1,0:T(8,128)(2,1)S(1)} %collective-permute-done.10.low_ref.refs_6_), channel_id=1, source_target_pairs={{0,4},{4,0},{8,12},{12,8},{16,20},{20,16},{24,28},{28,24},{1,5},{5... | collective-permute-start | bytes 3342344 | tf_op jit(solution)/shard_map/ppermute | solution.py:477
  78.8 15.4 %collective-permute-start.21 = (bf16[144,2048]{1,0:T(8,128)(2,1)S(1)}, bf16[144,2048]{1,0:T(8,128)(2,1)S(1)}, u32[]{:S(2)}, u32[]{:S(2)}) collective-permute-start(bf16[144,2048]{1,0:T(8,128)(2,1)S(1)} %get-tuple-element.44), channel_id=1, source_target_pairs={{0,8},{4,12},{8,0},{12,4},{16,24},{20,28},{24,16},{28,20},{1,9},{5... | collective-permute-start | bytes 1769480 | tf_op jit(solution)/shard_map/ppermute | solution.py:477
  79.4 14.9 %collective-permute-start.20 = (bf16[128,2048]{1,0:T(8,128)(2,1)S(1)}, bf16[128,2048]{1,0:T(8,128)(2,1)S(1)}, u32[]{:S(2)}, u32[]{:S(2)}) collective-permute-start(bf16[128,2048]{1,0:T(8,128)(2,1)S(1)} %get-tuple-element.42), channel_id=1, source_target_pairs={{0,16},{4,20},{8,24},{12,28},{16,0},{20,4},{24,8},{28,12},{1,17},{... | collective-permute-start | bytes 1572872 | tf_op jit(solution)/shard_map/ppermute | solution.py:477
  80.9 5.7 %copy-start.23 = (bf16[272,2048]{1,0:T(8,128)(2,1)}, bf16[272,2048]{1,0:T(8,128)(2,1)S(1)}, u32[]{:S(2)}) copy-start(bf16[272,2048]{1,0:T(8,128)(2,1)S(1)} %collective-permute-done.16.refs_12_) | copy-start | bytes 3342340
  82.5 4.1 %copy-start.24 = (bf16[272,2048]{1,0:T(8,128)(2,1)}, bf16[272,2048]{1,0:T(8,128)(2,1)S(1)}, u32[]{:S(2)}) copy-start(bf16[272,2048]{1,0:T(8,128)(2,1)S(1)} %collective-permute-done.14.refs_11_) | copy-start | bytes 3342340
  82.6 14.4 %copy-start.5 = (f32[2048,2]{0,1:T(2,128)S(1)}, f32[2048,2]{0,1:T(2,128)}, u32[]{:S(2)}) copy-start(f32[2048,2]{0,1:T(2,128)} %param.31) | copy-start | bytes 49156
  82.6 14.4 %copy-start.7 = (f32[2048]{0:T(1024)S(1)}, f32[2048]{0:T(1024)}, u32[]{:S(2)}) copy-start(f32[2048]{0:T(1024)} %param.28) | copy-start | bytes 24580
  82.6 14.4 %copy-start.17 = (f32[2]{0:T(128)S(1)}, f32[2]{0:T(128)}, u32[]{:S(2)}) copy-start(f32[2]{0:T(128)} %bias_ref.1) | copy-start | bytes 28
  86.7 7.5 %collective-permute-start.19 = (bf16[32,512]{1,0:T(8,128)(2,1)S(1)}, bf16[32,512]{1,0:T(8,128)(2,1)S(1)}, u32[]{:S(2)}, u32[]{:S(2)}) collective-permute-start(bf16[32,512]{1,0:T(8,128)(2,1)S(1)} %get-tuple-element.40.refs_0_), channel_id=1, source_target_pairs={{0,3},{1,2},{2,1},{3,0},{4,7},{5,6},{6,5},{7,4},{8,11},{9,10},{10,... | collective-permute-start | bytes 98312 | tf_op jit(solution)/shard_map/ppermute | solution.py:477
  88.2 6.0 %collective-permute-start.18 = (bf16[32,512]{1,0:T(8,128)(2,1)S(1)}, bf16[32,512]{1,0:T(8,128)(2,1)S(1)}, u32[]{:S(2)}, u32[]{:S(2)}) collective-permute-start(bf16[32,512]{1,0:T(8,128)(2,1)S(1)} %get-tuple-element.40.refs_0_), channel_id=1, source_target_pairs={{0,2},{1,3},{2,0},{3,1},{4,6},{5,7},{6,4},{7,5},{8,10},{9,11},{10,... | collective-permute-start | bytes 98312 | tf_op jit(solution)/shard_map/ppermute | solution.py:477
  88.8 5.3 %collective-permute-start.17 = (bf16[32,512]{1,0:T(8,128)(2,1)S(1)}, bf16[32,512]{1,0:T(8,128)(2,1)S(1)}, u32[]{:S(2)}, u32[]{:S(2)}) collective-permute-start(bf16[32,512]{1,0:T(8,128)(2,1)S(1)} %get-tuple-element.40.refs_0_), channel_id=1, source_target_pairs={{0,1},{1,0},{2,3},{3,2},{4,5},{5,4},{6,7},{7,6},{8,9},{9,8},{10,11... | collective-permute-start | bytes 98312 | tf_op jit(solution)/shard_map/ppermute | solution.py:477
  94.2 2.8 %collective-permute-start.23 = (bf16[144,2048]{1,0:T(8,128)(2,1)S(1)}, bf16[144,2048]{1,0:T(8,128)(2,1)S(1)}, u32[]{:S(2)}, u32[]{:S(2)}) collective-permute-start(bf16[144,2048]{1,0:T(8,128)(2,1)S(1)} %collective-permute-done.21.refs_9_), channel_id=1, source_target_pairs={{0,4},{4,0},{8,12},{12,8},{16,20},{20,16},{24,28},{28,24},{1,5},{5... | collective-permute-start | bytes 1769480 | tf_op jit(solution)/shard_map/ppermute | solution.py:477
  94.2 2.7 %collective-permute-start.22 = (bf16[128,2048]{1,0:T(8,128)(2,1)S(1)}, bf16[128,2048]{1,0:T(8,128)(2,1)S(1)}, u32[]{:S(2)}, u32[]{:S(2)}) collective-permute-start(bf16[128,2048]{1,0:T(8,128)(2,1)S(1)} %collective-permute-done.20.refs_8_), channel_id=1, source_target_pairs={{0,4},{4,0},{8,12},{12,8},{16,20},{20,16},{24,28},{28,24},{1,5},{5... | collective-permute-start | bytes 1572872 | tf_op jit(solution)/shard_map/ppermute | solution.py:477
  103.5 4.5 %collective-permute-start.24 = (bf16[32,640]{1,0:T(8,128)(2,1)S(1)}, bf16[32,640]{1,0:T(8,128)(2,1)S(1)}, u32[]{:S(2)}, u32[]{:S(2)}) collective-permute-start(bf16[32,640]{1,0:T(8,128)(2,1)S(1)} %get-tuple-element.48), channel_id=1, source_target_pairs={{0,1},{1,0},{2,3},{3,2},{4,5},{5,4},{6,7},{7,6},{8,9},{9,8},{10,11... | collective-permute-start | bytes 122888 | tf_op jit(solution)/shard_map/ppermute | solution.py:477
  104.4 6.2 %collective-permute-start.25 = (bf16[32,640]{1,0:T(8,128)(2,1)S(1)}, bf16[32,640]{1,0:T(8,128)(2,1)S(1)}, u32[]{:S(2)}, u32[]{:S(2)}) collective-permute-start(bf16[32,640]{1,0:T(8,128)(2,1)S(1)} %get-tuple-element.49), channel_id=1, source_target_pairs={{0,2},{1,3},{2,0},{3,1},{4,6},{5,7},{6,4},{7,5},{8,10},{9,11},{10,... | collective-permute-start | bytes 122888 | tf_op jit(solution)/shard_map/ppermute | solution.py:477
  105.7 5.9 %collective-permute-start.26 = (bf16[32,640]{1,0:T(8,128)(2,1)S(1)}, bf16[32,640]{1,0:T(8,128)(2,1)S(1)}, u32[]{:S(2)}, u32[]{:S(2)}) collective-permute-start(bf16[32,640]{1,0:T(8,128)(2,1)S(1)} %get-tuple-element.50), channel_id=1, source_target_pairs={{0,3},{1,2},{2,1},{3,0},{4,7},{5,6},{6,5},{7,4},{8,11},{9,10},{10,... | collective-permute-start | bytes 122888 | tf_op jit(solution)/shard_map/ppermute | solution.py:477
  111.6 16.6 %copy-start.16 = (s32[6]{0:T(128)S(1)}, s32[6]{0:T(128)}, u32[]{:S(2)}) copy-start(s32[6]{0:T(128)} %count_ref.3) | copy-start | bytes 76
  111.6 24.5 %copy-start.4 = (bf16[768,64]{1,0:T(8,128)(2,1)S(1)}, bf16[768,64]{1,0:T(8,128)(2,1)}, u32[]{:S(2)}) copy-start(bf16[768,64]{1,0:T(8,128)(2,1)} %compare_convert_fusion.pick) | copy-start | bytes 294916
  119.8 5.2 %collective-permute-start.27 = (bf16[8,1152]{1,0:T(8,128)(2,1)S(1)}, bf16[8,1152]{1,0:T(8,128)(2,1)S(1)}, u32[]{:S(2)}, u32[]{:S(2)}) collective-permute-start(bf16[8,1152]{1,0:T(8,128)(2,1)S(1)} %get-tuple-element.55), channel_id=1, source_target_pairs={{0,1},{1,0},{2,3},{3,2},{4,5},{5,4},{6,7},{7,6},{8,9},{9,8},{10,11... | collective-permute-start | bytes 55304 | tf_op jit(solution)/shard_map/ppermute | solution.py:477
  120.5 4.9 %collective-permute-start.28 = (bf16[8,1152]{1,0:T(8,128)(2,1)S(1)}, bf16[8,1152]{1,0:T(8,128)(2,1)S(1)}, u32[]{:S(2)}, u32[]{:S(2)}) collective-permute-start(bf16[8,1152]{1,0:T(8,128)(2,1)S(1)} %get-tuple-element.56), channel_id=1, source_target_pairs={{0,2},{1,3},{2,0},{3,1},{4,6},{5,7},{6,4},{7,5},{8,10},{9,11},{10,... | collective-permute-start | bytes 55304 | tf_op jit(solution)/shard_map/ppermute | solution.py:477
  122.6 5.6 %collective-permute-start.29 = (bf16[8,1152]{1,0:T(8,128)(2,1)S(1)}, bf16[8,1152]{1,0:T(8,128)(2,1)S(1)}, u32[]{:S(2)}, u32[]{:S(2)}) collective-permute-start(bf16[8,1152]{1,0:T(8,128)(2,1)S(1)} %get-tuple-element.57), channel_id=1, source_target_pairs={{0,3},{1,2},{2,1},{3,0},{4,7},{5,6},{6,5},{7,4},{8,11},{9,10},{10,... | collective-permute-start | bytes 55304 | tf_op jit(solution)/shard_map/ppermute | solution.py:477
  128.9 4.8 %collective-permute-start.32 = (f32[8,1024]{1,0:T(8,128)S(1)}, f32[8,1024]{1,0:T(8,128)S(1)}, u32[]{:S(2)}, u32[]{:S(2)}) collective-permute-start(f32[8,1024]{1,0:T(8,128)S(1)} %finish.1.refs_0_), channel_id=1, source_target_pairs={{0,24},{4,28},{8,16},{12,20},{16,8},{20,12},{24,0},{28,4},{1,25},{... | collective-permute-start | bytes 98312 | tf_op jit(solution)/shard_map/ppermute | solution.py:477
  130.5 3.9 %collective-permute-start.31 = (f32[8,1024]{1,0:T(8,128)S(1)}, f32[8,1024]{1,0:T(8,128)S(1)}, u32[]{:S(2)}, u32[]{:S(2)}) collective-permute-start(f32[8,1024]{1,0:T(8,128)S(1)} %finish.1.refs_0_), channel_id=1, source_target_pairs={{0,16},{4,20},{8,24},{12,28},{16,0},{20,4},{24,8},{28,12},{1,17},{... | collective-permute-start | bytes 98312 | tf_op jit(solution)/shard_map/ppermute | solution.py:477
  131.0 3.9 %collective-permute-start.30 = (f32[8,1024]{1,0:T(8,128)S(1)}, f32[8,1024]{1,0:T(8,128)S(1)}, u32[]{:S(2)}, u32[]{:S(2)}) collective-permute-start(f32[8,1024]{1,0:T(8,128)S(1)} %finish.1.refs_0_), channel_id=1, source_target_pairs={{0,8},{4,12},{8,0},{12,4},{16,24},{20,28},{24,16},{28,20},{1,9},{5... | collective-permute-start | bytes 98312 | tf_op jit(solution)/shard_map/ppermute | solution.py:477
  132.4 2.5 %collective-permute-start.33 = (f32[8,1024]{1,0:T(8,128)S(1)}, f32[8,1024]{1,0:T(8,128)S(1)}, u32[]{:S(2)}, u32[]{:S(2)}) collective-permute-start(f32[8,1024]{1,0:T(8,128)S(1)} %finish.1.refs_0_), channel_id=1, source_target_pairs={{0,4},{4,0},{8,12},{12,8},{16,20},{20,16},{24,28},{28,24},{1,5},{5... | collective-permute-start | bytes 98312 | tf_op jit(solution)/shard_map/ppermute | solution.py:477
  133.7 1.2 collective-permute-start.36
  134.4 1.2 collective-permute-start.35
  134.9 1.2 collective-permute-start.34

commit v5 on v4

--- a/solution.py
+++ b/solution.py
@@ -56,10 +56,20 @@
     return lax.optimization_barrier((value, *others))[0]
 
 
-def strict_upper(rows):
-    a = lax.broadcasted_iota(jnp.int32, (rows, rows), 0)
-    b = lax.broadcasted_iota(jnp.int32, (rows, rows), 1)
-    return (a < b).astype(BF16)
+def rank_before(hot):
+    classes, rows = hot.shape
+    tiles = [hot[:, c : c + LANES] for c in range(0, rows, LANES)]
+    a = lax.broadcasted_iota(jnp.int32, (LANES, LANES), 0)
+    b = lax.broadcasted_iota(jnp.int32, (LANES, LANES), 1)
+    stacked = jnp.concatenate(tiles, axis=0)
+    inside = dot(stacked.astype(BF16), (a < b).astype(BF16))
+    sizes = jnp.sum(stacked, axis=1, keepdims=True)
+    offset, ranks = jnp.zeros((classes, 1), F32), []
+    for t in range(len(tiles)):
+        span = slice(t * classes, (t + 1) * classes)
+        ranks.append(inside[span] + offset)
+        offset = offset + sizes[span]
+    return jnp.concatenate(ranks, axis=1)
 
 
 def pick_rows(position, first, count, rows):
@@ -76,7 +86,7 @@
     owners = lax.broadcasted_iota(jnp.int32, (senders, rows), 0)
     hot = (ids >= owners * per_owner) & (ids < (owners + 1) * per_owner)
     hot_f = hot.astype(F32)
-    before = dot(hot.astype(BF16), strict_upper(rows))
+    before = rank_before(hot_f)
     base = (owners * cap_rows + 1).astype(F32)
     position = (jnp.sum(hot_f * (base + before), axis=0, keepdims=True)).astype(jnp.int32) - 1
     first = (owners * per_owner + where_ref[1] * visits_dev).astype(F32)
@@ -159,7 +169,7 @@
     hot = label == (visits + 1).astype(F32)
     hot_b = hot.astype(BF16)
     hot_f = hot.astype(F32)
-    before = dot(hot_b, strict_upper(rows))
+    before = rank_before(hot_f)
     base = (visits * VB + 1).astype(F32)
     position = (jnp.sum(hot_f * (base + before), axis=0, keepdims=True)).astype(jnp.int32) - 1
     inputs[1].wait()
@@ -188,7 +198,7 @@
 
     def one_visit(v, carry):
         count = count_ref[v]
-        at = pl.ds(pl.multiple_of(v * VB, VB), VB)
+        at = slice(v * VB, (v + 1) * VB)
         live_key = key_slot < count
         weight = (query_slot < count).astype(F32) / count.astype(F32)
         for p in range(HEADS // 2):
@@ -204,7 +214,8 @@
         ctx[v] = dot(pbar[v].astype(BF16), normed[at, :]).astype(BF16)
         return carry
 
-    lax.fori_loop(0, visits_dev, one_visit, 0)
+    for v in range(visits_dev):
+        one_visit(v, 0)
     copies[1].wait()
     copies[2].wait()
     vals = dot(ctx[...].reshape(visits_dev * HEADS, D), wv[...]).reshape(visits_dev, HEADS, D)
@@ -355,12 +366,9 @@
         outcome.append(jnp.sum(act * fw[j : j + 1, :], axis=-1, keepdims=True) + first * base)
     chosen = jnp.where(meta_ref[:, 0:1] > 0.5, fw[1:2, :], fw[0:1, :])
     slope = (chosen * sigma * (1.0 + pre * (1.0 - sigma))).astype(BF16)
+    moment = jnp.sum(slope.astype(F32) * pre, axis=-1, keepdims=True) / factor
     for i, (k, lo, size) in enumerate(plan):
         grads[e ^ k, :, lo : lo + size] = dot(slope, scratch[i][:size, :], NT)
-    moment = jnp.zeros((rows, 1), F32)
-    for j in range(n_ev):
-        span = slice(j * width, (j + 1) * width)
-        moment = moment + jnp.sum(grads[j] * gain[:, span] * mid[:, span], axis=-1, keepdims=True)
     scalars = pack_scalars([outcome[0], outcome[1], moment], rows)
     each = n_ev // n_mp
     for k in range(n_mp):
@@ -425,12 +433,14 @@
     vec = kept[:, :DV]
     spread = rms_factor(vec)
     moment = jnp.zeros((rows, 1), F32)
-    for j in range(n_ev):
+    for t in range(3):
+        forward = kept[:, DV + t * cols : DV + (t + 1) * cols]
+        moment = moment + jnp.sum(three[t].astype(F32) * forward, axis=-1, keepdims=True)
+    moment = moment / spread
+    for j in range(D // width):
         span = slice(j * width, (j + 1) * width)
         scaled = grads[j] * vgain_ref[:, span]
-        moment = moment + jnp.sum(scaled * vec[:, span], axis=-1, keepdims=True)
-        if (j + 1) * width <= D:
-            table[:, :, span] = (scaled * spread).reshape(n_mp, VPAD, width)
+        table[:, :, span] = (scaled * spread).reshape(n_mp, VPAD, width)
 
     @pl.when(m * cols < D)
     def _():

time: 138 us -> 137 us (level)
  transfers between devices with their start and end apart: 38 -> 38, of which waited for: 20 -> 19; matrix products, arithmetic and copies ran while one was open for 2% -> 2% of each run, Pallas kernels for 17% -> 17%
where the time goes in v5:
time: 137 us
  waiting for transfers between devices  49.1 us (36%)
  starting transfers between devices  39.5 us (29%)
  Pallas kernels  39.5 us (29%)
  local copies, waits for them, and re-layouts  5.97 us (4%)
  other arithmetic  1.85 us (1%)
    ppermute x37, waiting for transfers between devices, swap(): return lax.ppermute(x, axis, [(i, i ^ k) for i in range(size)])  49.1 us
    ppermute x37, starting transfers between devices, swap(): return lax.ppermute(x, axis, [(i, i ^ k) for i in range(size)])  35 us
    pallas_call x1, Pallas kernels, local(): pl.pallas_call(functools.partial(encode_kernel, visits_dev), out_shape=ja...  12.5 us
    pallas_call x1, Pallas kernels, local(): pl.pallas_call(functools.partial(back_kernel, n_mp, n_ev, qkv_plan), out_...  8.08 us
    pallas_call x1, Pallas kernels, local(): pl.pallas_call(functools.partial(ffn_kernel, n_mp, n_ev, ffn_plan), out_s...  6.42 us
    unnamed x53, local copies, waits for them, and re-layouts  5.16 us
    all_to_all x1, starting transfers between devices, local(): lax.all_to_all(send.reshape(n_ev, rows_dev // n_ev, D + LANES), 'events',...  4.45 us
    pallas_call x1, Pallas kernels, local(): pl.pallas_call(functools.partial(project_kernel, n_mp, n_ev, qkv_plan), o...  4.02 us
  transfers between devices with their start and end apart: 38, of which 19 were waited for; matrix products, arithmetic and copies ran while one was open for 2% of the time, Pallas kernels for 17%

profile of v5, /device:TPU:0, one launch (start us, length us, event | category | flops | bytes accessed | tf_op | source)
XLA Modules:
  0.0 137.1 jit_solution(1062375700918693096)
XLA Ops:
  0.6 3.0 %collective-permute-start.1 = (bf16[3,256,512]{2,1,0:T(8,128)(2,1)}, bf16[3,256,512]{2,1,0:T(8,128)(2,1)S(1)}, u32[]{:S(2)}, u32[]{:S(2)}) collective-permute-start(bf16[3,256,512]{2,1,0:T(8,128)(2,1)} %refs_5_.1), channel_id=1, source_target_pairs={{0,16},{4,20},{8,24},{12,28},{16,0},{20,4},{24,8},{28,12},{1,17},{... | collective-permute-start | bytes 2359304 | tf_op jit(solution)/shard_map/ppermute | solution.py:487
  3.7 1.5 %collective-permute-start = (bf16[3,256,512]{2,1,0:T(8,128)(2,1)}, bf16[3,256,512]{2,1,0:T(8,128)(2,1)S(1)}, u32[]{:S(2)}, u32[]{:S(2)}) collective-permute-start(bf16[3,256,512]{2,1,0:T(8,128)(2,1)} %refs_5_.1), channel_id=1, source_target_pairs={{0,8},{4,12},{8,0},{12,4},{16,24},{20,28},{24,16},{28,20},{1,9},{5... | collective-permute-start | bytes 2359304 | tf_op jit(solution)/shard_map/ppermute | solution.py:487
  5.2 1.4 %copy-done.3 = bf16[768,1024]{1,0:T(8,128)(2,1)S(1)} copy-done((bf16[768,1024]{1,0:T(8,128)(2,1)S(1)}, bf16[768,1024]{1,0:T(8,128)(2,1)}, u32[]{:S(2)}) %copy-start.3) | copy-done | bytes 1572888
  6.6 0.7 copy-done.8
  7.3 3.7 %pack.1 = bf16[768,1152]{1,0:T(8,128)(2,1)} custom-call(s32[2]{0:T(128)S(1)} %pad_add_fusion.where_ref, s32[6,128]{1,0:T(8,128)S(1)} %bitcast.29, bf16[768,1024]{1,0:T(8,128)(2,1)S(1)} %copy-done.3), custom_call_target="tpu_custom_call" | custom-call | flops 1 | bytes 1 | tf_op jit(solution)/shard_map/pack/pallas_call | solution.py:616
  11.2 4.5 %all-to-all-start = ((bf16[8,96,1152]{2,1,0:T(8,128)(2,1)}), bf16[8,96,1152]{2,1,0:T(8,128)(2,1)}, u32[]{:S(2)}, u32[]{:S(2)}) async-start(bf16[8,96,1152]{2,1,0:T(8,128)(2,1)} %bitcast.6), calls=%async_computation | async-start | bytes 3538944 | tf_op jit(solution)/shard_map/all_to_all | solution.py:626
  15.6 0.6 prep.1
  16.3 6.0 %collective-permute-done.1.high_ref.refs_9_.refs_7_ = bf16[3,256,512]{2,1,0:T(8,128)(2,1)S(1)} collective-permute-done((bf16[3,256,512]{2,1,0:T(8,128)(2,1)}, bf16[3,256,512]{2,1,0:T(8,128)(2,1)S(1)}, u32[]{:S(2)}, u32[]{:S(2)}) %collective-permute-start.1) | collective-permute-done | bytes 786464 | tf_op jit(solution)/shard_map/ppermute | solution.py:487
  22.2 2.1 %collective-permute-done.low_ref.refs_8_.refs_6_ = bf16[3,256,512]{2,1,0:T(8,128)(2,1)S(1)} collective-permute-done((bf16[3,256,512]{2,1,0:T(8,128)(2,1)}, bf16[3,256,512]{2,1,0:T(8,128)(2,1)S(1)}, u32[]{:S(2)}, u32[]{:S(2)}) %collective-permute-start) | collective-permute-done | bytes 786464 | tf_op jit(solution)/shard_map/ppermute | solution.py:487
  24.4 0.1 select_n.16
  24.5 0.1 pad.3.clone
  24.6 0.8 subtract_convert_fusion
  25.4 0.8 compare_convert_fusion.pick
  26.3 0.5 split.1
  26.8 0.5 collective-permute-start.6
  27.4 2.9 %collective-permute-start.8 = (bf16[3,128,512]{2,1,0:T(8,128)(2,1)S(1)}, bf16[3,128,512]{2,1,0:T(8,128)(2,1)}, u32[]{:S(2)}, u32[]{:S(2)}) collective-permute-start(bf16[3,128,512]{2,1,0:T(8,128)(2,1)S(1)} %get-tuple-element.33), channel_id=1, source_target_pairs={{0,8},{4,12},{8,0},{12,4},{16,24},{20,28},{24,16},{28,20},{1,9},{5... | collective-permute-start | bytes 1179656 | tf_op jit(solution)/shard_map/ppermute | solution.py:487
  30.3 1.5 %copy-done.19 = bf16[256,2048]{1,0:T(8,128)(2,1)S(1)} copy-done((bf16[256,2048]{1,0:T(8,128)(2,1)S(1)}, bf16[256,2048]{1,0:T(8,128)(2,1)}, u32[]{:S(2)}) %copy-start.19) | copy-done | bytes 1048600
  31.8 1.4 %fold.1.refs_5_ = bf16[272,2048]{1,0:T(8,128)(2,1)} custom-call(bf16[2048,256]{1,0:T(8,128)(2,1)S(1)} %copy-done.18, bf16[8,256]{1,0:T(8,128)(2,1)S(1)} %maximum_maximum_fusion.head_ref, bf16[256,2048]{1,0:T(8,128)(2,1)S(1)} %copy-done.19), custom_call_target="tpu_custom_call" | custom-call | flops 30000001024 | bytes 30000000 | tf_op jit(solution)/shard_map/fold/pallas_call | solution.py:662
  33.2 15.6 %collective-permute-done.6.refs_10_.refs_8_ = bf16[3,128,512]{2,1,0:T(8,128)(2,1)S(1)} collective-permute-done((bf16[3,128,512]{2,1,0:T(8,128)(2,1)S(1)}, bf16[3,128,512]{2,1,0:T(8,128)(2,1)S(1)}, u32[]{:S(2)}, u32[]{:S(2)}) %collective-permute-start.6) | collective-permute-done | bytes 393248 | tf_op jit(solution)/shard_map/ppermute | solution.py:487
  48.8 1.7 %collective-permute-done.8.refs_11_.refs_9_ = bf16[3,128,512]{2,1,0:T(8,128)(2,1)} collective-permute-done((bf16[3,128,512]{2,1,0:T(8,128)(2,1)S(1)}, bf16[3,128,512]{2,1,0:T(8,128)(2,1)}, u32[]{:S(2)}, u32[]{:S(2)}) %collective-permute-start.8) | collective-permute-done | bytes 393248 | tf_op jit(solution)/shard_map/ppermute | solution.py:487
  50.5 0.4 collective-permute-start.15
  50.8 1.6 %collective-permute-start.10 = (bf16[272,2048]{1,0:T(8,128)(2,1)}, bf16[272,2048]{1,0:T(8,128)(2,1)S(1)}, u32[]{:S(2)}, u32[]{:S(2)}) collective-permute-start(bf16[272,2048]{1,0:T(8,128)(2,1)} %fold.1.refs_5_), channel_id=1, source_target_pairs={{0,8},{4,12},{8,0},{12,4},{16,24},{20,28},{24,16},{28,20},{1,9},{5... | collective-permute-start | bytes 3342344 | tf_op jit(solution)/shard_map/ppermute | solution.py:487
  52.5 0.5 collective-permute-start.9
  53.0 1.7 %collective-permute-done.7.refs_15_.refs_13_ = bf16[3,128,512]{2,1,0:T(8,128)(2,1)S(1)} collective-permute-done((bf16[3,128,512]{2,1,0:T(8,128)(2,1)S(1)}, bf16[3,128,512]{2,1,0:T(8,128)(2,1)S(1)}, u32[]{:S(2)}, u32[]{:S(2)}) %collective-permute-start.7) | collective-permute-done | bytes 393248 | tf_op jit(solution)/shard_map/ppermute | solution.py:487
  54.7 0.2 collective-permute-done.9.refs_16_.refs_14_
  55.0 0.7 copy-done.12
  55.6 0.7 copy-done.15
  56.3 12.5 %encode.1.refs_0_ = bf16[8,2048]{1,0:T(8,128)(2,1)S(1)} custom-call(s32[6]{0:T(128)S(1)} %copy-done.15, f32[1,1024]{1,0:T(1,128)S(1)} %bitcast.30, bf16[768,1152]{1,0:T(8,128)(2,1)} %bitcast.7.got_hbm, bf16[1024,3072]{1,0:T(8,128)(2,1)} %qkv_ref.1, bf16[1024,1024]{1,0:T(8,128)(2,1)} %proj_ref.1), custom_call_target="tpu_custom_call" | custom-call | flops 1 | bytes 1 | tf_op jit(solution)/shard_map/encode/pallas_call | solution.py:682
  68.9 3.7 %collective-permute-start.13 = (bf16[8,2048]{1,0:T(8,128)(2,1)S(1)}, bf16[8,2048]{1,0:T(8,128)(2,1)S(1)}, u32[]{:S(2)}, u32[]{:S(2)}) collective-permute-start(bf16[8,2048]{1,0:T(8,128)(2,1)S(1)} %encode.1.refs_0_), channel_id=1, source_target_pairs={{0,3},{1,2},{2,1},{3,0},{4,7},{5,6},{6,5},{7,4},{8,11},{9,10},{10,... | collective-permute-start | bytes 98312 | tf_op jit(solution)/shard_map/ppermute | solution.py:487
  72.5 0.8 collective-permute-start.11
  73.3 2.5 %collective-permute-done.15.high_ref.refs_7_ = bf16[272,2048]{1,0:T(8,128)(2,1)S(1)} collective-permute-done((bf16[272,2048]{1,0:T(8,128)(2,1)}, bf16[272,2048]{1,0:T(8,128)(2,1)S(1)}, u32[]{:S(2)}, u32[]{:S(2)}) %collective-permute-start.15) | collective-permute-done | bytes 1114144 | tf_op jit(solution)/shard_map/ppermute | solution.py:487
  75.8 1.6 %collective-permute-done.12.refs_2_ = bf16[8,2048]{1,0:T(8,128)(2,1)S(1)} collective-permute-done((bf16[8,2048]{1,0:T(8,128)(2,1)S(1)}, bf16[8,2048]{1,0:T(8,128)(2,1)S(1)}, u32[]{:S(2)}, u32[]{:S(2)}) %collective-permute-start.12) | collective-permute-done | bytes 32800 | tf_op jit(solution)/shard_map/ppermute | solution.py:487
  77.4 0.5 collective-permute-start.14
  77.9 0.6 collective-permute-start.21
  78.6 1.5 %collective-permute-start.20 = (bf16[128,2048]{1,0:T(8,128)(2,1)S(1)}, bf16[128,2048]{1,0:T(8,128)(2,1)S(1)}, u32[]{:S(2)}, u32[]{:S(2)}) collective-permute-start(bf16[128,2048]{1,0:T(8,128)(2,1)S(1)} %get-tuple-element.42), channel_id=1, source_target_pairs={{0,16},{4,20},{8,24},{12,28},{16,0},{20,4},{24,8},{28,12},{1,17},{... | collective-permute-start | bytes 1572872 | tf_op jit(solution)/shard_map/ppermute | solution.py:487
  80.1 1.6 %collective-permute-done.14.refs_11_ = bf16[272,2048]{1,0:T(8,128)(2,1)S(1)} collective-permute-done((bf16[272,2048]{1,0:T(8,128)(2,1)S(1)}, bf16[272,2048]{1,0:T(8,128)(2,1)S(1)}, u32[]{:S(2)}, u32[]{:S(2)}) %collective-permute-start.14) | collective-permute-done | bytes 1114144 | tf_op jit(solution)/shard_map/ppermute | solution.py:487
  81.8 4.0 %project.1 = (bf16[32,512]{1,0:T(8,128)(2,1)S(1)}, f32[32,3712]{1,0:T(8,128)S(1)}) custom-call(s32[2]{0:T(128)S(1)} %copy-done.11, bf16[8,2048]{1,0:T(8,128)(2,1)S(1)} %encode.1.refs_0_, bf16[8,2048]{1,0:T(8,128)(2,1)S(1)} %collective-permute-done.11.refs_1_, bf16[8,2048]{1,0:T(8,128)(2,1)S(1)} %collective-permute-done.12.refs_2_, ...), custom_call_target="tpu_custom_call" | custom-call | flops 1 | bytes 1 | tf_op jit(solution)/shard_map/project/pallas_call | solution.py:715
  85.8 2.2 %collective-permute-start.19 = (bf16[32,512]{1,0:T(8,128)(2,1)S(1)}, bf16[32,512]{1,0:T(8,128)(2,1)S(1)}, u32[]{:S(2)}, u32[]{:S(2)}) collective-permute-start(bf16[32,512]{1,0:T(8,128)(2,1)S(1)} %get-tuple-element.40.refs_0_), channel_id=1, source_target_pairs={{0,3},{1,2},{2,1},{3,0},{4,7},{5,6},{6,5},{7,4},{8,11},{9,10},{10,... | collective-permute-start | bytes 98312 | tf_op jit(solution)/shard_map/ppermute | solution.py:487
  88.0 2.3 %collective-permute-start.17 = (bf16[32,512]{1,0:T(8,128)(2,1)S(1)}, bf16[32,512]{1,0:T(8,128)(2,1)S(1)}, u32[]{:S(2)}, u32[]{:S(2)}) collective-permute-start(bf16[32,512]{1,0:T(8,128)(2,1)S(1)} %get-tuple-element.40.refs_0_), channel_id=1, source_target_pairs={{0,1},{1,0},{2,3},{3,2},{4,5},{5,4},{6,7},{7,6},{8,9},{9,8},{10,11... | collective-permute-start | bytes 98312 | tf_op jit(solution)/shard_map/ppermute | solution.py:487
  90.3 3.0 %collective-permute-done.21.refs_9_ = bf16[144,2048]{1,0:T(8,128)(2,1)S(1)} collective-permute-done((bf16[144,2048]{1,0:T(8,128)(2,1)S(1)}, bf16[144,2048]{1,0:T(8,128)(2,1)S(1)}, u32[]{:S(2)}, u32[]{:S(2)}) %collective-permute-start.21) | collective-permute-done | bytes 589856 | tf_op jit(solution)/shard_map/ppermute | solution.py:487
  93.4 0.5 collective-permute-start.22
  93.9 2.2 %collective-permute-done.22.refs_13_ = bf16[128,2048]{1,0:T(8,128)(2,1)S(1)} collective-permute-done((bf16[128,2048]{1,0:T(8,128)(2,1)S(1)}, bf16[128,2048]{1,0:T(8,128)(2,1)S(1)}, u32[]{:S(2)}, u32[]{:S(2)}) %collective-permute-start.22) | collective-permute-done | bytes 524320 | tf_op jit(solution)/shard_map/ppermute | solution.py:487
  96.2 6.4 %ffn.1 = (bf16[32,640]{1,0:T(8,128)(2,1)S(1)}, bf16[32,640]{1,0:T(8,128)(2,1)S(1)}, bf16[32,640]{1,0:T(8,128)(2,1)S(1)}, bf16[32,640]{1,0:T(8,128)(2,1)S(1)}, f32[32,640]{1,0:T(8,128)S(1)}) custom-call(s32[2]{0:T(128)S(1)} %copy-done.11, f32[2]{0:T(128)S(1)} %copy-done.17, f32[1,2048]{1,0:T(1,128)S(1)} %bitcast.27, ...), custom_call_target="tpu_custom_call" | custom-call | flops 1 | bytes 1 | tf_op jit(solution)/shard_map/ffn/pallas_call | solution.py:744
  102.6 0.9 collective-permute-start.24
  103.5 1.9 %collective-permute-start.25 = (bf16[32,640]{1,0:T(8,128)(2,1)S(1)}, bf16[32,640]{1,0:T(8,128)(2,1)S(1)}, u32[]{:S(2)}, u32[]{:S(2)}) collective-permute-start(bf16[32,640]{1,0:T(8,128)(2,1)S(1)} %get-tuple-element.49), channel_id=1, source_target_pairs={{0,2},{1,3},{2,0},{3,1},{4,6},{5,7},{6,4},{7,5},{8,10},{9,11},{10,... | collective-permute-start | bytes 122888 | tf_op jit(solution)/shard_map/ppermute | solution.py:487
  105.4 1.6 %collective-permute-start.26 = (bf16[32,640]{1,0:T(8,128)(2,1)S(1)}, bf16[32,640]{1,0:T(8,128)(2,1)S(1)}, u32[]{:S(2)}, u32[]{:S(2)}) collective-permute-start(bf16[32,640]{1,0:T(8,128)(2,1)S(1)} %get-tuple-element.50), channel_id=1, source_target_pairs={{0,3},{1,2},{2,1},{3,0},{4,7},{5,6},{6,5},{7,4},{8,11},{9,10},{10,... | collective-permute-start | bytes 122888 | tf_op jit(solution)/shard_map/ppermute | solution.py:487
  107.1 2.1 %collective-permute-done.25.refs_2_ = bf16[32,640]{1,0:T(8,128)(2,1)S(1)} collective-permute-done((bf16[32,640]{1,0:T(8,128)(2,1)S(1)}, bf16[32,640]{1,0:T(8,128)(2,1)S(1)}, u32[]{:S(2)}, u32[]{:S(2)}) %collective-permute-start.25) | collective-permute-done | bytes 40992 | tf_op jit(solution)/shard_map/ppermute | solution.py:487
  109.2 2.0 %collective-permute-done.26.refs_3_ = bf16[32,640]{1,0:T(8,128)(2,1)S(1)} collective-permute-done((bf16[32,640]{1,0:T(8,128)(2,1)S(1)}, bf16[32,640]{1,0:T(8,128)(2,1)S(1)}, u32[]{:S(2)}, u32[]{:S(2)}) %collective-permute-start.26) | collective-permute-done | bytes 40992 | tf_op jit(solution)/shard_map/ppermute | solution.py:487
  111.2 8.1 %back.1 = (bf16[8,1152]{1,0:T(8,128)(2,1)S(1)}, bf16[8,1152]{1,0:T(8,128)(2,1)S(1)}, bf16[8,1152]{1,0:T(8,128)(2,1)S(1)}, bf16[8,1152]{1,0:T(8,128)(2,1)S(1)}, f...) custom-call(s32[2]{0:T(128)S(1)} %copy-done.11, f32[32,640]{1,0:T(8,128)S(1)} %get-tuple-element.46.mid_ref, ...), custom_call_target="tpu_custom_call" | custom-call | flops 1 | bytes 1 | tf_op jit(solution)/shard_map/back/pallas_call | solution.py:765
  119.4 2.3 %collective-permute-start.28 = (bf16[8,1152]{1,0:T(8,128)(2,1)S(1)}, bf16[8,1152]{1,0:T(8,128)(2,1)S(1)}, u32[]{:S(2)}, u32[]{:S(2)}) collective-permute-start(bf16[8,1152]{1,0:T(8,128)(2,1)S(1)} %get-tuple-element.56), channel_id=1, source_target_pairs={{0,2},{1,3},{2,0},{3,1},{4,6},{5,7},{6,4},{7,5},{8,10},{9,11},{10,... | collective-permute-start | bytes 55304 | tf_op jit(solution)/shard_map/ppermute | solution.py:487
  121.7 2.1 %collective-permute-start.29 = (bf16[8,1152]{1,0:T(8,128)(2,1)S(1)}, bf16[8,1152]{1,0:T(8,128)(2,1)S(1)}, u32[]{:S(2)}, u32[]{:S(2)}) collective-permute-start(bf16[8,1152]{1,0:T(8,128)(2,1)S(1)} %get-tuple-element.57), channel_id=1, source_target_pairs={{0,3},{1,2},{2,1},{3,0},{4,7},{5,6},{6,5},{7,4},{8,11},{9,10},{10,... | collective-permute-start | bytes 55304 | tf_op jit(solution)/shard_map/ppermute | solution.py:487
  123.8 0.1 copy.21
  123.9 0.6 reshape.62
  124.5 2.7 %collective-permute-done.29.refs_3_ = bf16[8,1152]{1,0:T(8,128)(2,1)S(1)} collective-permute-done((bf16[8,1152]{1,0:T(8,128)(2,1)S(1)}, bf16[8,1152]{1,0:T(8,128)(2,1)S(1)}, u32[]{:S(2)}, u32[]{:S(2)}) %collective-permute-start.29) | collective-permute-done | bytes 18464 | tf_op jit(solution)/shard_map/ppermute | solution.py:487
  127.2 0.7 finish.1.refs_0_
  127.9 1.5 %collective-permute-start.32 = (f32[8,1024]{1,0:T(8,128)S(1)}, f32[8,1024]{1,0:T(8,128)S(1)}, u32[]{:S(2)}, u32[]{:S(2)}) collective-permute-start(f32[8,1024]{1,0:T(8,128)S(1)} %finish.1.refs_0_), channel_id=1, source_target_pairs={{0,24},{4,28},{8,16},{12,20},{16,8},{20,12},{24,0},{28,4},{1,25},{... | collective-permute-start | bytes 98312 | tf_op jit(solution)/shard_map/ppermute | solution.py:487
  129.4 0.9 collective-permute-start.31
  130.4 1.1 collective-permute-start.30
  131.4 1.3 collective-permute-done.32.refs_3_
  132.8 0.6 collective-permute-done.31.refs_2_
  133.3 0.9 collective-permute-done.30.refs_1_
  134.3 0.2 collective-permute-done.35.refs_6_
  134.5 0.9 collective-permute-done.34.refs_5_
  135.5 1.4 %spread.1 = bf16[768,1024]{1,0:T(8,128)(2,1)} custom-call(bf16[768,64]{1,0:T(8,128)(2,1)S(1)} %copy-done.4, f32[8,1024]{1,0:T(8,128)S(1)} %finish.1.refs_0_, f32[8,1024]{1,0:T(8,128)S(1)} %collective-permute-done.30.refs_1_, f32[8,1024]{1,0:T(8,128)S(1)} %collective-permute-done.31.refs_2_, f32[8,1024]{1,0:T(8,128)S(1)} %collective-permute-done.32.refs_3_, ...), custom_call_target="tpu_custom_call" | custom-call | flops 1 | bytes 1 | tf_op jit(solution)/shard_map/spread/pallas_call | solution.py:795
  (88 shorter events, 0.7 us)
Async XLA Ops:
  0.6 21.6 %collective-permute-start.1 = (bf16[3,256,512]{2,1,0:T(8,128)(2,1)}, bf16[3,256,512]{2,1,0:T(8,128)(2,1)S(1)}, u32[]{:S(2)}, u32[]{:S(2)}) collective-permute-start(bf16[3,256,512]{2,1,0:T(8,128)(2,1)} %refs_5_.1), channel_id=1, source_target_pairs={{0,16},{4,20},{8,24},{12,28},{16,0},{20,4},{24,8},{28,12},{1,17},{... | collective-permute-start | bytes 2359304 | tf_op jit(solution)/shard_map/ppermute | solution.py:487
  3.7 20.7 %collective-permute-start = (bf16[3,256,512]{2,1,0:T(8,128)(2,1)}, bf16[3,256,512]{2,1,0:T(8,128)(2,1)S(1)}, u32[]{:S(2)}, u32[]{:S(2)}) collective-permute-start(bf16[3,256,512]{2,1,0:T(8,128)(2,1)} %refs_5_.1), channel_id=1, source_target_pairs={{0,8},{4,12},{8,0},{12,4},{16,24},{20,28},{24,16},{28,20},{1,9},{5... | collective-permute-start | bytes 2359304 | tf_op jit(solution)/shard_map/ppermute | solution.py:487
  5.2 25.1 %collective-permute-start.2 = (bf16[3,256,512]{2,1,0:T(8,128)(2,1)}, bf16[3,256,512]{2,1,0:T(8,128)(2,1)S(1)}, u32[]{:S(2)}, u32[]{:S(2)}) collective-permute-start(bf16[3,256,512]{2,1,0:T(8,128)(2,1)} %refs_5_.1), channel_id=1, source_target_pairs={{0,4},{4,0},{8,12},{12,8},{16,20},{20,16},{24,28},{28,24},{1,5},{5... | collective-permute-start | bytes 2359304 | tf_op jit(solution)/shard_map/ppermute | solution.py:487
  5.2 5.9 %copy-start.10 = (s32[2]{0:T(128)}, s32[2]{0:T(128)S(1)}, u32[]{:S(2)}) copy-start(s32[2]{0:T(128)S(1)} %pad_add_fusion.where_ref) | copy-start | bytes 28
  5.2 1.4 %copy-start.3 = (bf16[768,1024]{1,0:T(8,128)(2,1)S(1)}, bf16[768,1024]{1,0:T(8,128)(2,1)}, u32[]{:S(2)}) copy-start(bf16[768,1024]{1,0:T(8,128)(2,1)} %x_hbm.1) | copy-start | bytes 4718596
  6.6 0.7 copy-start.8
  11.1 4.5 %copy-start.20 = (s32[24]{0:T(128)S(1)}, s32[24]{0:T(128)}, u32[]{:S(2)}) copy-start(s32[24]{0:T(128)} %patient_ref.1) | copy-start | bytes 292
  11.1 4.5 %copy-start.21 = (s32[24]{0:T(128)S(1)}, s32[24]{0:T(128)}, u32[]{:S(2)}) copy-start(s32[24]{0:T(128)} %treat_ref.1) | copy-start | bytes 292
  11.1 4.5 %copy-start.22 = (f32[24]{0:T(128)S(1)}, f32[24]{0:T(128)}, u32[]{:S(2)}) copy-start(f32[24]{0:T(128)} %target_ref.1) | copy-start | bytes 292
  11.1 5.1 %copy-start.25 = (s32[8]{0:T(128)S(1)}, s32[8]{0:T(128)}, u32[]{:S(2)}) copy-start(s32[8]{0:T(128)} %constant.26.clone) | copy-start | bytes 100
  11.1 14.3 %copy-start.9 = (s32[768]{0:T(1024)S(1)}, s32[768]{0:T(1024)}, u32[]{:S(2)}) copy-start(s32[768]{0:T(1024)} %param.18) | copy-start | bytes 9220
  11.2 39.3 %all-to-all-start = ((bf16[8,96,1152]{2,1,0:T(8,128)(2,1)}), bf16[8,96,1152]{2,1,0:T(8,128)(2,1)}, u32[]{:S(2)}, u32[]{:S(2)}) async-start(bf16[8,96,1152]{2,1,0:T(8,128)(2,1)} %bitcast.6), calls=%async_computation | async-start | bytes 3538944 | tf_op jit(solution)/shard_map/all_to_all | solution.py:626
  16.2 10.6 %copy-start.13 = (f32[8,32]{1,0:T(8,128)}, f32[8,32]{1,0:T(8,128)S(1)}, u32[]{:S(2)}) copy-start(f32[8,32]{1,0:T(8,128)S(1)} %get-tuple-element.31.refs_6_) | copy-start | bytes 3076
  22.2 8.0 %collective-permute-start.4 = (bf16[3,256,512]{2,1,0:T(8,128)(2,1)S(1)}, bf16[3,256,512]{2,1,0:T(8,128)(2,1)}, u32[]{:S(2)}, u32[]{:S(2)}) collective-permute-start(bf16[3,256,512]{2,1,0:T(8,128)(2,1)S(1)} %collective-permute-done.1.high_ref.refs_9_.refs_7_), channel_id=1, source_target_pairs={{0,4},{4,0},{8,12},{12,8},{16,20},{20,16},{24,28},{28,24},{1,5},{5... | collective-permute-start | bytes 2359304 | tf_op jit(solution)/shard_map/ppermute | solution.py:487
  24.3 5.9 %collective-permute-start.3 = (bf16[3,256,512]{2,1,0:T(8,128)(2,1)S(1)}, bf16[3,256,512]{2,1,0:T(8,128)(2,1)S(1)}, u32[]{:S(2)}, u32[]{:S(2)}) collective-permute-start(bf16[3,256,512]{2,1,0:T(8,128)(2,1)S(1)} %collective-permute-done.low_ref.refs_8_.refs_6_), channel_id=1, source_target_pairs={{0,4},{4,0},{8,12},{12,8},{16,20},{20,16},{24,28},{28,24},{1,5},{5... | collective-permute-start | bytes 2359304 | tf_op jit(solution)/shard_map/ppermute | solution.py:487
  24.5 5.8 %copy-start.18 = (bf16[2048,256]{1,0:T(8,128)(2,1)S(1)}, bf16[2048,256]{1,0:T(8,128)(2,1)}, u32[]{:S(2)}) copy-start(bf16[2048,256]{1,0:T(8,128)(2,1)} %weight_ref.1) | copy-start | bytes 3145732
  26.8 22.0 %collective-permute-start.6 = (bf16[3,128,512]{2,1,0:T(8,128)(2,1)S(1)}, bf16[3,128,512]{2,1,0:T(8,128)(2,1)S(1)}, u32[]{:S(2)}, u32[]{:S(2)}) collective-permute-start(bf16[3,128,512]{2,1,0:T(8,128)(2,1)S(1)} %get-tuple-element.32), channel_id=1, source_target_pairs={{0,16},{4,20},{8,24},{12,28},{16,0},{20,4},{24,8},{28,12},{1,17},{... | collective-permute-start | bytes 1179656 | tf_op jit(solution)/shard_map/ppermute | solution.py:487
  27.4 23.1 %collective-permute-start.8 = (bf16[3,128,512]{2,1,0:T(8,128)(2,1)S(1)}, bf16[3,128,512]{2,1,0:T(8,128)(2,1)}, u32[]{:S(2)}, u32[]{:S(2)}) collective-permute-start(bf16[3,128,512]{2,1,0:T(8,128)(2,1)S(1)} %get-tuple-element.33), channel_id=1, source_target_pairs={{0,8},{4,12},{8,0},{12,4},{16,24},{20,28},{24,16},{28,20},{1,9},{5... | collective-permute-start | bytes 1179656 | tf_op jit(solution)/shard_map/ppermute | solution.py:487
  30.3 51.4 %copy-start.2 = (bf16[3,256,512]{2,1,0:T(8,128)(2,1)}, bf16[3,256,512]{2,1,0:T(8,128)(2,1)S(1)}, u32[]{:S(2)}) copy-start(bf16[3,256,512]{2,1,0:T(8,128)(2,1)S(1)} %collective-permute-done.3.refs_13_.refs_11_) | copy-start | bytes 2359300
  30.3 1.5 %copy-start.19 = (bf16[256,2048]{1,0:T(8,128)(2,1)S(1)}, bf16[256,2048]{1,0:T(8,128)(2,1)}, u32[]{:S(2)}) copy-start(bf16[256,2048]{1,0:T(8,128)(2,1)} %ffn_ref) | copy-start | bytes 3145732
  33.2 21.7 %collective-permute-start.5 = (bf16[272,2048]{1,0:T(8,128)(2,1)}, bf16[272,2048]{1,0:T(8,128)(2,1)}, u32[]{:S(2)}, u32[]{:S(2)}) collective-permute-start(bf16[272,2048]{1,0:T(8,128)(2,1)} %fold.1.refs_5_), channel_id=1, source_target_pairs={{0,4},{4,0},{8,12},{12,8},{16,20},{20,16},{24,28},{28,24},{1,5},{5... | collective-permute-start | bytes 3342344 | tf_op jit(solution)/shard_map/ppermute | solution.py:487
  50.5 25.3 %collective-permute-start.15 = (bf16[272,2048]{1,0:T(8,128)(2,1)}, bf16[272,2048]{1,0:T(8,128)(2,1)S(1)}, u32[]{:S(2)}, u32[]{:S(2)}) collective-permute-start(bf16[272,2048]{1,0:T(8,128)(2,1)} %fold.1.refs_5_), channel_id=1, source_target_pairs={{0,16},{4,20},{8,24},{12,28},{16,0},{20,4},{24,8},{28,12},{1,17},{... | collective-permute-start | bytes 3342344 | tf_op jit(solution)/shard_map/ppermute | solution.py:487
  50.8 26.5 %collective-permute-start.10 = (bf16[272,2048]{1,0:T(8,128)(2,1)}, bf16[272,2048]{1,0:T(8,128)(2,1)S(1)}, u32[]{:S(2)}, u32[]{:S(2)}) collective-permute-start(bf16[272,2048]{1,0:T(8,128)(2,1)} %fold.1.refs_5_), channel_id=1, source_target_pairs={{0,8},{4,12},{8,0},{12,4},{16,24},{20,28},{24,16},{28,20},{1,9},{5... | collective-permute-start | bytes 3342344 | tf_op jit(solution)/shard_map/ppermute | solution.py:487
  52.5 2.3 %collective-permute-start.7 = (bf16[3,128,512]{2,1,0:T(8,128)(2,1)S(1)}, bf16[3,128,512]{2,1,0:T(8,128)(2,1)S(1)}, u32[]{:S(2)}, u32[]{:S(2)}) collective-permute-start(bf16[3,128,512]{2,1,0:T(8,128)(2,1)S(1)} %collective-permute-done.6.refs_10_.refs_8_), channel_id=1, source_target_pairs={{0,4},{4,0},{8,12},{12,8},{16,20},{20,16},{24,28},{28,24},{1,5},{5... | collective-permute-start | bytes 1179656 | tf_op jit(solution)/shard_map/ppermute | solution.py:487
  52.5 2.5 %collective-permute-start.9 = (bf16[3,128,512]{2,1,0:T(8,128)(2,1)}, bf16[3,128,512]{2,1,0:T(8,128)(2,1)S(1)}, u32[]{:S(2)}, u32[]{:S(2)}) collective-permute-start(bf16[3,128,512]{2,1,0:T(8,128)(2,1)} %collective-permute-done.8.refs_11_.refs_9_), channel_id=1, source_target_pairs={{0,4},{4,0},{8,12},{12,8},{16,20},{20,16},{24,28},{28,24},{1,5},{5... | collective-permute-start | bytes 1179656 | tf_op jit(solution)/shard_map/ppermute | solution.py:487
  55.0 0.7 copy-start.12
  55.6 0.7 copy-start.15
  68.8 12.9 %copy-start.1 = (bf16[3,256,512]{2,1,0:T(8,128)(2,1)S(1)}, bf16[3,256,512]{2,1,0:T(8,128)(2,1)}, u32[]{:S(2)}) copy-start(bf16[3,256,512]{2,1,0:T(8,128)(2,1)} %refs_5_.1) | copy-start | bytes 2359300
  68.8 12.9 %copy-start.6 = (f32[2048]{0:T(1024)S(1)}, f32[2048]{0:T(1024)}, u32[]{:S(2)}) copy-start(f32[2048]{0:T(1024)} %param.26) | copy-start | bytes 24580
  68.8 12.9 %copy-start.11 = (s32[2]{0:T(128)S(1)}, s32[2]{0:T(128)}, u32[]{:S(2)}) copy-start(s32[2]{0:T(128)} %copy-done.10) | copy-start | bytes 28
  68.9 12.9 %copy-start.14 = (f32[8,32]{1,0:T(8,128)S(1)}, f32[8,32]{1,0:T(8,128)}, u32[]{:S(2)}) copy-start(f32[8,32]{1,0:T(8,128)} %copy-done.13) | copy-start | bytes 3076
  68.9 6.9 %collective-permute-start.13 = (bf16[8,2048]{1,0:T(8,128)(2,1)S(1)}, bf16[8,2048]{1,0:T(8,128)(2,1)S(1)}, u32[]{:S(2)}, u32[]{:S(2)}) collective-permute-start(bf16[8,2048]{1,0:T(8,128)(2,1)S(1)} %encode.1.refs_0_), channel_id=1, source_target_pairs={{0,3},{1,2},{2,1},{3,0},{4,7},{5,6},{6,5},{7,4},{8,11},{9,10},{10,... | collective-permute-start | bytes 98312 | tf_op jit(solution)/shard_map/ppermute | solution.py:487
  72.5 4.8 %collective-permute-start.12 = (bf16[8,2048]{1,0:T(8,128)(2,1)S(1)}, bf16[8,2048]{1,0:T(8,128)(2,1)S(1)}, u32[]{:S(2)}, u32[]{:S(2)}) collective-permute-start(bf16[8,2048]{1,0:T(8,128)(2,1)S(1)} %encode.1.refs_0_), channel_id=1, source_target_pairs={{0,2},{1,3},{2,0},{3,1},{4,6},{5,7},{6,4},{7,5},{8,10},{9,11},{10,... | collective-permute-start | bytes 98312 | tf_op jit(solution)/shard_map/ppermute | solution.py:487
  72.5 4.8 %collective-permute-start.11 = (bf16[8,2048]{1,0:T(8,128)(2,1)S(1)}, bf16[8,2048]{1,0:T(8,128)(2,1)S(1)}, u32[]{:S(2)}, u32[]{:S(2)}) collective-permute-start(bf16[8,2048]{1,0:T(8,128)(2,1)S(1)} %encode.1.refs_0_), channel_id=1, source_target_pairs={{0,1},{1,0},{2,3},{3,2},{4,5},{5,4},{6,7},{7,6},{8,9},{9,8},{10,11... | collective-permute-start | bytes 98312 | tf_op jit(solution)/shard_map/ppermute | solution.py:487
  75.8 10.0 %copy-start = (bf16[272,2048]{1,0:T(8,128)(2,1)}, bf16[272,2048]{1,0:T(8,128)(2,1)S(1)}, u32[]{:S(2)}) copy-start(bf16[272,2048]{1,0:T(8,128)(2,1)S(1)} %collective-permute-done.15.high_ref.refs_7_) | copy-start | bytes 3342340
  77.4 2.8 %collective-permute-start.16 = (bf16[272,2048]{1,0:T(8,128)(2,1)S(1)}, bf16[272,2048]{1,0:T(8,128)(2,1)S(1)}, u32[]{:S(2)}, u32[]{:S(2)}) collective-permute-start(bf16[272,2048]{1,0:T(8,128)(2,1)S(1)} %collective-permute-done.15.high_ref.refs_7_), channel_id=1, source_target_pairs={{0,4},{4,0},{8,12},{12,8},{16,20},{20,16},{24,28},{28,24},{1,5},{5... | collective-permute-start | bytes 3342344 | tf_op jit(solution)/shard_map/ppermute | solution.py:487
  77.4 4.3 %collective-permute-start.14 = (bf16[272,2048]{1,0:T(8,128)(2,1)S(1)}, bf16[272,2048]{1,0:T(8,128)(2,1)S(1)}, u32[]{:S(2)}, u32[]{:S(2)}) collective-permute-start(bf16[272,2048]{1,0:T(8,128)(2,1)S(1)} %collective-permute-done.10.low_ref.refs_6_), channel_id=1, source_target_pairs={{0,4},{4,0},{8,12},{12,8},{16,20},{20,16},{24,28},{28,24},{1,5},{5... | collective-permute-start | bytes 3342344 | tf_op jit(solution)/shard_map/ppermute | solution.py:487
  77.9 15.4 %collective-permute-start.21 = (bf16[144,2048]{1,0:T(8,128)(2,1)S(1)}, bf16[144,2048]{1,0:T(8,128)(2,1)S(1)}, u32[]{:S(2)}, u32[]{:S(2)}) collective-permute-start(bf16[144,2048]{1,0:T(8,128)(2,1)S(1)} %get-tuple-element.44), channel_id=1, source_target_pairs={{0,8},{4,12},{8,0},{12,4},{16,24},{20,28},{24,16},{28,20},{1,9},{5... | collective-permute-start | bytes 1769480 | tf_op jit(solution)/shard_map/ppermute | solution.py:487
  78.6 14.8 %collective-permute-start.20 = (bf16[128,2048]{1,0:T(8,128)(2,1)S(1)}, bf16[128,2048]{1,0:T(8,128)(2,1)S(1)}, u32[]{:S(2)}, u32[]{:S(2)}) collective-permute-start(bf16[128,2048]{1,0:T(8,128)(2,1)S(1)} %get-tuple-element.42), channel_id=1, source_target_pairs={{0,16},{4,20},{8,24},{12,28},{16,0},{20,4},{24,8},{28,12},{1,17},{... | collective-permute-start | bytes 1572872 | tf_op jit(solution)/shard_map/ppermute | solution.py:487
  80.1 5.7 %copy-start.23 = (bf16[272,2048]{1,0:T(8,128)(2,1)}, bf16[272,2048]{1,0:T(8,128)(2,1)S(1)}, u32[]{:S(2)}) copy-start(bf16[272,2048]{1,0:T(8,128)(2,1)S(1)} %collective-permute-done.16.refs_12_) | copy-start | bytes 3342340
  81.7 4.1 %copy-start.24 = (bf16[272,2048]{1,0:T(8,128)(2,1)}, bf16[272,2048]{1,0:T(8,128)(2,1)S(1)}, u32[]{:S(2)}) copy-start(bf16[272,2048]{1,0:T(8,128)(2,1)S(1)} %collective-permute-done.14.refs_11_) | copy-start | bytes 3342340
  81.7 14.4 %copy-start.5 = (f32[2048,2]{0,1:T(2,128)S(1)}, f32[2048,2]{0,1:T(2,128)}, u32[]{:S(2)}) copy-start(f32[2048,2]{0,1:T(2,128)} %param.31) | copy-start | bytes 49156
  81.8 14.4 %copy-start.7 = (f32[2048]{0:T(1024)S(1)}, f32[2048]{0:T(1024)}, u32[]{:S(2)}) copy-start(f32[2048]{0:T(1024)} %param.28) | copy-start | bytes 24580
  81.8 14.4 %copy-start.17 = (f32[2]{0:T(128)S(1)}, f32[2]{0:T(128)}, u32[]{:S(2)}) copy-start(f32[2]{0:T(128)} %bias_ref.1) | copy-start | bytes 28
  85.8 7.5 %collective-permute-start.19 = (bf16[32,512]{1,0:T(8,128)(2,1)S(1)}, bf16[32,512]{1,0:T(8,128)(2,1)S(1)}, u32[]{:S(2)}, u32[]{:S(2)}) collective-permute-start(bf16[32,512]{1,0:T(8,128)(2,1)S(1)} %get-tuple-element.40.refs_0_), channel_id=1, source_target_pairs={{0,3},{1,2},{2,1},{3,0},{4,7},{5,6},{6,5},{7,4},{8,11},{9,10},{10,... | collective-permute-start | bytes 98312 | tf_op jit(solution)/shard_map/ppermute | solution.py:487
  88.0 5.3 %collective-permute-start.18 = (bf16[32,512]{1,0:T(8,128)(2,1)S(1)}, bf16[32,512]{1,0:T(8,128)(2,1)S(1)}, u32[]{:S(2)}, u32[]{:S(2)}) collective-permute-start(bf16[32,512]{1,0:T(8,128)(2,1)S(1)} %get-tuple-element.40.refs_0_), channel_id=1, source_target_pairs={{0,2},{1,3},{2,0},{3,1},{4,6},{5,7},{6,4},{7,5},{8,10},{9,11},{10,... | collective-permute-start | bytes 98312 | tf_op jit(solution)/shard_map/ppermute | solution.py:487
  88.0 5.3 %collective-permute-start.17 = (bf16[32,512]{1,0:T(8,128)(2,1)S(1)}, bf16[32,512]{1,0:T(8,128)(2,1)S(1)}, u32[]{:S(2)}, u32[]{:S(2)}) collective-permute-start(bf16[32,512]{1,0:T(8,128)(2,1)S(1)} %get-tuple-element.40.refs_0_), channel_id=1, source_target_pairs={{0,1},{1,0},{2,3},{3,2},{4,5},{5,4},{6,7},{7,6},{8,9},{9,8},{10,11... | collective-permute-start | bytes 98312 | tf_op jit(solution)/shard_map/ppermute | solution.py:487
  93.3 2.8 %collective-permute-start.23 = (bf16[144,2048]{1,0:T(8,128)(2,1)S(1)}, bf16[144,2048]{1,0:T(8,128)(2,1)S(1)}, u32[]{:S(2)}, u32[]{:S(2)}) collective-permute-start(bf16[144,2048]{1,0:T(8,128)(2,1)S(1)} %collective-permute-done.21.refs_9_), channel_id=1, source_target_pairs={{0,4},{4,0},{8,12},{12,8},{16,20},{20,16},{24,28},{28,24},{1,5},{5... | collective-permute-start | bytes 1769480 | tf_op jit(solution)/shard_map/ppermute | solution.py:487
  93.4 2.7 %collective-permute-start.22 = (bf16[128,2048]{1,0:T(8,128)(2,1)S(1)}, bf16[128,2048]{1,0:T(8,128)(2,1)S(1)}, u32[]{:S(2)}, u32[]{:S(2)}) collective-permute-start(bf16[128,2048]{1,0:T(8,128)(2,1)S(1)} %collective-permute-done.20.refs_8_), channel_id=1, source_target_pairs={{0,4},{4,0},{8,12},{12,8},{16,20},{20,16},{24,28},{28,24},{1,5},{5... | collective-permute-start | bytes 1572872 | tf_op jit(solution)/shard_map/ppermute | solution.py:487
  102.6 4.5 %collective-permute-start.24 = (bf16[32,640]{1,0:T(8,128)(2,1)S(1)}, bf16[32,640]{1,0:T(8,128)(2,1)S(1)}, u32[]{:S(2)}, u32[]{:S(2)}) collective-permute-start(bf16[32,640]{1,0:T(8,128)(2,1)S(1)} %get-tuple-element.48), channel_id=1, source_target_pairs={{0,1},{1,0},{2,3},{3,2},{4,5},{5,4},{6,7},{7,6},{8,9},{9,8},{10,11... | collective-permute-start | bytes 122888 | tf_op jit(solution)/shard_map/ppermute | solution.py:487
  103.5 5.7 %collective-permute-start.25 = (bf16[32,640]{1,0:T(8,128)(2,1)S(1)}, bf16[32,640]{1,0:T(8,128)(2,1)S(1)}, u32[]{:S(2)}, u32[]{:S(2)}) collective-permute-start(bf16[32,640]{1,0:T(8,128)(2,1)S(1)} %get-tuple-element.49), channel_id=1, source_target_pairs={{0,2},{1,3},{2,0},{3,1},{4,6},{5,7},{6,4},{7,5},{8,10},{9,11},{10,... | collective-permute-start | bytes 122888 | tf_op jit(solution)/shard_map/ppermute | solution.py:487
  105.4 5.8 %collective-permute-start.26 = (bf16[32,640]{1,0:T(8,128)(2,1)S(1)}, bf16[32,640]{1,0:T(8,128)(2,1)S(1)}, u32[]{:S(2)}, u32[]{:S(2)}) collective-permute-start(bf16[32,640]{1,0:T(8,128)(2,1)S(1)} %get-tuple-element.50), channel_id=1, source_target_pairs={{0,3},{1,2},{2,1},{3,0},{4,7},{5,6},{6,5},{7,4},{8,11},{9,10},{10,... | collective-permute-start | bytes 122888 | tf_op jit(solution)/shard_map/ppermute | solution.py:487
  111.2 16.0 %copy-start.16 = (s32[6]{0:T(128)S(1)}, s32[6]{0:T(128)}, u32[]{:S(2)}) copy-start(s32[6]{0:T(128)} %count_ref.3) | copy-start | bytes 76
  111.2 24.3 %copy-start.4 = (bf16[768,64]{1,0:T(8,128)(2,1)S(1)}, bf16[768,64]{1,0:T(8,128)(2,1)}, u32[]{:S(2)}) copy-start(bf16[768,64]{1,0:T(8,128)(2,1)} %compare_convert_fusion.pick) | copy-start | bytes 294916
  119.3 5.2 %collective-permute-start.27 = (bf16[8,1152]{1,0:T(8,128)(2,1)S(1)}, bf16[8,1152]{1,0:T(8,128)(2,1)S(1)}, u32[]{:S(2)}, u32[]{:S(2)}) collective-permute-start(bf16[8,1152]{1,0:T(8,128)(2,1)S(1)} %get-tuple-element.55), channel_id=1, source_target_pairs={{0,1},{1,0},{2,3},{3,2},{4,5},{5,4},{6,7},{7,6},{8,9},{9,8},{10,11... | collective-permute-start | bytes 55304 | tf_op jit(solution)/shard_map/ppermute | solution.py:487
  119.4 5.1 %collective-permute-start.28 = (bf16[8,1152]{1,0:T(8,128)(2,1)S(1)}, bf16[8,1152]{1,0:T(8,128)(2,1)S(1)}, u32[]{:S(2)}, u32[]{:S(2)}) collective-permute-start(bf16[8,1152]{1,0:T(8,128)(2,1)S(1)} %get-tuple-element.56), channel_id=1, source_target_pairs={{0,2},{1,3},{2,0},{3,1},{4,6},{5,7},{6,4},{7,5},{8,10},{9,11},{10,... | collective-permute-start | bytes 55304 | tf_op jit(solution)/shard_map/ppermute | solution.py:487
  121.7 5.6 %collective-permute-start.29 = (bf16[8,1152]{1,0:T(8,128)(2,1)S(1)}, bf16[8,1152]{1,0:T(8,128)(2,1)S(1)}, u32[]{:S(2)}, u32[]{:S(2)}) collective-permute-start(bf16[8,1152]{1,0:T(8,128)(2,1)S(1)} %get-tuple-element.57), channel_id=1, source_target_pairs={{0,3},{1,2},{2,1},{3,0},{4,7},{5,6},{6,5},{7,4},{8,11},{9,10},{10,... | collective-permute-start | bytes 55304 | tf_op jit(solution)/shard_map/ppermute | solution.py:487
  127.9 4.8 %collective-permute-start.32 = (f32[8,1024]{1,0:T(8,128)S(1)}, f32[8,1024]{1,0:T(8,128)S(1)}, u32[]{:S(2)}, u32[]{:S(2)}) collective-permute-start(f32[8,1024]{1,0:T(8,128)S(1)} %finish.1.refs_0_), channel_id=1, source_target_pairs={{0,24},{4,28},{8,16},{12,20},{16,8},{20,12},{24,0},{28,4},{1,25},{... | collective-permute-start | bytes 98312 | tf_op jit(solution)/shard_map/ppermute | solution.py:487
  129.4 3.9 %collective-permute-start.31 = (f32[8,1024]{1,0:T(8,128)S(1)}, f32[8,1024]{1,0:T(8,128)S(1)}, u32[]{:S(2)}, u32[]{:S(2)}) collective-permute-start(f32[8,1024]{1,0:T(8,128)S(1)} %finish.1.refs_0_), channel_id=1, source_target_pairs={{0,16},{4,20},{8,24},{12,28},{16,0},{20,4},{24,8},{28,12},{1,17},{... | collective-permute-start | bytes 98312 | tf_op jit(solution)/shard_map/ppermute | solution.py:487
  130.4 3.9 %collective-permute-start.30 = (f32[8,1024]{1,0:T(8,128)S(1)}, f32[8,1024]{1,0:T(8,128)S(1)}, u32[]{:S(2)}, u32[]{:S(2)}) collective-permute-start(f32[8,1024]{1,0:T(8,128)S(1)} %finish.1.refs_0_), channel_id=1, source_target_pairs={{0,8},{4,12},{8,0},{12,4},{16,24},{20,28},{24,16},{28,20},{1,9},{5... | collective-permute-start | bytes 98312 | tf_op jit(solution)/shard_map/ppermute | solution.py:487
  131.4 2.9 %collective-permute-start.33 = (f32[8,1024]{1,0:T(8,128)S(1)}, f32[8,1024]{1,0:T(8,128)S(1)}, u32[]{:S(2)}, u32[]{:S(2)}) collective-permute-start(f32[8,1024]{1,0:T(8,128)S(1)} %finish.1.refs_0_), channel_id=1, source_target_pairs={{0,4},{4,0},{8,12},{12,8},{16,20},{20,16},{24,28},{28,24},{1,5},{5... | collective-permute-start | bytes 98312 | tf_op jit(solution)/shard_map/ppermute | solution.py:487
  132.8 1.5 %collective-permute-start.36 = (f32[8,1024]{1,0:T(8,128)S(1)}, f32[8,1024]{1,0:T(8,128)S(1)}, u32[]{:S(2)}, u32[]{:S(2)}) collective-permute-start(f32[8,1024]{1,0:T(8,128)S(1)} %collective-permute-done.32.refs_3_), channel_id=1, source_target_pairs={{0,4},{4,0},{8,12},{12,8},{16,20},{20,16},{24,28},{28,24},{1,5},{5... | collective-permute-start | bytes 98312 | tf_op jit(solution)/shard_map/ppermute | solution.py:487
  133.3 1.2 collective-permute-start.35
  134.3 1.2 collective-permute-start.34

commit v6 on v5

--- a/solution.py
+++ b/solution.py
@@ -250,14 +250,27 @@
     return copies
 
 
+def fetch_parts(pieces, plan, scratch, sems):
+    copies = []
+    for (_, parts), buffer in zip(plan, scratch, strict=True):
+        group = []
+        for i, first, rows in parts:
+            span = slice(first, first + rows)
+            place = buffer.at[:, span, :] if len(buffer.shape) == 3 else buffer.at[span, :]
+            group.append(pltpu.make_async_copy(pieces[i], place, sems.at[i]))
+            group[-1].start()
+        copies.append(group)
+    return copies
+
+
 def project_kernel(n_mp, n_ev, plan, where_ref, *refs):
-    n = len(plan)
+    n, groups = sum(len(parts) for _, parts in plan), len(plan)
     vec_in, (gain_ref, meta_ref, patient_ref), refs = refs[:n_mp], refs[n_mp : n_mp + 3], refs[n_mp + 3 :]
     pieces, refs = refs[:n], refs[n:]
     attended_ref, state, refs = refs[0], refs[1], refs[2:]
-    scratch, refs = refs[:n], refs[n:]
+    scratch, refs = refs[:groups], refs[groups:]
     vec, blocks, sems, kept, out_sems = refs
-    copies = fetch(pieces, scratch, sems)
+    copies = fetch_parts(pieces, plan, scratch, sems)
     e, m = where_ref[0], where_ref[1]
     cols = attended_ref.shape[1]
     saves = [
@@ -275,11 +288,12 @@
     for j in range(n_ev):
         blocks[j] = normed[:, j * width : (j + 1) * width]
     totals = [jnp.zeros((rows, cols), F32) for _ in range(3)]
-    for i, (k, lo, size) in enumerate(plan):
-        copies[i].wait()
-        block = blocks[e ^ k][:, lo : lo + size]
+    for i, (k, _) in enumerate(plan):
+        for copy in copies[i]:
+            copy.wait()
+        block = blocks[e ^ k]
         for t in range(3):
-            totals[t] = totals[t] + dot(block, scratch[i][t, :size, :])
+            totals[t] = totals[t] + dot(block, scratch[i][t])
     parts = [total.astype(BF16) for total in totals]
     for t in range(3):
         kept[:, DV + t * cols : DV + (t + 1) * cols] = parts[t].astype(F32)
@@ -323,16 +337,16 @@
 def ffn_kernel(
     n_mp, n_ev, plan, where_ref, bias_ref, gain_ref, meta_ref, head_ref, *refs
 ):
-    n = len(plan)
+    n, groups = sum(len(parts) for _, parts in plan), len(plan)
     attn_in, state, refs = refs[:n_mp], refs[n_mp], refs[n_mp + 1 :]
     pieces, refs = refs[:n], refs[n:]
     outs, mid_ref, refs = refs[:n_mp], refs[n_mp], refs[n_mp + 1 :]
-    scratch, refs = refs[:n], refs[n:]
+    scratch, refs = refs[:groups], refs[groups:]
     attn, vec_ref, blocks, grads, sems = refs
     e, m = where_ref[0], where_ref[1]
     cols = DV // n_mp
     small = fetch([state.at[:, :DV]], [vec_ref], sems, n)
-    copies = fetch(pieces, scratch, sems)
+    copies = fetch_parts(pieces, plan, scratch, sems)
     for k in range(n_mp):
         attn[m ^ k] = attn_in[k][...]
     for copy in small:
@@ -351,12 +365,12 @@
     hidden = scratch[0].shape[1]
     pre = jnp.zeros((rows, hidden), F32)
     fw = jnp.zeros((2, hidden), F32)
-    for i, (k, lo, size) in enumerate(plan):
-        copies[i].wait()
-        pre = pre + dot(blocks[e ^ k][:, lo : lo + size], scratch[i][:size, :])
-        if scratch[i].shape[0] > size:
-            parts = scratch[i][size : size + FW_ROWS, :].astype(F32)
-            fw = fw + (parts[0:2] + parts[2:4] + parts[4:6])
+    for i, (k, _) in enumerate(plan):
+        for copy in copies[i]:
+            copy.wait()
+        pre = pre + dot(blocks[e ^ k], scratch[i][:width, :])
+        parts = scratch[i][width : width + FW_ROWS, :].astype(F32)
+        fw = fw + (parts[0:2] + parts[2:4] + parts[4:6])
     sigma = 1.0 / (1.0 + jnp.exp(-pre))
     act = (pre * sigma).astype(BF16).astype(F32)
     first = (m == 0).astype(F32)
@@ -367,8 +381,8 @@
     chosen = jnp.where(meta_ref[:, 0:1] > 0.5, fw[1:2, :], fw[0:1, :])
     slope = (chosen * sigma * (1.0 + pre * (1.0 - sigma))).astype(BF16)
     moment = jnp.sum(slope.astype(F32) * pre, axis=-1, keepdims=True) / factor
-    for i, (k, lo, size) in enumerate(plan):
-        grads[e ^ k, :, lo : lo + size] = dot(slope, scratch[i][:size, :], NT)
+    for i, (k, _) in enumerate(plan):
+        grads[e ^ k] = dot(slope, scratch[i][:width, :], NT)
     scalars = pack_scalars([outcome[0], outcome[1], moment], rows)
     each = n_ev // n_mp
     for k in range(n_mp):
@@ -380,14 +394,14 @@
 def back_kernel(
     n_mp, n_ev, plan, where_ref, mid_ref, meta_ref, gain_ref, vgain_ref, head_ref, *refs
 ):
-    n = len(plan)
+    n, groups = sum(len(parts) for _, parts in plan), len(plan)
     pay_in, state, refs = refs[:n_mp], refs[n_mp], refs[n_mp + 1 :]
     pieces, refs = refs[:n], refs[n:]
     outs, outcome_ref, coef_ref, refs = refs[:n_mp], refs[n_mp], refs[n_mp + 1], refs[n_mp + 2 :]
-    scratch, refs = refs[:n], refs[n:]
+    scratch, refs = refs[:groups], refs[groups:]
     kept, grads, table, sems = refs
     (stored,) = fetch([state], [kept], sems, n)
-    copies = fetch(pieces, scratch, sems)
+    copies = fetch_parts(pieces, plan, scratch, sems)
     e, m = where_ref[0], where_ref[1]
     rows = mid_ref.shape[0]
     cols = DV // n_mp
@@ -423,12 +437,13 @@
         three[1].append(dot(grad_s, queries[:, span], TN).astype(BF16))
         three[2].append(dot(prob.astype(BF16), grad_c[:, span], TN).astype(BF16))
     three = [jnp.concatenate(parts, axis=1) for parts in three]
-    for i, (k, lo, size) in enumerate(plan):
-        copies[i].wait()
-        part = dot(three[0], scratch[i][0, :size, :], NT)
-        part = part + dot(three[1], scratch[i][1, :size, :], NT)
-        part = part + dot(three[2], scratch[i][2, :size, :], NT)
-        grads[e ^ k, :, lo : lo + size] = part
+    for i, (k, _) in enumerate(plan):
+        for copy in copies[i]:
+            copy.wait()
+        part = dot(three[0], scratch[i][0], NT)
+        part = part + dot(three[1], scratch[i][1], NT)
+        part = part + dot(three[2], scratch[i][2], NT)
+        grads[e ^ k] = part
     width = DV // n_ev
     vec = kept[:, :DV]
     spread = rms_factor(vec)
@@ -558,17 +573,27 @@
     return [swap(piece, "events", n_ev, 1) for piece in pieces]
 
 
-def direct_plan(n_ev, width):
-    order = range(n_ev) if n_ev != 8 else (0, 2, 4, 6, 1, 3, 5, 7)
-    return [(k, 0, width) for k in order]
-
-
-def hop_plan(n_ev, width):
+def hop_places(n_ev, width):
     if n_ev != 8:
-        return direct_plan(n_ev, width)
-    half = width // 2
-    near = [(0, 0, width), (2, 0, width), (4, 0, width), (6, 0, half), (6, half, half)]
-    return near + [(k ^ 1, lo, size) for k, lo, size in near]
+        return [(k, 0) for k in range(n_ev)]
+    near = [(0, 0), (2, 0), (4, 0), (6, 0), (6, width // 2)]
+    return near + [(k ^ 1, first) for k, first in near]
+
+
+def grouped(places, pieces, row_axis):
+    plan = {}
+    for i, (k, first) in enumerate(places):
+        plan.setdefault(k, []).append((i, first, pieces[i].shape[row_axis]))
+    return list(plan.items())
+
+
+def room(plan, piece, row_axis):
+    shapes = []
+    for _, parts in plan:
+        shape = list(piece.shape)
+        shape[row_axis] = max(first + rows for _, first, rows in parts)
+        shapes.append(pltpu.VMEM(tuple(shape), BF16))
+    return shapes
 
 
 def event_order(n_ev):
@@ -668,8 +693,6 @@
         cost_estimate=cost(30),
         name="fold",
     )(ffn_out, heads, after(ffn_in, *ready))
-    qkv_plan = hop_plan(n_ev, width)
-    ffn_plan = hop_plan(n_ev, width)
     gate = [got]
     if two_hops:
         qkv_second = second_hop(*qkv_halves, n_ev)
@@ -709,7 +732,8 @@
         vecs[0] = after(vec, *ffn_far[1:])
     else:
         qkv_pieces = qkv_first
-    n_q = len(qkv_plan)
+    n_q = len(qkv_pieces)
+    qkv_plan = grouped(hop_places(n_ev, width), qkv_pieces, 1)
     vgain = visit_gain.reshape(1, DV)
     state_shape = (group, state_spans(cols)[2][1])
     attended, state = pl.pallas_call(
@@ -720,7 +744,7 @@
         ],
         in_specs=[smem()] + [vmem()] * (n_mp + 3) + [hbm()] * n_q,
         out_specs=[vmem(), hbm()],
-        scratch_shapes=[pltpu.VMEM(piece.shape, BF16) for piece in qkv_pieces]
+        scratch_shapes=room(qkv_plan, visit_qkv, 1)
         + [
             pltpu.VMEM((n_mp, VPAD, DV), BF16),
             pltpu.VMEM((n_ev, group, width), BF16),
@@ -739,7 +763,8 @@
         ffn_pieces = ffn_first + ffn_second + ffn_far + across(ffn_second, n_ev)
     else:
         ffn_pieces = ffn_first
-    n_f = len(ffn_plan)
+    n_f = len(ffn_pieces)
+    ffn_plan = grouped(hop_places(n_ev, width), ffn_pieces, 0)
     fgain = ffn_gain.reshape(1, DV)
     ffn_outs = pl.pallas_call(
         functools.partial(ffn_kernel, n_mp, n_ev, ffn_plan),
@@ -747,7 +772,7 @@
         + [jax.ShapeDtypeStruct((group, cols + LANES), F32)],
         in_specs=[smem()] * 2 + [vmem()] * (3 + n_mp) + [hbm()] * (1 + n_f),
         out_specs=[vmem()] * (n_mp + 1),
-        scratch_shapes=[pltpu.VMEM(piece.shape, BF16) for piece in ffn_pieces]
+        scratch_shapes=room(ffn_plan, ffn_shard, 0)
         + [
             pltpu.VMEM((n_mp, group, cols), BF16),
             pltpu.VMEM((group, DV), F32),
@@ -768,7 +793,7 @@
         + [jax.ShapeDtypeStruct((group, LANES), F32), jax.ShapeDtypeStruct((VPAD, D), F32)],
         in_specs=[smem()] + [vmem()] * (5 + n_mp) + [hbm()] * (1 + n_q),
         out_specs=[vmem()] * (n_mp + 2),
-        scratch_shapes=[pltpu.VMEM(piece.shape, BF16) for piece in qkv_pieces]
+        scratch_shapes=room(qkv_plan, visit_qkv, 1)
         + [
             pltpu.VMEM(state_shape, F32),
             pltpu.VMEM((n_ev, group, width), F32),

time: 137 us -> 136 us (level)
  transfers between devices with their start and end apart: 38 -> 38, of which waited for: 19 -> 20; matrix products, arithmetic and copies ran while one was open for 2% -> 2% of each run, Pallas kernels for 17% -> 17%
where the time goes in v6:
time: 136 us
  waiting for transfers between devices  49 us (36%)
  starting transfers between devices  39.5 us (29%)
  Pallas kernels  38.6 us (28%)
  local copies, waits for them, and re-layouts  5.97 us (4%)
  other arithmetic  1.85 us (1%)
    ppermute x37, waiting for transfers between devices, swap(): return lax.ppermute(x, axis, [(i, i ^ k) for i in range(size)])  49 us
    ppermute x37, starting transfers between devices, swap(): return lax.ppermute(x, axis, [(i, i ^ k) for i in range(size)])  35 us
    pallas_call x1, Pallas kernels, local(): pl.pallas_call(functools.partial(encode_kernel, visits_dev), out_shape=ja...  12.5 us
    pallas_call x1, Pallas kernels, local(): pl.pallas_call(functools.partial(back_kernel, n_mp, n_ev, qkv_plan), out_...  7.46 us
    pallas_call x1, Pallas kernels, local(): pl.pallas_call(functools.partial(ffn_kernel, n_mp, n_ev, ffn_plan), out_s...  6.39 us
    unnamed x53, local copies, waits for them, and re-layouts  5.16 us
    all_to_all x1, starting transfers between devices, local(): lax.all_to_all(send.reshape(n_ev, rows_dev // n_ev, D + LANES), 'events',...  4.45 us
    pallas_call x1, Pallas kernels, local(): pl.pallas_call(functools.partial(project_kernel, n_mp, n_ev, qkv_plan), o...  3.76 us
  transfers between devices with their start and end apart: 38, of which 20 were waited for; matrix products, arithmetic and copies ran while one was open for 2% of the time, Pallas kernels for 17%

profile of v6, /device:TPU:0, one launch (start us, length us, event | category | flops | bytes accessed | tf_op | source)
XLA Modules:
  0.0 136.1 jit_solution(2425524431639202145)
XLA Ops:
  0.6 3.0 %collective-permute-start.1 = (bf16[3,256,512]{2,1,0:T(8,128)(2,1)}, bf16[3,256,512]{2,1,0:T(8,128)(2,1)S(1)}, u32[]{:S(2)}, u32[]{:S(2)}) collective-permute-start(bf16[3,256,512]{2,1,0:T(8,128)(2,1)} %refs_5_.1), channel_id=1, source_target_pairs={{0,16},{4,20},{8,24},{12,28},{16,0},{20,4},{24,8},{28,12},{1,17},{... | collective-permute-start | bytes 2359304 | tf_op jit(solution)/shard_map/ppermute | solution.py:502
  3.7 1.5 %collective-permute-start = (bf16[3,256,512]{2,1,0:T(8,128)(2,1)}, bf16[3,256,512]{2,1,0:T(8,128)(2,1)S(1)}, u32[]{:S(2)}, u32[]{:S(2)}) collective-permute-start(bf16[3,256,512]{2,1,0:T(8,128)(2,1)} %refs_5_.1), channel_id=1, source_target_pairs={{0,8},{4,12},{8,0},{12,4},{16,24},{20,28},{24,16},{28,20},{1,9},{5... | collective-permute-start | bytes 2359304 | tf_op jit(solution)/shard_map/ppermute | solution.py:502
  5.2 1.4 %copy-done.3 = bf16[768,1024]{1,0:T(8,128)(2,1)S(1)} copy-done((bf16[768,1024]{1,0:T(8,128)(2,1)S(1)}, bf16[768,1024]{1,0:T(8,128)(2,1)}, u32[]{:S(2)}) %copy-start.3) | copy-done | bytes 1572888
  6.6 0.7 copy-done.8
  7.3 3.7 %pack.1 = bf16[768,1152]{1,0:T(8,128)(2,1)} custom-call(s32[2]{0:T(128)S(1)} %pad_add_fusion.where_ref, s32[6,128]{1,0:T(8,128)S(1)} %bitcast.29, bf16[768,1024]{1,0:T(8,128)(2,1)S(1)} %copy-done.3), custom_call_target="tpu_custom_call" | custom-call | flops 1 | bytes 1 | tf_op jit(solution)/shard_map/pack/pallas_call | solution.py:641
  11.2 4.5 %all-to-all-start = ((bf16[8,96,1152]{2,1,0:T(8,128)(2,1)}), bf16[8,96,1152]{2,1,0:T(8,128)(2,1)}, u32[]{:S(2)}, u32[]{:S(2)}) async-start(bf16[8,96,1152]{2,1,0:T(8,128)(2,1)} %bitcast.6), calls=%async_computation | async-start | bytes 3538944 | tf_op jit(solution)/shard_map/all_to_all | solution.py:651
  15.6 0.6 prep.1
  16.3 6.0 %collective-permute-done.1.high_ref.refs_9_.refs_7_ = bf16[3,256,512]{2,1,0:T(8,128)(2,1)S(1)} collective-permute-done((bf16[3,256,512]{2,1,0:T(8,128)(2,1)}, bf16[3,256,512]{2,1,0:T(8,128)(2,1)S(1)}, u32[]{:S(2)}, u32[]{:S(2)}) %collective-permute-start.1) | collective-permute-done | bytes 786464 | tf_op jit(solution)/shard_map/ppermute | solution.py:502
  22.2 2.1 %collective-permute-done.low_ref.refs_8_.refs_6_ = bf16[3,256,512]{2,1,0:T(8,128)(2,1)S(1)} collective-permute-done((bf16[3,256,512]{2,1,0:T(8,128)(2,1)}, bf16[3,256,512]{2,1,0:T(8,128)(2,1)S(1)}, u32[]{:S(2)}, u32[]{:S(2)}) %collective-permute-start) | collective-permute-done | bytes 786464 | tf_op jit(solution)/shard_map/ppermute | solution.py:502
  24.4 0.1 select_n.16
  24.5 0.1 pad.3.clone
  24.6 0.8 subtract_convert_fusion
  25.4 0.8 compare_convert_fusion.pick
  26.3 0.5 split.1
  26.8 0.5 collective-permute-start.6
  27.4 2.9 %collective-permute-start.8 = (bf16[3,128,512]{2,1,0:T(8,128)(2,1)S(1)}, bf16[3,128,512]{2,1,0:T(8,128)(2,1)}, u32[]{:S(2)}, u32[]{:S(2)}) collective-permute-start(bf16[3,128,512]{2,1,0:T(8,128)(2,1)S(1)} %get-tuple-element.33), channel_id=1, source_target_pairs={{0,8},{4,12},{8,0},{12,4},{16,24},{20,28},{24,16},{28,20},{1,9},{5... | collective-permute-start | bytes 1179656 | tf_op jit(solution)/shard_map/ppermute | solution.py:502
  30.3 1.5 %copy-done.19 = bf16[256,2048]{1,0:T(8,128)(2,1)S(1)} copy-done((bf16[256,2048]{1,0:T(8,128)(2,1)S(1)}, bf16[256,2048]{1,0:T(8,128)(2,1)}, u32[]{:S(2)}) %copy-start.19) | copy-done | bytes 1048600
  31.8 1.4 %fold.1.refs_5_ = bf16[272,2048]{1,0:T(8,128)(2,1)} custom-call(bf16[2048,256]{1,0:T(8,128)(2,1)S(1)} %copy-done.18, bf16[8,256]{1,0:T(8,128)(2,1)S(1)} %maximum_maximum_fusion.head_ref, bf16[256,2048]{1,0:T(8,128)(2,1)S(1)} %copy-done.19), custom_call_target="tpu_custom_call" | custom-call | flops 30000001024 | bytes 30000000 | tf_op jit(solution)/shard_map/fold/pallas_call | solution.py:687
  33.2 15.6 %collective-permute-done.6.refs_10_.refs_8_ = bf16[3,128,512]{2,1,0:T(8,128)(2,1)S(1)} collective-permute-done((bf16[3,128,512]{2,1,0:T(8,128)(2,1)S(1)}, bf16[3,128,512]{2,1,0:T(8,128)(2,1)S(1)}, u32[]{:S(2)}, u32[]{:S(2)}) %collective-permute-start.6) | collective-permute-done | bytes 393248 | tf_op jit(solution)/shard_map/ppermute | solution.py:502
  48.8 1.7 %collective-permute-done.8.refs_11_.refs_9_ = bf16[3,128,512]{2,1,0:T(8,128)(2,1)} collective-permute-done((bf16[3,128,512]{2,1,0:T(8,128)(2,1)S(1)}, bf16[3,128,512]{2,1,0:T(8,128)(2,1)}, u32[]{:S(2)}, u32[]{:S(2)}) %collective-permute-start.8) | collective-permute-done | bytes 393248 | tf_op jit(solution)/shard_map/ppermute | solution.py:502
  50.5 0.4 collective-permute-start.15
  50.8 1.6 %collective-permute-start.10 = (bf16[272,2048]{1,0:T(8,128)(2,1)}, bf16[272,2048]{1,0:T(8,128)(2,1)S(1)}, u32[]{:S(2)}, u32[]{:S(2)}) collective-permute-start(bf16[272,2048]{1,0:T(8,128)(2,1)} %fold.1.refs_5_), channel_id=1, source_target_pairs={{0,8},{4,12},{8,0},{12,4},{16,24},{20,28},{24,16},{28,20},{1,9},{5... | collective-permute-start | bytes 3342344 | tf_op jit(solution)/shard_map/ppermute | solution.py:502
  52.5 0.5 collective-permute-start.9
  53.0 1.7 %collective-permute-done.7.refs_15_.refs_13_ = bf16[3,128,512]{2,1,0:T(8,128)(2,1)S(1)} collective-permute-done((bf16[3,128,512]{2,1,0:T(8,128)(2,1)S(1)}, bf16[3,128,512]{2,1,0:T(8,128)(2,1)S(1)}, u32[]{:S(2)}, u32[]{:S(2)}) %collective-permute-start.7) | collective-permute-done | bytes 393248 | tf_op jit(solution)/shard_map/ppermute | solution.py:502
  54.7 0.2 collective-permute-done.9.refs_16_.refs_14_
  55.0 0.7 copy-done.12
  55.6 0.7 copy-done.15
  56.3 12.5 %encode.1.refs_0_ = bf16[8,2048]{1,0:T(8,128)(2,1)S(1)} custom-call(s32[6]{0:T(128)S(1)} %copy-done.15, f32[1,1024]{1,0:T(1,128)S(1)} %bitcast.30, bf16[768,1152]{1,0:T(8,128)(2,1)} %bitcast.7.got_hbm, bf16[1024,3072]{1,0:T(8,128)(2,1)} %qkv_ref.1, bf16[1024,1024]{1,0:T(8,128)(2,1)} %proj_ref.1), custom_call_target="tpu_custom_call" | custom-call | flops 1 | bytes 1 | tf_op jit(solution)/shard_map/encode/pallas_call | solution.py:705
  68.9 3.7 %collective-permute-start.13 = (bf16[8,2048]{1,0:T(8,128)(2,1)S(1)}, bf16[8,2048]{1,0:T(8,128)(2,1)S(1)}, u32[]{:S(2)}, u32[]{:S(2)}) collective-permute-start(bf16[8,2048]{1,0:T(8,128)(2,1)S(1)} %encode.1.refs_0_), channel_id=1, source_target_pairs={{0,3},{1,2},{2,1},{3,0},{4,7},{5,6},{6,5},{7,4},{8,11},{9,10},{10,... | collective-permute-start | bytes 98312 | tf_op jit(solution)/shard_map/ppermute | solution.py:502
  72.5 0.8 collective-permute-start.11
  73.3 2.5 %collective-permute-done.15.high_ref.refs_7_ = bf16[272,2048]{1,0:T(8,128)(2,1)S(1)} collective-permute-done((bf16[272,2048]{1,0:T(8,128)(2,1)}, bf16[272,2048]{1,0:T(8,128)(2,1)S(1)}, u32[]{:S(2)}, u32[]{:S(2)}) %collective-permute-start.15) | collective-permute-done | bytes 1114144 | tf_op jit(solution)/shard_map/ppermute | solution.py:502
  75.8 1.6 %collective-permute-done.12.refs_2_ = bf16[8,2048]{1,0:T(8,128)(2,1)S(1)} collective-permute-done((bf16[8,2048]{1,0:T(8,128)(2,1)S(1)}, bf16[8,2048]{1,0:T(8,128)(2,1)S(1)}, u32[]{:S(2)}, u32[]{:S(2)}) %collective-permute-start.12) | collective-permute-done | bytes 32800 | tf_op jit(solution)/shard_map/ppermute | solution.py:502
  77.4 0.5 collective-permute-start.14
  77.9 0.6 collective-permute-start.21
  78.6 1.5 %collective-permute-start.20 = (bf16[128,2048]{1,0:T(8,128)(2,1)S(1)}, bf16[128,2048]{1,0:T(8,128)(2,1)S(1)}, u32[]{:S(2)}, u32[]{:S(2)}) collective-permute-start(bf16[128,2048]{1,0:T(8,128)(2,1)S(1)} %get-tuple-element.42), channel_id=1, source_target_pairs={{0,16},{4,20},{8,24},{12,28},{16,0},{20,4},{24,8},{28,12},{1,17},{... | collective-permute-start | bytes 1572872 | tf_op jit(solution)/shard_map/ppermute | solution.py:502
  80.1 1.6 %collective-permute-done.14.refs_11_ = bf16[272,2048]{1,0:T(8,128)(2,1)S(1)} collective-permute-done((bf16[272,2048]{1,0:T(8,128)(2,1)S(1)}, bf16[272,2048]{1,0:T(8,128)(2,1)S(1)}, u32[]{:S(2)}, u32[]{:S(2)}) %collective-permute-start.14) | collective-permute-done | bytes 1114144 | tf_op jit(solution)/shard_map/ppermute | solution.py:502
  81.8 3.8 %project.1 = (bf16[32,512]{1,0:T(8,128)(2,1)S(1)}, f32[32,3712]{1,0:T(8,128)S(1)}) custom-call(s32[2]{0:T(128)S(1)} %copy-done.11, bf16[8,2048]{1,0:T(8,128)(2,1)S(1)} %encode.1.refs_0_, bf16[8,2048]{1,0:T(8,128)(2,1)S(1)} %collective-permute-done.11.refs_1_, bf16[8,2048]{1,0:T(8,128)(2,1)S(1)} %collective-permute-done.12.refs_2_, ...), custom_call_target="tpu_custom_call" | custom-call | flops 1 | bytes 1 | tf_op jit(solution)/shard_map/project/pallas_call | solution.py:739
  85.6 2.2 %collective-permute-start.19 = (bf16[32,512]{1,0:T(8,128)(2,1)S(1)}, bf16[32,512]{1,0:T(8,128)(2,1)S(1)}, u32[]{:S(2)}, u32[]{:S(2)}) collective-permute-start(bf16[32,512]{1,0:T(8,128)(2,1)S(1)} %get-tuple-element.40.refs_0_), channel_id=1, source_target_pairs={{0,3},{1,2},{2,1},{3,0},{4,7},{5,6},{6,5},{7,4},{8,11},{9,10},{10,... | collective-permute-start | bytes 98312 | tf_op jit(solution)/shard_map/ppermute | solution.py:502
  87.8 2.3 %collective-permute-start.17 = (bf16[32,512]{1,0:T(8,128)(2,1)S(1)}, bf16[32,512]{1,0:T(8,128)(2,1)S(1)}, u32[]{:S(2)}, u32[]{:S(2)}) collective-permute-start(bf16[32,512]{1,0:T(8,128)(2,1)S(1)} %get-tuple-element.40.refs_0_), channel_id=1, source_target_pairs={{0,1},{1,0},{2,3},{3,2},{4,5},{5,4},{6,7},{7,6},{8,9},{9,8},{10,11... | collective-permute-start | bytes 98312 | tf_op jit(solution)/shard_map/ppermute | solution.py:502
  90.0 3.3 %collective-permute-done.21.refs_9_ = bf16[144,2048]{1,0:T(8,128)(2,1)S(1)} collective-permute-done((bf16[144,2048]{1,0:T(8,128)(2,1)S(1)}, bf16[144,2048]{1,0:T(8,128)(2,1)S(1)}, u32[]{:S(2)}, u32[]{:S(2)}) %collective-permute-start.21) | collective-permute-done | bytes 589856 | tf_op jit(solution)/shard_map/ppermute | solution.py:502
  93.4 0.5 collective-permute-start.22
  93.9 2.2 %collective-permute-done.22.refs_13_ = bf16[128,2048]{1,0:T(8,128)(2,1)S(1)} collective-permute-done((bf16[128,2048]{1,0:T(8,128)(2,1)S(1)}, bf16[128,2048]{1,0:T(8,128)(2,1)S(1)}, u32[]{:S(2)}, u32[]{:S(2)}) %collective-permute-start.22) | collective-permute-done | bytes 524320 | tf_op jit(solution)/shard_map/ppermute | solution.py:502
  96.2 6.4 %ffn.1 = (bf16[32,640]{1,0:T(8,128)(2,1)S(1)}, bf16[32,640]{1,0:T(8,128)(2,1)S(1)}, bf16[32,640]{1,0:T(8,128)(2,1)S(1)}, bf16[32,640]{1,0:T(8,128)(2,1)S(1)}, f32[32,640]{1,0:T(8,128)S(1)}) custom-call(s32[2]{0:T(128)S(1)} %copy-done.11, f32[2]{0:T(128)S(1)} %copy-done.17, f32[1,2048]{1,0:T(1,128)S(1)} %bitcast.27, ...), custom_call_target="tpu_custom_call" | custom-call | flops 1 | bytes 1 | tf_op jit(solution)/shard_map/ffn/pallas_call | solution.py:769
  102.6 0.6 collective-permute-start.24
  103.2 2.2 %collective-permute-start.25 = (bf16[32,640]{1,0:T(8,128)(2,1)S(1)}, bf16[32,640]{1,0:T(8,128)(2,1)S(1)}, u32[]{:S(2)}, u32[]{:S(2)}) collective-permute-start(bf16[32,640]{1,0:T(8,128)(2,1)S(1)} %get-tuple-element.49), channel_id=1, source_target_pairs={{0,2},{1,3},{2,0},{3,1},{4,6},{5,7},{6,4},{7,5},{8,10},{9,11},{10,... | collective-permute-start | bytes 122888 | tf_op jit(solution)/shard_map/ppermute | solution.py:502
  105.4 1.6 %collective-permute-start.26 = (bf16[32,640]{1,0:T(8,128)(2,1)S(1)}, bf16[32,640]{1,0:T(8,128)(2,1)S(1)}, u32[]{:S(2)}, u32[]{:S(2)}) collective-permute-start(bf16[32,640]{1,0:T(8,128)(2,1)S(1)} %get-tuple-element.50), channel_id=1, source_target_pairs={{0,3},{1,2},{2,1},{3,0},{4,7},{5,6},{6,5},{7,4},{8,11},{9,10},{10,... | collective-permute-start | bytes 122888 | tf_op jit(solution)/shard_map/ppermute | solution.py:502
  107.1 1.4 %collective-permute-done.25.refs_2_ = bf16[32,640]{1,0:T(8,128)(2,1)S(1)} collective-permute-done((bf16[32,640]{1,0:T(8,128)(2,1)S(1)}, bf16[32,640]{1,0:T(8,128)(2,1)S(1)}, u32[]{:S(2)}, u32[]{:S(2)}) %collective-permute-start.25) | collective-permute-done | bytes 40992 | tf_op jit(solution)/shard_map/ppermute | solution.py:502
  108.5 2.7 %collective-permute-done.26.refs_3_ = bf16[32,640]{1,0:T(8,128)(2,1)S(1)} collective-permute-done((bf16[32,640]{1,0:T(8,128)(2,1)S(1)}, bf16[32,640]{1,0:T(8,128)(2,1)S(1)}, u32[]{:S(2)}, u32[]{:S(2)}) %collective-permute-start.26) | collective-permute-done | bytes 40992 | tf_op jit(solution)/shard_map/ppermute | solution.py:502
  111.2 7.5 %back.1 = (bf16[8,1152]{1,0:T(8,128)(2,1)S(1)}, bf16[8,1152]{1,0:T(8,128)(2,1)S(1)}, bf16[8,1152]{1,0:T(8,128)(2,1)S(1)}, bf16[8,1152]{1,0:T(8,128)(2,1)S(1)}, f...) custom-call(s32[2]{0:T(128)S(1)} %copy-done.11, f32[32,640]{1,0:T(8,128)S(1)} %get-tuple-element.46.mid_ref, ...), custom_call_target="tpu_custom_call" | custom-call | flops 1 | bytes 1 | tf_op jit(solution)/shard_map/back/pallas_call | solution.py:790
  118.7 2.3 %collective-permute-start.28 = (bf16[8,1152]{1,0:T(8,128)(2,1)S(1)}, bf16[8,1152]{1,0:T(8,128)(2,1)S(1)}, u32[]{:S(2)}, u32[]{:S(2)}) collective-permute-start(bf16[8,1152]{1,0:T(8,128)(2,1)S(1)} %get-tuple-element.56), channel_id=1, source_target_pairs={{0,2},{1,3},{2,0},{3,1},{4,6},{5,7},{6,4},{7,5},{8,10},{9,11},{10,... | collective-permute-start | bytes 55304 | tf_op jit(solution)/shard_map/ppermute | solution.py:502
  121.0 2.1 %collective-permute-start.29 = (bf16[8,1152]{1,0:T(8,128)(2,1)S(1)}, bf16[8,1152]{1,0:T(8,128)(2,1)S(1)}, u32[]{:S(2)}, u32[]{:S(2)}) collective-permute-start(bf16[8,1152]{1,0:T(8,128)(2,1)S(1)} %get-tuple-element.57), channel_id=1, source_target_pairs={{0,3},{1,2},{2,1},{3,0},{4,7},{5,6},{6,5},{7,4},{8,11},{9,10},{10,... | collective-permute-start | bytes 55304 | tf_op jit(solution)/shard_map/ppermute | solution.py:502
  123.1 0.1 copy.21
  123.2 0.6 reshape.62
  123.9 2.7 %collective-permute-done.29.refs_3_ = bf16[8,1152]{1,0:T(8,128)(2,1)S(1)} collective-permute-done((bf16[8,1152]{1,0:T(8,128)(2,1)S(1)}, bf16[8,1152]{1,0:T(8,128)(2,1)S(1)}, u32[]{:S(2)}, u32[]{:S(2)}) %collective-permute-start.29) | collective-permute-done | bytes 18464 | tf_op jit(solution)/shard_map/ppermute | solution.py:502
  126.6 0.7 finish.1.refs_0_
  127.3 1.5 %collective-permute-start.32 = (f32[8,1024]{1,0:T(8,128)S(1)}, f32[8,1024]{1,0:T(8,128)S(1)}, u32[]{:S(2)}, u32[]{:S(2)}) collective-permute-start(f32[8,1024]{1,0:T(8,128)S(1)} %finish.1.refs_0_), channel_id=1, source_target_pairs={{0,24},{4,28},{8,16},{12,20},{16,8},{20,12},{24,0},{28,4},{1,25},{... | collective-permute-start | bytes 98312 | tf_op jit(solution)/shard_map/ppermute | solution.py:502
  128.8 0.6 collective-permute-start.31
  129.4 1.4 %collective-permute-start.30 = (f32[8,1024]{1,0:T(8,128)S(1)}, f32[8,1024]{1,0:T(8,128)S(1)}, u32[]{:S(2)}, u32[]{:S(2)}) collective-permute-start(f32[8,1024]{1,0:T(8,128)S(1)} %finish.1.refs_0_), channel_id=1, source_target_pairs={{0,8},{4,12},{8,0},{12,4},{16,24},{20,28},{24,16},{28,20},{1,9},{5... | collective-permute-start | bytes 98312 | tf_op jit(solution)/shard_map/ppermute | solution.py:502
  130.8 1.3 collective-permute-done.32.refs_3_
  132.1 0.6 collective-permute-done.31.refs_2_
  132.7 0.6 collective-permute-done.30.refs_1_
  133.3 0.6 collective-permute-done.35.refs_6_
  133.9 0.6 collective-permute-done.34.refs_5_
  134.5 1.4 %spread.1 = bf16[768,1024]{1,0:T(8,128)(2,1)} custom-call(bf16[768,64]{1,0:T(8,128)(2,1)S(1)} %copy-done.4, f32[8,1024]{1,0:T(8,128)S(1)} %finish.1.refs_0_, f32[8,1024]{1,0:T(8,128)S(1)} %collective-permute-done.30.refs_1_, f32[8,1024]{1,0:T(8,128)S(1)} %collective-permute-done.31.refs_2_, f32[8,1024]{1,0:T(8,128)S(1)} %collective-permute-done.32.refs_3_, ...), custom_call_target="tpu_custom_call" | custom-call | flops 1 | bytes 1 | tf_op jit(solution)/shard_map/spread/pallas_call | solution.py:820
  (88 shorter events, 0.7 us)
Async XLA Ops:
  0.6 21.6 %collective-permute-start.1 = (bf16[3,256,512]{2,1,0:T(8,128)(2,1)}, bf16[3,256,512]{2,1,0:T(8,128)(2,1)S(1)}, u32[]{:S(2)}, u32[]{:S(2)}) collective-permute-start(bf16[3,256,512]{2,1,0:T(8,128)(2,1)} %refs_5_.1), channel_id=1, source_target_pairs={{0,16},{4,20},{8,24},{12,28},{16,0},{20,4},{24,8},{28,12},{1,17},{... | collective-permute-start | bytes 2359304 | tf_op jit(solution)/shard_map/ppermute | solution.py:502
  3.7 20.7 %collective-permute-start = (bf16[3,256,512]{2,1,0:T(8,128)(2,1)}, bf16[3,256,512]{2,1,0:T(8,128)(2,1)S(1)}, u32[]{:S(2)}, u32[]{:S(2)}) collective-permute-start(bf16[3,256,512]{2,1,0:T(8,128)(2,1)} %refs_5_.1), channel_id=1, source_target_pairs={{0,8},{4,12},{8,0},{12,4},{16,24},{20,28},{24,16},{28,20},{1,9},{5... | collective-permute-start | bytes 2359304 | tf_op jit(solution)/shard_map/ppermute | solution.py:502
  5.2 25.1 %collective-permute-start.2 = (bf16[3,256,512]{2,1,0:T(8,128)(2,1)}, bf16[3,256,512]{2,1,0:T(8,128)(2,1)S(1)}, u32[]{:S(2)}, u32[]{:S(2)}) collective-permute-start(bf16[3,256,512]{2,1,0:T(8,128)(2,1)} %refs_5_.1), channel_id=1, source_target_pairs={{0,4},{4,0},{8,12},{12,8},{16,20},{20,16},{24,28},{28,24},{1,5},{5... | collective-permute-start | bytes 2359304 | tf_op jit(solution)/shard_map/ppermute | solution.py:502
  5.2 5.9 %copy-start.10 = (s32[2]{0:T(128)}, s32[2]{0:T(128)S(1)}, u32[]{:S(2)}) copy-start(s32[2]{0:T(128)S(1)} %pad_add_fusion.where_ref) | copy-start | bytes 28
  5.2 1.4 %copy-start.3 = (bf16[768,1024]{1,0:T(8,128)(2,1)S(1)}, bf16[768,1024]{1,0:T(8,128)(2,1)}, u32[]{:S(2)}) copy-start(bf16[768,1024]{1,0:T(8,128)(2,1)} %x_hbm.1) | copy-start | bytes 4718596
  6.6 0.7 copy-start.8
  11.1 4.5 %copy-start.20 = (s32[24]{0:T(128)S(1)}, s32[24]{0:T(128)}, u32[]{:S(2)}) copy-start(s32[24]{0:T(128)} %patient_ref.1) | copy-start | bytes 292
  11.1 4.5 %copy-start.21 = (s32[24]{0:T(128)S(1)}, s32[24]{0:T(128)}, u32[]{:S(2)}) copy-start(s32[24]{0:T(128)} %treat_ref.1) | copy-start | bytes 292
  11.1 4.5 %copy-start.22 = (f32[24]{0:T(128)S(1)}, f32[24]{0:T(128)}, u32[]{:S(2)}) copy-start(f32[24]{0:T(128)} %target_ref.1) | copy-start | bytes 292
  11.1 5.1 %copy-start.25 = (s32[8]{0:T(128)S(1)}, s32[8]{0:T(128)}, u32[]{:S(2)}) copy-start(s32[8]{0:T(128)} %constant.26.clone) | copy-start | bytes 100
  11.1 14.3 %copy-start.9 = (s32[768]{0:T(1024)S(1)}, s32[768]{0:T(1024)}, u32[]{:S(2)}) copy-start(s32[768]{0:T(1024)} %param.18) | copy-start | bytes 9220
  11.2 39.3 %all-to-all-start = ((bf16[8,96,1152]{2,1,0:T(8,128)(2,1)}), bf16[8,96,1152]{2,1,0:T(8,128)(2,1)}, u32[]{:S(2)}, u32[]{:S(2)}) async-start(bf16[8,96,1152]{2,1,0:T(8,128)(2,1)} %bitcast.6), calls=%async_computation | async-start | bytes 3538944 | tf_op jit(solution)/shard_map/all_to_all | solution.py:651
  16.2 10.6 %copy-start.13 = (f32[8,32]{1,0:T(8,128)}, f32[8,32]{1,0:T(8,128)S(1)}, u32[]{:S(2)}) copy-start(f32[8,32]{1,0:T(8,128)S(1)} %get-tuple-element.31.refs_6_) | copy-start | bytes 3076
  22.2 8.0 %collective-permute-start.4 = (bf16[3,256,512]{2,1,0:T(8,128)(2,1)S(1)}, bf16[3,256,512]{2,1,0:T(8,128)(2,1)}, u32[]{:S(2)}, u32[]{:S(2)}) collective-permute-start(bf16[3,256,512]{2,1,0:T(8,128)(2,1)S(1)} %collective-permute-done.1.high_ref.refs_9_.refs_7_), channel_id=1, source_target_pairs={{0,4},{4,0},{8,12},{12,8},{16,20},{20,16},{24,28},{28,24},{1,5},{5... | collective-permute-start | bytes 2359304 | tf_op jit(solution)/shard_map/ppermute | solution.py:502
  24.3 5.9 %collective-permute-start.3 = (bf16[3,256,512]{2,1,0:T(8,128)(2,1)S(1)}, bf16[3,256,512]{2,1,0:T(8,128)(2,1)S(1)}, u32[]{:S(2)}, u32[]{:S(2)}) collective-permute-start(bf16[3,256,512]{2,1,0:T(8,128)(2,1)S(1)} %collective-permute-done.low_ref.refs_8_.refs_6_), channel_id=1, source_target_pairs={{0,4},{4,0},{8,12},{12,8},{16,20},{20,16},{24,28},{28,24},{1,5},{5... | collective-permute-start | bytes 2359304 | tf_op jit(solution)/shard_map/ppermute | solution.py:502
  24.5 5.8 %copy-start.18 = (bf16[2048,256]{1,0:T(8,128)(2,1)S(1)}, bf16[2048,256]{1,0:T(8,128)(2,1)}, u32[]{:S(2)}) copy-start(bf16[2048,256]{1,0:T(8,128)(2,1)} %weight_ref.1) | copy-start | bytes 3145732
  26.8 22.0 %collective-permute-start.6 = (bf16[3,128,512]{2,1,0:T(8,128)(2,1)S(1)}, bf16[3,128,512]{2,1,0:T(8,128)(2,1)S(1)}, u32[]{:S(2)}, u32[]{:S(2)}) collective-permute-start(bf16[3,128,512]{2,1,0:T(8,128)(2,1)S(1)} %get-tuple-element.32), channel_id=1, source_target_pairs={{0,16},{4,20},{8,24},{12,28},{16,0},{20,4},{24,8},{28,12},{1,17},{... | collective-permute-start | bytes 1179656 | tf_op jit(solution)/shard_map/ppermute | solution.py:502
  27.4 23.1 %collective-permute-start.8 = (bf16[3,128,512]{2,1,0:T(8,128)(2,1)S(1)}, bf16[3,128,512]{2,1,0:T(8,128)(2,1)}, u32[]{:S(2)}, u32[]{:S(2)}) collective-permute-start(bf16[3,128,512]{2,1,0:T(8,128)(2,1)S(1)} %get-tuple-element.33), channel_id=1, source_target_pairs={{0,8},{4,12},{8,0},{12,4},{16,24},{20,28},{24,16},{28,20},{1,9},{5... | collective-permute-start | bytes 1179656 | tf_op jit(solution)/shard_map/ppermute | solution.py:502
  30.3 51.4 %copy-start.2 = (bf16[3,256,512]{2,1,0:T(8,128)(2,1)}, bf16[3,256,512]{2,1,0:T(8,128)(2,1)S(1)}, u32[]{:S(2)}) copy-start(bf16[3,256,512]{2,1,0:T(8,128)(2,1)S(1)} %collective-permute-done.3.refs_13_.refs_11_) | copy-start | bytes 2359300
  30.3 1.5 %copy-start.19 = (bf16[256,2048]{1,0:T(8,128)(2,1)S(1)}, bf16[256,2048]{1,0:T(8,128)(2,1)}, u32[]{:S(2)}) copy-start(bf16[256,2048]{1,0:T(8,128)(2,1)} %ffn_ref) | copy-start | bytes 3145732
  33.2 21.7 %collective-permute-start.5 = (bf16[272,2048]{1,0:T(8,128)(2,1)}, bf16[272,2048]{1,0:T(8,128)(2,1)}, u32[]{:S(2)}, u32[]{:S(2)}) collective-permute-start(bf16[272,2048]{1,0:T(8,128)(2,1)} %fold.1.refs_5_), channel_id=1, source_target_pairs={{0,4},{4,0},{8,12},{12,8},{16,20},{20,16},{24,28},{28,24},{1,5},{5... | collective-permute-start | bytes 3342344 | tf_op jit(solution)/shard_map/ppermute | solution.py:502
  50.5 25.3 %collective-permute-start.15 = (bf16[272,2048]{1,0:T(8,128)(2,1)}, bf16[272,2048]{1,0:T(8,128)(2,1)S(1)}, u32[]{:S(2)}, u32[]{:S(2)}) collective-permute-start(bf16[272,2048]{1,0:T(8,128)(2,1)} %fold.1.refs_5_), channel_id=1, source_target_pairs={{0,16},{4,20},{8,24},{12,28},{16,0},{20,4},{24,8},{28,12},{1,17},{... | collective-permute-start | bytes 3342344 | tf_op jit(solution)/shard_map/ppermute | solution.py:502
  50.8 26.5 %collective-permute-start.10 = (bf16[272,2048]{1,0:T(8,128)(2,1)}, bf16[272,2048]{1,0:T(8,128)(2,1)S(1)}, u32[]{:S(2)}, u32[]{:S(2)}) collective-permute-start(bf16[272,2048]{1,0:T(8,128)(2,1)} %fold.1.refs_5_), channel_id=1, source_target_pairs={{0,8},{4,12},{8,0},{12,4},{16,24},{20,28},{24,16},{28,20},{1,9},{5... | collective-permute-start | bytes 3342344 | tf_op jit(solution)/shard_map/ppermute | solution.py:502
  52.5 2.3 %collective-permute-start.7 = (bf16[3,128,512]{2,1,0:T(8,128)(2,1)S(1)}, bf16[3,128,512]{2,1,0:T(8,128)(2,1)S(1)}, u32[]{:S(2)}, u32[]{:S(2)}) collective-permute-start(bf16[3,128,512]{2,1,0:T(8,128)(2,1)S(1)} %collective-permute-done.6.refs_10_.refs_8_), channel_id=1, source_target_pairs={{0,4},{4,0},{8,12},{12,8},{16,20},{20,16},{24,28},{28,24},{1,5},{5... | collective-permute-start | bytes 1179656 | tf_op jit(solution)/shard_map/ppermute | solution.py:502
  52.5 2.5 %collective-permute-start.9 = (bf16[3,128,512]{2,1,0:T(8,128)(2,1)}, bf16[3,128,512]{2,1,0:T(8,128)(2,1)S(1)}, u32[]{:S(2)}, u32[]{:S(2)}) collective-permute-start(bf16[3,128,512]{2,1,0:T(8,128)(2,1)} %collective-permute-done.8.refs_11_.refs_9_), channel_id=1, source_target_pairs={{0,4},{4,0},{8,12},{12,8},{16,20},{20,16},{24,28},{28,24},{1,5},{5... | collective-permute-start | bytes 1179656 | tf_op jit(solution)/shard_map/ppermute | solution.py:502
  55.0 0.7 copy-start.12
  55.6 0.7 copy-start.15
  68.8 12.9 %copy-start.1 = (bf16[3,256,512]{2,1,0:T(8,128)(2,1)S(1)}, bf16[3,256,512]{2,1,0:T(8,128)(2,1)}, u32[]{:S(2)}) copy-start(bf16[3,256,512]{2,1,0:T(8,128)(2,1)} %refs_5_.1) | copy-start | bytes 2359300
  68.8 12.9 %copy-start.6 = (f32[2048]{0:T(1024)S(1)}, f32[2048]{0:T(1024)}, u32[]{:S(2)}) copy-start(f32[2048]{0:T(1024)} %param.26) | copy-start | bytes 24580
  68.8 12.9 %copy-start.11 = (s32[2]{0:T(128)S(1)}, s32[2]{0:T(128)}, u32[]{:S(2)}) copy-start(s32[2]{0:T(128)} %copy-done.10) | copy-start | bytes 28
  68.9 12.9 %copy-start.14 = (f32[8,32]{1,0:T(8,128)S(1)}, f32[8,32]{1,0:T(8,128)}, u32[]{:S(2)}) copy-start(f32[8,32]{1,0:T(8,128)} %copy-done.13) | copy-start | bytes 3076
  68.9 6.9 %collective-permute-start.13 = (bf16[8,2048]{1,0:T(8,128)(2,1)S(1)}, bf16[8,2048]{1,0:T(8,128)(2,1)S(1)}, u32[]{:S(2)}, u32[]{:S(2)}) collective-permute-start(bf16[8,2048]{1,0:T(8,128)(2,1)S(1)} %encode.1.refs_0_), channel_id=1, source_target_pairs={{0,3},{1,2},{2,1},{3,0},{4,7},{5,6},{6,5},{7,4},{8,11},{9,10},{10,... | collective-permute-start | bytes 98312 | tf_op jit(solution)/shard_map/ppermute | solution.py:502
  72.5 4.8 %collective-permute-start.12 = (bf16[8,2048]{1,0:T(8,128)(2,1)S(1)}, bf16[8,2048]{1,0:T(8,128)(2,1)S(1)}, u32[]{:S(2)}, u32[]{:S(2)}) collective-permute-start(bf16[8,2048]{1,0:T(8,128)(2,1)S(1)} %encode.1.refs_0_), channel_id=1, source_target_pairs={{0,2},{1,3},{2,0},{3,1},{4,6},{5,7},{6,4},{7,5},{8,10},{9,11},{10,... | collective-permute-start | bytes 98312 | tf_op jit(solution)/shard_map/ppermute | solution.py:502
  72.5 4.8 %collective-permute-start.11 = (bf16[8,2048]{1,0:T(8,128)(2,1)S(1)}, bf16[8,2048]{1,0:T(8,128)(2,1)S(1)}, u32[]{:S(2)}, u32[]{:S(2)}) collective-permute-start(bf16[8,2048]{1,0:T(8,128)(2,1)S(1)} %encode.1.refs_0_), channel_id=1, source_target_pairs={{0,1},{1,0},{2,3},{3,2},{4,5},{5,4},{6,7},{7,6},{8,9},{9,8},{10,11... | collective-permute-start | bytes 98312 | tf_op jit(solution)/shard_map/ppermute | solution.py:502
  75.8 9.8 %copy-start = (bf16[272,2048]{1,0:T(8,128)(2,1)}, bf16[272,2048]{1,0:T(8,128)(2,1)S(1)}, u32[]{:S(2)}) copy-start(bf16[272,2048]{1,0:T(8,128)(2,1)S(1)} %collective-permute-done.15.high_ref.refs_7_) | copy-start | bytes 3342340
  77.4 2.8 %collective-permute-start.16 = (bf16[272,2048]{1,0:T(8,128)(2,1)S(1)}, bf16[272,2048]{1,0:T(8,128)(2,1)S(1)}, u32[]{:S(2)}, u32[]{:S(2)}) collective-permute-start(bf16[272,2048]{1,0:T(8,128)(2,1)S(1)} %collective-permute-done.15.high_ref.refs_7_), channel_id=1, source_target_pairs={{0,4},{4,0},{8,12},{12,8},{16,20},{20,16},{24,28},{28,24},{1,5},{5... | collective-permute-start | bytes 3342344 | tf_op jit(solution)/shard_map/ppermute | solution.py:502
  77.4 4.3 %collective-permute-start.14 = (bf16[272,2048]{1,0:T(8,128)(2,1)S(1)}, bf16[272,2048]{1,0:T(8,128)(2,1)S(1)}, u32[]{:S(2)}, u32[]{:S(2)}) collective-permute-start(bf16[272,2048]{1,0:T(8,128)(2,1)S(1)} %collective-permute-done.10.low_ref.refs_6_), channel_id=1, source_target_pairs={{0,4},{4,0},{8,12},{12,8},{16,20},{20,16},{24,28},{28,24},{1,5},{5... | collective-permute-start | bytes 3342344 | tf_op jit(solution)/shard_map/ppermute | solution.py:502
  77.9 15.4 %collective-permute-start.21 = (bf16[144,2048]{1,0:T(8,128)(2,1)S(1)}, bf16[144,2048]{1,0:T(8,128)(2,1)S(1)}, u32[]{:S(2)}, u32[]{:S(2)}) collective-permute-start(bf16[144,2048]{1,0:T(8,128)(2,1)S(1)} %get-tuple-element.44), channel_id=1, source_target_pairs={{0,8},{4,12},{8,0},{12,4},{16,24},{20,28},{24,16},{28,20},{1,9},{5... | collective-permute-start | bytes 1769480 | tf_op jit(solution)/shard_map/ppermute | solution.py:502
  78.6 14.8 %collective-permute-start.20 = (bf16[128,2048]{1,0:T(8,128)(2,1)S(1)}, bf16[128,2048]{1,0:T(8,128)(2,1)S(1)}, u32[]{:S(2)}, u32[]{:S(2)}) collective-permute-start(bf16[128,2048]{1,0:T(8,128)(2,1)S(1)} %get-tuple-element.42), channel_id=1, source_target_pairs={{0,16},{4,20},{8,24},{12,28},{16,0},{20,4},{24,8},{28,12},{1,17},{... | collective-permute-start | bytes 1572872 | tf_op jit(solution)/shard_map/ppermute | solution.py:502
  80.1 5.4 %copy-start.23 = (bf16[272,2048]{1,0:T(8,128)(2,1)}, bf16[272,2048]{1,0:T(8,128)(2,1)S(1)}, u32[]{:S(2)}) copy-start(bf16[272,2048]{1,0:T(8,128)(2,1)S(1)} %collective-permute-done.16.refs_12_) | copy-start | bytes 3342340
  81.7 3.9 %copy-start.24 = (bf16[272,2048]{1,0:T(8,128)(2,1)}, bf16[272,2048]{1,0:T(8,128)(2,1)S(1)}, u32[]{:S(2)}) copy-start(bf16[272,2048]{1,0:T(8,128)(2,1)S(1)} %collective-permute-done.14.refs_11_) | copy-start | bytes 3342340
  81.7 14.4 %copy-start.5 = (f32[2048,2]{0,1:T(2,128)S(1)}, f32[2048,2]{0,1:T(2,128)}, u32[]{:S(2)}) copy-start(f32[2048,2]{0,1:T(2,128)} %param.31) | copy-start | bytes 49156
  81.8 14.4 %copy-start.7 = (f32[2048]{0:T(1024)S(1)}, f32[2048]{0:T(1024)}, u32[]{:S(2)}) copy-start(f32[2048]{0:T(1024)} %param.28) | copy-start | bytes 24580
  81.8 14.4 %copy-start.17 = (f32[2]{0:T(128)S(1)}, f32[2]{0:T(128)}, u32[]{:S(2)}) copy-start(f32[2]{0:T(128)} %bias_ref.1) | copy-start | bytes 28
  85.6 7.7 %collective-permute-start.19 = (bf16[32,512]{1,0:T(8,128)(2,1)S(1)}, bf16[32,512]{1,0:T(8,128)(2,1)S(1)}, u32[]{:S(2)}, u32[]{:S(2)}) collective-permute-start(bf16[32,512]{1,0:T(8,128)(2,1)S(1)} %get-tuple-element.40.refs_0_), channel_id=1, source_target_pairs={{0,3},{1,2},{2,1},{3,0},{4,7},{5,6},{6,5},{7,4},{8,11},{9,10},{10,... | collective-permute-start | bytes 98312 | tf_op jit(solution)/shard_map/ppermute | solution.py:502
  87.8 5.6 %collective-permute-start.18 = (bf16[32,512]{1,0:T(8,128)(2,1)S(1)}, bf16[32,512]{1,0:T(8,128)(2,1)S(1)}, u32[]{:S(2)}, u32[]{:S(2)}) collective-permute-start(bf16[32,512]{1,0:T(8,128)(2,1)S(1)} %get-tuple-element.40.refs_0_), channel_id=1, source_target_pairs={{0,2},{1,3},{2,0},{3,1},{4,6},{5,7},{6,4},{7,5},{8,10},{9,11},{10,... | collective-permute-start | bytes 98312 | tf_op jit(solution)/shard_map/ppermute | solution.py:502
  87.8 5.6 %collective-permute-start.17 = (bf16[32,512]{1,0:T(8,128)(2,1)S(1)}, bf16[32,512]{1,0:T(8,128)(2,1)S(1)}, u32[]{:S(2)}, u32[]{:S(2)}) collective-permute-start(bf16[32,512]{1,0:T(8,128)(2,1)S(1)} %get-tuple-element.40.refs_0_), channel_id=1, source_target_pairs={{0,1},{1,0},{2,3},{3,2},{4,5},{5,4},{6,7},{7,6},{8,9},{9,8},{10,11... | collective-permute-start | bytes 98312 | tf_op jit(solution)/shard_map/ppermute | solution.py:502
  93.3 2.8 %collective-permute-start.23 = (bf16[144,2048]{1,0:T(8,128)(2,1)S(1)}, bf16[144,2048]{1,0:T(8,128)(2,1)S(1)}, u32[]{:S(2)}, u32[]{:S(2)}) collective-permute-start(bf16[144,2048]{1,0:T(8,128)(2,1)S(1)} %collective-permute-done.21.refs_9_), channel_id=1, source_target_pairs={{0,4},{4,0},{8,12},{12,8},{16,20},{20,16},{24,28},{28,24},{1,5},{5... | collective-permute-start | bytes 1769480 | tf_op jit(solution)/shard_map/ppermute | solution.py:502
  93.4 2.7 %collective-permute-start.22 = (bf16[128,2048]{1,0:T(8,128)(2,1)S(1)}, bf16[128,2048]{1,0:T(8,128)(2,1)S(1)}, u32[]{:S(2)}, u32[]{:S(2)}) collective-permute-start(bf16[128,2048]{1,0:T(8,128)(2,1)S(1)} %collective-permute-done.20.refs_8_), channel_id=1, source_target_pairs={{0,4},{4,0},{8,12},{12,8},{16,20},{20,16},{24,28},{28,24},{1,5},{5... | collective-permute-start | bytes 1572872 | tf_op jit(solution)/shard_map/ppermute | solution.py:502
  102.6 4.5 %collective-permute-start.24 = (bf16[32,640]{1,0:T(8,128)(2,1)S(1)}, bf16[32,640]{1,0:T(8,128)(2,1)S(1)}, u32[]{:S(2)}, u32[]{:S(2)}) collective-permute-start(bf16[32,640]{1,0:T(8,128)(2,1)S(1)} %get-tuple-element.48), channel_id=1, source_target_pairs={{0,1},{1,0},{2,3},{3,2},{4,5},{5,4},{6,7},{7,6},{8,9},{9,8},{10,11... | collective-permute-start | bytes 122888 | tf_op jit(solution)/shard_map/ppermute | solution.py:502
  103.2 5.3 %collective-permute-start.25 = (bf16[32,640]{1,0:T(8,128)(2,1)S(1)}, bf16[32,640]{1,0:T(8,128)(2,1)S(1)}, u32[]{:S(2)}, u32[]{:S(2)}) collective-permute-start(bf16[32,640]{1,0:T(8,128)(2,1)S(1)} %get-tuple-element.49), channel_id=1, source_target_pairs={{0,2},{1,3},{2,0},{3,1},{4,6},{5,7},{6,4},{7,5},{8,10},{9,11},{10,... | collective-permute-start | bytes 122888 | tf_op jit(solution)/shard_map/ppermute | solution.py:502
  105.4 5.8 %collective-permute-start.26 = (bf16[32,640]{1,0:T(8,128)(2,1)S(1)}, bf16[32,640]{1,0:T(8,128)(2,1)S(1)}, u32[]{:S(2)}, u32[]{:S(2)}) collective-permute-start(bf16[32,640]{1,0:T(8,128)(2,1)S(1)} %get-tuple-element.50), channel_id=1, source_target_pairs={{0,3},{1,2},{2,1},{3,0},{4,7},{5,6},{6,5},{7,4},{8,11},{9,10},{10,... | collective-permute-start | bytes 122888 | tf_op jit(solution)/shard_map/ppermute | solution.py:502
  111.2 15.4 %copy-start.16 = (s32[6]{0:T(128)S(1)}, s32[6]{0:T(128)}, u32[]{:S(2)}) copy-start(s32[6]{0:T(128)} %count_ref.3) | copy-start | bytes 76
  111.2 23.3 %copy-start.4 = (bf16[768,64]{1,0:T(8,128)(2,1)S(1)}, bf16[768,64]{1,0:T(8,128)(2,1)}, u32[]{:S(2)}) copy-start(bf16[768,64]{1,0:T(8,128)(2,1)} %compare_convert_fusion.pick) | copy-start | bytes 294916
  118.7 5.2 %collective-permute-start.27 = (bf16[8,1152]{1,0:T(8,128)(2,1)S(1)}, bf16[8,1152]{1,0:T(8,128)(2,1)S(1)}, u32[]{:S(2)}, u32[]{:S(2)}) collective-permute-start(bf16[8,1152]{1,0:T(8,128)(2,1)S(1)} %get-tuple-element.55), channel_id=1, source_target_pairs={{0,1},{1,0},{2,3},{3,2},{4,5},{5,4},{6,7},{7,6},{8,9},{9,8},{10,11... | collective-permute-start | bytes 55304 | tf_op jit(solution)/shard_map/ppermute | solution.py:502
  118.7 5.1 %collective-permute-start.28 = (bf16[8,1152]{1,0:T(8,128)(2,1)S(1)}, bf16[8,1152]{1,0:T(8,128)(2,1)S(1)}, u32[]{:S(2)}, u32[]{:S(2)}) collective-permute-start(bf16[8,1152]{1,0:T(8,128)(2,1)S(1)} %get-tuple-element.56), channel_id=1, source_target_pairs={{0,2},{1,3},{2,0},{3,1},{4,6},{5,7},{6,4},{7,5},{8,10},{9,11},{10,... | collective-permute-start | bytes 55304 | tf_op jit(solution)/shard_map/ppermute | solution.py:502
  121.0 5.6 %collective-permute-start.29 = (bf16[8,1152]{1,0:T(8,128)(2,1)S(1)}, bf16[8,1152]{1,0:T(8,128)(2,1)S(1)}, u32[]{:S(2)}, u32[]{:S(2)}) collective-permute-start(bf16[8,1152]{1,0:T(8,128)(2,1)S(1)} %get-tuple-element.57), channel_id=1, source_target_pairs={{0,3},{1,2},{2,1},{3,0},{4,7},{5,6},{6,5},{7,4},{8,11},{9,10},{10,... | collective-permute-start | bytes 55304 | tf_op jit(solution)/shard_map/ppermute | solution.py:502
  127.3 4.8 %collective-permute-start.32 = (f32[8,1024]{1,0:T(8,128)S(1)}, f32[8,1024]{1,0:T(8,128)S(1)}, u32[]{:S(2)}, u32[]{:S(2)}) collective-permute-start(f32[8,1024]{1,0:T(8,128)S(1)} %finish.1.refs_0_), channel_id=1, source_target_pairs={{0,24},{4,28},{8,16},{12,20},{16,8},{20,12},{24,0},{28,4},{1,25},{... | collective-permute-start | bytes 98312 | tf_op jit(solution)/shard_map/ppermute | solution.py:502
  128.8 3.9 %collective-permute-start.31 = (f32[8,1024]{1,0:T(8,128)S(1)}, f32[8,1024]{1,0:T(8,128)S(1)}, u32[]{:S(2)}, u32[]{:S(2)}) collective-permute-start(f32[8,1024]{1,0:T(8,128)S(1)} %finish.1.refs_0_), channel_id=1, source_target_pairs={{0,16},{4,20},{8,24},{12,28},{16,0},{20,4},{24,8},{28,12},{1,17},{... | collective-permute-start | bytes 98312 | tf_op jit(solution)/shard_map/ppermute | solution.py:502
  129.4 3.9 %collective-permute-start.30 = (f32[8,1024]{1,0:T(8,128)S(1)}, f32[8,1024]{1,0:T(8,128)S(1)}, u32[]{:S(2)}, u32[]{:S(2)}) collective-permute-start(f32[8,1024]{1,0:T(8,128)S(1)} %finish.1.refs_0_), channel_id=1, source_target_pairs={{0,8},{4,12},{8,0},{12,4},{16,24},{20,28},{24,16},{28,20},{1,9},{5... | collective-permute-start | bytes 98312 | tf_op jit(solution)/shard_map/ppermute | solution.py:502
  130.8 2.5 %collective-permute-start.33 = (f32[8,1024]{1,0:T(8,128)S(1)}, f32[8,1024]{1,0:T(8,128)S(1)}, u32[]{:S(2)}, u32[]{:S(2)}) collective-permute-start(f32[8,1024]{1,0:T(8,128)S(1)} %finish.1.refs_0_), channel_id=1, source_target_pairs={{0,4},{4,0},{8,12},{12,8},{16,20},{20,16},{24,28},{28,24},{1,5},{5... | collective-permute-start | bytes 98312 | tf_op jit(solution)/shard_map/ppermute | solution.py:502
  132.1 1.2 collective-permute-start.36
  132.7 1.2 collective-permute-start.35
  133.3 1.2 collective-permute-start.34

commit v7 on v6

--- a/solution.py
+++ b/solution.py
@@ -133,7 +133,6 @@
 
 def encode_kernel(
     visits_dev,
-    count_ref,
     gain_ref,
     got_hbm,
     qkv_ref,
@@ -170,6 +169,7 @@
     hot_b = hot.astype(BF16)
     hot_f = hot.astype(F32)
     before = rank_before(hot_f)
+    counts = jnp.maximum(jnp.sum(hot_f, axis=1, keepdims=True), 1.0)
     base = (visits * VB + 1).astype(F32)
     position = (jnp.sum(hot_f * (base + before), axis=0, keepdims=True)).astype(jnp.int32) - 1
     inputs[1].wait()
@@ -197,10 +197,10 @@
     halves = ((lanes8 >= rows8 * VB) & (lanes8 < (rows8 + 1) * VB)).astype(BF16)
 
     def one_visit(v, carry):
-        count = count_ref[v]
+        count = counts[v : v + 1, :]
         at = slice(v * VB, (v + 1) * VB)
-        live_key = key_slot < count
-        weight = (query_slot < count).astype(F32) / count.astype(F32)
+        live_key = key_slot.astype(F32) < count
+        weight = (query_slot.astype(F32) < count).astype(F32) / count
         for p in range(HEADS // 2):
             q = qk[at, p * LANES : (p + 1) * LANES].astype(F32)
             k = qk[at, D + p * LANES : D + (p + 1) * LANES]
@@ -227,10 +227,7 @@
     head_part = attended.astype(BF16)
     rest = (attended - head_part.astype(F32)).astype(BF16)
     mixed = dot(head_part, wo[...]) + dot(rest, wo[...])
-    row = lax.broadcasted_iota(jnp.int32, (VPAD, 1), 0)
-    inverse = jnp.zeros((VPAD, 1), F32)
-    for v in range(visits_dev):
-        inverse = jnp.where(row == v, 1.0 / count_ref[v].astype(F32), inverse)
+    inverse = 1.0 / counts
     mean_input = sums * inverse
     vec_ref[:, :D] = (mean_input + mixed).astype(BF16)
     vec_ref[:, D:] = mean_input.astype(BF16)
@@ -705,7 +702,7 @@
     vec = pl.pallas_call(
         functools.partial(encode_kernel, visits_dev),
         out_shape=jax.ShapeDtypeStruct((VPAD, DV), BF16),
-        in_specs=[smem(), vmem(), hbm(), hbm(), hbm()],
+        in_specs=[vmem(), hbm(), hbm(), hbm()],
         out_specs=vmem(),
         scratch_shapes=[
             pltpu.VMEM((rows_dev, D + LANES), BF16),
@@ -721,7 +718,7 @@
         compiler_params=params(53),
         cost_estimate=cost(0),
         name="encode",
-    )(visit_count, enc_gain.reshape(1, D), got, enc_qkv, enc_out)
+    )(enc_gain.reshape(1, D), got, enc_qkv, enc_out)
 
     vecs = [vec] + [swap(vec, "mp", n_mp, k) for k in range(1, n_mp)]
     if two_hops:

time: 136 us -> 136 us (level)
    unnamed x53 -> x51, local copies, waits for them, and re-layouts: 5.16 us -> 4.51 us
  transfers between devices with their start and end apart: 38 -> 38, of which waited for: 20 -> 20; matrix products, arithmetic and copies ran while one was open for 2% -> 2% of each run, Pallas kernels for 17% -> 16%
where the time goes in v7:
time: 136 us
  waiting for transfers between devices  50.1 us (37%)
  starting transfers between devices  39.7 us (29%)
  Pallas kernels  38 us (28%)
  local copies, waits for them, and re-layouts  5.32 us (4%)
  other arithmetic  1.86 us (1%)
    ppermute x37, waiting for transfers between devices, swap(): return lax.ppermute(x, axis, [(i, i ^ k) for i in range(size)])  50.1 us
    ppermute x37, starting transfers between devices, swap(): return lax.ppermute(x, axis, [(i, i ^ k) for i in range(size)])  35.2 us
    pallas_call x1, Pallas kernels, local(): pl.pallas_call(functools.partial(encode_kernel, visits_dev), out_shape=ja...  12 us
    pallas_call x1, Pallas kernels, local(): pl.pallas_call(functools.partial(back_kernel, n_mp, n_ev, qkv_plan), out_...  7.46 us
    pallas_call x1, Pallas kernels, local(): pl.pallas_call(functools.partial(ffn_kernel, n_mp, n_ev, ffn_plan), out_s...  6.39 us
    unnamed x51, local copies, waits for them, and re-layouts  4.51 us
    all_to_all x1, starting transfers between devices, local(): lax.all_to_all(send.reshape(n_ev, rows_dev // n_ev, D + LANES), 'events',...  4.45 us
    pallas_call x1, Pallas kernels, local(): pl.pallas_call(functools.partial(project_kernel, n_mp, n_ev, qkv_plan), o...  3.76 us
  transfers between devices with their start and end apart: 38, of which 20 were waited for; matrix products, arithmetic and copies ran while one was open for 2% of the time, Pallas kernels for 16%

profile of v7, /device:TPU:0, one launch (start us, length us, event | category | flops | bytes accessed | tf_op | source)
XLA Modules:
  0.0 136.1 jit_solution(9211327124948543215)
XLA Ops:
  0.6 3.0 %collective-permute-start.1 = (bf16[3,256,512]{2,1,0:T(8,128)(2,1)}, bf16[3,256,512]{2,1,0:T(8,128)(2,1)S(1)}, u32[]{:S(2)}, u32[]{:S(2)}) collective-permute-start(bf16[3,256,512]{2,1,0:T(8,128)(2,1)} %refs_5_.1), channel_id=1, source_target_pairs={{0,16},{4,20},{8,24},{12,28},{16,0},{20,4},{24,8},{28,12},{1,17},{... | collective-permute-start | bytes 2359304 | tf_op jit(solution)/shard_map/ppermute | solution.py:499
  3.7 1.5 %collective-permute-start = (bf16[3,256,512]{2,1,0:T(8,128)(2,1)}, bf16[3,256,512]{2,1,0:T(8,128)(2,1)S(1)}, u32[]{:S(2)}, u32[]{:S(2)}) collective-permute-start(bf16[3,256,512]{2,1,0:T(8,128)(2,1)} %refs_5_.1), channel_id=1, source_target_pairs={{0,8},{4,12},{8,0},{12,4},{16,24},{20,28},{24,16},{28,20},{1,9},{5... | collective-permute-start | bytes 2359304 | tf_op jit(solution)/shard_map/ppermute | solution.py:499
  5.2 1.4 %copy-done.3 = bf16[768,1024]{1,0:T(8,128)(2,1)S(1)} copy-done((bf16[768,1024]{1,0:T(8,128)(2,1)S(1)}, bf16[768,1024]{1,0:T(8,128)(2,1)}, u32[]{:S(2)}) %copy-start.3) | copy-done | bytes 1572888
  6.6 0.7 copy-done.8
  7.3 3.7 %pack.1 = bf16[768,1152]{1,0:T(8,128)(2,1)} custom-call(s32[2]{0:T(128)S(1)} %pad_add_fusion.where_ref, s32[6,128]{1,0:T(8,128)S(1)} %bitcast.29, bf16[768,1024]{1,0:T(8,128)(2,1)S(1)} %copy-done.3), custom_call_target="tpu_custom_call" | custom-call | flops 1 | bytes 1 | tf_op jit(solution)/shard_map/pack/pallas_call | solution.py:638
  11.1 4.4 %all-to-all-start = ((bf16[8,96,1152]{2,1,0:T(8,128)(2,1)}), bf16[8,96,1152]{2,1,0:T(8,128)(2,1)}, u32[]{:S(2)}, u32[]{:S(2)}) async-start(bf16[8,96,1152]{2,1,0:T(8,128)(2,1)} %bitcast.6), calls=%async_computation | async-start | bytes 3538944 | tf_op jit(solution)/shard_map/all_to_all | solution.py:648
  15.6 0.6 prep.1
  16.3 6.0 %collective-permute-done.1.high_ref.refs_9_.refs_7_ = bf16[3,256,512]{2,1,0:T(8,128)(2,1)S(1)} collective-permute-done((bf16[3,256,512]{2,1,0:T(8,128)(2,1)}, bf16[3,256,512]{2,1,0:T(8,128)(2,1)S(1)}, u32[]{:S(2)}, u32[]{:S(2)}) %collective-permute-start.1) | collective-permute-done | bytes 786464 | tf_op jit(solution)/shard_map/ppermute | solution.py:499
  22.2 2.1 %collective-permute-done.low_ref.refs_8_.refs_6_ = bf16[3,256,512]{2,1,0:T(8,128)(2,1)S(1)} collective-permute-done((bf16[3,256,512]{2,1,0:T(8,128)(2,1)}, bf16[3,256,512]{2,1,0:T(8,128)(2,1)S(1)}, u32[]{:S(2)}, u32[]{:S(2)}) %collective-permute-start) | collective-permute-done | bytes 786464 | tf_op jit(solution)/shard_map/ppermute | solution.py:499
  24.4 0.1 select_n.16
  24.5 0.1 pad.3.clone
  24.6 0.8 subtract_convert_fusion
  25.4 0.8 compare_convert_fusion.pick
  26.3 0.5 split.1
  26.8 0.5 collective-permute-start.6
  27.4 2.9 %collective-permute-start.8 = (bf16[3,128,512]{2,1,0:T(8,128)(2,1)S(1)}, bf16[3,128,512]{2,1,0:T(8,128)(2,1)}, u32[]{:S(2)}, u32[]{:S(2)}) collective-permute-start(bf16[3,128,512]{2,1,0:T(8,128)(2,1)S(1)} %get-tuple-element.33), channel_id=1, source_target_pairs={{0,8},{4,12},{8,0},{12,4},{16,24},{20,28},{24,16},{28,20},{1,9},{5... | collective-permute-start | bytes 1179656 | tf_op jit(solution)/shard_map/ppermute | solution.py:499
  30.3 1.5 %copy-done.18 = bf16[256,2048]{1,0:T(8,128)(2,1)S(1)} copy-done((bf16[256,2048]{1,0:T(8,128)(2,1)S(1)}, bf16[256,2048]{1,0:T(8,128)(2,1)}, u32[]{:S(2)}) %copy-start.18) | copy-done | bytes 1048600
  31.8 1.4 %fold.1.refs_5_ = bf16[272,2048]{1,0:T(8,128)(2,1)} custom-call(bf16[2048,256]{1,0:T(8,128)(2,1)S(1)} %copy-done.17, bf16[8,256]{1,0:T(8,128)(2,1)S(1)} %maximum_maximum_fusion.head_ref, bf16[256,2048]{1,0:T(8,128)(2,1)S(1)} %copy-done.18), custom_call_target="tpu_custom_call" | custom-call | flops 30000001024 | bytes 30000000 | tf_op jit(solution)/shard_map/fold/pallas_call | solution.py:684
  33.2 15.6 %collective-permute-done.6.refs_10_.refs_8_ = bf16[3,128,512]{2,1,0:T(8,128)(2,1)S(1)} collective-permute-done((bf16[3,128,512]{2,1,0:T(8,128)(2,1)S(1)}, bf16[3,128,512]{2,1,0:T(8,128)(2,1)S(1)}, u32[]{:S(2)}, u32[]{:S(2)}) %collective-permute-start.6) | collective-permute-done | bytes 393248 | tf_op jit(solution)/shard_map/ppermute | solution.py:499
  48.8 1.7 %collective-permute-done.8.refs_11_.refs_9_ = bf16[3,128,512]{2,1,0:T(8,128)(2,1)} collective-permute-done((bf16[3,128,512]{2,1,0:T(8,128)(2,1)S(1)}, bf16[3,128,512]{2,1,0:T(8,128)(2,1)}, u32[]{:S(2)}, u32[]{:S(2)}) %collective-permute-start.8) | collective-permute-done | bytes 393248 | tf_op jit(solution)/shard_map/ppermute | solution.py:499
  50.5 0.4 collective-permute-start.15
  50.8 1.6 %collective-permute-start.10 = (bf16[272,2048]{1,0:T(8,128)(2,1)}, bf16[272,2048]{1,0:T(8,128)(2,1)S(1)}, u32[]{:S(2)}, u32[]{:S(2)}) collective-permute-start(bf16[272,2048]{1,0:T(8,128)(2,1)} %fold.1.refs_5_), channel_id=1, source_target_pairs={{0,8},{4,12},{8,0},{12,4},{16,24},{20,28},{24,16},{28,20},{1,9},{5... | collective-permute-start | bytes 3342344 | tf_op jit(solution)/shard_map/ppermute | solution.py:499
  52.5 0.5 collective-permute-start.9
  53.0 1.7 %collective-permute-done.7.refs_15_.refs_13_ = bf16[3,128,512]{2,1,0:T(8,128)(2,1)S(1)} collective-permute-done((bf16[3,128,512]{2,1,0:T(8,128)(2,1)S(1)}, bf16[3,128,512]{2,1,0:T(8,128)(2,1)S(1)}, u32[]{:S(2)}, u32[]{:S(2)}) %collective-permute-start.7) | collective-permute-done | bytes 393248 | tf_op jit(solution)/shard_map/ppermute | solution.py:499
  54.7 0.2 collective-permute-done.9.refs_16_.refs_14_
  55.0 0.7 copy-done.12
  55.6 12.0 %encode.1.refs_0_ = bf16[8,2048]{1,0:T(8,128)(2,1)S(1)} custom-call(f32[1,1024]{1,0:T(1,128)S(1)} %bitcast.30, bf16[768,1152]{1,0:T(8,128)(2,1)} %bitcast.7.got_hbm, bf16[1024,3072]{1,0:T(8,128)(2,1)} %qkv_ref.1, bf16[1024,1024]{1,0:T(8,128)(2,1)} %proj_ref.1), custom_call_target="tpu_custom_call" | custom-call | flops 1 | bytes 1 | tf_op jit(solution)/shard_map/encode/pallas_call | solution.py:702
  67.7 3.7 %collective-permute-start.13 = (bf16[8,2048]{1,0:T(8,128)(2,1)S(1)}, bf16[8,2048]{1,0:T(8,128)(2,1)S(1)}, u32[]{:S(2)}, u32[]{:S(2)}) collective-permute-start(bf16[8,2048]{1,0:T(8,128)(2,1)S(1)} %encode.1.refs_0_), channel_id=1, source_target_pairs={{0,3},{1,2},{2,1},{3,0},{4,7},{5,6},{6,5},{7,4},{8,11},{9,10},{10,... | collective-permute-start | bytes 98312 | tf_op jit(solution)/shard_map/ppermute | solution.py:499
  71.3 0.8 collective-permute-start.11
  72.1 3.7 %collective-permute-done.15.high_ref.refs_7_ = bf16[272,2048]{1,0:T(8,128)(2,1)S(1)} collective-permute-done((bf16[272,2048]{1,0:T(8,128)(2,1)}, bf16[272,2048]{1,0:T(8,128)(2,1)S(1)}, u32[]{:S(2)}, u32[]{:S(2)}) %collective-permute-start.15) | collective-permute-done | bytes 1114144 | tf_op jit(solution)/shard_map/ppermute | solution.py:499
  75.8 0.3 collective-permute-done.12.refs_2_
  76.2 0.5 collective-permute-start.14
  76.7 1.3 collective-permute-start.21
  78.0 1.1 collective-permute-start.20
  79.2 1.3 collective-permute-done.14.refs_11_
  80.6 3.8 %project.1 = (bf16[32,512]{1,0:T(8,128)(2,1)S(1)}, f32[32,3712]{1,0:T(8,128)S(1)}) custom-call(s32[2]{0:T(128)S(1)} %copy-done.11, bf16[8,2048]{1,0:T(8,128)(2,1)S(1)} %encode.1.refs_0_, bf16[8,2048]{1,0:T(8,128)(2,1)S(1)} %collective-permute-done.11.refs_1_, bf16[8,2048]{1,0:T(8,128)(2,1)S(1)} %collective-permute-done.12.refs_2_, ...), custom_call_target="tpu_custom_call" | custom-call | flops 1 | bytes 1 | tf_op jit(solution)/shard_map/project/pallas_call | solution.py:736
  84.4 3.4 %collective-permute-start.19 = (bf16[32,512]{1,0:T(8,128)(2,1)S(1)}, bf16[32,512]{1,0:T(8,128)(2,1)S(1)}, u32[]{:S(2)}, u32[]{:S(2)}) collective-permute-start(bf16[32,512]{1,0:T(8,128)(2,1)S(1)} %get-tuple-element.40.refs_0_), channel_id=1, source_target_pairs={{0,3},{1,2},{2,1},{3,0},{4,7},{5,6},{6,5},{7,4},{8,11},{9,10},{10,... | collective-permute-start | bytes 98312 | tf_op jit(solution)/shard_map/ppermute | solution.py:499
  87.8 1.1 collective-permute-start.17
  88.8 3.3 %collective-permute-done.21.refs_9_ = bf16[144,2048]{1,0:T(8,128)(2,1)S(1)} collective-permute-done((bf16[144,2048]{1,0:T(8,128)(2,1)S(1)}, bf16[144,2048]{1,0:T(8,128)(2,1)S(1)}, u32[]{:S(2)}, u32[]{:S(2)}) %collective-permute-start.21) | collective-permute-done | bytes 589856 | tf_op jit(solution)/shard_map/ppermute | solution.py:499
  92.1 0.5 collective-permute-done.18.refs_2_
  92.6 0.5 collective-permute-start.22
  93.1 2.2 %collective-permute-done.22.refs_13_ = bf16[128,2048]{1,0:T(8,128)(2,1)S(1)} collective-permute-done((bf16[128,2048]{1,0:T(8,128)(2,1)S(1)}, bf16[128,2048]{1,0:T(8,128)(2,1)S(1)}, u32[]{:S(2)}, u32[]{:S(2)}) %collective-permute-start.22) | collective-permute-done | bytes 524320 | tf_op jit(solution)/shard_map/ppermute | solution.py:499
  95.3 6.4 %ffn.1 = (bf16[32,640]{1,0:T(8,128)(2,1)S(1)}, bf16[32,640]{1,0:T(8,128)(2,1)S(1)}, bf16[32,640]{1,0:T(8,128)(2,1)S(1)}, bf16[32,640]{1,0:T(8,128)(2,1)S(1)}, f32[32,640]{1,0:T(8,128)S(1)}) custom-call(s32[2]{0:T(128)S(1)} %copy-done.11, f32[2]{0:T(128)S(1)} %copy-done.15, f32[1,2048]{1,0:T(1,128)S(1)} %bitcast.27, ...), custom_call_target="tpu_custom_call" | custom-call | flops 1 | bytes 1 | tf_op jit(solution)/shard_map/ffn/pallas_call | solution.py:766
  101.7 1.0 collective-permute-start.24
  102.8 2.6 %collective-permute-start.25 = (bf16[32,640]{1,0:T(8,128)(2,1)S(1)}, bf16[32,640]{1,0:T(8,128)(2,1)S(1)}, u32[]{:S(2)}, u32[]{:S(2)}) collective-permute-start(bf16[32,640]{1,0:T(8,128)(2,1)S(1)} %get-tuple-element.49), channel_id=1, source_target_pairs={{0,2},{1,3},{2,0},{3,1},{4,6},{5,7},{6,4},{7,5},{8,10},{9,11},{10,... | collective-permute-start | bytes 122888 | tf_op jit(solution)/shard_map/ppermute | solution.py:499
  105.4 0.8 collective-permute-start.26
  106.2 2.2 %collective-permute-done.25.refs_2_ = bf16[32,640]{1,0:T(8,128)(2,1)S(1)} collective-permute-done((bf16[32,640]{1,0:T(8,128)(2,1)S(1)}, bf16[32,640]{1,0:T(8,128)(2,1)S(1)}, u32[]{:S(2)}, u32[]{:S(2)}) %collective-permute-start.25) | collective-permute-done | bytes 40992 | tf_op jit(solution)/shard_map/ppermute | solution.py:499
  108.4 2.8 %collective-permute-done.26.refs_3_ = bf16[32,640]{1,0:T(8,128)(2,1)S(1)} collective-permute-done((bf16[32,640]{1,0:T(8,128)(2,1)S(1)}, bf16[32,640]{1,0:T(8,128)(2,1)S(1)}, u32[]{:S(2)}, u32[]{:S(2)}) %collective-permute-start.26) | collective-permute-done | bytes 40992 | tf_op jit(solution)/shard_map/ppermute | solution.py:499
  111.2 7.5 %back.1 = (bf16[8,1152]{1,0:T(8,128)(2,1)S(1)}, bf16[8,1152]{1,0:T(8,128)(2,1)S(1)}, bf16[8,1152]{1,0:T(8,128)(2,1)S(1)}, bf16[8,1152]{1,0:T(8,128)(2,1)S(1)}, f...) custom-call(s32[2]{0:T(128)S(1)} %copy-done.11, f32[32,640]{1,0:T(8,128)S(1)} %get-tuple-element.46.mid_ref, ...), custom_call_target="tpu_custom_call" | custom-call | flops 1 | bytes 1 | tf_op jit(solution)/shard_map/back/pallas_call | solution.py:787
  118.7 1.4 %collective-permute-start.28 = (bf16[8,1152]{1,0:T(8,128)(2,1)S(1)}, bf16[8,1152]{1,0:T(8,128)(2,1)S(1)}, u32[]{:S(2)}, u32[]{:S(2)}) collective-permute-start(bf16[8,1152]{1,0:T(8,128)(2,1)S(1)} %get-tuple-element.56), channel_id=1, source_target_pairs={{0,2},{1,3},{2,0},{3,1},{4,6},{5,7},{6,4},{7,5},{8,10},{9,11},{10,... | collective-permute-start | bytes 55304 | tf_op jit(solution)/shard_map/ppermute | solution.py:499
  120.1 3.0 %collective-permute-start.29 = (bf16[8,1152]{1,0:T(8,128)(2,1)S(1)}, bf16[8,1152]{1,0:T(8,128)(2,1)S(1)}, u32[]{:S(2)}, u32[]{:S(2)}) collective-permute-start(bf16[8,1152]{1,0:T(8,128)(2,1)S(1)} %get-tuple-element.57), channel_id=1, source_target_pairs={{0,3},{1,2},{2,1},{3,0},{4,7},{5,6},{6,5},{7,4},{8,11},{9,10},{10,... | collective-permute-start | bytes 55304 | tf_op jit(solution)/shard_map/ppermute | solution.py:499
  123.1 0.1 copy.21
  123.2 0.6 reshape.62
  123.9 1.8 %collective-permute-done.29.refs_3_ = bf16[8,1152]{1,0:T(8,128)(2,1)S(1)} collective-permute-done((bf16[8,1152]{1,0:T(8,128)(2,1)S(1)}, bf16[8,1152]{1,0:T(8,128)(2,1)S(1)}, u32[]{:S(2)}, u32[]{:S(2)}) %collective-permute-start.29) | collective-permute-done | bytes 18464 | tf_op jit(solution)/shard_map/ppermute | solution.py:499
  125.7 0.7 finish.1.refs_0_
  126.4 2.3 %collective-permute-start.32 = (f32[8,1024]{1,0:T(8,128)S(1)}, f32[8,1024]{1,0:T(8,128)S(1)}, u32[]{:S(2)}, u32[]{:S(2)}) collective-permute-start(f32[8,1024]{1,0:T(8,128)S(1)} %finish.1.refs_0_), channel_id=1, source_target_pairs={{0,24},{4,28},{8,16},{12,20},{16,8},{20,12},{24,0},{28,4},{1,25},{... | collective-permute-start | bytes 98312 | tf_op jit(solution)/shard_map/ppermute | solution.py:499
  128.7 0.7 collective-permute-start.31
  129.4 0.5 collective-permute-start.30
  129.9 1.3 collective-permute-done.32.refs_3_
  131.2 1.3 collective-permute-done.31.refs_2_
  132.6 0.7 collective-permute-done.30.refs_1_
  133.3 0.5 collective-permute-done.35.refs_6_
  133.8 0.7 collective-permute-done.34.refs_5_
  134.5 1.4 %spread.1 = bf16[768,1024]{1,0:T(8,128)(2,1)} custom-call(bf16[768,64]{1,0:T(8,128)(2,1)S(1)} %copy-done.4, f32[8,1024]{1,0:T(8,128)S(1)} %finish.1.refs_0_, f32[8,1024]{1,0:T(8,128)S(1)} %collective-permute-done.30.refs_1_, f32[8,1024]{1,0:T(8,128)S(1)} %collective-permute-done.31.refs_2_, f32[8,1024]{1,0:T(8,128)S(1)} %collective-permute-done.32.refs_3_, ...), custom_call_target="tpu_custom_call" | custom-call | flops 1 | bytes 1 | tf_op jit(solution)/shard_map/spread/pallas_call | solution.py:817
  (86 shorter events, 0.6 us)
Async XLA Ops:
  0.6 21.6 %collective-permute-start.1 = (bf16[3,256,512]{2,1,0:T(8,128)(2,1)}, bf16[3,256,512]{2,1,0:T(8,128)(2,1)S(1)}, u32[]{:S(2)}, u32[]{:S(2)}) collective-permute-start(bf16[3,256,512]{2,1,0:T(8,128)(2,1)} %refs_5_.1), channel_id=1, source_target_pairs={{0,16},{4,20},{8,24},{12,28},{16,0},{20,4},{24,8},{28,12},{1,17},{... | collective-permute-start | bytes 2359304 | tf_op jit(solution)/shard_map/ppermute | solution.py:499
  3.7 20.7 %collective-permute-start = (bf16[3,256,512]{2,1,0:T(8,128)(2,1)}, bf16[3,256,512]{2,1,0:T(8,128)(2,1)S(1)}, u32[]{:S(2)}, u32[]{:S(2)}) collective-permute-start(bf16[3,256,512]{2,1,0:T(8,128)(2,1)} %refs_5_.1), channel_id=1, source_target_pairs={{0,8},{4,12},{8,0},{12,4},{16,24},{20,28},{24,16},{28,20},{1,9},{5... | collective-permute-start | bytes 2359304 | tf_op jit(solution)/shard_map/ppermute | solution.py:499
  5.2 25.1 %collective-permute-start.2 = (bf16[3,256,512]{2,1,0:T(8,128)(2,1)}, bf16[3,256,512]{2,1,0:T(8,128)(2,1)S(1)}, u32[]{:S(2)}, u32[]{:S(2)}) collective-permute-start(bf16[3,256,512]{2,1,0:T(8,128)(2,1)} %refs_5_.1), channel_id=1, source_target_pairs={{0,4},{4,0},{8,12},{12,8},{16,20},{20,16},{24,28},{28,24},{1,5},{5... | collective-permute-start | bytes 2359304 | tf_op jit(solution)/shard_map/ppermute | solution.py:499
  5.2 5.8 %copy-start.10 = (s32[2]{0:T(128)}, s32[2]{0:T(128)S(1)}, u32[]{:S(2)}) copy-start(s32[2]{0:T(128)S(1)} %pad_add_fusion.where_ref) | copy-start | bytes 28
  5.2 1.4 %copy-start.3 = (bf16[768,1024]{1,0:T(8,128)(2,1)S(1)}, bf16[768,1024]{1,0:T(8,128)(2,1)}, u32[]{:S(2)}) copy-start(bf16[768,1024]{1,0:T(8,128)(2,1)} %x_hbm.1) | copy-start | bytes 4718596
  6.6 0.7 copy-start.8
  11.1 4.5 %copy-start.19 = (s32[24]{0:T(128)S(1)}, s32[24]{0:T(128)}, u32[]{:S(2)}) copy-start(s32[24]{0:T(128)} %patient_ref.1) | copy-start | bytes 292
  11.1 4.5 %copy-start.20 = (s32[24]{0:T(128)S(1)}, s32[24]{0:T(128)}, u32[]{:S(2)}) copy-start(s32[24]{0:T(128)} %treat_ref.1) | copy-start | bytes 292
  11.1 4.5 %copy-start.21 = (f32[24]{0:T(128)S(1)}, f32[24]{0:T(128)}, u32[]{:S(2)}) copy-start(f32[24]{0:T(128)} %target_ref.1) | copy-start | bytes 292
  11.1 5.1 %copy-start.24 = (s32[8]{0:T(128)S(1)}, s32[8]{0:T(128)}, u32[]{:S(2)}) copy-start(s32[8]{0:T(128)} %constant.26.clone) | copy-start | bytes 100
  11.1 14.3 %copy-start.9 = (s32[768]{0:T(1024)S(1)}, s32[768]{0:T(1024)}, u32[]{:S(2)}) copy-start(s32[768]{0:T(1024)} %param.18) | copy-start | bytes 9220
  11.1 39.3 %all-to-all-start = ((bf16[8,96,1152]{2,1,0:T(8,128)(2,1)}), bf16[8,96,1152]{2,1,0:T(8,128)(2,1)}, u32[]{:S(2)}, u32[]{:S(2)}) async-start(bf16[8,96,1152]{2,1,0:T(8,128)(2,1)} %bitcast.6), calls=%async_computation | async-start | bytes 3538944 | tf_op jit(solution)/shard_map/all_to_all | solution.py:648
  16.2 10.6 %copy-start.13 = (f32[8,32]{1,0:T(8,128)}, f32[8,32]{1,0:T(8,128)S(1)}, u32[]{:S(2)}) copy-start(f32[8,32]{1,0:T(8,128)S(1)} %get-tuple-element.31.refs_6_) | copy-start | bytes 3076
  22.2 8.0 %collective-permute-start.4 = (bf16[3,256,512]{2,1,0:T(8,128)(2,1)S(1)}, bf16[3,256,512]{2,1,0:T(8,128)(2,1)}, u32[]{:S(2)}, u32[]{:S(2)}) collective-permute-start(bf16[3,256,512]{2,1,0:T(8,128)(2,1)S(1)} %collective-permute-done.1.high_ref.refs_9_.refs_7_), channel_id=1, source_target_pairs={{0,4},{4,0},{8,12},{12,8},{16,20},{20,16},{24,28},{28,24},{1,5},{5... | collective-permute-start | bytes 2359304 | tf_op jit(solution)/shard_map/ppermute | solution.py:499
  24.3 6.0 %collective-permute-start.3 = (bf16[3,256,512]{2,1,0:T(8,128)(2,1)S(1)}, bf16[3,256,512]{2,1,0:T(8,128)(2,1)S(1)}, u32[]{:S(2)}, u32[]{:S(2)}) collective-permute-start(bf16[3,256,512]{2,1,0:T(8,128)(2,1)S(1)} %collective-permute-done.low_ref.refs_8_.refs_6_), channel_id=1, source_target_pairs={{0,4},{4,0},{8,12},{12,8},{16,20},{20,16},{24,28},{28,24},{1,5},{5... | collective-permute-start | bytes 2359304 | tf_op jit(solution)/shard_map/ppermute | solution.py:499
  24.5 5.8 %copy-start.17 = (bf16[2048,256]{1,0:T(8,128)(2,1)S(1)}, bf16[2048,256]{1,0:T(8,128)(2,1)}, u32[]{:S(2)}) copy-start(bf16[2048,256]{1,0:T(8,128)(2,1)} %weight_ref.1) | copy-start | bytes 3145732
  26.8 22.0 %collective-permute-start.6 = (bf16[3,128,512]{2,1,0:T(8,128)(2,1)S(1)}, bf16[3,128,512]{2,1,0:T(8,128)(2,1)S(1)}, u32[]{:S(2)}, u32[]{:S(2)}) collective-permute-start(bf16[3,128,512]{2,1,0:T(8,128)(2,1)S(1)} %get-tuple-element.32), channel_id=1, source_target_pairs={{0,16},{4,20},{8,24},{12,28},{16,0},{20,4},{24,8},{28,12},{1,17},{... | collective-permute-start | bytes 1179656 | tf_op jit(solution)/shard_map/ppermute | solution.py:499
  27.4 23.1 %collective-permute-start.8 = (bf16[3,128,512]{2,1,0:T(8,128)(2,1)S(1)}, bf16[3,128,512]{2,1,0:T(8,128)(2,1)}, u32[]{:S(2)}, u32[]{:S(2)}) collective-permute-start(bf16[3,128,512]{2,1,0:T(8,128)(2,1)S(1)} %get-tuple-element.33), channel_id=1, source_target_pairs={{0,8},{4,12},{8,0},{12,4},{16,24},{20,28},{24,16},{28,20},{1,9},{5... | collective-permute-start | bytes 1179656 | tf_op jit(solution)/shard_map/ppermute | solution.py:499
  30.3 50.2 %copy-start.2 = (bf16[3,256,512]{2,1,0:T(8,128)(2,1)}, bf16[3,256,512]{2,1,0:T(8,128)(2,1)S(1)}, u32[]{:S(2)}) copy-start(bf16[3,256,512]{2,1,0:T(8,128)(2,1)S(1)} %collective-permute-done.3.refs_13_.refs_11_) | copy-start | bytes 2359300
  30.3 1.5 %copy-start.18 = (bf16[256,2048]{1,0:T(8,128)(2,1)S(1)}, bf16[256,2048]{1,0:T(8,128)(2,1)}, u32[]{:S(2)}) copy-start(bf16[256,2048]{1,0:T(8,128)(2,1)} %ffn_ref) | copy-start | bytes 3145732
  33.2 21.7 %collective-permute-start.5 = (bf16[272,2048]{1,0:T(8,128)(2,1)}, bf16[272,2048]{1,0:T(8,128)(2,1)}, u32[]{:S(2)}, u32[]{:S(2)}) collective-permute-start(bf16[272,2048]{1,0:T(8,128)(2,1)} %fold.1.refs_5_), channel_id=1, source_target_pairs={{0,4},{4,0},{8,12},{12,8},{16,20},{20,16},{24,28},{28,24},{1,5},{5... | collective-permute-start | bytes 3342344 | tf_op jit(solution)/shard_map/ppermute | solution.py:499
  50.5 25.3 %collective-permute-start.15 = (bf16[272,2048]{1,0:T(8,128)(2,1)}, bf16[272,2048]{1,0:T(8,128)(2,1)S(1)}, u32[]{:S(2)}, u32[]{:S(2)}) collective-permute-start(bf16[272,2048]{1,0:T(8,128)(2,1)} %fold.1.refs_5_), channel_id=1, source_target_pairs={{0,16},{4,20},{8,24},{12,28},{16,0},{20,4},{24,8},{28,12},{1,17},{... | collective-permute-start | bytes 3342344 | tf_op jit(solution)/shard_map/ppermute | solution.py:499
  50.8 25.4 %collective-permute-start.10 = (bf16[272,2048]{1,0:T(8,128)(2,1)}, bf16[272,2048]{1,0:T(8,128)(2,1)S(1)}, u32[]{:S(2)}, u32[]{:S(2)}) collective-permute-start(bf16[272,2048]{1,0:T(8,128)(2,1)} %fold.1.refs_5_), channel_id=1, source_target_pairs={{0,8},{4,12},{8,0},{12,4},{16,24},{20,28},{24,16},{28,20},{1,9},{5... | collective-permute-start | bytes 3342344 | tf_op jit(solution)/shard_map/ppermute | solution.py:499
  52.5 2.3 %collective-permute-start.7 = (bf16[3,128,512]{2,1,0:T(8,128)(2,1)S(1)}, bf16[3,128,512]{2,1,0:T(8,128)(2,1)S(1)}, u32[]{:S(2)}, u32[]{:S(2)}) collective-permute-start(bf16[3,128,512]{2,1,0:T(8,128)(2,1)S(1)} %collective-permute-done.6.refs_10_.refs_8_), channel_id=1, source_target_pairs={{0,4},{4,0},{8,12},{12,8},{16,20},{20,16},{24,28},{28,24},{1,5},{5... | collective-permute-start | bytes 1179656 | tf_op jit(solution)/shard_map/ppermute | solution.py:499
  52.5 2.5 %collective-permute-start.9 = (bf16[3,128,512]{2,1,0:T(8,128)(2,1)}, bf16[3,128,512]{2,1,0:T(8,128)(2,1)S(1)}, u32[]{:S(2)}, u32[]{:S(2)}) collective-permute-start(bf16[3,128,512]{2,1,0:T(8,128)(2,1)} %collective-permute-done.8.refs_11_.refs_9_), channel_id=1, source_target_pairs={{0,4},{4,0},{8,12},{12,8},{16,20},{20,16},{24,28},{28,24},{1,5},{5... | collective-permute-start | bytes 1179656 | tf_op jit(solution)/shard_map/ppermute | solution.py:499
  55.0 0.7 copy-start.12
  67.6 12.9 %copy-start.1 = (bf16[3,256,512]{2,1,0:T(8,128)(2,1)S(1)}, bf16[3,256,512]{2,1,0:T(8,128)(2,1)}, u32[]{:S(2)}) copy-start(bf16[3,256,512]{2,1,0:T(8,128)(2,1)} %refs_5_.1) | copy-start | bytes 2359300
  67.6 12.9 %copy-start.6 = (f32[2048]{0:T(1024)S(1)}, f32[2048]{0:T(1024)}, u32[]{:S(2)}) copy-start(f32[2048]{0:T(1024)} %param.26) | copy-start | bytes 24580
  67.6 12.9 %copy-start.11 = (s32[2]{0:T(128)S(1)}, s32[2]{0:T(128)}, u32[]{:S(2)}) copy-start(s32[2]{0:T(128)} %copy-done.10) | copy-start | bytes 28
  67.6 12.9 %copy-start.14 = (f32[8,32]{1,0:T(8,128)S(1)}, f32[8,32]{1,0:T(8,128)}, u32[]{:S(2)}) copy-start(f32[8,32]{1,0:T(8,128)} %copy-done.13) | copy-start | bytes 3076
  67.7 8.1 %collective-permute-start.13 = (bf16[8,2048]{1,0:T(8,128)(2,1)S(1)}, bf16[8,2048]{1,0:T(8,128)(2,1)S(1)}, u32[]{:S(2)}, u32[]{:S(2)}) collective-permute-start(bf16[8,2048]{1,0:T(8,128)(2,1)S(1)} %encode.1.refs_0_), channel_id=1, source_target_pairs={{0,3},{1,2},{2,1},{3,0},{4,7},{5,6},{6,5},{7,4},{8,11},{9,10},{10,... | collective-permute-start | bytes 98312 | tf_op jit(solution)/shard_map/ppermute | solution.py:499
  71.3 4.8 %collective-permute-start.12 = (bf16[8,2048]{1,0:T(8,128)(2,1)S(1)}, bf16[8,2048]{1,0:T(8,128)(2,1)S(1)}, u32[]{:S(2)}, u32[]{:S(2)}) collective-permute-start(bf16[8,2048]{1,0:T(8,128)(2,1)S(1)} %encode.1.refs_0_), channel_id=1, source_target_pairs={{0,2},{1,3},{2,0},{3,1},{4,6},{5,7},{6,4},{7,5},{8,10},{9,11},{10,... | collective-permute-start | bytes 98312 | tf_op jit(solution)/shard_map/ppermute | solution.py:499
  71.3 4.8 %collective-permute-start.11 = (bf16[8,2048]{1,0:T(8,128)(2,1)S(1)}, bf16[8,2048]{1,0:T(8,128)(2,1)S(1)}, u32[]{:S(2)}, u32[]{:S(2)}) collective-permute-start(bf16[8,2048]{1,0:T(8,128)(2,1)S(1)} %encode.1.refs_0_), channel_id=1, source_target_pairs={{0,1},{1,0},{2,3},{3,2},{4,5},{5,4},{6,7},{7,6},{8,9},{9,8},{10,11... | collective-permute-start | bytes 98312 | tf_op jit(solution)/shard_map/ppermute | solution.py:499
  75.8 8.5 %copy-start = (bf16[272,2048]{1,0:T(8,128)(2,1)}, bf16[272,2048]{1,0:T(8,128)(2,1)S(1)}, u32[]{:S(2)}) copy-start(bf16[272,2048]{1,0:T(8,128)(2,1)S(1)} %collective-permute-done.15.high_ref.refs_7_) | copy-start | bytes 3342340
  76.1 3.0 %collective-permute-start.16 = (bf16[272,2048]{1,0:T(8,128)(2,1)S(1)}, bf16[272,2048]{1,0:T(8,128)(2,1)S(1)}, u32[]{:S(2)}, u32[]{:S(2)}) collective-permute-start(bf16[272,2048]{1,0:T(8,128)(2,1)S(1)} %collective-permute-done.15.high_ref.refs_7_), channel_id=1, source_target_pairs={{0,4},{4,0},{8,12},{12,8},{16,20},{20,16},{24,28},{28,24},{1,5},{5... | collective-permute-start | bytes 3342344 | tf_op jit(solution)/shard_map/ppermute | solution.py:499
  76.2 4.3 %collective-permute-start.14 = (bf16[272,2048]{1,0:T(8,128)(2,1)S(1)}, bf16[272,2048]{1,0:T(8,128)(2,1)S(1)}, u32[]{:S(2)}, u32[]{:S(2)}) collective-permute-start(bf16[272,2048]{1,0:T(8,128)(2,1)S(1)} %collective-permute-done.10.low_ref.refs_6_), channel_id=1, source_target_pairs={{0,4},{4,0},{8,12},{12,8},{16,20},{20,16},{24,28},{28,24},{1,5},{5... | collective-permute-start | bytes 3342344 | tf_op jit(solution)/shard_map/ppermute | solution.py:499
  76.7 15.4 %collective-permute-start.21 = (bf16[144,2048]{1,0:T(8,128)(2,1)S(1)}, bf16[144,2048]{1,0:T(8,128)(2,1)S(1)}, u32[]{:S(2)}, u32[]{:S(2)}) collective-permute-start(bf16[144,2048]{1,0:T(8,128)(2,1)S(1)} %get-tuple-element.44), channel_id=1, source_target_pairs={{0,8},{4,12},{8,0},{12,4},{16,24},{20,28},{24,16},{28,20},{1,9},{5... | collective-permute-start | bytes 1769480 | tf_op jit(solution)/shard_map/ppermute | solution.py:499
  78.0 14.6 %collective-permute-start.20 = (bf16[128,2048]{1,0:T(8,128)(2,1)S(1)}, bf16[128,2048]{1,0:T(8,128)(2,1)S(1)}, u32[]{:S(2)}, u32[]{:S(2)}) collective-permute-start(bf16[128,2048]{1,0:T(8,128)(2,1)S(1)} %get-tuple-element.42), channel_id=1, source_target_pairs={{0,16},{4,20},{8,24},{12,28},{16,0},{20,4},{24,8},{28,12},{1,17},{... | collective-permute-start | bytes 1572872 | tf_op jit(solution)/shard_map/ppermute | solution.py:499
  79.2 5.2 %copy-start.22 = (bf16[272,2048]{1,0:T(8,128)(2,1)}, bf16[272,2048]{1,0:T(8,128)(2,1)S(1)}, u32[]{:S(2)}) copy-start(bf16[272,2048]{1,0:T(8,128)(2,1)S(1)} %collective-permute-done.16.refs_12_) | copy-start | bytes 3342340
  80.5 3.9 %copy-start.23 = (bf16[272,2048]{1,0:T(8,128)(2,1)}, bf16[272,2048]{1,0:T(8,128)(2,1)S(1)}, u32[]{:S(2)}) copy-start(bf16[272,2048]{1,0:T(8,128)(2,1)S(1)} %collective-permute-done.14.refs_11_) | copy-start | bytes 3342340
  80.5 14.8 %copy-start.5 = (f32[2048,2]{0,1:T(2,128)S(1)}, f32[2048,2]{0,1:T(2,128)}, u32[]{:S(2)}) copy-start(f32[2048,2]{0,1:T(2,128)} %param.31) | copy-start | bytes 49156
  80.5 14.8 %copy-start.7 = (f32[2048]{0:T(1024)S(1)}, f32[2048]{0:T(1024)}, u32[]{:S(2)}) copy-start(f32[2048]{0:T(1024)} %param.28) | copy-start | bytes 24580
  80.5 14.8 %copy-start.15 = (f32[2]{0:T(128)S(1)}, f32[2]{0:T(128)}, u32[]{:S(2)}) copy-start(f32[2]{0:T(128)} %bias_ref.1) | copy-start | bytes 28
  84.4 7.7 %collective-permute-start.19 = (bf16[32,512]{1,0:T(8,128)(2,1)S(1)}, bf16[32,512]{1,0:T(8,128)(2,1)S(1)}, u32[]{:S(2)}, u32[]{:S(2)}) collective-permute-start(bf16[32,512]{1,0:T(8,128)(2,1)S(1)} %get-tuple-element.40.refs_0_), channel_id=1, source_target_pairs={{0,3},{1,2},{2,1},{3,0},{4,7},{5,6},{6,5},{7,4},{8,11},{9,10},{10,... | collective-permute-start | bytes 98312 | tf_op jit(solution)/shard_map/ppermute | solution.py:499
  87.8 4.8 %collective-permute-start.18 = (bf16[32,512]{1,0:T(8,128)(2,1)S(1)}, bf16[32,512]{1,0:T(8,128)(2,1)S(1)}, u32[]{:S(2)}, u32[]{:S(2)}) collective-permute-start(bf16[32,512]{1,0:T(8,128)(2,1)S(1)} %get-tuple-element.40.refs_0_), channel_id=1, source_target_pairs={{0,2},{1,3},{2,0},{3,1},{4,6},{5,7},{6,4},{7,5},{8,10},{9,11},{10,... | collective-permute-start | bytes 98312 | tf_op jit(solution)/shard_map/ppermute | solution.py:499
  87.8 4.8 %collective-permute-start.17 = (bf16[32,512]{1,0:T(8,128)(2,1)S(1)}, bf16[32,512]{1,0:T(8,128)(2,1)S(1)}, u32[]{:S(2)}, u32[]{:S(2)}) collective-permute-start(bf16[32,512]{1,0:T(8,128)(2,1)S(1)} %get-tuple-element.40.refs_0_), channel_id=1, source_target_pairs={{0,1},{1,0},{2,3},{3,2},{4,5},{5,4},{6,7},{7,6},{8,9},{9,8},{10,11... | collective-permute-start | bytes 98312 | tf_op jit(solution)/shard_map/ppermute | solution.py:499
  92.6 2.8 %collective-permute-start.23 = (bf16[144,2048]{1,0:T(8,128)(2,1)S(1)}, bf16[144,2048]{1,0:T(8,128)(2,1)S(1)}, u32[]{:S(2)}, u32[]{:S(2)}) collective-permute-start(bf16[144,2048]{1,0:T(8,128)(2,1)S(1)} %collective-permute-done.21.refs_9_), channel_id=1, source_target_pairs={{0,4},{4,0},{8,12},{12,8},{16,20},{20,16},{24,28},{28,24},{1,5},{5... | collective-permute-start | bytes 1769480 | tf_op jit(solution)/shard_map/ppermute | solution.py:499
  92.6 2.7 %collective-permute-start.22 = (bf16[128,2048]{1,0:T(8,128)(2,1)S(1)}, bf16[128,2048]{1,0:T(8,128)(2,1)S(1)}, u32[]{:S(2)}, u32[]{:S(2)}) collective-permute-start(bf16[128,2048]{1,0:T(8,128)(2,1)S(1)} %collective-permute-done.20.refs_8_), channel_id=1, source_target_pairs={{0,4},{4,0},{8,12},{12,8},{16,20},{20,16},{24,28},{28,24},{1,5},{5... | collective-permute-start | bytes 1572872 | tf_op jit(solution)/shard_map/ppermute | solution.py:499
  101.7 4.5 %collective-permute-start.24 = (bf16[32,640]{1,0:T(8,128)(2,1)S(1)}, bf16[32,640]{1,0:T(8,128)(2,1)S(1)}, u32[]{:S(2)}, u32[]{:S(2)}) collective-permute-start(bf16[32,640]{1,0:T(8,128)(2,1)S(1)} %get-tuple-element.48), channel_id=1, source_target_pairs={{0,1},{1,0},{2,3},{3,2},{4,5},{5,4},{6,7},{7,6},{8,9},{9,8},{10,11... | collective-permute-start | bytes 122888 | tf_op jit(solution)/shard_map/ppermute | solution.py:499
  102.8 5.6 %collective-permute-start.25 = (bf16[32,640]{1,0:T(8,128)(2,1)S(1)}, bf16[32,640]{1,0:T(8,128)(2,1)S(1)}, u32[]{:S(2)}, u32[]{:S(2)}) collective-permute-start(bf16[32,640]{1,0:T(8,128)(2,1)S(1)} %get-tuple-element.49), channel_id=1, source_target_pairs={{0,2},{1,3},{2,0},{3,1},{4,6},{5,7},{6,4},{7,5},{8,10},{9,11},{10,... | collective-permute-start | bytes 122888 | tf_op jit(solution)/shard_map/ppermute | solution.py:499
  105.4 5.8 %collective-permute-start.26 = (bf16[32,640]{1,0:T(8,128)(2,1)S(1)}, bf16[32,640]{1,0:T(8,128)(2,1)S(1)}, u32[]{:S(2)}, u32[]{:S(2)}) collective-permute-start(bf16[32,640]{1,0:T(8,128)(2,1)S(1)} %get-tuple-element.50), channel_id=1, source_target_pairs={{0,3},{1,2},{2,1},{3,0},{4,7},{5,6},{6,5},{7,4},{8,11},{9,10},{10,... | collective-permute-start | bytes 122888 | tf_op jit(solution)/shard_map/ppermute | solution.py:499
  111.2 14.5 %copy-start.16 = (s32[6]{0:T(128)S(1)}, s32[6]{0:T(128)}, u32[]{:S(2)}) copy-start(s32[6]{0:T(128)} %count_ref.1) | copy-start | bytes 76
  111.2 23.3 %copy-start.4 = (bf16[768,64]{1,0:T(8,128)(2,1)S(1)}, bf16[768,64]{1,0:T(8,128)(2,1)}, u32[]{:S(2)}) copy-start(bf16[768,64]{1,0:T(8,128)(2,1)} %compare_convert_fusion.pick) | copy-start | bytes 294916
  118.7 5.2 %collective-permute-start.27 = (bf16[8,1152]{1,0:T(8,128)(2,1)S(1)}, bf16[8,1152]{1,0:T(8,128)(2,1)S(1)}, u32[]{:S(2)}, u32[]{:S(2)}) collective-permute-start(bf16[8,1152]{1,0:T(8,128)(2,1)S(1)} %get-tuple-element.55), channel_id=1, source_target_pairs={{0,1},{1,0},{2,3},{3,2},{4,5},{5,4},{6,7},{7,6},{8,9},{9,8},{10,11... | collective-permute-start | bytes 55304 | tf_op jit(solution)/shard_map/ppermute | solution.py:499
  118.7 5.1 %collective-permute-start.28 = (bf16[8,1152]{1,0:T(8,128)(2,1)S(1)}, bf16[8,1152]{1,0:T(8,128)(2,1)S(1)}, u32[]{:S(2)}, u32[]{:S(2)}) collective-permute-start(bf16[8,1152]{1,0:T(8,128)(2,1)S(1)} %get-tuple-element.56), channel_id=1, source_target_pairs={{0,2},{1,3},{2,0},{3,1},{4,6},{5,7},{6,4},{7,5},{8,10},{9,11},{10,... | collective-permute-start | bytes 55304 | tf_op jit(solution)/shard_map/ppermute | solution.py:499
  120.1 5.6 %collective-permute-start.29 = (bf16[8,1152]{1,0:T(8,128)(2,1)S(1)}, bf16[8,1152]{1,0:T(8,128)(2,1)S(1)}, u32[]{:S(2)}, u32[]{:S(2)}) collective-permute-start(bf16[8,1152]{1,0:T(8,128)(2,1)S(1)} %get-tuple-element.57), channel_id=1, source_target_pairs={{0,3},{1,2},{2,1},{3,0},{4,7},{5,6},{6,5},{7,4},{8,11},{9,10},{10,... | collective-permute-start | bytes 55304 | tf_op jit(solution)/shard_map/ppermute | solution.py:499
  126.4 4.8 %collective-permute-start.32 = (f32[8,1024]{1,0:T(8,128)S(1)}, f32[8,1024]{1,0:T(8,128)S(1)}, u32[]{:S(2)}, u32[]{:S(2)}) collective-permute-start(f32[8,1024]{1,0:T(8,128)S(1)} %finish.1.refs_0_), channel_id=1, source_target_pairs={{0,24},{4,28},{8,16},{12,20},{16,8},{20,12},{24,0},{28,4},{1,25},{... | collective-permute-start | bytes 98312 | tf_op jit(solution)/shard_map/ppermute | solution.py:499
  128.7 3.9 %collective-permute-start.31 = (f32[8,1024]{1,0:T(8,128)S(1)}, f32[8,1024]{1,0:T(8,128)S(1)}, u32[]{:S(2)}, u32[]{:S(2)}) collective-permute-start(f32[8,1024]{1,0:T(8,128)S(1)} %finish.1.refs_0_), channel_id=1, source_target_pairs={{0,16},{4,20},{8,24},{12,28},{16,0},{20,4},{24,8},{28,12},{1,17},{... | collective-permute-start | bytes 98312 | tf_op jit(solution)/shard_map/ppermute | solution.py:499
  129.4 3.9 %collective-permute-start.30 = (f32[8,1024]{1,0:T(8,128)S(1)}, f32[8,1024]{1,0:T(8,128)S(1)}, u32[]{:S(2)}, u32[]{:S(2)}) collective-permute-start(f32[8,1024]{1,0:T(8,128)S(1)} %finish.1.refs_0_), channel_id=1, source_target_pairs={{0,8},{4,12},{8,0},{12,4},{16,24},{20,28},{24,16},{28,20},{1,9},{5... | collective-permute-start | bytes 98312 | tf_op jit(solution)/shard_map/ppermute | solution.py:499
  129.9 3.4 %collective-permute-start.33 = (f32[8,1024]{1,0:T(8,128)S(1)}, f32[8,1024]{1,0:T(8,128)S(1)}, u32[]{:S(2)}, u32[]{:S(2)}) collective-permute-start(f32[8,1024]{1,0:T(8,128)S(1)} %finish.1.refs_0_), channel_id=1, source_target_pairs={{0,4},{4,0},{8,12},{12,8},{16,20},{20,16},{24,28},{28,24},{1,5},{5... | collective-permute-start | bytes 98312 | tf_op jit(solution)/shard_map/ppermute | solution.py:499
  131.2 2.1 %collective-permute-start.36 = (f32[8,1024]{1,0:T(8,128)S(1)}, f32[8,1024]{1,0:T(8,128)S(1)}, u32[]{:S(2)}, u32[]{:S(2)}) collective-permute-start(f32[8,1024]{1,0:T(8,128)S(1)} %collective-permute-done.32.refs_3_), channel_id=1, source_target_pairs={{0,4},{4,0},{8,12},{12,8},{16,20},{20,16},{24,28},{28,24},{1,5},{5... | collective-permute-start | bytes 98312 | tf_op jit(solution)/shard_map/ppermute | solution.py:499
  132.6 1.2 collective-permute-start.35
  133.3 1.2 collective-permute-start.34
